TPU v7x, 32 devices: a whole 2x2x4 slice. The times are simulated.
32 devices in a mesh: group: 4 (over z), within: 8 (over y, x, core).
Axes of the slice: x: 2, y: 2, z: 4, core: 2. Of those that a mesh axis runs over, the one named last changes fastest.
Arguments:
- vectors: bfloat16 [16384, 768], P(('group', 'within')), may hold values from -6 to 6
- centroids: float32 [2048, 768], P(('group', 'within')), may hold values from -6 to 6
- list_ids: int32 [16384], P(('group', 'within')), may hold values from 0 to 2047, as said below
- codes: int32 [16384, 96], P(('group', 'within')), may hold values from 0 to 255, as said below
- rotation: float32 [768, 768], replicated, may hold values from -0.21875 to 0.21875
Outputs:
- rotated_out: bfloat16 [16384, 768], P(('group', 'within'))
- codebooks: float32 [96, 2048], P('within')
Inputs may be any that keep to these rules, and one draw needn't show every extreme that they name: `list_ids`: the rows of the d-th block of 512 rows name only lists d * 64 to (d + 1) * 64 - 1, each of them at least once. `codes`: in subspace m, the rows of the d-th block of 512 rows name codeword 256/2 + (d + m) mod (128) in 2 to 5 consecutive rows (counted round the block) and codewords below 128 elsewhere.
All inputs are finite; a program needn't handle non-finite values.
Results may differ from a plain program's by a relative error of at most 0.012.
Values may be sent and summed in bfloat16 or wider, within the bound.
No kernel may reach another device: no remote copies, remote signals or barrier semaphores. Data moves between devices by JAX's collectives and lax.ppermute only.
A program may use at most 64 MiB of HBM per device.

v0:
```python
import math

import jax
import jax.numpy as jnp
from jax import lax
from jax.sharding import PartitionSpec as P

K = 256
ALTS = 2
NS_STEPS = 2


exact_mode = lax.Precision.HIGHEST
epsilon = 1e-06


def block_rows(row_count):
    return math.gcd(row_count, 256)


def code_table(codes_block):
    levels = jnp.arange(K, dtype=jnp.int32)
    return (codes_block[:, :, None] == levels[None, None, :]).astype(jnp.bfloat16)


def code_counts_local(codes):
    row_count, subspaces = codes.shape
    step_rows = block_rows(row_count)
    blocked = codes.reshape(row_count // step_rows, step_rows, subspaces)

    def code_add_block(total, codes_block):
        return (total + jnp.sum(code_table(codes_block).astype(jnp.float32), axis=0), None)

    total, unused = lax.scan(code_add_block, jnp.zeros((subspaces, K), jnp.float32), blocked)
    return total


def word_sums(codes, rotated, extent):
    row_count = codes.shape[0]
    sub_width = rotated.shape[1] // codes.shape[1]
    step_rows = block_rows(row_count)
    picked = codes
    values = rotated
    picked = picked.reshape(row_count // step_rows, step_rows, extent)
    values = values.reshape(row_count // step_rows, step_rows, extent, sub_width)

    def word_add_block(total, pieces):
        codes_block, value_block = pieces
        table = code_table(codes_block)
        return (
            total
            + jnp.einsum("rmk,rmj->mkj", table, value_block, preferred_element_type=jnp.float32),
            None,
        )

    total, unused = lax.scan(
        word_add_block, jnp.zeros((extent, K, sub_width), jnp.float32), (picked, values)
    )
    return total.reshape(extent, K * sub_width)


def rebuild_rows(codes, book_table):
    row_count, subspaces = codes.shape
    sub_width = book_table.shape[1] // K
    step_rows = block_rows(row_count)
    book = book_table.reshape(subspaces, K, sub_width)
    blocked = codes.reshape(row_count // step_rows, step_rows, subspaces)

    def one_block(carry, codes_block):
        table = code_table(codes_block)
        rows_out = jnp.einsum("rmk,mkj->rmj", table, book, preferred_element_type=jnp.float32)
        return (carry, rows_out.astype(jnp.bfloat16).reshape(step_rows, subspaces * sub_width))

    unused, stacked = lax.scan(one_block, jnp.zeros((), jnp.float32), blocked)
    return stacked.reshape(row_count, subspaces * sub_width)


def polar_factor(cross):
    gram_matrix = jnp.einsum("ik,jk->ij", cross, cross, precision=exact_mode)
    norm_square = jnp.sqrt(jnp.sum(gram_matrix * gram_matrix) + epsilon)
    norm_scale = jnp.sqrt(norm_square)
    current = cross / norm_scale
    gram_matrix = gram_matrix / norm_square
    for iteration in range(NS_STEPS):
        if iteration > 0:
            gram_matrix = jnp.einsum("ik,jk->ij", current, current, precision=exact_mode)
        current = 1.5 * current - 0.5 * jnp.dot(gram_matrix, current, precision=exact_mode)
    return current


def per_device(vectors, centroids, list_ids, codes, rotation):
    lists_local = centroids.shape[0]
    row_count = vectors.shape[0]
    feature_width = vectors.shape[1]
    subspaces = codes.shape[1]
    sub_width = feature_width // subspaces
    owners = lax.axis_size("within")
    owned_rows = subspaces // owners
    owner_index = lax.axis_index("within")
    total_rows = row_count * lax.axis_size("group") * owners
    local_list = list_ids % lists_local
    residual = (vectors.astype(jnp.float32) - jnp.take(centroids, local_list, axis=0)).astype(
        jnp.bfloat16
    )
    counts = lax.psum(code_counts_local(codes), ("group", "within"))
    current = rotation
    owned_book = jnp.zeros((owned_rows, K * sub_width), jnp.float32)
    for alternation in range(ALTS):
        rotated = jnp.dot(
            residual, current.astype(jnp.bfloat16), preferred_element_type=jnp.float32
        ).astype(jnp.bfloat16)
        sums = lax.psum(word_sums(codes, rotated, subspaces), ("group", "within"))
        codebook = sums.reshape(subspaces, K, sub_width) / (counts[:, :, None] + 1.0)
        book_table = codebook.astype(jnp.bfloat16).reshape(subspaces, K * sub_width)
        owned_book = lax.dynamic_slice_in_dim(
            codebook.reshape(subspaces, K * sub_width), owner_index * owned_rows, owned_rows, 0
        )
        recon = rebuild_rows(codes, book_table)
        cross_term = jnp.einsum("rd,re->de", residual, recon, preferred_element_type=jnp.float32)
        cross = lax.psum(cross_term, ("group", "within")) / total_rows
        current = polar_factor(cross)
    rotated_out = jnp.dot(
        residual, current.astype(jnp.bfloat16), preferred_element_type=jnp.float32
    ).astype(jnp.bfloat16)
    return (rotated_out, owned_book)


def solution(mesh):
    in_specs = (
        P(("group", "within"), None),
        P(("group", "within"), None),
        P(("group", "within")),
        P(("group", "within"), None),
        P(),
    )
    out_specs = (P(("group", "within"), None), P("within", None))
    return jax.shard_map(
        per_device, mesh=mesh, in_specs=in_specs, out_specs=out_specs, check_vma=False
    )
```

profile of v0, /device:TPU:0, one launch (start us, length us, event | category | flops | bytes accessed | tf_op | source)
XLA Modules:
  0.0 708.2 jit_solution(1984195488075929537)
XLA Ops:
  14.3 15.0 %while.55 = (s32[]{:T(128)}, f32[96,256,8]{1,2,0:T(8,128)}, s32[2,256,96]{1,2,0:T(8,128)S(1)}, bf16[2,256,96,8]{1,3,2,0:T(8,128)(2,1)}, s32[]{:T(128)}, /*index=5*/s32[]{:T(128)}) while((s32[]{:T(128)}, f32[96,256,8]{1,2,0:T(8,128)}, s32[2,256,96]{1,2,0:T(8,128)S(1)}, bf16[2,256,96,8]{1,3,2,0:T(8,128)(2,1)}, s32[]{:T(128)}, ...), condition=%wide.region_1.2_spmd.clone, body=%wide.region_0.1_spmd.clone.sunk | while | flops 107347968 | bytes 2261587 | solution.py:56
  14.4 7.2 %fusion.84 = f32[96,256,8]{1,2,0:T(8,128)} fusion(s32[256,96]{0,1:T(8,128)S(1)} %dynamic-slice_bitcast_fusion.10, f32[96,256,8]{1,2,0:T(8,128)} %get-tuple-element.381, bf16[2,256,96,8]{1,3,2,0:T(8,128)(2,1)} %get-tuple-element.389, s32[]{:T(128)} %get-tuple-element.380, pred[]{:T(512)S(6)} %compare.10), kind=kOutput, calls=%fused_computation.18.clone.1 | convolution fusion | flops 107347968 | bytes 2064897 | tf_op jit(solution)/shard_map/while/body/eval_jaxpr/rmk,rmj->mkj/dot_general | solution.py:52
  21.6 7.8 %fusion.84 = f32[96,256,8]{1,2,0:T(8,128)} fusion(s32[256,96]{0,1:T(8,128)S(1)} %dynamic-slice_bitcast_fusion.10, f32[96,256,8]{1,2,0:T(8,128)} %get-tuple-element.381, bf16[2,256,96,8]{1,3,2,0:T(8,128)(2,1)} %get-tuple-element.389, s32[]{:T(128)} %get-tuple-element.380, pred[]{:T(512)S(6)} %compare.10), kind=kOutput, calls=%fused_computation.18.clone.1 | convolution fusion | flops 107347968 | bytes 2064897 | tf_op jit(solution)/shard_map/while/body/eval_jaxpr/rmk,rmj->mkj/dot_general | solution.py:52
  29.3 2.5 copy.33
  31.8 9.5 %while.56 = (s32[]{:T(128)}, f32[96,256]{1,0:T(8,128)S(1)}, s32[2,256,96]{1,0,2:T(2,128)S(1)}, s32[]{:T(128)}, s32[]{:T(128)}) while((s32[]{:T(128)}, f32[96,256]{1,0:T(8,128)S(1)}, s32[2,256,96]{1,0,2:T(2,128)S(1)}, s32[]{:T(128)}, s32[]{:T(128)}) %tuple.108), condition=%wide.region_5.6_spmd.clone, body=%wide.region_3.5_spmd.clone.sunk | while | flops 25190400 | bytes 884811 | solution.py:34
  32.0 4.5 convert_reduce_fusion.2
  36.8 4.5 convert_reduce_fusion.2
  42.1 133.8 %all-reduce.12.cloned.1.call-done = (f32[96,256,8]{0,2,1:T(8,128)}, f32[96,256]{1,0:T(8,128)}) async-done(((f32[96,256,8]{0,2,1:T(8,128)}, f32[96,256]{1,0:T(8,128)}), (f32[96,256,8]{0,2,1:T(8,128)}, f32[96,256]{1,0:T(8,128)})) %all-reduce.12.cloned.1.call-update) | async-done | bytes 884752 | tf_op jit(solution)/shard_map/psum | solution.py:112
  178.8 14.2 %while.53 = (s32[]{:T(128)}, bf16[2,256,768]{2,1,0:T(8,128)(2,1)S(1)}, s32[2,256,96]{1,2,0:T(8,128)S(1)}, bf16[96,256,8]{1,2,0:T(8,128)(2,1)S(1)}, s32[]{:T(128)}) while((s32[]{:T(128)}, bf16[2,256,768]{2,1,0:T(8,128)(2,1)S(1)}, s32[2,256,96]{1,2,0:T(8,128)S(1)}, bf16[96,256,8]{1,2,0:T(8,128)(2,1)S(1)}, s32[]{:T(128)}) %tuple.130), condition=%wide.region_8.9_spmd, body=%wide.region_7.8_spmd.sunk | while | flops 107151360 | bytes 2654277 | solution.py:74
  178.8 6.8 fusion.80
  185.9 6.8 fusion.80
  193.0 2.2 fusion.48
  195.8 133.8 %all-reduce.6.cloned.1.call-done = f32[768,768]{1,0:T(8,128)} async-done(((f32[768,768]{1,0:T(8,128)}), f32[768,768]{1,0:T(8,128)}) %all-reduce.6.cloned.1.call-update) | async-done | bytes 2359312 | tf_op jit(solution)/shard_map/psum | solution.py:120
  329.6 10.2 %multiply_reduce_fusion.1 = (f32[]{:T(128)}, f32[768,768]{1,0:T(8,128)}) fusion(f32[768,768]{1,0:T(8,128)} %all-reduce.6.cloned.1.call-done), kind=kOutput, calls=%fused_computation.45 | convolution fusion | flops 5437587456 | bytes 4718596 | tf_op jit(solution)/shard_map/ik,jk->ij/dot_general | solution.py:79
  340.6 9.6 %multiply_subtract_fusion.1 = f32[768,768]{1,0:T(8,128)S(1)} fusion(f32[768,768]{1,0:T(8,128)} %get-tuple-element.252, f32[768,768]{1,0:T(8,128)} %all-reduce.6.cloned.1.call-done, f32[]{:T(128)S(6)} %sqrt.12, f32[]{:T(128)S(6)} %sqrt.13), kind=kOutput, calls=%fused_computation.42 | convolution fusion | flops 5440536576 | bytes 7077896 | tf_op jit(solution)/shard_map/dot_general | solution.py:87
  350.2 6.0 fusion.49
  356.2 6.0 subtract_convert_fusion.1
  364.7 15.0 %while.57 = (s32[]{:T(128)}, f32[96,256,8]{1,2,0:T(8,128)}, s32[2,256,96]{1,2,0:T(8,128)S(1)}, bf16[2,256,96,8]{1,3,2,0:T(8,128)(2,1)}, s32[]{:T(128)}, /*index=5*/s32[]{:T(128)}) while((s32[]{:T(128)}, f32[96,256,8]{1,2,0:T(8,128)}, s32[2,256,96]{1,2,0:T(8,128)S(1)}, bf16[2,256,96,8]{1,3,2,0:T(8,128)(2,1)}, s32[]{:T(128)}, ...), condition=%wide.region_12.13_spmd.clone, body=%wide.region_11.12_spmd.clone.sunk | while | flops 107347968 | bytes 2261587 | solution.py:56
  364.7 7.2 %fusion.86 = f32[96,256,8]{1,2,0:T(8,128)} fusion(s32[256,96]{0,1:T(8,128)S(1)} %dynamic-slice_bitcast_fusion.11, f32[96,256,8]{1,2,0:T(8,128)} %get-tuple-element.429, bf16[2,256,96,8]{1,3,2,0:T(8,128)(2,1)} %get-tuple-element.437, s32[]{:T(128)} %get-tuple-element.428, pred[]{:T(512)S(6)} %compare.12), kind=kOutput, calls=%fused_computation.31.clone.1 | convolution fusion | flops 107347968 | bytes 2064897 | tf_op jit(solution)/shard_map/while/body/eval_jaxpr/rmk,rmj->mkj/dot_general | solution.py:52
  371.9 7.8 %fusion.86 = f32[96,256,8]{1,2,0:T(8,128)} fusion(s32[256,96]{0,1:T(8,128)S(1)} %dynamic-slice_bitcast_fusion.11, f32[96,256,8]{1,2,0:T(8,128)} %get-tuple-element.429, bf16[2,256,96,8]{1,3,2,0:T(8,128)(2,1)} %get-tuple-element.437, s32[]{:T(128)} %get-tuple-element.428, pred[]{:T(512)S(6)} %compare.12), kind=kOutput, calls=%fused_computation.31.clone.1 | convolution fusion | flops 107347968 | bytes 2064897 | tf_op jit(solution)/shard_map/while/body/eval_jaxpr/rmk,rmj->mkj/dot_general | solution.py:52
  379.6 2.5 copy.42
  382.2 128.9 %all-reduce.8.cloned.1.call-done = f32[96,2048]{0,1:T(8,128)} async-done(((f32[96,2048]{0,1:T(8,128)}), f32[96,2048]{0,1:T(8,128)}) %all-reduce.8.cloned.1.call-update) | async-done | bytes 786448 | tf_op jit(solution)/shard_map/psum | solution.py:112
  513.9 15.6 %while.54 = (s32[]{:T(128)}, bf16[2,256,768]{2,1,0:T(8,128)(2,1)}, s32[2,256,96]{1,2,0:T(8,128)S(1)}, bf16[96,256,8]{1,2,0:T(8,128)(2,1)S(1)}, s32[]{:T(128)}) while((s32[]{:T(128)}, bf16[2,256,768]{2,1,0:T(8,128)(2,1)}, s32[2,256,96]{1,2,0:T(8,128)S(1)}, bf16[96,256,8]{1,2,0:T(8,128)(2,1)S(1)}, s32[]{:T(128)}) %tuple.132), condition=%wide.region_15.16_spmd, body=%wide.region_14.15_spmd.sunk | while | flops 107151360 | bytes 2654785 | solution.py:74
  513.9 6.8 fusion.82
  521.7 6.8 fusion.82
  529.5 3.3 fusion.50
  535.7 2.2 copy.46
  537.9 129.1 %all-reduce.10.cloned.1.call-done = f32[768,768]{1,0:T(8,128)} async-done(((f32[768,768]{1,0:T(8,128)}), f32[768,768]{1,0:T(8,128)}) %all-reduce.10.cloned.1.call-update) | async-done | bytes 2359312 | tf_op jit(solution)/shard_map/psum | solution.py:120
  667.0 10.1 %multiply_reduce_fusion = (f32[]{:T(128)}, f32[768,768]{1,0:T(8,128)}) fusion(f32[768,768]{1,0:T(8,128)} %all-reduce.10.cloned.1.call-done), kind=kOutput, calls=%fused_computation.40 | convolution fusion | flops 5437587456 | bytes 4718596 | tf_op jit(solution)/shard_map/ik,jk->ij/dot_general | solution.py:79
  677.9 9.7 %multiply_subtract_fusion = f32[768,768]{1,0:T(8,128)S(1)} fusion(f32[768,768]{1,0:T(8,128)} %get-tuple-element.254, f32[768,768]{1,0:T(8,128)} %all-reduce.10.cloned.1.call-done, f32[]{:T(128)S(6)} %sqrt.14, f32[]{:T(128)S(6)} %sqrt.15), kind=kOutput, calls=%fused_computation.37 | convolution fusion | flops 5440536576 | bytes 7077896 | tf_op jit(solution)/shard_map/dot_general | solution.py:87
  687.6 6.0 fusion.51
  693.6 6.0 subtract_convert_fusion
  (67 shorter events, 23.9 us)
Async XLA Ops:
  7.2 0.9 copy-start
  7.2 168.7 %all-reduce.12.cloned.1.call-start = ((), (), s32[]{:S(2)}) async-start(), calls=%async_computation.3 | async-start | bytes 2293760 | tf_op jit(solution)/shard_map/psum | solution.py:112
  10.0 1.9 copy-start.3
  12.7 1.5 copy-start.4
  41.3 0.6 copy-start.2
  42.0 287.6 %all-reduce.6.cloned.1.call-start = ((), (), s32[]{:S(2)}) async-start(), calls=%async_computation | async-start | bytes 4718592 | tf_op jit(solution)/shard_map/psum | solution.py:120
  195.2 315.8 %all-reduce.8.cloned.1.call-start = ((), (), s32[]{:S(2)}) async-start(), calls=%async_computation.1 | async-start | bytes 2097152 | tf_op jit(solution)/shard_map/psum | solution.py:112
  382.2 284.9 %all-reduce.10.cloned.1.call-start = ((), (), s32[]{:S(2)}) async-start(), calls=%async_computation.2 | async-start | bytes 4718592 | tf_op jit(solution)/shard_map/psum | solution.py:120
  532.8 1.2 copy-start.1
Sparse Core Ops, SparseCore 0:
  42.1 133.6 all-reduce.11
  195.3 134.2 all-reduce.5
  382.3 128.7 all-reduce.7
  533.0 133.9 all-reduce.9
where the time goes:
time: 715 us; the launch traced here: 708 us
  waiting for transfers between devices  526 us (74%)
  matrix products  130 us (18%)
  local copies, waits for them, and re-layouts  19.5 us (3%)
  other arithmetic  16.6 us (2%)
  between operations  16 us (2%)
    psum x2, waiting for transfers between devices, per_device(): cross = lax.psum(cross_term, ('group', 'within')) / total_rows  263 us
    psum x2, waiting for transfers between devices, per_device(): sums = lax.psum(word_sums(codes, rotated, subspaces), ('group', 'within'))  263 us
    dot_general x4, matrix products, polar_factor(): jnp.dot(gram_matrix, current, precision=exact_mode)  31.3 us
    dot_general x4, matrix products, word_add_block(): jnp.einsum('rmk,rmj->mkj', table, value_block, preferred_element_type=jnp...  29.9 us
    dot_general x4, matrix products, one_block(): jnp.einsum('rmk,mkj->rmj', table, book, preferred_element_type=jnp.float32)  27.3 us
    dot_general x2, matrix products, polar_factor(): gram_matrix = jnp.einsum('ik,jk->ij', cross, cross, precision=exact_mode)  20.4 us
  transfers between devices with their start and end apart: 4, of which 4 were waited for; matrix products, arithmetic and copies ran while one was open for 1% of the time, Pallas kernels for 0%

commit v1 on v0

v1 whole, which is shorter than its diff:
```python
import functools

import jax
import jax.numpy as jnp
from jax import lax
from jax.experimental import pallas as pl
from jax.experimental.pallas import tpu as pltpu
from jax.sharding import PartitionSpec as P

K = 256
ALTS = 2
LO = 8
HI = K // LO
SUB = 8
PACK = 128 // HI
EPSILON = 1e-06
VMEM_BYTES = 56 * 1024 * 1024

F32 = jnp.float32
BF16 = jnp.bfloat16
NT = (((1,), (1,)), ((), ()))
NN = (((1,), (0,)), ((), ()))
TN = (((0,), (0,)), ((), ()))


def mm(a, b, dims=NN):
    return lax.dot_general(a, b, dims, preferred_element_type=F32)


def vmem_spec():
    return pl.BlockSpec(memory_space=pltpu.VMEM)


def any_spec():
    return pl.BlockSpec(memory_space=pl.ANY)


def params():
    return pltpu.CompilerParams(vmem_limit_bytes=VMEM_BYTES)


def swap(x, axis, size, bits):
    return lax.ppermute(x, axis, [(i, i ^ bits) for i in range(size)])


def residual_kernel(vectors_ref, centroids_ref, ids_ref, codes_ref, out_ref, codes_out_ref):
    lists = centroids_ref.shape[0]
    rows = vectors_ref.shape[0]
    local = lax.rem(ids_ref[...], lists)
    level = lax.broadcasted_iota(jnp.int32, (lists, rows), 0)
    table = jnp.where(level == local, 1.0, 0.0).astype(BF16)
    center = centroids_ref[...]
    first = center.astype(BF16)
    rest = center - first.astype(F32)
    second = rest.astype(BF16)
    third = (rest - second.astype(F32)).astype(BF16)
    picked = mm(table, first, TN) + mm(table, second, TN) + mm(table, third, TN)
    out_ref[...] = (vectors_ref[...].astype(F32) - picked).astype(BF16)
    codes_out_ref[...] = codes_ref[...].astype(F32).T.astype(BF16)


def residual_call(vectors, centroids, ids, codes):
    rows, width = vectors.shape
    return pl.pallas_call(
        residual_kernel,
        out_shape=(
            jax.ShapeDtypeStruct((rows, width), BF16),
            jax.ShapeDtypeStruct((codes.shape[1], rows), BF16),
        ),
        in_specs=[vmem_spec()] * 4,
        out_specs=(vmem_spec(), vmem_spec()),
        compiler_params=params(),
        name="residual",
    )(vectors, centroids, ids.reshape(1, rows), codes)


def split_codes(codes):
    whole = codes.astype(F32).astype(jnp.int32)
    return whole >> 3, whole & 7


def packs_of(owned):
    return [range(first, min(first + PACK, owned)) for first in range(0, owned, PACK)]


def hi_table(hi, pack):
    rows = hi.shape[1]
    level = lax.broadcasted_iota(jnp.int32, (HI, rows), 0)
    parts = [jnp.where(level == hi[m : m + 1, :], 1.0, 0.0) for m in pack]
    parts += [jnp.zeros((HI, rows), F32)] * (PACK - len(pack))
    return jnp.concatenate(parts, axis=0).astype(BF16)


def lane_owner(rows):
    return lax.broadcasted_iota(jnp.int32, (rows, 128), 1) // HI


def diagonal(wide, block):
    owner = lane_owner(block)
    total = jnp.zeros((block, 128), F32)
    for i in range(wide.shape[0] // block):
        total = jnp.where(owner == i, wide[i * block : (i + 1) * block, :], total)
    return total


def add_chunk(residual, rotation_rows, codes, totals, first, with_counts):
    owned = codes.shape[0]
    rotated = mm(rotation_rows, residual, NT).astype(BF16).astype(F32)
    hi, lo = split_codes(codes)
    rows = residual.shape[0]
    low_level = lax.broadcasted_iota(jnp.int32, (LO, rows), 0)
    for g, pack in enumerate(packs_of(owned)):
        table = hi_table(hi, pack)
        parts = []
        for m in pack:
            value = rotated[m * SUB : (m + 1) * SUB, :]
            low = jnp.broadcast_to(lo[m : m + 1, :], (SUB, rows))
            parts += [jnp.where(low == level, value, 0.0) for level in range(LO)]
        if with_counts:
            parts += [jnp.where(low_level == lo[m : m + 1, :], 1.0, 0.0) for m in pack]
        part = mm(jnp.concatenate(parts, axis=0).astype(BF16), table, NT)
        height = part.shape[0]
        if first:
            totals[g, :height, :] = part
        else:
            totals[g, :height, :] += part


def pack_sums(totals, owned, out_ref, with_counts):
    packs = packs_of(owned)
    block = LO * SUB
    counts = []
    for g, pack in enumerate(packs):
        size = len(pack)
        out_ref[g * block : (g + 1) * block, :] = diagonal(totals[g, : size * block, :], block).astype(BF16)
        if with_counts:
            counts.append(diagonal(totals[g, size * block : size * (block + LO), :], LO))
    if with_counts:
        every = jnp.concatenate(counts, axis=0)
        above = jnp.floor(every * (1.0 / 256.0))
        below = every - above * 256.0
        base = len(packs) * block
        height = len(packs) * LO
        pad = out_ref.shape[0] - base - 2 * height
        pieces = [above, below] + ([jnp.zeros((pad, 128), F32)] if pad else [])
        out_ref[base:, :] = jnp.concatenate(pieces, axis=0).astype(BF16)


def sums_rows(owned, with_counts):
    packs = len(packs_of(owned))
    rows = packs * LO * SUB
    if with_counts:
        rows += -(-2 * packs * LO // 16) * 16
    return rows


def totals_shape(owned):
    return pltpu.VMEM((len(packs_of(owned)), PACK * LO * (SUB + 1), 128), F32)


def start_copies(sources, held, sems):
    copies = [pltpu.make_async_copy(src, held.at[i], sems.at[i]) for i, src in enumerate(sources)]
    for copy in copies:
        copy.start()
    return copies


def sums_kernel(count, rotation_ref, codes_ref, *refs):
    chunks, out_ref, held, totals, sems = refs[:count], refs[count], *refs[count + 1 :]
    owned = codes_ref.shape[1]
    copies = start_copies(chunks, held, sems)
    rotation_rows = rotation_ref[...]
    for i, copy in enumerate(copies):
        copy.wait()
        add_chunk(held[i], rotation_rows, codes_ref[i], totals, i == 0, True)
    pack_sums(totals, owned, out_ref, True)


def sums_call(rotation_rows, codes, chunks):
    count, owned = codes.shape[:2]
    return pl.pallas_call(
        functools.partial(sums_kernel, count),
        out_shape=jax.ShapeDtypeStruct((sums_rows(owned, True), 128), BF16),
        in_specs=[vmem_spec()] * 2 + [any_spec()] * count,
        out_specs=vmem_spec(),
        scratch_shapes=[
            pltpu.VMEM((count,) + chunks[0].shape, BF16),
            totals_shape(owned),
            pltpu.SemaphoreType.DMA((count,)),
        ],
        compiler_params=params(),
        name="sums",
    )(rotation_rows, codes, *chunks)


def tree(values):
    while len(values) > 1:
        values = [values[i] + values[i + 1] for i in range(0, len(values), 2)]
    return values[0]


def cross_kernel(count, groups, with_counts, total_rows, codes_ref, *refs):
    sums = refs[:groups]
    refs = refs[groups:]
    owned = codes_ref.shape[1]
    packs = packs_of(owned)
    block = LO * SUB
    base = len(packs) * block
    height = len(packs) * LO
    if with_counts:
        chunks, refs = refs[:count], refs[count:]
        cross_ref, counts_ref, held, sems = refs
    else:
        counts_in, chunks, refs = refs[0], refs[1 : count + 1], refs[count + 1 :]
        cross_ref, book_ref, held, sems = refs
    copies = start_copies(chunks, held, sems)
    everything = tree([ref[...].astype(F32) for ref in sums])
    if with_counts:
        counts = everything[base : base + height] * 256.0 + everything[base + height : base + 2 * height]
        counts_ref[...] = counts
    else:
        counts = counts_in[...]
    books = []
    for g in range(len(packs)):
        rows = []
        for level in range(LO):
            at = g * block + level * SUB
            rows.append(everything[at : at + SUB] / (counts[g * LO + level : g * LO + level + 1] + 1.0))
        book = jnp.concatenate(rows, axis=0)
        if not with_counts:
            book_ref[g * block : (g + 1) * block, :] = book
        books.append(book)
    owner = lane_owner(block)
    wide = [
        jnp.concatenate([jnp.where(owner == i, book, 0.0) for i in range(len(pack))], axis=0).astype(BF16)
        for book, pack in zip(books, packs)
    ]
    total = jnp.zeros(cross_ref.shape, F32)
    for i, copy in enumerate(copies):
        hi, lo = split_codes(codes_ref[i])
        rows = hi.shape[1]
        rebuilt = []
        for g, pack in enumerate(packs):
            spread = mm(wide[g], hi_table(hi, pack))
            for j, m in enumerate(pack):
                low = jnp.broadcast_to(lo[m : m + 1, :], (SUB, rows))
                at = j * block
                value = spread[at : at + SUB]
                for level in range(1, LO):
                    value = jnp.where(low == level, spread[at + level * SUB : at + (level + 1) * SUB], value)
                rebuilt.append(value)
        copy.wait()
        total += mm(jnp.concatenate(rebuilt, axis=0).astype(BF16), held[i])
    cross_ref[...] = (total * (1.0 / total_rows)).astype(BF16)


def cross_call(codes, sums, counts, chunks, total_rows):
    count, owned = codes.shape[:2]
    packs = len(packs_of(owned))
    width = chunks[0].shape[1]
    with_counts = counts is None
    extra = (
        jax.ShapeDtypeStruct((packs * LO, 128), F32)
        if with_counts
        else jax.ShapeDtypeStruct((packs * LO * SUB, 128), F32)
    )
    small = list(sums) + ([] if with_counts else [counts])
    return pl.pallas_call(
        functools.partial(cross_kernel, count, len(sums), with_counts, total_rows),
        out_shape=(jax.ShapeDtypeStruct((owned * SUB, width), BF16), extra),
        in_specs=[vmem_spec()] * (1 + len(small)) + [any_spec()] * count,
        out_specs=(vmem_spec(), vmem_spec()),
        scratch_shapes=[
            pltpu.VMEM((count,) + chunks[0].shape, BF16),
            pltpu.SemaphoreType.DMA((count,)),
        ],
        compiler_params=params(),
        name="cross",
    )(codes, *small, *chunks)


def gather_blocks(place_ref, blocks, whole):
    height = blocks[0].shape[0]
    for k, ref in enumerate(blocks):
        at = pl.multiple_of((place_ref[0] ^ k) * height, 8)
        whole[pl.ds(at, height), :] = ref[...].astype(F32)


def first_step(whole):
    x = whole[...]
    xb = x.astype(BF16)
    gram = mm(xb, xb, NT)
    norm_square = jnp.sqrt(jnp.sum(gram * gram, keepdims=True) + EPSILON)
    scale = lax.rsqrt(norm_square)
    step = mm((gram * (1.0 / norm_square)).astype(BF16), xb)
    return (1.5 * x - 0.5 * step) * scale


def next_sums_kernel(count, blocks, place_ref, codes_ref, *refs):
    parts, refs = refs[:blocks], refs[blocks:]
    chunks, out_ref, held, totals, whole, sems = refs[:count], refs[count], *refs[count + 1 :]
    owned = codes_ref.shape[1]
    copies = start_copies(chunks, held, sems)
    gather_blocks(place_ref, parts, whole)
    x = first_step(whole)
    whole[...] = x
    height = parts[0].shape[0]
    mine = whole[pl.ds(pl.multiple_of(place_ref[0] * height, 8), height), :]
    xb = x.astype(BF16)
    gram = mm(mine.astype(BF16), xb, NT)
    rotation_rows = (1.5 * mine - 0.5 * mm(gram.astype(BF16), xb)).astype(BF16)
    for i, copy in enumerate(copies):
        copy.wait()
        add_chunk(held[i], rotation_rows, codes_ref[i], totals, i == 0, False)
    pack_sums(totals, owned, out_ref, False)


def next_sums_call(place, codes, blocks, chunks):
    count, owned = codes.shape[:2]
    width = chunks[0].shape[1]
    return pl.pallas_call(
        functools.partial(next_sums_kernel, count, len(blocks)),
        out_shape=jax.ShapeDtypeStruct((sums_rows(owned, False), 128), BF16),
        in_specs=[pl.BlockSpec(memory_space=pltpu.SMEM)] + [vmem_spec()] * (1 + len(blocks)) + [any_spec()] * count,
        out_specs=vmem_spec(),
        scratch_shapes=[
            pltpu.VMEM((count,) + chunks[0].shape, BF16),
            totals_shape(owned),
            pltpu.VMEM((width, width), F32),
            pltpu.SemaphoreType.DMA((count,)),
        ],
        compiler_params=params(),
        name="next_sums",
    )(place, codes, *blocks, *chunks)


def final_kernel(blocks, place_ref, residual_ref, *refs):
    parts, out_ref, whole = refs[:blocks], refs[blocks], refs[blocks + 1]
    gather_blocks(place_ref, parts, whole)
    x = first_step(whole)
    xb = x.astype(BF16)
    gram = mm(xb, xb, NT)
    rotation = (1.5 * x - 0.5 * mm(gram.astype(BF16), xb)).astype(BF16)
    out_ref[...] = mm(residual_ref[...], rotation, NT).astype(BF16)


def final_call(place, residual, blocks):
    width = residual.shape[1]
    return pl.pallas_call(
        functools.partial(final_kernel, len(blocks)),
        out_shape=jax.ShapeDtypeStruct(residual.shape, BF16),
        in_specs=[pl.BlockSpec(memory_space=pltpu.SMEM)] + [vmem_spec()] * (1 + len(blocks)),
        out_specs=vmem_spec(),
        scratch_shapes=[pltpu.VMEM((width, width), F32)],
        compiler_params=params(),
        name="final",
    )(place, residual, *blocks)


def gather_rows(residual, size):
    half = residual.shape[0] // 2
    bits = [1 << b for b in range(1, size.bit_length() - 1)]
    held = [{0: residual[:half]}, {0: residual[half:]}]
    for step in range(len(bits)):
        for h in range(2):
            bit = bits[step] if h == 0 else bits[len(bits) - 1 - step]
            for k in list(held[h]):
                held[h][k ^ bit] = swap(held[h][k], "within", size, bit)
    for h in range(2):
        for k in list(held[h]):
            held[h][k ^ 1] = swap(held[h][k], "within", size, 1)
    return [held[h][k] for k in range(size) for h in range(2)]


def gather_group(x, size):
    blocks = {k: swap(x, "within", size, k) if k else x for k in range(0, size, 2)}
    for k in list(blocks):
        blocks[k ^ 1] = swap(blocks[k], "within", size, 1)
    return [blocks[k] for k in range(size)]


def everywhere(x, size):
    return [x] + [swap(x, "group", size, k) for k in range(1, size)]


def per_device(vectors, centroids, list_ids, codes, rotation):
    groups = lax.axis_size("group")
    size = lax.axis_size("within")
    rows, width = vectors.shape
    subspaces = codes.shape[1]
    owned = subspaces // size
    total_rows = rows * size * groups
    place = lax.axis_index("within").astype(jnp.int32)
    places = place.reshape(1)
    residual, codes_t = residual_call(vectors, centroids, list_ids, codes)
    chunks = gather_rows(residual, size)
    moved = lax.all_to_all(codes_t.reshape(size, owned, rows), "within", 0, 0)
    order = jnp.arange(size, dtype=jnp.int32) ^ place
    moved = jnp.take(moved, order, axis=0)
    half = rows // 2
    own_codes = moved.reshape(size, owned, 2, half).transpose(0, 2, 1, 3).reshape(2 * size, owned, half)
    rotation_rows = lax.dynamic_slice_in_dim(rotation, place * owned * SUB, owned * SUB, 1).T.astype(BF16)
    sums = sums_call(rotation_rows, own_codes, chunks)
    counts = None
    for alternation in range(ALTS):
        parts = everywhere(sums, groups)
        cross, extra = cross_call(own_codes, parts, counts, chunks, total_rows)
        block = tree([p.astype(F32) for p in everywhere(cross, groups)]).astype(BF16)
        blocks = gather_group(block, size)
        if alternation + 1 < ALTS:
            counts = extra
            sums = next_sums_call(places, own_codes, blocks, chunks)
    rotated_out = final_call(places, residual, blocks)
    packs = len(packs_of(owned))
    book = extra.reshape(packs, LO * SUB, PACK, HI).transpose(0, 2, 3, 1).reshape(packs * PACK, K * SUB)
    return (rotated_out, book[:owned])


def solution(mesh):
    in_specs = (
        P(("group", "within"), None),
        P(("group", "within"), None),
        P(("group", "within")),
        P(("group", "within"), None),
        P(),
    )
    out_specs = (P(("group", "within"), None), P("within", None))
    return jax.shard_map(per_device, mesh=mesh, in_specs=in_specs, out_specs=out_specs, check_vma=False)
```

time: 715 us -> 169 us (0.24)
  waiting for transfers between devices: 526 us -> 56.8 us
  matrix products: 130 us -> 0 us
  Pallas kernels: 0 us -> 53.5 us
  starting transfers between devices: 0.69 us -> 37.9 us
  between operations: 16 us -> 0.98 us
  other arithmetic: 16.6 us -> 3.65 us
    psum x4 -> x0, waiting for transfers between devices: 526 us -> none  [the longest x2 263 us: per_device(): cross = lax.psum(cross_term, ('group', 'within')) / total_rows]
    dot_general x21 -> x0, matrix products: 130 us -> none  [the longest x4 31.3 us: polar_factor(): jnp.dot(gram_matrix, current, precision=exact_mode)]
    ppermute x0 -> x40, waiting for transfers between devices: none -> 56.8 us  [swap(): return lax.ppermute(x, axis, [(i, i ^ bits) for i in range(size)])]
    pallas_call x0 -> x6, Pallas kernels: none -> 53.5 us  [the longest x2 16 us: cross_call(): pl.pallas_call(functools.partial(cross_kernel, count, len(sums), with_cou...]
    ppermute x0 -> x40, starting transfers between devices: none -> 33.7 us  [swap(): return lax.ppermute(x, axis, [(i, i ^ bits) for i in range(size)])]
    reduce_sum x2 -> x0, other arithmetic: 8.99 us -> none  [code_add_block(): jnp.sum(code_table(codes_block).astype(jnp.float32), axis=0)]
  transfers between devices with their start and end apart: 4 -> 41, of which waited for: 4 -> 18; matrix products, arithmetic and copies ran while one was open for 1% -> 7% of each run, Pallas kernels for 0% -> 0%
where the time goes in v1:
time: 169 us
  waiting for transfers between devices  56.8 us (34%)
  Pallas kernels  53.5 us (32%)
  starting transfers between devices  37.9 us (22%)
  local copies, waits for them, and re-layouts  16 us (9%)
  other arithmetic  3.65 us (2%)
    ppermute x40, waiting for transfers between devices, swap(): return lax.ppermute(x, axis, [(i, i ^ bits) for i in range(size)])  56.8 us
    ppermute x40, starting transfers between devices, swap(): return lax.ppermute(x, axis, [(i, i ^ bits) for i in range(size)])  33.7 us
    pallas_call x2, Pallas kernels, cross_call(): pl.pallas_call(functools.partial(cross_kernel, count, len(sums), with_cou...  16 us
    pallas_call x1, Pallas kernels, next_sums_call(): pl.pallas_call(functools.partial(next_sums_kernel, count, len(blocks)), o...  14.3 us
    pallas_call x1, Pallas kernels, sums_call(): pl.pallas_call(functools.partial(sums_kernel, count), out_shape=jax.Shape...  11.8 us
    pallas_call x1, Pallas kernels, final_call(): pl.pallas_call(functools.partial(final_kernel, len(blocks)), out_shape=ja...  8.43 us
    unnamed x48, local copies, waits for them, and re-layouts  6.82 us
    all_to_all x1, starting transfers between devices, per_device(): moved = lax.all_to_all(codes_t.reshape(size, owned, rows), 'within', 0, 0)  4.16 us
  transfers between devices with their start and end apart: 41, of which 18 were waited for; matrix products, arithmetic and copies ran while one was open for 7% of the time, Pallas kernels for 0%

profile of v1, /device:TPU:0, one launch (start us, length us, event | category | flops | bytes accessed | tf_op | source)
XLA Modules:
  0.0 168.7 jit_solution(11308020824214261223)
XLA Ops:
  0.6 1.9 %copy.13.codes_ref = s32[512,96]{1,0:T(8,128)} copy(s32[512,96]{0,1:T(8,128)} %param.8) | data formatting | bytes 393216 | tf_op args[3]
  2.6 3.0 %residual.1 = (bf16[512,768]{1,0:T(8,128)(2,1)}, bf16[96,512]{1,0:T(8,128)(2,1)}) custom-call(bf16[512,768]{1,0:T(8,128)(2,1)} %vectors_ref.1, f32[64,768]{1,0:T(8,128)} %centroids_ref.1, s32[1,512]{1,0:T(1,128)} %bitcast.14, s32[512,96]{1,0:T(8,128)} %copy.13.codes_ref), custom_call_target="tpu_custom_call" | custom-call | tf_op jit(solution)/shard_map/residual/pallas_call | solution.py:64
  6.8 3.0 %collective-permute-start.7 = (bf16[256,768]{1,0:T(8,128)(2,1)S(1)}, bf16[256,768]{1,0:T(8,128)(2,1)S(1)}, u32[]{:S(2)}, u32[]{:S(2)}) collective-permute-start(bf16[256,768]{1,0:T(8,128)(2,1)S(1)} %get-tuple-element.14.refs_1_.refs_5_.refs_9_.refs_6_), channel_id=1, source_target_pairs={{0,4},{1,5},{2,6},{3,7},{4,0},{5,1},{6,2},{7,3},{8,12},{9,13},{10,... | collective-permute-start | bytes 1179656 | tf_op jit(solution)/shard_map/ppermute | solution.py:43
  13.5 4.2 %all-to-all-start = ((bf16[8,12,512]{2,1,0:T(8,128)(2,1)}), bf16[8,12,512]{2,1,0:T(8,128)(2,1)}, u32[]{:S(2)}, u32[]{:S(2)}) async-start(bf16[8,12,512]{2,1,0:T(8,128)(2,1)} %reshape.46), calls=%async_computation | async-start | bytes 262144 | tf_op jit(solution)/shard_map/all_to_all | solution.py:397
  17.6 2.1 %collective-permute-done.7.refs_9_.refs_13_.refs_17_.refs_14_ = bf16[256,768]{1,0:T(8,128)(2,1)S(1)} collective-permute-done((bf16[256,768]{1,0:T(8,128)(2,1)S(1)}, bf16[256,768]{1,0:T(8,128)(2,1)S(1)}, u32[]{:S(2)}, u32[]{:S(2)}) %collective-permute-start.7) | collective-permute-done | bytes 393248 | tf_op jit(solution)/shard_map/ppermute | solution.py:43
  19.8 2.2 %collective-permute-done.3.refs_5_.refs_9_.refs_13_.refs_10_ = bf16[256,768]{1,0:T(8,128)(2,1)} collective-permute-done((bf16[256,768]{1,0:T(8,128)(2,1)S(1)}, bf16[256,768]{1,0:T(8,128)(2,1)}, u32[]{:S(2)}, u32[]{:S(2)}) %collective-permute-start.3) | collective-permute-done | bytes 393248 | tf_op jit(solution)/shard_map/ppermute | solution.py:43
  23.5 6.9 %collective-permute-done.2.refs_4_.refs_8_.refs_12_.refs_9_ = bf16[256,768]{1,0:T(8,128)(2,1)} collective-permute-done((bf16[256,768]{1,0:T(8,128)(2,1)S(1)}, bf16[256,768]{1,0:T(8,128)(2,1)}, u32[]{:S(2)}, u32[]{:S(2)}) %collective-permute-start.2) | collective-permute-done | bytes 393248 | tf_op jit(solution)/shard_map/ppermute | solution.py:43
  31.2 1.7 %copy.17 = bf16[768,96]{0,1:T(8,128)(2,1)} copy(bf16[768,96]{1,0:T(8,128)(2,1)} %constant_dynamic-slice_fusion) | data formatting | bytes 294912
  33.0 2.1 %gather_fusion = bf16[8,12,512]{2,1,0:T(8,128)(2,1)} fusion(bf16[8,12,512]{2,1,0:T(8,128)(2,1)} %all-to-all-done, s32[1024]{0:T(1024)S(1)} %pad_clamp_fusion), kind=kCustom, calls=%fused_computation | custom fusion | bytes 196640 | tf_op jit(solution)/shard_map/jit(_take)/gather | solution.py:399
  35.6 3.1 %collective-permute-done.11.refs_13_.refs_17_.refs_21_.refs_18_ = bf16[256,768]{1,0:T(8,128)(2,1)} collective-permute-done((bf16[256,768]{1,0:T(8,128)(2,1)S(1)}, bf16[256,768]{1,0:T(8,128)(2,1)}, u32[]{:S(2)}, u32[]{:S(2)}) %collective-permute-start.11) | collective-permute-done | bytes 393248 | tf_op jit(solution)/shard_map/ppermute | solution.py:43
  42.7 11.8 %sums.1.refs_0_ = bf16[240,128]{1,0:T(8,128)(2,1)} custom-call(bf16[96,768]{1,0:T(8,128)(2,1)} %bitcast.13, bf16[16,12,256]{2,1,0:T(8,128)(2,1)} %reshape.47.codes_ref, bf16[256,768]{1,0:T(8,128)(2,1)} %copy-done.2, bf16[256,768]{1,0:T(8,128)(2,1)} %copy-done.1, bf16[256,768]{1,0:T(8,128)(2,1)} %collective-permute-done.refs_2_.refs_6_.refs_10_.refs_7_, ...), custom_call_target="tpu_custom_call" | custom-call | tf_op jit(solution)/shard_map/sums/pallas_call | solution.py:181
  54.4 3.7 %collective-permute-start.16 = (bf16[240,128]{1,0:T(8,128)(2,1)}, bf16[240,128]{1,0:T(8,128)(2,1)S(1)}, u32[]{:S(2)}, u32[]{:S(2)}) collective-permute-start(bf16[240,128]{1,0:T(8,128)(2,1)} %sums.1.refs_0_), channel_id=1, source_target_pairs={{0,24},{8,16},{16,8},{24,0},{1,25},{9,17},{17,9},{25,1},{2,26},{10... | collective-permute-start | bytes 184328 | tf_op jit(solution)/shard_map/ppermute | solution.py:43
  58.9 2.2 %collective-permute-done.16.refs_3_ = bf16[240,128]{1,0:T(8,128)(2,1)S(1)} collective-permute-done((bf16[240,128]{1,0:T(8,128)(2,1)}, bf16[240,128]{1,0:T(8,128)(2,1)S(1)}, u32[]{:S(2)}, u32[]{:S(2)}) %collective-permute-start.16) | collective-permute-done | bytes 61472 | tf_op jit(solution)/shard_map/ppermute | solution.py:43
  61.0 3.0 %collective-permute-done.15.refs_2_ = bf16[240,128]{1,0:T(8,128)(2,1)S(1)} collective-permute-done((bf16[240,128]{1,0:T(8,128)(2,1)}, bf16[240,128]{1,0:T(8,128)(2,1)S(1)}, u32[]{:S(2)}, u32[]{:S(2)}) %collective-permute-start.15) | collective-permute-done | bytes 61472 | tf_op jit(solution)/shard_map/ppermute | solution.py:43
  65.3 8.0 %cross.2 = (bf16[96,768]{1,0:T(8,128)(2,1)}, f32[24,128]{1,0:T(8,128)}) custom-call(bf16[16,12,256]{2,1,0:T(8,128)(2,1)} %reshape.47.codes_ref, bf16[240,128]{1,0:T(8,128)(2,1)} %sums.1.refs_0_, bf16[240,128]{1,0:T(8,128)(2,1)} %copy-done.19, bf16[240,128]{1,0:T(8,128)(2,1)} %copy-done.18, bf16[240,128]{1,0:T(8,128)(2,1)} %copy-done.17, ...), custom_call_target="tpu_custom_call" | custom-call | tf_op jit(solution)/shard_map/cross/pallas_call | solution.py:268
  73.3 2.5 %collective-permute-start.19 = (bf16[96,768]{1,0:T(8,128)(2,1)}, bf16[96,768]{1,0:T(8,128)(2,1)S(1)}, u32[]{:S(2)}, u32[]{:S(2)}) collective-permute-start(bf16[96,768]{1,0:T(8,128)(2,1)} %get-tuple-element.10), channel_id=1, source_target_pairs={{0,24},{8,16},{16,8},{24,0},{1,25},{9,17},{17,9},{25,1},{2,26},{10... | collective-permute-start | bytes 442376 | tf_op jit(solution)/shard_map/ppermute | solution.py:43
  75.8 1.9 %collective-permute-start.17 = (bf16[96,768]{1,0:T(8,128)(2,1)}, bf16[96,768]{1,0:T(8,128)(2,1)S(1)}, u32[]{:S(2)}, u32[]{:S(2)}) collective-permute-start(bf16[96,768]{1,0:T(8,128)(2,1)} %get-tuple-element.10), channel_id=1, source_target_pairs={{0,8},{8,0},{16,24},{24,16},{1,9},{9,1},{17,25},{25,17},{2,10},{10... | collective-permute-start | bytes 442376 | tf_op jit(solution)/shard_map/ppermute | solution.py:43
  77.7 4.4 %collective-permute-done.19 = bf16[96,768]{1,0:T(8,128)(2,1)S(1)} collective-permute-done((bf16[96,768]{1,0:T(8,128)(2,1)}, bf16[96,768]{1,0:T(8,128)(2,1)S(1)}, u32[]{:S(2)}, u32[]{:S(2)}) %collective-permute-start.19) | collective-permute-done | bytes 147488 | tf_op jit(solution)/shard_map/ppermute | solution.py:43
  82.2 6.4 %collective-permute-done.18 = bf16[96,768]{1,0:T(8,128)(2,1)S(1)} collective-permute-done((bf16[96,768]{1,0:T(8,128)(2,1)}, bf16[96,768]{1,0:T(8,128)(2,1)S(1)}, u32[]{:S(2)}, u32[]{:S(2)}) %collective-permute-start.18) | collective-permute-done | bytes 147488 | tf_op jit(solution)/shard_map/ppermute | solution.py:43
  93.1 3.8 %collective-permute-done.25.refs_6_ = bf16[96,768]{1,0:T(8,128)(2,1)S(1)} collective-permute-done((bf16[96,768]{1,0:T(8,128)(2,1)S(1)}, bf16[96,768]{1,0:T(8,128)(2,1)S(1)}, u32[]{:S(2)}, u32[]{:S(2)}) %collective-permute-start.25) | collective-permute-done | bytes 147488 | tf_op jit(solution)/shard_map/ppermute | solution.py:43
  100.7 14.3 %next_sums.1.refs_0_ = bf16[192,128]{1,0:T(8,128)(2,1)} custom-call(s32[1]{0:T(128)} %bitcast.place_ref, bf16[16,12,256]{2,1,0:T(8,128)(2,1)} %reshape.47.codes_ref, bf16[96,768]{1,0:T(8,128)(2,1)} %copy-done.5, bf16[96,768]{1,0:T(8,128)(2,1)} %copy-done.13, bf16[96,768]{1,0:T(8,128)(2,1)} %copy-done.12, bf16[96,768]{1,0:T(8,128)(2,1)} %copy-done.16, ...), custom_call_target="tpu_custom_call" | custom-call | tf_op jit(solution)/shard_map/next_sums/pallas_call | solution.py:321
  115.0 2.1 %collective-permute-start.29 = (bf16[192,128]{1,0:T(8,128)(2,1)}, bf16[192,128]{1,0:T(8,128)(2,1)S(1)}, u32[]{:S(2)}, u32[]{:S(2)}) collective-permute-start(bf16[192,128]{1,0:T(8,128)(2,1)} %next_sums.1.refs_0_), channel_id=1, source_target_pairs={{0,24},{8,16},{16,8},{24,0},{1,25},{9,17},{17,9},{25,1},{2,26},{10... | collective-permute-start | bytes 147464 | tf_op jit(solution)/shard_map/ppermute | solution.py:43
  117.1 2.3 %collective-permute-start.27 = (bf16[192,128]{1,0:T(8,128)(2,1)}, bf16[192,128]{1,0:T(8,128)(2,1)S(1)}, u32[]{:S(2)}, u32[]{:S(2)}) collective-permute-start(bf16[192,128]{1,0:T(8,128)(2,1)} %next_sums.1.refs_0_), channel_id=1, source_target_pairs={{0,8},{8,0},{16,24},{24,16},{1,9},{9,1},{17,25},{25,17},{2,10},{10... | collective-permute-start | bytes 147464 | tf_op jit(solution)/shard_map/ppermute | solution.py:43
  119.5 2.2 %collective-permute-done.29.refs_3_ = bf16[192,128]{1,0:T(8,128)(2,1)S(1)} collective-permute-done((bf16[192,128]{1,0:T(8,128)(2,1)}, bf16[192,128]{1,0:T(8,128)(2,1)S(1)}, u32[]{:S(2)}, u32[]{:S(2)}) %collective-permute-start.29) | collective-permute-done | bytes 49184 | tf_op jit(solution)/shard_map/ppermute | solution.py:43
  123.8 8.0 %cross.3 = (bf16[96,768]{1,0:T(8,128)(2,1)}, f32[192,128]{1,0:T(8,128)}) custom-call(bf16[16,12,256]{2,1,0:T(8,128)(2,1)} %reshape.47.codes_ref, bf16[192,128]{1,0:T(8,128)(2,1)} %next_sums.1.refs_0_, bf16[192,128]{1,0:T(8,128)(2,1)} %copy-done.22, bf16[192,128]{1,0:T(8,128)(2,1)} %copy-done.21, bf16[192,128]{1,0:T(8,128)(2,1)} %copy-done.20, ...), custom_call_target="tpu_custom_call" | custom-call | tf_op jit(solution)/shard_map/cross/pallas_call | solution.py:268
  131.8 2.1 %collective-permute-start.32 = (bf16[96,768]{1,0:T(8,128)(2,1)}, bf16[96,768]{1,0:T(8,128)(2,1)S(1)}, u32[]{:S(2)}, u32[]{:S(2)}) collective-permute-start(bf16[96,768]{1,0:T(8,128)(2,1)} %get-tuple-element.12), channel_id=1, source_target_pairs={{0,24},{8,16},{16,8},{24,0},{1,25},{9,17},{17,9},{25,1},{2,26},{10... | collective-permute-start | bytes 442376 | tf_op jit(solution)/shard_map/ppermute | solution.py:43
  133.9 2.3 %collective-permute-start.30 = (bf16[96,768]{1,0:T(8,128)(2,1)}, bf16[96,768]{1,0:T(8,128)(2,1)S(1)}, u32[]{:S(2)}, u32[]{:S(2)}) collective-permute-start(bf16[96,768]{1,0:T(8,128)(2,1)} %get-tuple-element.12), channel_id=1, source_target_pairs={{0,8},{8,0},{16,24},{24,16},{1,9},{9,1},{17,25},{25,17},{2,10},{10... | collective-permute-start | bytes 442376 | tf_op jit(solution)/shard_map/ppermute | solution.py:43
  136.3 4.5 %collective-permute-done.32 = bf16[96,768]{1,0:T(8,128)(2,1)S(1)} collective-permute-done((bf16[96,768]{1,0:T(8,128)(2,1)}, bf16[96,768]{1,0:T(8,128)(2,1)S(1)}, u32[]{:S(2)}, u32[]{:S(2)}) %collective-permute-start.32) | collective-permute-done | bytes 147488 | tf_op jit(solution)/shard_map/ppermute | solution.py:43
  140.7 6.0 %collective-permute-done.31 = bf16[96,768]{1,0:T(8,128)(2,1)S(1)} collective-permute-done((bf16[96,768]{1,0:T(8,128)(2,1)}, bf16[96,768]{1,0:T(8,128)(2,1)S(1)}, u32[]{:S(2)}, u32[]{:S(2)}) %collective-permute-start.31) | collective-permute-done | bytes 147488 | tf_op jit(solution)/shard_map/ppermute | solution.py:43
  151.3 4.2 %collective-permute-done.38.refs_6_ = bf16[96,768]{1,0:T(8,128)(2,1)S(1)} collective-permute-done((bf16[96,768]{1,0:T(8,128)(2,1)S(1)}, bf16[96,768]{1,0:T(8,128)(2,1)S(1)}, u32[]{:S(2)}, u32[]{:S(2)}) %collective-permute-start.38) | collective-permute-done | bytes 147488 | tf_op jit(solution)/shard_map/ppermute | solution.py:43
  155.5 1.6 collective-permute-done.36.refs_4_
  160.2 8.4 %final.1 = bf16[512,768]{1,0:T(8,128)(2,1)} custom-call(s32[1]{0:T(128)} %bitcast.place_ref, bf16[512,768]{1,0:T(8,128)(2,1)} %get-tuple-element.8.residual_ref, bf16[96,768]{1,0:T(8,128)(2,1)} %copy-done.4, bf16[96,768]{1,0:T(8,128)(2,1)} %copy-done.9, bf16[96,768]{1,0:T(8,128)(2,1)} %copy-done.8, bf16[96,768]{1,0:T(8,128)(2,1)} %collective-permute-done.35.refs_3_, ...), custom_call_target="tpu_custom_call" | custom-call | tf_op jit(solution)/shard_map/final/pallas_call | solution.py:349
  (121 shorter events, 31.7 us)
Async XLA Ops:
  6.8 13.0 %collective-permute-start.7 = (bf16[256,768]{1,0:T(8,128)(2,1)S(1)}, bf16[256,768]{1,0:T(8,128)(2,1)S(1)}, u32[]{:S(2)}, u32[]{:S(2)}) collective-permute-start(bf16[256,768]{1,0:T(8,128)(2,1)S(1)} %get-tuple-element.14.refs_1_.refs_5_.refs_9_.refs_6_), channel_id=1, source_target_pairs={{0,4},{1,5},{2,6},{3,7},{4,0},{5,1},{6,2},{7,3},{8,12},{9,13},{10,... | collective-permute-start | bytes 1179656 | tf_op jit(solution)/shard_map/ppermute | solution.py:43
  9.8 12.1 %collective-permute-start.3 = (bf16[256,768]{1,0:T(8,128)(2,1)S(1)}, bf16[256,768]{1,0:T(8,128)(2,1)}, u32[]{:S(2)}, u32[]{:S(2)}) collective-permute-start(bf16[256,768]{1,0:T(8,128)(2,1)S(1)} %get-tuple-element.14.refs_1_.refs_5_.refs_9_.refs_6_), channel_id=1, source_target_pairs={{0,2},{1,3},{2,0},{3,1},{4,6},{5,7},{6,4},{7,5},{8,10},{9,11},{10,... | collective-permute-start | bytes 1179656 | tf_op jit(solution)/shard_map/ppermute | solution.py:43
  11.3 12.2 %collective-permute-start.1 = (bf16[256,768]{1,0:T(8,128)(2,1)S(1)}, bf16[256,768]{1,0:T(8,128)(2,1)}, u32[]{:S(2)}, u32[]{:S(2)}) collective-permute-start(bf16[256,768]{1,0:T(8,128)(2,1)S(1)} %get-tuple-element.14.refs_1_.refs_5_.refs_9_.refs_6_), channel_id=1, source_target_pairs={{0,1},{1,0},{2,3},{3,2},{4,5},{5,4},{6,7},{7,6},{8,9},{9,8},{10,11... | collective-permute-start | bytes 1179656 | tf_op jit(solution)/shard_map/ppermute | solution.py:43
  11.3 19.1 %collective-permute-start.2 = (bf16[256,768]{1,0:T(8,128)(2,1)S(1)}, bf16[256,768]{1,0:T(8,128)(2,1)}, u32[]{:S(2)}, u32[]{:S(2)}) collective-permute-start(bf16[256,768]{1,0:T(8,128)(2,1)S(1)} %get-tuple-element.15.refs_0_.refs_4_.refs_8_.refs_5_), channel_id=1, source_target_pairs={{0,2},{1,3},{2,0},{3,1},{4,6},{5,7},{6,4},{7,5},{8,10},{9,11},{10,... | collective-permute-start | bytes 1179656 | tf_op jit(solution)/shard_map/ppermute | solution.py:43
  11.8 23.3 %collective-permute-start.6 = (bf16[256,768]{1,0:T(8,128)(2,1)S(1)}, bf16[256,768]{1,0:T(8,128)(2,1)}, u32[]{:S(2)}, u32[]{:S(2)}) collective-permute-start(bf16[256,768]{1,0:T(8,128)(2,1)S(1)} %get-tuple-element.15.refs_0_.refs_4_.refs_8_.refs_5_), channel_id=1, source_target_pairs={{0,4},{1,5},{2,6},{3,7},{4,0},{5,1},{6,2},{7,3},{8,12},{9,13},{10,... | collective-permute-start | bytes 1179656 | tf_op jit(solution)/shard_map/ppermute | solution.py:43
  13.5 19.5 %all-to-all-start = ((bf16[8,12,512]{2,1,0:T(8,128)(2,1)}), bf16[8,12,512]{2,1,0:T(8,128)(2,1)}, u32[]{:S(2)}, u32[]{:S(2)}) async-start(bf16[8,12,512]{2,1,0:T(8,128)(2,1)} %reshape.46), calls=%async_computation | async-start | bytes 262144 | tf_op jit(solution)/shard_map/all_to_all | solution.py:397
  19.8 15.4 %collective-permute-start = (bf16[256,768]{1,0:T(8,128)(2,1)S(1)}, bf16[256,768]{1,0:T(8,128)(2,1)}, u32[]{:S(2)}, u32[]{:S(2)}) collective-permute-start(bf16[256,768]{1,0:T(8,128)(2,1)S(1)} %get-tuple-element.15.refs_0_.refs_4_.refs_8_.refs_5_), channel_id=1, source_target_pairs={{0,1},{1,0},{2,3},{3,2},{4,5},{5,4},{6,7},{7,6},{8,9},{9,8},{10,11... | collective-permute-start | bytes 1179656 | tf_op jit(solution)/shard_map/ppermute | solution.py:43
  22.0 16.8 %collective-permute-start.11 = (bf16[256,768]{1,0:T(8,128)(2,1)S(1)}, bf16[256,768]{1,0:T(8,128)(2,1)}, u32[]{:S(2)}, u32[]{:S(2)}) collective-permute-start(bf16[256,768]{1,0:T(8,128)(2,1)S(1)} %collective-permute-done.7.refs_9_.refs_13_.refs_17_.refs_14_), channel_id=1, source_target_pairs={{0,2},{1,3},{2,0},{3,1},{4,6},{5,7},{6,4},{7,5},{8,10},{9,11},{10,... | collective-permute-start | bytes 1179656 | tf_op jit(solution)/shard_map/ppermute | solution.py:43
  23.5 15.3 %collective-permute-start.9 = (bf16[256,768]{1,0:T(8,128)(2,1)S(1)}, bf16[256,768]{1,0:T(8,128)(2,1)}, u32[]{:S(2)}, u32[]{:S(2)}) collective-permute-start(bf16[256,768]{1,0:T(8,128)(2,1)S(1)} %collective-permute-done.7.refs_9_.refs_13_.refs_17_.refs_14_), channel_id=1, source_target_pairs={{0,1},{1,0},{2,3},{3,2},{4,5},{5,4},{6,7},{7,6},{8,9},{9,8},{10,11... | collective-permute-start | bytes 1179656 | tf_op jit(solution)/shard_map/ppermute | solution.py:43
  30.4 8.9 %collective-permute-start.10 = (bf16[256,768]{1,0:T(8,128)(2,1)}, bf16[256,768]{1,0:T(8,128)(2,1)}, u32[]{:S(2)}, u32[]{:S(2)}) collective-permute-start(bf16[256,768]{1,0:T(8,128)(2,1)} %collective-permute-done.2.refs_4_.refs_8_.refs_12_.refs_9_), channel_id=1, source_target_pairs={{0,4},{1,5},{2,6},{3,7},{4,0},{5,1},{6,2},{7,3},{8,12},{9,13},{10,... | collective-permute-start | bytes 1179656 | tf_op jit(solution)/shard_map/ppermute | solution.py:43
  35.1 7.5 %collective-permute-start.4 = (bf16[256,768]{1,0:T(8,128)(2,1)}, bf16[256,768]{1,0:T(8,128)(2,1)}, u32[]{:S(2)}, u32[]{:S(2)}) collective-permute-start(bf16[256,768]{1,0:T(8,128)(2,1)} %collective-permute-done.2.refs_4_.refs_8_.refs_12_.refs_9_), channel_id=1, source_target_pairs={{0,1},{1,0},{2,3},{3,2},{4,5},{5,4},{6,7},{7,6},{8,9},{9,8},{10,11... | collective-permute-start | bytes 1179656 | tf_op jit(solution)/shard_map/ppermute | solution.py:43
  35.1 7.5 %collective-permute-start.5 = (bf16[256,768]{1,0:T(8,128)(2,1)}, bf16[256,768]{1,0:T(8,128)(2,1)}, u32[]{:S(2)}, u32[]{:S(2)}) collective-permute-start(bf16[256,768]{1,0:T(8,128)(2,1)} %collective-permute-done.3.refs_5_.refs_9_.refs_13_.refs_10_), channel_id=1, source_target_pairs={{0,1},{1,0},{2,3},{3,2},{4,5},{5,4},{6,7},{7,6},{8,9},{9,8},{10,11... | collective-permute-start | bytes 1179656 | tf_op jit(solution)/shard_map/ppermute | solution.py:43
  54.4 6.6 %collective-permute-start.16 = (bf16[240,128]{1,0:T(8,128)(2,1)}, bf16[240,128]{1,0:T(8,128)(2,1)S(1)}, u32[]{:S(2)}, u32[]{:S(2)}) collective-permute-start(bf16[240,128]{1,0:T(8,128)(2,1)} %sums.1.refs_0_), channel_id=1, source_target_pairs={{0,24},{8,16},{16,8},{24,0},{1,25},{9,17},{17,9},{25,1},{2,26},{10... | collective-permute-start | bytes 184328 | tf_op jit(solution)/shard_map/ppermute | solution.py:43
  58.1 5.9 %collective-permute-start.15 = (bf16[240,128]{1,0:T(8,128)(2,1)}, bf16[240,128]{1,0:T(8,128)(2,1)S(1)}, u32[]{:S(2)}, u32[]{:S(2)}) collective-permute-start(bf16[240,128]{1,0:T(8,128)(2,1)} %sums.1.refs_0_), channel_id=1, source_target_pairs={{0,16},{8,24},{16,0},{24,8},{1,17},{9,25},{17,1},{25,9},{2,18},{10... | collective-permute-start | bytes 184328 | tf_op jit(solution)/shard_map/ppermute | solution.py:43
  58.1 5.9 %collective-permute-start.14 = (bf16[240,128]{1,0:T(8,128)(2,1)}, bf16[240,128]{1,0:T(8,128)(2,1)S(1)}, u32[]{:S(2)}, u32[]{:S(2)}) collective-permute-start(bf16[240,128]{1,0:T(8,128)(2,1)} %sums.1.refs_0_), channel_id=1, source_target_pairs={{0,8},{8,0},{16,24},{24,16},{1,9},{9,1},{17,25},{25,17},{2,10},{10... | collective-permute-start | bytes 184328 | tf_op jit(solution)/shard_map/ppermute | solution.py:43
  73.3 8.9 %collective-permute-start.19 = (bf16[96,768]{1,0:T(8,128)(2,1)}, bf16[96,768]{1,0:T(8,128)(2,1)S(1)}, u32[]{:S(2)}, u32[]{:S(2)}) collective-permute-start(bf16[96,768]{1,0:T(8,128)(2,1)} %get-tuple-element.10), channel_id=1, source_target_pairs={{0,24},{8,16},{16,8},{24,0},{1,25},{9,17},{17,9},{25,1},{2,26},{10... | collective-permute-start | bytes 442376 | tf_op jit(solution)/shard_map/ppermute | solution.py:43
  75.8 12.7 %collective-permute-start.18 = (bf16[96,768]{1,0:T(8,128)(2,1)}, bf16[96,768]{1,0:T(8,128)(2,1)S(1)}, u32[]{:S(2)}, u32[]{:S(2)}) collective-permute-start(bf16[96,768]{1,0:T(8,128)(2,1)} %get-tuple-element.10), channel_id=1, source_target_pairs={{0,16},{8,24},{16,0},{24,8},{1,17},{9,25},{17,1},{25,9},{2,18},{10... | collective-permute-start | bytes 442376 | tf_op jit(solution)/shard_map/ppermute | solution.py:43
  75.8 12.7 %collective-permute-start.17 = (bf16[96,768]{1,0:T(8,128)(2,1)}, bf16[96,768]{1,0:T(8,128)(2,1)S(1)}, u32[]{:S(2)}, u32[]{:S(2)}) collective-permute-start(bf16[96,768]{1,0:T(8,128)(2,1)} %get-tuple-element.10), channel_id=1, source_target_pairs={{0,8},{8,0},{16,24},{24,16},{1,9},{9,1},{17,25},{25,17},{2,10},{10... | collective-permute-start | bytes 442376 | tf_op jit(solution)/shard_map/ppermute | solution.py:43
  89.6 7.4 %collective-permute-start.25 = (bf16[96,768]{1,0:T(8,128)(2,1)S(1)}, bf16[96,768]{1,0:T(8,128)(2,1)S(1)}, u32[]{:S(2)}, u32[]{:S(2)}) collective-permute-start(bf16[96,768]{1,0:T(8,128)(2,1)S(1)} %add_convert_fusion.1.refs_0_), channel_id=1, source_target_pairs={{0,6},{1,7},{2,4},{3,5},{4,2},{5,3},{6,0},{7,1},{8,14},{9,15},{10,... | collective-permute-start | bytes 442376 | tf_op jit(solution)/shard_map/ppermute | solution.py:43
  91.1 7.4 %collective-permute-start.23 = (bf16[96,768]{1,0:T(8,128)(2,1)S(1)}, bf16[96,768]{1,0:T(8,128)(2,1)S(1)}, u32[]{:S(2)}, u32[]{:S(2)}) collective-permute-start(bf16[96,768]{1,0:T(8,128)(2,1)S(1)} %add_convert_fusion.1.refs_0_), channel_id=1, source_target_pairs={{0,4},{1,5},{2,6},{3,7},{4,0},{5,1},{6,2},{7,3},{8,12},{9,13},{10,... | collective-permute-start | bytes 442376 | tf_op jit(solution)/shard_map/ppermute | solution.py:43
  92.6 5.9 %collective-permute-start.21 = (bf16[96,768]{1,0:T(8,128)(2,1)S(1)}, bf16[96,768]{1,0:T(8,128)(2,1)S(1)}, u32[]{:S(2)}, u32[]{:S(2)}) collective-permute-start(bf16[96,768]{1,0:T(8,128)(2,1)S(1)} %add_convert_fusion.1.refs_0_), channel_id=1, source_target_pairs={{0,2},{1,3},{2,0},{3,1},{4,6},{5,7},{6,4},{7,5},{8,10},{9,11},{10,... | collective-permute-start | bytes 442376 | tf_op jit(solution)/shard_map/ppermute | solution.py:43
  93.1 5.9 %collective-permute-start.20 = (bf16[96,768]{1,0:T(8,128)(2,1)S(1)}, bf16[96,768]{1,0:T(8,128)(2,1)S(1)}, u32[]{:S(2)}, u32[]{:S(2)}) collective-permute-start(bf16[96,768]{1,0:T(8,128)(2,1)S(1)} %add_convert_fusion.1.refs_0_), channel_id=1, source_target_pairs={{0,1},{1,0},{2,3},{3,2},{4,5},{5,4},{6,7},{7,6},{8,9},{9,8},{10,11... | collective-permute-start | bytes 442376 | tf_op jit(solution)/shard_map/ppermute | solution.py:43
  115.0 6.6 %collective-permute-start.29 = (bf16[192,128]{1,0:T(8,128)(2,1)}, bf16[192,128]{1,0:T(8,128)(2,1)S(1)}, u32[]{:S(2)}, u32[]{:S(2)}) collective-permute-start(bf16[192,128]{1,0:T(8,128)(2,1)} %next_sums.1.refs_0_), channel_id=1, source_target_pairs={{0,24},{8,16},{16,8},{24,0},{1,25},{9,17},{17,9},{25,1},{2,26},{10... | collective-permute-start | bytes 147464 | tf_op jit(solution)/shard_map/ppermute | solution.py:43
  117.1 6.0 %collective-permute-start.28 = (bf16[192,128]{1,0:T(8,128)(2,1)}, bf16[192,128]{1,0:T(8,128)(2,1)S(1)}, u32[]{:S(2)}, u32[]{:S(2)}) collective-permute-start(bf16[192,128]{1,0:T(8,128)(2,1)} %next_sums.1.refs_0_), channel_id=1, source_target_pairs={{0,16},{8,24},{16,0},{24,8},{1,17},{9,25},{17,1},{25,9},{2,18},{10... | collective-permute-start | bytes 147464 | tf_op jit(solution)/shard_map/ppermute | solution.py:43
  117.1 6.0 %collective-permute-start.27 = (bf16[192,128]{1,0:T(8,128)(2,1)}, bf16[192,128]{1,0:T(8,128)(2,1)S(1)}, u32[]{:S(2)}, u32[]{:S(2)}) collective-permute-start(bf16[192,128]{1,0:T(8,128)(2,1)} %next_sums.1.refs_0_), channel_id=1, source_target_pairs={{0,8},{8,0},{16,24},{24,16},{1,9},{9,1},{17,25},{25,17},{2,10},{10... | collective-permute-start | bytes 147464 | tf_op jit(solution)/shard_map/ppermute | solution.py:43
  131.8 8.9 %collective-permute-start.32 = (bf16[96,768]{1,0:T(8,128)(2,1)}, bf16[96,768]{1,0:T(8,128)(2,1)S(1)}, u32[]{:S(2)}, u32[]{:S(2)}) collective-permute-start(bf16[96,768]{1,0:T(8,128)(2,1)} %get-tuple-element.12), channel_id=1, source_target_pairs={{0,24},{8,16},{16,8},{24,0},{1,25},{9,17},{17,9},{25,1},{2,26},{10... | collective-permute-start | bytes 442376 | tf_op jit(solution)/shard_map/ppermute | solution.py:43
  133.9 12.8 %collective-permute-start.31 = (bf16[96,768]{1,0:T(8,128)(2,1)}, bf16[96,768]{1,0:T(8,128)(2,1)S(1)}, u32[]{:S(2)}, u32[]{:S(2)}) collective-permute-start(bf16[96,768]{1,0:T(8,128)(2,1)} %get-tuple-element.12), channel_id=1, source_target_pairs={{0,16},{8,24},{16,0},{24,8},{1,17},{9,25},{17,1},{25,9},{2,18},{10... | collective-permute-start | bytes 442376 | tf_op jit(solution)/shard_map/ppermute | solution.py:43
  133.9 12.8 %collective-permute-start.30 = (bf16[96,768]{1,0:T(8,128)(2,1)}, bf16[96,768]{1,0:T(8,128)(2,1)S(1)}, u32[]{:S(2)}, u32[]{:S(2)}) collective-permute-start(bf16[96,768]{1,0:T(8,128)(2,1)} %get-tuple-element.12), channel_id=1, source_target_pairs={{0,8},{8,0},{16,24},{24,16},{1,9},{9,1},{17,25},{25,17},{2,10},{10... | collective-permute-start | bytes 442376 | tf_op jit(solution)/shard_map/ppermute | solution.py:43
  147.7 7.7 %collective-permute-start.38 = (bf16[96,768]{1,0:T(8,128)(2,1)S(1)}, bf16[96,768]{1,0:T(8,128)(2,1)S(1)}, u32[]{:S(2)}, u32[]{:S(2)}) collective-permute-start(bf16[96,768]{1,0:T(8,128)(2,1)S(1)} %add_convert_fusion.refs_0_), channel_id=1, source_target_pairs={{0,6},{1,7},{2,4},{3,5},{4,2},{5,3},{6,0},{7,1},{8,14},{9,15},{10,... | collective-permute-start | bytes 442376 | tf_op jit(solution)/shard_map/ppermute | solution.py:43
  149.2 7.9 %collective-permute-start.36 = (bf16[96,768]{1,0:T(8,128)(2,1)S(1)}, bf16[96,768]{1,0:T(8,128)(2,1)S(1)}, u32[]{:S(2)}, u32[]{:S(2)}) collective-permute-start(bf16[96,768]{1,0:T(8,128)(2,1)S(1)} %add_convert_fusion.refs_0_), channel_id=1, source_target_pairs={{0,4},{1,5},{2,6},{3,7},{4,0},{5,1},{6,2},{7,3},{8,12},{9,13},{10,... | collective-permute-start | bytes 442376 | tf_op jit(solution)/shard_map/ppermute | solution.py:43
  150.1 7.1 %collective-permute-start.34 = (bf16[96,768]{1,0:T(8,128)(2,1)S(1)}, bf16[96,768]{1,0:T(8,128)(2,1)S(1)}, u32[]{:S(2)}, u32[]{:S(2)}) collective-permute-start(bf16[96,768]{1,0:T(8,128)(2,1)S(1)} %add_convert_fusion.refs_0_), channel_id=1, source_target_pairs={{0,2},{1,3},{2,0},{3,1},{4,6},{5,7},{6,4},{7,5},{8,10},{9,11},{10,... | collective-permute-start | bytes 442376 | tf_op jit(solution)/shard_map/ppermute | solution.py:43
  151.3 8.3 %collective-permute-start.33 = (bf16[96,768]{1,0:T(8,128)(2,1)S(1)}, bf16[96,768]{1,0:T(8,128)(2,1)S(1)}, u32[]{:S(2)}, u32[]{:S(2)}) collective-permute-start(bf16[96,768]{1,0:T(8,128)(2,1)S(1)} %add_convert_fusion.refs_0_), channel_id=1, source_target_pairs={{0,1},{1,0},{2,3},{3,2},{4,5},{5,4},{6,7},{7,6},{8,9},{9,8},{10,11... | collective-permute-start | bytes 442376 | tf_op jit(solution)/shard_map/ppermute | solution.py:43
  (32 other events, 198.5 us)

commit v2 on v1

v2 whole, which is shorter than its diff:
```python
import functools
import math

import jax
import jax.numpy as jnp
from jax import lax
from jax.experimental import pallas as pl
from jax.experimental.pallas import tpu as pltpu
from jax.sharding import PartitionSpec as P

K = 256
ALTS = 2
LO = 8
HI = K // LO
SUB = 8
PACK = 128 // HI
EPSILON = 1e-06
MIB = 1024 * 1024
BAND = 256

F32 = jnp.float32
BF16 = jnp.bfloat16
NT = (((1,), (1,)), ((), ()))
NN = (((1,), (0,)), ((), ()))
TN = (((0,), (0,)), ((), ()))


def mm(a, b, dims=NN):
    return lax.dot_general(a, b, dims, preferred_element_type=F32)


def vmem_spec():
    return pl.BlockSpec(memory_space=pltpu.VMEM)


def smem_spec():
    return pl.BlockSpec(memory_space=pltpu.SMEM)


def cost(us):
    return pl.CostEstimate(flops=int(us * 1e9), bytes_accessed=0, transcendentals=0)


def params(*arrays):
    held = sum(math.prod(a.shape) * a.dtype.itemsize for a in arrays)
    return pltpu.CompilerParams(vmem_limit_bytes=held + 12 * MIB)


def swap(x, axis, size, bits):
    return lax.ppermute(x, axis, [(i, i ^ bits) for i in range(size)])


def residual_kernel(vectors_ref, centroids_ref, ids_ref, *outs):
    lists = centroids_ref.shape[0]
    rows = vectors_ref.shape[0]
    half = rows // 2
    local = lax.rem(ids_ref[...], lists)
    level = lax.broadcasted_iota(jnp.int32, (lists, rows), 0)
    table = jnp.where(level == local, 1.0, 0.0).astype(BF16)
    center = centroids_ref[...]
    first = center.astype(BF16)
    rest = center - first.astype(F32)
    second = rest.astype(BF16)
    third = (rest - second.astype(F32)).astype(BF16)
    for h, out_ref in enumerate(outs):
        part = table[:, h * half : (h + 1) * half]
        picked = mm(part, first, TN) + mm(part, second, TN) + mm(part, third, TN)
        out_ref[...] = (vectors_ref[h * half : (h + 1) * half, :].astype(F32) - picked).astype(BF16)


def residual_call(vectors, centroids, ids):
    rows, width = vectors.shape
    return pl.pallas_call(
        residual_kernel,
        out_shape=(jax.ShapeDtypeStruct((rows // 2, width), BF16),) * 2,
        in_specs=[vmem_spec()] * 3,
        out_specs=(vmem_spec(),) * 2,
        compiler_params=params(),
        name="residual",
    )(vectors, centroids, ids.reshape(1, rows))


def packs_of(owned):
    return [range(first, min(first + PACK, owned)) for first in range(0, owned, PACK)]


def hi_table(hi, pack):
    rows = hi.shape[1]
    level = lax.broadcasted_iota(jnp.int32, (HI, rows), 0)
    parts = [jnp.where(level == hi[m : m + 1, :], 1.0, 0.0) for m in pack]
    parts += [jnp.zeros((HI, rows), F32)] * (PACK - len(pack))
    return jnp.concatenate(parts, axis=0).astype(BF16)


def lane_owner(rows):
    return lax.broadcasted_iota(jnp.int32, (rows, 128), 1) // HI


def diagonal(wide, block):
    owner = lane_owner(block)
    total = jnp.zeros((block, 128), F32)
    for i in range(wide.shape[0] // block):
        total = jnp.where(owner == i, wide[i * block : (i + 1) * block, :], total)
    return total


def pack_sums(rotated, codes, pack, with_counts):
    rows = codes.shape[1]
    hi, lo = codes >> 3, codes & 7
    table = hi_table(hi, pack)
    parts = []
    for m in pack:
        value = rotated[m * SUB : (m + 1) * SUB, :]
        low = jnp.broadcast_to(lo[m : m + 1, :], (SUB, rows))
        parts += [jnp.where(low == level, value, 0.0) for level in range(LO)]
    if with_counts:
        low_level = lax.broadcasted_iota(jnp.int32, (LO, rows), 0)
        parts += [jnp.where(low_level == lo[m : m + 1, :], 1.0, 0.0) for m in pack]
    return mm(jnp.concatenate(parts, axis=0).astype(BF16), table, NT)


def pack_layout(owned, with_counts):
    packs = len(packs_of(owned))
    base, height = packs * LO * SUB, packs * LO
    return base, height, base + (-(-2 * height // 16) * 16 if with_counts else 0)


def write_sums(sums, counts, owned, out_ref):
    base, height, total = pack_layout(owned, counts is not None)
    out_ref[:base, :] = sums.astype(BF16)
    if counts is not None:
        above = jnp.floor(counts * (1.0 / 256.0))
        pieces = [above, counts - above * 256.0]
        pad = total - base - 2 * height
        pieces += [jnp.zeros((pad, 128), F32)] if pad else []
        out_ref[base:, :] = jnp.concatenate(pieces, axis=0).astype(BF16)


def pack_diagonals(totals, owned, with_counts):
    block = LO * SUB
    sums, counts = [], []
    for total, pack in zip(totals, packs_of(owned)):
        size = len(pack)
        sums.append(diagonal(total[: size * block], block))
        if with_counts:
            counts.append(diagonal(total[size * block :], LO))
    return jnp.concatenate(sums, axis=0), jnp.concatenate(counts, axis=0) if with_counts else None


def tree(values):
    while len(values) > 1:
        values = [values[i] + values[i + 1] for i in range(0, len(values), 2)]
    return values[0]


def merge_parts(parts, owned, with_counts):
    base, height, unused = pack_layout(owned, with_counts)
    whole = tree([ref[...].astype(F32) for ref in parts])
    if not with_counts:
        return whole, None
    return whole[:base], whole[base : base + height] * 256.0 + whole[base + height : base + 2 * height]


def code_rows(rows):
    return rows // 128 * 16


def write_codes(codes, out_ref, at):
    owned, rows = codes.shape
    filled = jnp.concatenate([codes, jnp.zeros((16 - owned, rows), F32)], axis=0).astype(BF16)
    for c in range(rows // 128):
        out_ref[at + 16 * c : at + 16 * c + 16, :] = filled[:, 128 * c : 128 * c + 128]


def local_sums_kernel(size, place_ref, rotation_ref, codes_ref, upper_ref, lower_ref, *refs):
    outs, turned, staged = refs[:2], refs[2], refs[3]
    subspaces = codes_ref.shape[0]
    owned = subspaces // size
    base = pack_layout(owned, True)[2]
    residual = jnp.concatenate([upper_ref[...], lower_ref[...]], axis=0)
    rotated = mm(residual, rotation_ref[...].astype(BF16)).astype(BF16).astype(F32)
    turned[...] = rotated.T
    for j in range(size):
        staged[j, :owned, :] = codes_ref[j * owned : (j + 1) * owned, :]
    for k in range(size):
        other = place_ref[0] ^ k
        codes = staged[other][:owned]
        value = turned[pl.ds(pl.multiple_of(other * (owned * SUB), 8), owned * SUB), :]
        totals = [pack_sums(value, codes, pack, True) for pack in packs_of(owned)]
        sums, counts = pack_diagonals(totals, owned, True)
        slot = outs[k % 2].at[k // 2]
        write_sums(sums, counts, owned, slot.at[:base])
        write_codes(codes.astype(F32), slot, base)


def local_sums_call(place, rotation, codes, upper, lower, size):
    subspaces, rows = codes.shape
    owned = subspaces // size
    height = -(-owned // 8) * 8
    shape = jax.ShapeDtypeStruct((size // 2, pack_layout(owned, True)[2] + code_rows(rows), 128), BF16)
    return pl.pallas_call(
        functools.partial(local_sums_kernel, size),
        out_shape=(shape,) * 2,
        in_specs=[smem_spec()] + [vmem_spec()] * 4,
        out_specs=(vmem_spec(),) * 2,
        scratch_shapes=[pltpu.VMEM((rotation.shape[1], rows), F32), pltpu.VMEM((size, height, rows), jnp.int32)],
        compiler_params=params(rotation),
        cost_estimate=cost(4),
        name="local_sums",
    )(place, rotation, codes, upper, lower)


def merge_cores_kernel(owned, even_ref, came_ref, *outs):
    base = pack_layout(owned, True)[2]
    length = even_ref.shape[1] - base
    for i, out_ref in enumerate(outs):
        sums, counts = merge_parts([even_ref.at[i], came_ref.at[i]], owned, True)
        write_sums(sums, counts, owned, out_ref.at[:base])
        out_ref[base : base + length, :] = even_ref[i, base:, :]
        out_ref[base + length :, :] = came_ref[i, base:, :]


def merge_cores_call(even, came, owned):
    slots, height, lanes = even.shape
    shape = jax.ShapeDtypeStruct((2 * height - pack_layout(owned, True)[2], lanes), BF16)
    return pl.pallas_call(
        functools.partial(merge_cores_kernel, owned),
        out_shape=(shape,) * slots,
        in_specs=[vmem_spec()] * 2,
        out_specs=(vmem_spec(),) * slots,
        compiler_params=params(),
        cost_estimate=cost(1),
        name="merge_cores",
    )(even, came)


def merge_chips_kernel(owned, *refs):
    parts, (out_ref, codes_ref) = refs[:-2], refs[-2:]
    base = pack_layout(owned, True)[2]
    sums, counts = merge_parts(parts, owned, True)
    write_sums(sums, counts, owned, out_ref)
    length = (parts[0].shape[0] - base) // 2
    for i, part in enumerate(parts):
        for core in range(2):
            for c in range(length // 16):
                at = base + core * length + 16 * c
                piece = part[at : at + 16, :].astype(F32)
                codes_ref[2 * i + core, :, 128 * c : 128 * c + 128] = piece[:owned].astype(jnp.int32)


def merge_chips_call(parts, owned, rows):
    size = 2 * len(parts)
    return pl.pallas_call(
        functools.partial(merge_chips_kernel, owned),
        out_shape=(
            jax.ShapeDtypeStruct((pack_layout(owned, True)[2], 128), BF16),
            jax.ShapeDtypeStruct((size, owned, rows), jnp.int32),
        ),
        in_specs=[vmem_spec()] * len(parts),
        out_specs=(vmem_spec(),) * 2,
        compiler_params=params(),
        cost_estimate=cost(1),
        name="merge_chips",
    )(*parts)


def spans_of(size):
    step = min(2, size)
    return [range(first, first + step) for first in range(0, size, step)]


def span_codes(codes_ref, span):
    return jnp.concatenate([codes_ref[k] for k in span], axis=1)


def span_rows(chunks, span):
    return jnp.concatenate([chunks[2 * k + h][...] for k in span for h in range(2)], axis=0)


def cross_kernel(size, groups, with_counts, total_rows, codes_ref, *refs):
    sums, refs = refs[:groups], refs[groups:]
    owned = codes_ref.shape[1]
    packs = packs_of(owned)
    block = LO * SUB
    if with_counts:
        chunks, (cross_ref, counts_ref) = refs[: 2 * size], refs[2 * size :]
    else:
        counts_in, chunks, (cross_ref, book_ref) = refs[0], refs[1 : 2 * size + 1], refs[2 * size + 1 :]
    everything, counts = merge_parts(sums, owned, with_counts)
    if with_counts:
        counts_ref[...] = counts
    else:
        counts = counts_in[...]
    books = []
    for g in range(len(packs)):
        rows = []
        for level in range(LO):
            at = g * block + level * SUB
            rows.append(everything[at : at + SUB] / (counts[g * LO + level : g * LO + level + 1] + 1.0))
        book = jnp.concatenate(rows, axis=0)
        if not with_counts:
            book_ref[g * block : (g + 1) * block, :] = book
        books.append(book)
    owner = lane_owner(block)
    wide = [
        jnp.concatenate([jnp.where(owner == i, book, 0.0) for i in range(len(pack))], axis=0).astype(BF16)
        for book, pack in zip(books, packs)
    ]
    total = None
    for span in spans_of(size):
        codes = span_codes(codes_ref, span)
        hi, lo = codes >> 3, codes & 7
        rows = codes.shape[1]
        rebuilt = []
        for g, pack in enumerate(packs):
            spread = mm(wide[g], hi_table(hi, pack))
            for j, m in enumerate(pack):
                low = jnp.broadcast_to(lo[m : m + 1, :], (SUB, rows))
                at = j * block
                value = spread[at : at + SUB]
                for level in range(1, LO):
                    value = jnp.where(low == level, spread[at + level * SUB : at + (level + 1) * SUB], value)
                rebuilt.append(value)
        part = mm(jnp.concatenate(rebuilt, axis=0).astype(BF16), span_rows(chunks, span))
        total = part if total is None else total + part
    cross_ref[...] = (total * (1.0 / total_rows)).astype(BF16)


def cross_call(codes, sums, counts, chunks, total_rows):
    size, owned, unused = codes.shape
    packs = len(packs_of(owned))
    width = chunks[0].shape[1]
    with_counts = counts is None
    extra = jax.ShapeDtypeStruct((packs * LO * (1 if with_counts else SUB), 128), F32)
    small = list(sums) + ([] if with_counts else [counts])
    return pl.pallas_call(
        functools.partial(cross_kernel, size, len(sums), with_counts, total_rows),
        out_shape=(jax.ShapeDtypeStruct((owned * SUB, width), BF16), extra),
        in_specs=[vmem_spec()] * (1 + len(small) + len(chunks)),
        out_specs=(vmem_spec(), vmem_spec()),
        compiler_params=params(*chunks),
        name="cross",
    )(codes, *small, *chunks)


def bands(x):
    return [x[i : i + BAND] for i in range(0, x.shape[0], BAND)]


def first_step(xb):
    steps = []
    square = None
    for band in bands(xb):
        gram = mm(band, xb, NT)
        part = jnp.sum(gram * gram, keepdims=True)
        square = part if square is None else square + part
        steps.append(mm(gram.astype(BF16), xb))
    norm_square = jnp.sqrt(square + EPSILON)
    scale = lax.rsqrt(norm_square)
    less = 0.5 * scale / norm_square
    return [(1.5 * scale) * band.astype(F32) - less * step for band, step in zip(bands(xb), steps)]


def join(parts):
    if parts[0].shape[0] % 16 == 0:
        return jnp.concatenate(parts, axis=0)
    return jnp.concatenate([p.astype(F32) for p in parts], axis=0).astype(BF16)


def next_sums_kernel(size, codes_ref, *refs):
    parts, chunks, out_ref = refs[:size], refs[size : 3 * size], refs[3 * size]
    owned = codes_ref.shape[1]
    height = parts[0].shape[0]
    x = first_step(join([ref[...] for ref in parts]))
    xb = jnp.concatenate([band.astype(BF16) for band in x], axis=0)
    mine = x[0][:height]
    gram = mm(mine.astype(BF16), xb, NT)
    rotation_rows = (1.5 * mine - 0.5 * mm(gram.astype(BF16), xb)).astype(BF16)
    totals = None
    for span in spans_of(size):
        rotated = mm(rotation_rows, span_rows(chunks, span), NT).astype(BF16).astype(F32)
        codes = span_codes(codes_ref, span)
        more = [pack_sums(rotated, codes, pack, False) for pack in packs_of(owned)]
        totals = more if totals is None else [a + b for a, b in zip(totals, more)]
    write_sums(pack_diagonals(totals, owned, False)[0], None, owned, out_ref)


def next_sums_call(codes, blocks, chunks):
    size, owned, unused = codes.shape
    return pl.pallas_call(
        functools.partial(next_sums_kernel, size),
        out_shape=jax.ShapeDtypeStruct((pack_layout(owned, False)[2], 128), BF16),
        in_specs=[vmem_spec()] * (1 + len(blocks) + len(chunks)),
        out_specs=vmem_spec(),
        compiler_params=params(*chunks),
        name="next_sums",
    )(codes, *blocks, *chunks)


def final_kernel(size, place_ref, upper_ref, lower_ref, *refs):
    parts, out_ref, whole = refs[:size], refs[size], refs[size + 1]
    height = parts[0].shape[0]
    for k, ref in enumerate(parts):
        at = pl.multiple_of((place_ref[0] ^ k) * height, 16 if whole.dtype == BF16 else 8)
        whole[pl.ds(at, height), :] = ref[...].astype(whole.dtype)
    x = first_step(whole[...].astype(BF16))
    xb = jnp.concatenate([band.astype(BF16) for band in x], axis=0)
    residual = jnp.concatenate([upper_ref[...], lower_ref[...]], axis=0)
    for i, band in enumerate(x):
        gram = mm(xb[i * BAND : (i + 1) * BAND], xb, NT).astype(BF16)
        rotation = (1.5 * band - 0.5 * mm(gram, xb)).astype(BF16)
        out_ref[:, i * BAND : (i + 1) * BAND] = mm(residual, rotation, NT).astype(BF16)


def final_call(place, upper, lower, blocks):
    rows, width = upper.shape
    kind = BF16 if blocks[0].shape[0] % 16 == 0 else F32
    return pl.pallas_call(
        functools.partial(final_kernel, len(blocks)),
        out_shape=jax.ShapeDtypeStruct((2 * rows, width), BF16),
        in_specs=[smem_spec()] + [vmem_spec()] * (2 + len(blocks)),
        out_specs=vmem_spec(),
        scratch_shapes=[pltpu.VMEM((width, width), kind)],
        compiler_params=params(),
        name="final",
    )(place, upper, lower, *blocks)


def gather_rows(halves, size):
    bits = [1 << b for b in range(1, size.bit_length() - 1)]
    held = [{0: half} for half in halves]
    for h in range(2):
        held[h][1] = swap(held[h][0], "within", size, 1)
    for step in range(len(bits)):
        for h in range(2):
            bit = bits[step] if h == 0 else bits[len(bits) - 1 - step]
            for k in [k for k in held[h] if k % 2 == 0]:
                held[h][k ^ bit] = swap(held[h][k], "within", size, bit)
    for h in range(2):
        for k in [k for k in held[h] if k % 2 == 0 and k]:
            held[h][k ^ 1] = swap(held[h][k], "within", size, 1)
    return [held[h][k] for k in range(size) for h in range(2)]


def gather_group(x, size):
    blocks = {k: swap(x, "within", size, k) if k else x for k in range(0, size, 2)}
    for k in list(blocks):
        blocks[k ^ 1] = swap(blocks[k], "within", size, 1)
    return [blocks[k] for k in range(size)]


def scatter_sums(even, odd, owned, rows, size):
    merged = merge_cores_call(even, swap(odd, "within", size, 1), owned)
    parts = [merged[0]] + [swap(merged[k // 2], "within", size, k) for k in range(2, size, 2)]
    return merge_chips_call(parts, owned, rows)


def everywhere(x, size):
    return [x] + [swap(x, "group", size, k) for k in range(1, size)]


def per_device(vectors, centroids, list_ids, codes, rotation):
    groups = lax.axis_size("group")
    size = lax.axis_size("within")
    rows, width = vectors.shape
    owned = codes.shape[1] // size
    total_rows = rows * size * groups
    place = lax.axis_index("within").astype(jnp.int32).reshape(1)
    upper, lower = residual_call(vectors, centroids, list_ids)
    chunks = gather_rows((upper, lower), size)
    even, odd = local_sums_call(place, rotation, codes.T, upper, lower, size)
    sums, own_codes = scatter_sums(even, odd, owned, rows, size)
    counts = None
    for alternation in range(ALTS):
        parts = everywhere(sums, groups)
        cross, extra = cross_call(own_codes, parts, counts, chunks, total_rows)
        block = tree([p.astype(F32) for p in everywhere(cross, groups)]).astype(BF16)
        blocks = gather_group(block, size)
        if alternation + 1 < ALTS:
            counts = extra
            sums = next_sums_call(own_codes, blocks, chunks)
    rotated_out = final_call(place, upper, lower, blocks)
    packs = len(packs_of(owned))
    book = extra.reshape(packs, LO * SUB, PACK, HI).transpose(0, 2, 3, 1).reshape(packs * PACK, K * SUB)
    return (rotated_out, book[:owned])


def solution(mesh):
    in_specs = (
        P(("group", "within"), None),
        P(("group", "within"), None),
        P(("group", "within")),
        P(("group", "within"), None),
        P(),
    )
    out_specs = (P(("group", "within"), None), P("within", None))
    return jax.shard_map(per_device, mesh=mesh, in_specs=in_specs, out_specs=out_specs, check_vma=False)
```

time: 169 us -> 133 us (0.79)
  Pallas kernels: 53.5 us -> 23.1 us
  local copies, waits for them, and re-layouts: 16 us -> 6.32 us
  waiting for transfers between devices: 56.8 us -> 63.2 us
  other arithmetic: 3.65 us -> 0.15 us
    pallas_call x5 -> x7, Pallas kernels: 45 us -> 16.9 us  [the longest x1 6.79 us: next_sums_call(): pl.pallas_call(functools.partial(next_sums_kernel, size), out_shape=jax.S...]
    ppermute x40 -> x44, waiting for transfers between devices: 56.8 us -> 63.2 us  [swap(): return lax.ppermute(x, axis, [(i, i ^ bits) for i in range(size)])]
    ppermute x40 -> x44, starting transfers between devices: 33.7 us -> 38.7 us  [swap(): return lax.ppermute(x, axis, [(i, i ^ bits) for i in range(size)])]
    all_to_all x1 -> x0, starting transfers between devices: 4.16 us -> none  [per_device(): moved = lax.all_to_all(codes_t.reshape(size, owned, rows), 'within', 0, 0)]
    reshape x2 -> x0, local copies, waits for them, and re-layouts: 3.14 us -> none  [the longest x1 1.57 us: per_device(): moved.reshape(size, owned, 2, half).transpose(0, 2, 1, 3)]
    pallas_call x1, Pallas kernels: 8.43 us -> 6.21 us  [final_call(): pl.pallas_call(functools.partial(final_kernel, len(blocks)), out_shape=ja...]
    gather x1 -> x0, local copies, waits for them, and re-layouts: 2.11 us -> none  [per_device(): moved = jnp.take(moved, order, axis=0)]
    convert_element_type x2, other arithmetic: 1.97 us -> 0.15 us  [per_device(): tree([p.astype(F32) for p in everywhere(cross, groups)]).astype(BF16)]
  transfers between devices with their start and end apart: 41 -> 44, of which waited for: 18 -> 25; matrix products, arithmetic and copies ran while one was open for 7% -> 1% of each run, Pallas kernels for 0% -> 0%
where the time goes in v2:
time: 133 us; the launch traced here: 132 us
  waiting for transfers between devices  63.2 us (48%)
  starting transfers between devices  38.7 us (29%)
  Pallas kernels  23.1 us (17%)
  local copies, waits for them, and re-layouts  6.32 us (5%)
    ppermute x44, waiting for transfers between devices, swap(): return lax.ppermute(x, axis, [(i, i ^ bits) for i in range(size)])  63.2 us
    ppermute x44, starting transfers between devices, swap(): return lax.ppermute(x, axis, [(i, i ^ bits) for i in range(size)])  38.7 us
    pallas_call x1, Pallas kernels, next_sums_call(): pl.pallas_call(functools.partial(next_sums_kernel, size), out_shape=jax.S...  6.79 us
    pallas_call x1, Pallas kernels, final_call(): pl.pallas_call(functools.partial(final_kernel, len(blocks)), out_shape=ja...  6.21 us
    pallas_call x2, Pallas kernels, cross_call(): pl.pallas_call(functools.partial(cross_kernel, size, len(sums), with_coun...  5.95 us
    unnamed x10, local copies, waits for them, and re-layouts  5.32 us
    pallas_call x1, Pallas kernels, local_sums_call(): pl.pallas_call(functools.partial(local_sums_kernel, size), out_shape=(sha...  3.26 us
  transfers between devices with their start and end apart: 44, of which 25 were waited for; matrix products, arithmetic and copies ran while one was open for 1% of the time, Pallas kernels for 0%

profile of v2, /device:TPU:0, one launch (start us, length us, event | category | flops | bytes accessed | tf_op | source)
XLA Modules:
  0.0 132.3 jit_solution(7247044971845189848)
XLA Ops:
  4.2 1.7 %copy-done.3 = f32[768,768]{1,0:T(8,128)S(1)} copy-done((f32[768,768]{1,0:T(8,128)S(1)}, f32[768,768]{1,0:T(8,128)}, u32[]{:S(2)}) %copy-start.3) | copy-done | bytes 2359320
  6.8 3.3 %local_sums.1 = (bf16[4,304,128]{2,1,0:T(8,128)(2,1)S(1)}, bf16[4,304,128]{2,1,0:T(8,128)(2,1)S(1)}) custom-call(s32[1]{0:T(128)} %bitcast.place_ref, f32[768,768]{1,0:T(8,128)S(1)} %copy-done.3, s32[96,512]{1,0:T(8,128)S(1)} %bitcast.9, bf16[256,768]{1,0:T(8,128)(2,1)S(1)} %get-tuple-element.16.upper_ref.refs_4_.refs_8_.refs_5_, ...), custom_call_target="tpu_custom_call" | custom-call | flops 4000000000 | tf_op jit(solution)/shard_map/local_sums/pallas_call | solution.py:201
  10.6 2.6 %collective-permute-start.13 = (bf16[256,768]{1,0:T(8,128)(2,1)S(1)}, bf16[256,768]{1,0:T(8,128)(2,1)S(1)}, u32[]{:S(2)}, u32[]{:S(2)}) collective-permute-start(bf16[256,768]{1,0:T(8,128)(2,1)S(1)} %get-tuple-element.16.upper_ref.refs_4_.refs_8_.refs_5_), channel_id=1, source_target_pairs={{0,4},{1,5},{2,6},{3,7},{4,0},{5,1},{6,2},{7,3},{8,12},{9,13},{10,... | collective-permute-start | bytes 1179656 | tf_op jit(solution)/shard_map/ppermute | solution.py:50
  15.4 7.7 %collective-permute-done.13.refs_12_.refs_16_.refs_13_ = bf16[256,768]{1,0:T(8,128)(2,1)S(1)} collective-permute-done((bf16[256,768]{1,0:T(8,128)(2,1)S(1)}, bf16[256,768]{1,0:T(8,128)(2,1)S(1)}, u32[]{:S(2)}, u32[]{:S(2)}) %collective-permute-start.13) | collective-permute-done | bytes 393248 | tf_op jit(solution)/shard_map/ppermute | solution.py:50
  23.1 1.9 %collective-permute-start.1 = (bf16[368,128]{1,0:T(8,128)(2,1)S(1)}, bf16[368,128]{1,0:T(8,128)(2,1)S(1)}, u32[]{:S(2)}, u32[]{:S(2)}) collective-permute-start(bf16[368,128]{1,0:T(8,128)(2,1)S(1)} %get-tuple-element.21), channel_id=1, source_target_pairs={{0,2},{1,3},{2,0},{3,1},{4,6},{5,7},{6,4},{7,5},{8,10},{9,11},{10,... | collective-permute-start | bytes 282632 | tf_op jit(solution)/shard_map/ppermute | solution.py:50
  28.1 3.5 %collective-permute-done.14.refs_13_.refs_17_.refs_14_ = bf16[256,768]{1,0:T(8,128)(2,1)S(1)} collective-permute-done((bf16[256,768]{1,0:T(8,128)(2,1)S(1)}, bf16[256,768]{1,0:T(8,128)(2,1)S(1)}, u32[]{:S(2)}, u32[]{:S(2)}) %collective-permute-start.14) | collective-permute-done | bytes 393248 | tf_op jit(solution)/shard_map/ppermute | solution.py:50
  31.6 4.0 %collective-permute-done.1.refs_1_ = bf16[368,128]{1,0:T(8,128)(2,1)S(1)} collective-permute-done((bf16[368,128]{1,0:T(8,128)(2,1)S(1)}, bf16[368,128]{1,0:T(8,128)(2,1)S(1)}, u32[]{:S(2)}, u32[]{:S(2)}) %collective-permute-start.1) | collective-permute-done | bytes 94240 | tf_op jit(solution)/shard_map/ppermute | solution.py:50
  36.5 1.7 %collective-permute-start.18 = (bf16[256,768]{1,0:T(8,128)(2,1)S(1)}, bf16[256,768]{1,0:T(8,128)(2,1)S(1)}, u32[]{:S(2)}, u32[]{:S(2)}) collective-permute-start(bf16[256,768]{1,0:T(8,128)(2,1)S(1)} %collective-permute-done.14.refs_13_.refs_17_.refs_14_), channel_id=1, source_target_pairs={{0,2},{1,3},{2,0},{3,1},{4,6},{5,7},{6,4},{7,5},{8,10},{9,11},{10,... | collective-permute-start | bytes 1179656 | tf_op jit(solution)/shard_map/ppermute | solution.py:50
  38.3 3.7 %collective-permute-start.6 = (bf16[240,128]{1,0:T(8,128)(2,1)S(1)}, bf16[240,128]{1,0:T(8,128)(2,1)S(1)}, u32[]{:S(2)}, u32[]{:S(2)}) collective-permute-start(bf16[240,128]{1,0:T(8,128)(2,1)S(1)} %get-tuple-element.25.refs_0_), channel_id=1, source_target_pairs={{0,24},{8,16},{16,8},{24,0},{1,25},{9,17},{17,9},{25,1},{2,26},{10... | collective-permute-start | bytes 184328 | tf_op jit(solution)/shard_map/ppermute | solution.py:50
  42.0 2.9 %collective-permute-done.6.refs_3_ = bf16[240,128]{1,0:T(8,128)(2,1)S(1)} collective-permute-done((bf16[240,128]{1,0:T(8,128)(2,1)S(1)}, bf16[240,128]{1,0:T(8,128)(2,1)S(1)}, u32[]{:S(2)}, u32[]{:S(2)}) %collective-permute-start.6) | collective-permute-done | bytes 61472 | tf_op jit(solution)/shard_map/ppermute | solution.py:50
  45.5 1.6 %collective-permute-done.5.refs_2_ = bf16[240,128]{1,0:T(8,128)(2,1)S(1)} collective-permute-done((bf16[240,128]{1,0:T(8,128)(2,1)S(1)}, bf16[240,128]{1,0:T(8,128)(2,1)S(1)}, u32[]{:S(2)}, u32[]{:S(2)}) %collective-permute-start.5) | collective-permute-done | bytes 61472 | tf_op jit(solution)/shard_map/ppermute | solution.py:50
  47.1 2.0 %collective-permute-done.4.refs_1_ = bf16[240,128]{1,0:T(8,128)(2,1)S(1)} collective-permute-done((bf16[240,128]{1,0:T(8,128)(2,1)S(1)}, bf16[240,128]{1,0:T(8,128)(2,1)S(1)}, u32[]{:S(2)}, u32[]{:S(2)}) %collective-permute-start.4) | collective-permute-done | bytes 61472 | tf_op jit(solution)/shard_map/ppermute | solution.py:50
  52.5 3.0 %cross.2 = (bf16[96,768]{1,0:T(8,128)(2,1)S(1)}, f32[24,128]{1,0:T(8,128)S(1)}) custom-call(s32[8,12,512]{2,1,0:T(8,128)S(1)} %get-tuple-element.24.codes_ref, bf16[240,128]{1,0:T(8,128)(2,1)S(1)} %get-tuple-element.25.refs_0_, bf16[240,128]{1,0:T(8,128)(2,1)S(1)} %collective-permute-done.4.refs_1_, bf16[240,128]{1,0:T(8,128)(2,1)S(1)} %collective-permute-done.5.refs_2_, ...), custom_call_target="tpu_custom_call" | custom-call | tf_op jit(solution)/shard_map/cross/pallas_call | solution.py:336
  55.5 3.8 %collective-permute-start.23 = (bf16[96,768]{1,0:T(8,128)(2,1)S(1)}, bf16[96,768]{1,0:T(8,128)(2,1)S(1)}, u32[]{:S(2)}, u32[]{:S(2)}) collective-permute-start(bf16[96,768]{1,0:T(8,128)(2,1)S(1)} %get-tuple-element.26), channel_id=1, source_target_pairs={{0,24},{8,16},{16,8},{24,0},{1,25},{9,17},{17,9},{25,1},{2,26},{10... | collective-permute-start | bytes 442376 | tf_op jit(solution)/shard_map/ppermute | solution.py:50
  60.0 4.2 %collective-permute-done.23 = bf16[96,768]{1,0:T(8,128)(2,1)S(1)} collective-permute-done((bf16[96,768]{1,0:T(8,128)(2,1)S(1)}, bf16[96,768]{1,0:T(8,128)(2,1)S(1)}, u32[]{:S(2)}, u32[]{:S(2)}) %collective-permute-start.23) | collective-permute-done | bytes 147488 | tf_op jit(solution)/shard_map/ppermute | solution.py:50
  64.1 7.3 %collective-permute-done.22 = bf16[96,768]{1,0:T(8,128)(2,1)S(1)} collective-permute-done((bf16[96,768]{1,0:T(8,128)(2,1)S(1)}, bf16[96,768]{1,0:T(8,128)(2,1)S(1)}, u32[]{:S(2)}, u32[]{:S(2)}) %collective-permute-start.22) | collective-permute-done | bytes 147488 | tf_op jit(solution)/shard_map/ppermute | solution.py:50
  71.5 1.6 %collective-permute-start.29 = (bf16[96,768]{1,0:T(8,128)(2,1)S(1)}, bf16[96,768]{1,0:T(8,128)(2,1)S(1)}, u32[]{:S(2)}, u32[]{:S(2)}) collective-permute-start(bf16[96,768]{1,0:T(8,128)(2,1)S(1)} %add_convert_fusion.1.refs_0_), channel_id=1, source_target_pairs={{0,6},{1,7},{2,4},{3,5},{4,2},{5,3},{6,0},{7,1},{8,14},{9,15},{10,... | collective-permute-start | bytes 442376 | tf_op jit(solution)/shard_map/ppermute | solution.py:50
  75.1 4.2 %collective-permute-done.29.refs_6_ = bf16[96,768]{1,0:T(8,128)(2,1)S(1)} collective-permute-done((bf16[96,768]{1,0:T(8,128)(2,1)S(1)}, bf16[96,768]{1,0:T(8,128)(2,1)S(1)}, u32[]{:S(2)}, u32[]{:S(2)}) %collective-permute-start.29) | collective-permute-done | bytes 147488 | tf_op jit(solution)/shard_map/ppermute | solution.py:50
  79.3 1.8 %collective-permute-done.27.refs_4_ = bf16[96,768]{1,0:T(8,128)(2,1)S(1)} collective-permute-done((bf16[96,768]{1,0:T(8,128)(2,1)S(1)}, bf16[96,768]{1,0:T(8,128)(2,1)S(1)}, u32[]{:S(2)}, u32[]{:S(2)}) %collective-permute-start.27) | collective-permute-done | bytes 147488 | tf_op jit(solution)/shard_map/ppermute | solution.py:50
  82.6 6.8 %next_sums.1.refs_0_ = bf16[192,128]{1,0:T(8,128)(2,1)S(1)} custom-call(s32[8,12,512]{2,1,0:T(8,128)S(1)} %get-tuple-element.24.codes_ref, bf16[96,768]{1,0:T(8,128)(2,1)S(1)} %add_convert_fusion.1.refs_0_, bf16[96,768]{1,0:T(8,128)(2,1)S(1)} %collective-permute-done.24.refs_1_, bf16[96,768]{1,0:T(8,128)(2,1)S(1)} %collective-permute-done.25.refs_2_, ...), custom_call_target="tpu_custom_call" | custom-call | tf_op jit(solution)/shard_map/next_sums/pallas_call | solution.py:390
  89.4 2.4 %collective-permute-start.33 = (bf16[192,128]{1,0:T(8,128)(2,1)S(1)}, bf16[192,128]{1,0:T(8,128)(2,1)S(1)}, u32[]{:S(2)}, u32[]{:S(2)}) collective-permute-start(bf16[192,128]{1,0:T(8,128)(2,1)S(1)} %next_sums.1.refs_0_), channel_id=1, source_target_pairs={{0,24},{8,16},{16,8},{24,0},{1,25},{9,17},{17,9},{25,1},{2,26},{10... | collective-permute-start | bytes 147464 | tf_op jit(solution)/shard_map/ppermute | solution.py:50
  91.9 2.0 %collective-permute-start.31 = (bf16[192,128]{1,0:T(8,128)(2,1)S(1)}, bf16[192,128]{1,0:T(8,128)(2,1)S(1)}, u32[]{:S(2)}, u32[]{:S(2)}) collective-permute-start(bf16[192,128]{1,0:T(8,128)(2,1)S(1)} %next_sums.1.refs_0_), channel_id=1, source_target_pairs={{0,8},{8,0},{16,24},{24,16},{1,9},{9,1},{17,25},{25,17},{2,10},{10... | collective-permute-start | bytes 147464 | tf_op jit(solution)/shard_map/ppermute | solution.py:50
  93.9 1.9 %collective-permute-done.33.refs_3_ = bf16[192,128]{1,0:T(8,128)(2,1)S(1)} collective-permute-done((bf16[192,128]{1,0:T(8,128)(2,1)S(1)}, bf16[192,128]{1,0:T(8,128)(2,1)S(1)}, u32[]{:S(2)}, u32[]{:S(2)}) %collective-permute-start.33) | collective-permute-done | bytes 49184 | tf_op jit(solution)/shard_map/ppermute | solution.py:50
  97.3 3.0 %cross.3 = (bf16[96,768]{1,0:T(8,128)(2,1)S(1)}, f32[192,128]{1,0:T(8,128)S(1)}) custom-call(s32[8,12,512]{2,1,0:T(8,128)S(1)} %get-tuple-element.24.codes_ref, bf16[192,128]{1,0:T(8,128)(2,1)S(1)} %next_sums.1.refs_0_, bf16[192,128]{1,0:T(8,128)(2,1)S(1)} %collective-permute-done.31.refs_1_, bf16[192,128]{1,0:T(8,128)(2,1)S(1)} %collective-permute-done.32.refs_2_, ...), custom_call_target="tpu_custom_call" | custom-call | tf_op jit(solution)/shard_map/cross/pallas_call | solution.py:336
  100.3 2.4 %collective-permute-start.36 = (bf16[96,768]{1,0:T(8,128)(2,1)S(1)}, bf16[96,768]{1,0:T(8,128)(2,1)S(1)}, u32[]{:S(2)}, u32[]{:S(2)}) collective-permute-start(bf16[96,768]{1,0:T(8,128)(2,1)S(1)} %get-tuple-element.28), channel_id=1, source_target_pairs={{0,24},{8,16},{16,8},{24,0},{1,25},{9,17},{17,9},{25,1},{2,26},{10... | collective-permute-start | bytes 442376 | tf_op jit(solution)/shard_map/ppermute | solution.py:50
  102.7 2.0 %collective-permute-start.34 = (bf16[96,768]{1,0:T(8,128)(2,1)S(1)}, bf16[96,768]{1,0:T(8,128)(2,1)S(1)}, u32[]{:S(2)}, u32[]{:S(2)}) collective-permute-start(bf16[96,768]{1,0:T(8,128)(2,1)S(1)} %get-tuple-element.28), channel_id=1, source_target_pairs={{0,8},{8,0},{16,24},{24,16},{1,9},{9,1},{17,25},{25,17},{2,10},{10... | collective-permute-start | bytes 442376 | tf_op jit(solution)/shard_map/ppermute | solution.py:50
  104.8 4.3 %collective-permute-done.36 = bf16[96,768]{1,0:T(8,128)(2,1)S(1)} collective-permute-done((bf16[96,768]{1,0:T(8,128)(2,1)S(1)}, bf16[96,768]{1,0:T(8,128)(2,1)S(1)}, u32[]{:S(2)}, u32[]{:S(2)}) %collective-permute-start.36) | collective-permute-done | bytes 147488 | tf_op jit(solution)/shard_map/ppermute | solution.py:50
  109.0 6.0 %collective-permute-done.35 = bf16[96,768]{1,0:T(8,128)(2,1)S(1)} collective-permute-done((bf16[96,768]{1,0:T(8,128)(2,1)S(1)}, bf16[96,768]{1,0:T(8,128)(2,1)S(1)}, u32[]{:S(2)}, u32[]{:S(2)}) %collective-permute-start.35) | collective-permute-done | bytes 147488 | tf_op jit(solution)/shard_map/ppermute | solution.py:50
  115.1 1.6 %collective-permute-start.42 = (bf16[96,768]{1,0:T(8,128)(2,1)S(1)}, bf16[96,768]{1,0:T(8,128)(2,1)S(1)}, u32[]{:S(2)}, u32[]{:S(2)}) collective-permute-start(bf16[96,768]{1,0:T(8,128)(2,1)S(1)} %add_convert_fusion.refs_0_), channel_id=1, source_target_pairs={{0,6},{1,7},{2,4},{3,5},{4,2},{5,3},{6,0},{7,1},{8,14},{9,15},{10,... | collective-permute-start | bytes 442376 | tf_op jit(solution)/shard_map/ppermute | solution.py:50
  118.7 4.2 %collective-permute-done.42.refs_6_ = bf16[96,768]{1,0:T(8,128)(2,1)S(1)} collective-permute-done((bf16[96,768]{1,0:T(8,128)(2,1)S(1)}, bf16[96,768]{1,0:T(8,128)(2,1)S(1)}, u32[]{:S(2)}, u32[]{:S(2)}) %collective-permute-start.42) | collective-permute-done | bytes 147488 | tf_op jit(solution)/shard_map/ppermute | solution.py:50
  122.9 1.6 %collective-permute-done.40.refs_4_ = bf16[96,768]{1,0:T(8,128)(2,1)S(1)} collective-permute-done((bf16[96,768]{1,0:T(8,128)(2,1)S(1)}, bf16[96,768]{1,0:T(8,128)(2,1)S(1)}, u32[]{:S(2)}, u32[]{:S(2)}) %collective-permute-start.40) | collective-permute-done | bytes 147488 | tf_op jit(solution)/shard_map/ppermute | solution.py:50
  126.1 6.2 %final.1 = bf16[512,768]{1,0:T(8,128)(2,1)} custom-call(s32[1]{0:T(128)} %bitcast.place_ref, bf16[256,768]{1,0:T(8,128)(2,1)S(1)} %get-tuple-element.16.upper_ref.refs_4_.refs_8_.refs_5_, bf16[256,768]{1,0:T(8,128)(2,1)S(1)} %get-tuple-element.17.lower_ref.refs_5_.refs_9_.refs_6_, bf16[96,768]{1,0:T(8,128)(2,1)S(1)} %add_convert_fusion.refs_0_, ...), custom_call_target="tpu_custom_call" | custom-call | tf_op jit(solution)/shard_map/final/pallas_call | solution.py:418
  (80 shorter events, 24.8 us)
Async XLA Ops:
  10.0 5.1 %collective-permute-start = (bf16[4,304,128]{2,1,0:T(8,128)(2,1)S(1)}, bf16[4,304,128]{2,1,0:T(8,128)(2,1)S(1)}, u32[]{:S(2)}, u32[]{:S(2)}) collective-permute-start(bf16[4,304,128]{2,1,0:T(8,128)(2,1)S(1)} %get-tuple-element.19), channel_id=1, source_target_pairs={{0,1},{1,0},{2,3},{3,2},{4,5},{5,4},{6,7},{7,6},{8,9},{9,8},{10,11... | collective-permute-start | bytes 933896 | tf_op jit(solution)/shard_map/ppermute | solution.py:50
  10.6 12.5 %collective-permute-start.13 = (bf16[256,768]{1,0:T(8,128)(2,1)S(1)}, bf16[256,768]{1,0:T(8,128)(2,1)S(1)}, u32[]{:S(2)}, u32[]{:S(2)}) collective-permute-start(bf16[256,768]{1,0:T(8,128)(2,1)S(1)} %get-tuple-element.16.upper_ref.refs_4_.refs_8_.refs_5_), channel_id=1, source_target_pairs={{0,4},{1,5},{2,6},{3,7},{4,0},{5,1},{6,2},{7,3},{8,12},{9,13},{10,... | collective-permute-start | bytes 1179656 | tf_op jit(solution)/shard_map/ppermute | solution.py:50
  13.2 12.0 %collective-permute-start.9 = (bf16[256,768]{1,0:T(8,128)(2,1)S(1)}, bf16[256,768]{1,0:T(8,128)(2,1)S(1)}, u32[]{:S(2)}, u32[]{:S(2)}) collective-permute-start(bf16[256,768]{1,0:T(8,128)(2,1)S(1)} %get-tuple-element.16.upper_ref.refs_4_.refs_8_.refs_5_), channel_id=1, source_target_pairs={{0,2},{1,3},{2,0},{3,1},{4,6},{5,7},{6,4},{7,5},{8,10},{9,11},{10,... | collective-permute-start | bytes 1179656 | tf_op jit(solution)/shard_map/ppermute | solution.py:50
  14.7 11.9 %collective-permute-start.7 = (bf16[256,768]{1,0:T(8,128)(2,1)S(1)}, bf16[256,768]{1,0:T(8,128)(2,1)S(1)}, u32[]{:S(2)}, u32[]{:S(2)}) collective-permute-start(bf16[256,768]{1,0:T(8,128)(2,1)S(1)} %get-tuple-element.16.upper_ref.refs_4_.refs_8_.refs_5_), channel_id=1, source_target_pairs={{0,1},{1,0},{2,3},{3,2},{4,5},{5,4},{6,7},{7,6},{8,9},{9,8},{10,11... | collective-permute-start | bytes 1179656 | tf_op jit(solution)/shard_map/ppermute | solution.py:50
  14.7 16.9 %collective-permute-start.14 = (bf16[256,768]{1,0:T(8,128)(2,1)S(1)}, bf16[256,768]{1,0:T(8,128)(2,1)S(1)}, u32[]{:S(2)}, u32[]{:S(2)}) collective-permute-start(bf16[256,768]{1,0:T(8,128)(2,1)S(1)} %get-tuple-element.17.lower_ref.refs_5_.refs_9_.refs_6_), channel_id=1, source_target_pairs={{0,4},{1,5},{2,6},{3,7},{4,0},{5,1},{6,2},{7,3},{8,12},{9,13},{10,... | collective-permute-start | bytes 1179656 | tf_op jit(solution)/shard_map/ppermute | solution.py:50
  15.2 23.1 %collective-permute-start.10 = (bf16[256,768]{1,0:T(8,128)(2,1)S(1)}, bf16[256,768]{1,0:T(8,128)(2,1)S(1)}, u32[]{:S(2)}, u32[]{:S(2)}) collective-permute-start(bf16[256,768]{1,0:T(8,128)(2,1)S(1)} %get-tuple-element.17.lower_ref.refs_5_.refs_9_.refs_6_), channel_id=1, source_target_pairs={{0,2},{1,3},{2,0},{3,1},{4,6},{5,7},{6,4},{7,5},{8,10},{9,11},{10,... | collective-permute-start | bytes 1179656 | tf_op jit(solution)/shard_map/ppermute | solution.py:50
  23.1 12.4 %collective-permute-start.1 = (bf16[368,128]{1,0:T(8,128)(2,1)S(1)}, bf16[368,128]{1,0:T(8,128)(2,1)S(1)}, u32[]{:S(2)}, u32[]{:S(2)}) collective-permute-start(bf16[368,128]{1,0:T(8,128)(2,1)S(1)} %get-tuple-element.21), channel_id=1, source_target_pairs={{0,2},{1,3},{2,0},{3,1},{4,6},{5,7},{6,4},{7,5},{8,10},{9,11},{10,... | collective-permute-start | bytes 282632 | tf_op jit(solution)/shard_map/ppermute | solution.py:50
  25.1 10.5 %collective-permute-start.2 = (bf16[368,128]{1,0:T(8,128)(2,1)S(1)}, bf16[368,128]{1,0:T(8,128)(2,1)S(1)}, u32[]{:S(2)}, u32[]{:S(2)}) collective-permute-start(bf16[368,128]{1,0:T(8,128)(2,1)S(1)} %get-tuple-element.22), channel_id=1, source_target_pairs={{0,4},{1,5},{2,6},{3,7},{4,0},{5,1},{6,2},{7,3},{8,12},{9,13},{10,... | collective-permute-start | bytes 282632 | tf_op jit(solution)/shard_map/ppermute | solution.py:50
  26.6 9.9 %collective-permute-start.3 = (bf16[368,128]{1,0:T(8,128)(2,1)S(1)}, bf16[368,128]{1,0:T(8,128)(2,1)S(1)}, u32[]{:S(2)}, u32[]{:S(2)}) collective-permute-start(bf16[368,128]{1,0:T(8,128)(2,1)S(1)} %get-tuple-element.23), channel_id=1, source_target_pairs={{0,6},{1,7},{2,4},{3,5},{4,2},{5,3},{6,0},{7,1},{8,14},{9,15},{10,... | collective-permute-start | bytes 282632 | tf_op jit(solution)/shard_map/ppermute | solution.py:50
  31.5 10.4 %collective-permute-start.8 = (bf16[256,768]{1,0:T(8,128)(2,1)S(1)}, bf16[256,768]{1,0:T(8,128)(2,1)S(1)}, u32[]{:S(2)}, u32[]{:S(2)}) collective-permute-start(bf16[256,768]{1,0:T(8,128)(2,1)S(1)} %get-tuple-element.17.lower_ref.refs_5_.refs_9_.refs_6_), channel_id=1, source_target_pairs={{0,1},{1,0},{2,3},{3,2},{4,5},{5,4},{6,7},{7,6},{8,9},{9,8},{10,11... | collective-permute-start | bytes 1179656 | tf_op jit(solution)/shard_map/ppermute | solution.py:50
  35.6 13.6 %collective-permute-start.15 = (bf16[256,768]{1,0:T(8,128)(2,1)S(1)}, bf16[256,768]{1,0:T(8,128)(2,1)S(1)}, u32[]{:S(2)}, u32[]{:S(2)}) collective-permute-start(bf16[256,768]{1,0:T(8,128)(2,1)S(1)} %collective-permute-done.13.refs_12_.refs_16_.refs_13_), channel_id=1, source_target_pairs={{0,1},{1,0},{2,3},{3,2},{4,5},{5,4},{6,7},{7,6},{8,9},{9,8},{10,11... | collective-permute-start | bytes 1179656 | tf_op jit(solution)/shard_map/ppermute | solution.py:50
  35.6 14.1 %collective-permute-start.17 = (bf16[256,768]{1,0:T(8,128)(2,1)S(1)}, bf16[256,768]{1,0:T(8,128)(2,1)S(1)}, u32[]{:S(2)}, u32[]{:S(2)}) collective-permute-start(bf16[256,768]{1,0:T(8,128)(2,1)S(1)} %collective-permute-done.9.refs_8_.refs_12_.refs_9_), channel_id=1, source_target_pairs={{0,4},{1,5},{2,6},{3,7},{4,0},{5,1},{6,2},{7,3},{8,12},{9,13},{10,... | collective-permute-start | bytes 1179656 | tf_op jit(solution)/shard_map/ppermute | solution.py:50
  36.5 13.2 %collective-permute-start.18 = (bf16[256,768]{1,0:T(8,128)(2,1)S(1)}, bf16[256,768]{1,0:T(8,128)(2,1)S(1)}, u32[]{:S(2)}, u32[]{:S(2)}) collective-permute-start(bf16[256,768]{1,0:T(8,128)(2,1)S(1)} %collective-permute-done.14.refs_13_.refs_17_.refs_14_), channel_id=1, source_target_pairs={{0,2},{1,3},{2,0},{3,1},{4,6},{5,7},{6,4},{7,5},{8,10},{9,11},{10,... | collective-permute-start | bytes 1179656 | tf_op jit(solution)/shard_map/ppermute | solution.py:50
  38.3 6.5 %collective-permute-start.6 = (bf16[240,128]{1,0:T(8,128)(2,1)S(1)}, bf16[240,128]{1,0:T(8,128)(2,1)S(1)}, u32[]{:S(2)}, u32[]{:S(2)}) collective-permute-start(bf16[240,128]{1,0:T(8,128)(2,1)S(1)} %get-tuple-element.25.refs_0_), channel_id=1, source_target_pairs={{0,24},{8,16},{16,8},{24,0},{1,25},{9,17},{17,9},{25,1},{2,26},{10... | collective-permute-start | bytes 184328 | tf_op jit(solution)/shard_map/ppermute | solution.py:50
  42.0 5.1 %collective-permute-start.5 = (bf16[240,128]{1,0:T(8,128)(2,1)S(1)}, bf16[240,128]{1,0:T(8,128)(2,1)S(1)}, u32[]{:S(2)}, u32[]{:S(2)}) collective-permute-start(bf16[240,128]{1,0:T(8,128)(2,1)S(1)} %get-tuple-element.25.refs_0_), channel_id=1, source_target_pairs={{0,16},{8,24},{16,0},{24,8},{1,17},{9,25},{17,1},{25,9},{2,18},{10... | collective-permute-start | bytes 184328 | tf_op jit(solution)/shard_map/ppermute | solution.py:50
  55.5 8.6 %collective-permute-start.23 = (bf16[96,768]{1,0:T(8,128)(2,1)S(1)}, bf16[96,768]{1,0:T(8,128)(2,1)S(1)}, u32[]{:S(2)}, u32[]{:S(2)}) collective-permute-start(bf16[96,768]{1,0:T(8,128)(2,1)S(1)} %get-tuple-element.26), channel_id=1, source_target_pairs={{0,24},{8,16},{16,8},{24,0},{1,25},{9,17},{17,9},{25,1},{2,26},{10... | collective-permute-start | bytes 442376 | tf_op jit(solution)/shard_map/ppermute | solution.py:50
  59.3 12.2 %collective-permute-start.22 = (bf16[96,768]{1,0:T(8,128)(2,1)S(1)}, bf16[96,768]{1,0:T(8,128)(2,1)S(1)}, u32[]{:S(2)}, u32[]{:S(2)}) collective-permute-start(bf16[96,768]{1,0:T(8,128)(2,1)S(1)} %get-tuple-element.26), channel_id=1, source_target_pairs={{0,16},{8,24},{16,0},{24,8},{1,17},{9,25},{17,1},{25,9},{2,18},{10... | collective-permute-start | bytes 442376 | tf_op jit(solution)/shard_map/ppermute | solution.py:50
  59.3 12.2 %collective-permute-start.21 = (bf16[96,768]{1,0:T(8,128)(2,1)S(1)}, bf16[96,768]{1,0:T(8,128)(2,1)S(1)}, u32[]{:S(2)}, u32[]{:S(2)}) collective-permute-start(bf16[96,768]{1,0:T(8,128)(2,1)S(1)} %get-tuple-element.26), channel_id=1, source_target_pairs={{0,8},{8,0},{16,24},{24,16},{1,9},{9,1},{17,25},{25,17},{2,10},{10... | collective-permute-start | bytes 442376 | tf_op jit(solution)/shard_map/ppermute | solution.py:50
  71.5 7.7 %collective-permute-start.29 = (bf16[96,768]{1,0:T(8,128)(2,1)S(1)}, bf16[96,768]{1,0:T(8,128)(2,1)S(1)}, u32[]{:S(2)}, u32[]{:S(2)}) collective-permute-start(bf16[96,768]{1,0:T(8,128)(2,1)S(1)} %add_convert_fusion.1.refs_0_), channel_id=1, source_target_pairs={{0,6},{1,7},{2,4},{3,5},{4,2},{5,3},{6,0},{7,1},{8,14},{9,15},{10,... | collective-permute-start | bytes 442376 | tf_op jit(solution)/shard_map/ppermute | solution.py:50
  73.1 7.9 %collective-permute-start.27 = (bf16[96,768]{1,0:T(8,128)(2,1)S(1)}, bf16[96,768]{1,0:T(8,128)(2,1)S(1)}, u32[]{:S(2)}, u32[]{:S(2)}) collective-permute-start(bf16[96,768]{1,0:T(8,128)(2,1)S(1)} %add_convert_fusion.1.refs_0_), channel_id=1, source_target_pairs={{0,4},{1,5},{2,6},{3,7},{4,0},{5,1},{6,2},{7,3},{8,12},{9,13},{10,... | collective-permute-start | bytes 442376 | tf_op jit(solution)/shard_map/ppermute | solution.py:50
  73.6 7.5 %collective-permute-start.25 = (bf16[96,768]{1,0:T(8,128)(2,1)S(1)}, bf16[96,768]{1,0:T(8,128)(2,1)S(1)}, u32[]{:S(2)}, u32[]{:S(2)}) collective-permute-start(bf16[96,768]{1,0:T(8,128)(2,1)S(1)} %add_convert_fusion.1.refs_0_), channel_id=1, source_target_pairs={{0,2},{1,3},{2,0},{3,1},{4,6},{5,7},{6,4},{7,5},{8,10},{9,11},{10,... | collective-permute-start | bytes 442376 | tf_op jit(solution)/shard_map/ppermute | solution.py:50
  75.1 6.5 %collective-permute-start.24 = (bf16[96,768]{1,0:T(8,128)(2,1)S(1)}, bf16[96,768]{1,0:T(8,128)(2,1)S(1)}, u32[]{:S(2)}, u32[]{:S(2)}) collective-permute-start(bf16[96,768]{1,0:T(8,128)(2,1)S(1)} %add_convert_fusion.1.refs_0_), channel_id=1, source_target_pairs={{0,1},{1,0},{2,3},{3,2},{4,5},{5,4},{6,7},{7,6},{8,9},{9,8},{10,11... | collective-permute-start | bytes 442376 | tf_op jit(solution)/shard_map/ppermute | solution.py:50
  89.4 6.4 %collective-permute-start.33 = (bf16[192,128]{1,0:T(8,128)(2,1)S(1)}, bf16[192,128]{1,0:T(8,128)(2,1)S(1)}, u32[]{:S(2)}, u32[]{:S(2)}) collective-permute-start(bf16[192,128]{1,0:T(8,128)(2,1)S(1)} %next_sums.1.refs_0_), channel_id=1, source_target_pairs={{0,24},{8,16},{16,8},{24,0},{1,25},{9,17},{17,9},{25,1},{2,26},{10... | collective-permute-start | bytes 147464 | tf_op jit(solution)/shard_map/ppermute | solution.py:50
  91.8 5.5 %collective-permute-start.32 = (bf16[192,128]{1,0:T(8,128)(2,1)S(1)}, bf16[192,128]{1,0:T(8,128)(2,1)S(1)}, u32[]{:S(2)}, u32[]{:S(2)}) collective-permute-start(bf16[192,128]{1,0:T(8,128)(2,1)S(1)} %next_sums.1.refs_0_), channel_id=1, source_target_pairs={{0,16},{8,24},{16,0},{24,8},{1,17},{9,25},{17,1},{25,9},{2,18},{10... | collective-permute-start | bytes 147464 | tf_op jit(solution)/shard_map/ppermute | solution.py:50
  91.9 5.5 %collective-permute-start.31 = (bf16[192,128]{1,0:T(8,128)(2,1)S(1)}, bf16[192,128]{1,0:T(8,128)(2,1)S(1)}, u32[]{:S(2)}, u32[]{:S(2)}) collective-permute-start(bf16[192,128]{1,0:T(8,128)(2,1)S(1)} %next_sums.1.refs_0_), channel_id=1, source_target_pairs={{0,8},{8,0},{16,24},{24,16},{1,9},{9,1},{17,25},{25,17},{2,10},{10... | collective-permute-start | bytes 147464 | tf_op jit(solution)/shard_map/ppermute | solution.py:50
  100.3 8.7 %collective-permute-start.36 = (bf16[96,768]{1,0:T(8,128)(2,1)S(1)}, bf16[96,768]{1,0:T(8,128)(2,1)S(1)}, u32[]{:S(2)}, u32[]{:S(2)}) collective-permute-start(bf16[96,768]{1,0:T(8,128)(2,1)S(1)} %get-tuple-element.28), channel_id=1, source_target_pairs={{0,24},{8,16},{16,8},{24,0},{1,25},{9,17},{17,9},{25,1},{2,26},{10... | collective-permute-start | bytes 442376 | tf_op jit(solution)/shard_map/ppermute | solution.py:50
  102.7 12.3 %collective-permute-start.35 = (bf16[96,768]{1,0:T(8,128)(2,1)S(1)}, bf16[96,768]{1,0:T(8,128)(2,1)S(1)}, u32[]{:S(2)}, u32[]{:S(2)}) collective-permute-start(bf16[96,768]{1,0:T(8,128)(2,1)S(1)} %get-tuple-element.28), channel_id=1, source_target_pairs={{0,16},{8,24},{16,0},{24,8},{1,17},{9,25},{17,1},{25,9},{2,18},{10... | collective-permute-start | bytes 442376 | tf_op jit(solution)/shard_map/ppermute | solution.py:50
  102.7 12.3 %collective-permute-start.34 = (bf16[96,768]{1,0:T(8,128)(2,1)S(1)}, bf16[96,768]{1,0:T(8,128)(2,1)S(1)}, u32[]{:S(2)}, u32[]{:S(2)}) collective-permute-start(bf16[96,768]{1,0:T(8,128)(2,1)S(1)} %get-tuple-element.28), channel_id=1, source_target_pairs={{0,8},{8,0},{16,24},{24,16},{1,9},{9,1},{17,25},{25,17},{2,10},{10... | collective-permute-start | bytes 442376 | tf_op jit(solution)/shard_map/ppermute | solution.py:50
  115.1 7.7 %collective-permute-start.42 = (bf16[96,768]{1,0:T(8,128)(2,1)S(1)}, bf16[96,768]{1,0:T(8,128)(2,1)S(1)}, u32[]{:S(2)}, u32[]{:S(2)}) collective-permute-start(bf16[96,768]{1,0:T(8,128)(2,1)S(1)} %add_convert_fusion.refs_0_), channel_id=1, source_target_pairs={{0,6},{1,7},{2,4},{3,5},{4,2},{5,3},{6,0},{7,1},{8,14},{9,15},{10,... | collective-permute-start | bytes 442376 | tf_op jit(solution)/shard_map/ppermute | solution.py:50
  116.7 7.8 %collective-permute-start.40 = (bf16[96,768]{1,0:T(8,128)(2,1)S(1)}, bf16[96,768]{1,0:T(8,128)(2,1)S(1)}, u32[]{:S(2)}, u32[]{:S(2)}) collective-permute-start(bf16[96,768]{1,0:T(8,128)(2,1)S(1)} %add_convert_fusion.refs_0_), channel_id=1, source_target_pairs={{0,4},{1,5},{2,6},{3,7},{4,0},{5,1},{6,2},{7,3},{8,12},{9,13},{10,... | collective-permute-start | bytes 442376 | tf_op jit(solution)/shard_map/ppermute | solution.py:50
  117.2 7.3 %collective-permute-start.38 = (bf16[96,768]{1,0:T(8,128)(2,1)S(1)}, bf16[96,768]{1,0:T(8,128)(2,1)S(1)}, u32[]{:S(2)}, u32[]{:S(2)}) collective-permute-start(bf16[96,768]{1,0:T(8,128)(2,1)S(1)} %add_convert_fusion.refs_0_), channel_id=1, source_target_pairs={{0,2},{1,3},{2,0},{3,1},{4,6},{5,7},{6,4},{7,5},{8,10},{9,11},{10,... | collective-permute-start | bytes 442376 | tf_op jit(solution)/shard_map/ppermute | solution.py:50
  118.7 7.4 %collective-permute-start.37 = (bf16[96,768]{1,0:T(8,128)(2,1)S(1)}, bf16[96,768]{1,0:T(8,128)(2,1)S(1)}, u32[]{:S(2)}, u32[]{:S(2)}) collective-permute-start(bf16[96,768]{1,0:T(8,128)(2,1)S(1)} %add_convert_fusion.refs_0_), channel_id=1, source_target_pairs={{0,1},{1,0},{2,3},{3,2},{4,5},{5,4},{6,7},{7,6},{8,9},{9,8},{10,11... | collective-permute-start | bytes 442376 | tf_op jit(solution)/shard_map/ppermute | solution.py:50
  (17 other events, 33.2 us)

commit v3 on v2

--- a/solution.py
+++ b/solution.py
@@ -50,10 +50,9 @@
     return lax.ppermute(x, axis, [(i, i ^ bits) for i in range(size)])
 
 
-def residual_kernel(vectors_ref, centroids_ref, ids_ref, *outs):
+def residual_kernel(vectors_ref, centroids_ref, ids_ref, out_ref):
     lists = centroids_ref.shape[0]
     rows = vectors_ref.shape[0]
-    half = rows // 2
     local = lax.rem(ids_ref[...], lists)
     level = lax.broadcasted_iota(jnp.int32, (lists, rows), 0)
     table = jnp.where(level == local, 1.0, 0.0).astype(BF16)
@@ -62,19 +61,17 @@
     rest = center - first.astype(F32)
     second = rest.astype(BF16)
     third = (rest - second.astype(F32)).astype(BF16)
-    for h, out_ref in enumerate(outs):
-        part = table[:, h * half : (h + 1) * half]
-        picked = mm(part, first, TN) + mm(part, second, TN) + mm(part, third, TN)
-        out_ref[...] = (vectors_ref[h * half : (h + 1) * half, :].astype(F32) - picked).astype(BF16)
+    picked = mm(table, first, TN) + mm(table, second, TN) + mm(table, third, TN)
+    out_ref[...] = (vectors_ref[...].astype(F32) - picked).astype(BF16)
 
 
 def residual_call(vectors, centroids, ids):
     rows, width = vectors.shape
     return pl.pallas_call(
         residual_kernel,
-        out_shape=(jax.ShapeDtypeStruct((rows // 2, width), BF16),) * 2,
+        out_shape=jax.ShapeDtypeStruct((rows, width), BF16),
         in_specs=[vmem_spec()] * 3,
-        out_specs=(vmem_spec(),) * 2,
+        out_specs=vmem_spec(),
         compiler_params=params(),
         name="residual",
     )(vectors, centroids, ids.reshape(1, rows))
@@ -172,13 +169,12 @@
         out_ref[at + 16 * c : at + 16 * c + 16, :] = filled[:, 128 * c : 128 * c + 128]
 
 
-def local_sums_kernel(size, place_ref, rotation_ref, codes_ref, upper_ref, lower_ref, *refs):
+def local_sums_kernel(size, place_ref, rotation_ref, codes_ref, residual_ref, *refs):
     outs, turned, staged = refs[:2], refs[2], refs[3]
     subspaces = codes_ref.shape[0]
     owned = subspaces // size
     base = pack_layout(owned, True)[2]
-    residual = jnp.concatenate([upper_ref[...], lower_ref[...]], axis=0)
-    rotated = mm(residual, rotation_ref[...].astype(BF16)).astype(BF16).astype(F32)
+    rotated = mm(residual_ref[...], rotation_ref[...].astype(BF16)).astype(BF16).astype(F32)
     turned[...] = rotated.T
     for j in range(size):
         staged[j, :owned, :] = codes_ref[j * owned : (j + 1) * owned, :]
@@ -193,7 +189,7 @@
         write_codes(codes.astype(F32), slot, base)
 
 
-def local_sums_call(place, rotation, codes, upper, lower, size):
+def local_sums_call(place, rotation, codes, residual, size):
     subspaces, rows = codes.shape
     owned = subspaces // size
     height = -(-owned // 8) * 8
@@ -201,13 +197,13 @@
     return pl.pallas_call(
         functools.partial(local_sums_kernel, size),
         out_shape=(shape,) * 2,
-        in_specs=[smem_spec()] + [vmem_spec()] * 4,
+        in_specs=[smem_spec()] + [vmem_spec()] * 3,
         out_specs=(vmem_spec(),) * 2,
         scratch_shapes=[pltpu.VMEM((rotation.shape[1], rows), F32), pltpu.VMEM((size, height, rows), jnp.int32)],
         compiler_params=params(rotation),
-        cost_estimate=cost(4),
+        cost_estimate=cost(0),
         name="local_sums",
-    )(place, rotation, codes, upper, lower)
+    )(place, rotation, codes, residual)
 
 
 def merge_cores_kernel(owned, even_ref, came_ref, *outs):
@@ -229,7 +225,7 @@
         in_specs=[vmem_spec()] * 2,
         out_specs=(vmem_spec(),) * slots,
         compiler_params=params(),
-        cost_estimate=cost(1),
+        cost_estimate=cost(0),
         name="merge_cores",
     )(even, came)
 
@@ -259,88 +255,176 @@
         in_specs=[vmem_spec()] * len(parts),
         out_specs=(vmem_spec(),) * 2,
         compiler_params=params(),
-        cost_estimate=cost(1),
+        cost_estimate=cost(0),
         name="merge_chips",
     )(*parts)
 
 
-def spans_of(size):
-    step = min(2, size)
-    return [range(first, first + step) for first in range(0, size, step)]
+def merge_kernel(owned, first_ref, second_ref, out_ref):
+    sums, counts = merge_parts([first_ref, second_ref], owned, True)
+    write_sums(sums, counts, owned, out_ref)
+
+
+def merge_call(first, second, owned):
+    return pl.pallas_call(
+        functools.partial(merge_kernel, owned),
+        out_shape=jax.ShapeDtypeStruct(first.shape, BF16),
+        in_specs=[vmem_spec()] * 2,
+        out_specs=vmem_spec(),
+        compiler_params=params(),
+        cost_estimate=cost(0),
+        name="merge_groups",
+    )(first, second)
+
+
+def spans_of(held):
+    return [(k, k ^ 1) for k in held if k % 2 == 0]
 
 
 def span_codes(codes_ref, span):
     return jnp.concatenate([codes_ref[k] for k in span], axis=1)
 
 
-def span_rows(chunks, span):
-    return jnp.concatenate([chunks[2 * k + h][...] for k in span for h in range(2)], axis=0)
-
-
-def cross_kernel(size, groups, with_counts, total_rows, codes_ref, *refs):
-    sums, refs = refs[:groups], refs[groups:]
-    owned = codes_ref.shape[1]
-    packs = packs_of(owned)
+def span_rows(pieces, span):
+    return jnp.concatenate([ref[...] for k in span for ref in pieces[k]], axis=0)
+
+
+def pieces_of(held, refs):
+    at = 0
+    pieces = {}
+    for k, count in held.items():
+        pieces[k] = refs[at : at + count]
+        at += count
+    return pieces
+
+
+def read_books(sums, counts_in, owned):
+    everything, counts = merge_parts(sums, owned, counts_in is None)
+    if counts is None:
+        counts = counts_in[...]
     block = LO * SUB
-    if with_counts:
-        chunks, (cross_ref, counts_ref) = refs[: 2 * size], refs[2 * size :]
-    else:
-        counts_in, chunks, (cross_ref, book_ref) = refs[0], refs[1 : 2 * size + 1], refs[2 * size + 1 :]
-    everything, counts = merge_parts(sums, owned, with_counts)
-    if with_counts:
-        counts_ref[...] = counts
-    else:
-        counts = counts_in[...]
     books = []
-    for g in range(len(packs)):
+    for g in range(len(packs_of(owned))):
         rows = []
         for level in range(LO):
             at = g * block + level * SUB
             rows.append(everything[at : at + SUB] / (counts[g * LO + level : g * LO + level + 1] + 1.0))
-        book = jnp.concatenate(rows, axis=0)
-        if not with_counts:
-            book_ref[g * block : (g + 1) * block, :] = book
-        books.append(book)
-    owner = lane_owner(block)
-    wide = [
+        books.append(jnp.concatenate(rows, axis=0))
+    return books, counts
+
+
+def widen(books, owned):
+    owner = lane_owner(LO * SUB)
+    return [
         jnp.concatenate([jnp.where(owner == i, book, 0.0) for i in range(len(pack))], axis=0).astype(BF16)
-        for book, pack in zip(books, packs)
+        for book, pack in zip(books, packs_of(owned))
     ]
-    total = None
-    for span in spans_of(size):
+
+
+def add_spans(total, wide, codes_ref, pieces, spans):
+    owned = codes_ref.shape[1]
+    for span in spans:
         codes = span_codes(codes_ref, span)
         hi, lo = codes >> 3, codes & 7
         rows = codes.shape[1]
         rebuilt = []
-        for g, pack in enumerate(packs):
+        for g, pack in enumerate(packs_of(owned)):
             spread = mm(wide[g], hi_table(hi, pack))
             for j, m in enumerate(pack):
                 low = jnp.broadcast_to(lo[m : m + 1, :], (SUB, rows))
-                at = j * block
+                at = j * LO * SUB
                 value = spread[at : at + SUB]
                 for level in range(1, LO):
                     value = jnp.where(low == level, spread[at + level * SUB : at + (level + 1) * SUB], value)
                 rebuilt.append(value)
-        part = mm(jnp.concatenate(rebuilt, axis=0).astype(BF16), span_rows(chunks, span))
+        part = mm(jnp.concatenate(rebuilt, axis=0).astype(BF16), span_rows(pieces, span))
         total = part if total is None else total + part
+    return total
+
+
+def flat(chunks):
+    return {k: len(c) for k, c in chunks.items()}, [piece for c in chunks.values() for piece in c]
+
+
+def cross_near_kernel(held, groups, codes_ref, *refs):
+    sums, pieces, outs = refs[:groups], pieces_of(held, refs[groups:]), refs[groups + sum(held.values()) :]
+    total_ref, wide_ref, counts_ref = outs
+    owned = codes_ref.shape[1]
+    books, counts = read_books(sums, None, owned)
+    counts_ref[...] = counts
+    wide = widen(books, owned)
+    for g, one in enumerate(wide):
+        wide_ref[g, : one.shape[0], :] = one
+    total_ref[...] = add_spans(None, wide, codes_ref, pieces, spans_of(held))
+
+
+def cross_near_call(codes, sums, chunks):
+    owned = codes.shape[1]
+    packs = len(packs_of(owned))
+    held, rows = flat(chunks)
+    return pl.pallas_call(
+        functools.partial(cross_near_kernel, held, len(sums)),
+        out_shape=(
+            jax.ShapeDtypeStruct((owned * SUB, rows[0].shape[1]), F32),
+            jax.ShapeDtypeStruct((packs, PACK * LO * SUB, 128), BF16),
+            jax.ShapeDtypeStruct((packs * LO, 128), F32),
+        ),
+        in_specs=[vmem_spec()] * (1 + len(sums) + len(rows)),
+        out_specs=(vmem_spec(),) * 3,
+        compiler_params=params(*rows),
+        cost_estimate=cost(0),
+        name="cross_near",
+    )(codes, *sums, *rows)
+
+
+def cross_far_kernel(held, total_rows, codes_ref, total_ref, wide_ref, *refs):
+    pieces, cross_ref = pieces_of(held, refs), refs[-1]
+    packs = packs_of(codes_ref.shape[1])
+    wide = [wide_ref[g, : len(pack) * LO * SUB, :] for g, pack in enumerate(packs)]
+    total = add_spans(total_ref[...], wide, codes_ref, pieces, spans_of(held))
     cross_ref[...] = (total * (1.0 / total_rows)).astype(BF16)
 
 
+def cross_far_call(codes, total, wide, chunks, total_rows):
+    held, rows = flat(chunks)
+    return pl.pallas_call(
+        functools.partial(cross_far_kernel, held, total_rows),
+        out_shape=jax.ShapeDtypeStruct(total.shape, BF16),
+        in_specs=[vmem_spec()] * (3 + len(rows)),
+        out_specs=vmem_spec(),
+        compiler_params=params(*rows),
+        cost_estimate=cost(0),
+        name="cross_far",
+    )(codes, total, wide, *rows)
+
+
+def cross_kernel(held, groups, total_rows, codes_ref, *refs):
+    sums, counts_in, pieces = refs[:groups], refs[groups], pieces_of(held, refs[groups + 1 :])
+    cross_ref, book_ref = refs[-2:]
+    owned = codes_ref.shape[1]
+    block = LO * SUB
+    books, unused = read_books(sums, counts_in, owned)
+    for g, book in enumerate(books):
+        book_ref[g * block : (g + 1) * block, :] = book
+    total = add_spans(None, widen(books, owned), codes_ref, pieces, spans_of(held))
+    cross_ref[...] = (total * (1.0 / total_rows)).astype(BF16)
+
+
 def cross_call(codes, sums, counts, chunks, total_rows):
-    size, owned, unused = codes.shape
-    packs = len(packs_of(owned))
-    width = chunks[0].shape[1]
-    with_counts = counts is None
-    extra = jax.ShapeDtypeStruct((packs * LO * (1 if with_counts else SUB), 128), F32)
-    small = list(sums) + ([] if with_counts else [counts])
-    return pl.pallas_call(
-        functools.partial(cross_kernel, size, len(sums), with_counts, total_rows),
-        out_shape=(jax.ShapeDtypeStruct((owned * SUB, width), BF16), extra),
-        in_specs=[vmem_spec()] * (1 + len(small) + len(chunks)),
+    owned = codes.shape[1]
+    held, rows = flat(chunks)
+    return pl.pallas_call(
+        functools.partial(cross_kernel, held, len(sums), total_rows),
+        out_shape=(
+            jax.ShapeDtypeStruct((owned * SUB, rows[0].shape[1]), BF16),
+            jax.ShapeDtypeStruct((len(packs_of(owned)) * LO * SUB, 128), F32),
+        ),
+        in_specs=[vmem_spec()] * (2 + len(sums) + len(rows)),
         out_specs=(vmem_spec(), vmem_spec()),
-        compiler_params=params(*chunks),
+        compiler_params=params(*rows),
+        cost_estimate=cost(0),
         name="cross",
-    )(codes, *small, *chunks)
+    )(codes, *sums, counts, *rows)
 
 
 def bands(x):
@@ -367,8 +451,9 @@
     return jnp.concatenate([p.astype(F32) for p in parts], axis=0).astype(BF16)
 
 
-def next_sums_kernel(size, codes_ref, *refs):
-    parts, chunks, out_ref = refs[:size], refs[size : 3 * size], refs[3 * size]
+def next_sums_kernel(held, codes_ref, *refs):
+    size = len(held)
+    parts, pieces, out_ref = refs[:size], pieces_of(held, refs[size:]), refs[-1]
     owned = codes_ref.shape[1]
     height = parts[0].shape[0]
     x = first_step(join([ref[...] for ref in parts]))
@@ -377,8 +462,8 @@
     gram = mm(mine.astype(BF16), xb, NT)
     rotation_rows = (1.5 * mine - 0.5 * mm(gram.astype(BF16), xb)).astype(BF16)
     totals = None
-    for span in spans_of(size):
-        rotated = mm(rotation_rows, span_rows(chunks, span), NT).astype(BF16).astype(F32)
+    for span in spans_of(held):
+        rotated = mm(rotation_rows, span_rows(pieces, span), NT).astype(BF16).astype(F32)
         codes = span_codes(codes_ref, span)
         more = [pack_sums(rotated, codes, pack, False) for pack in packs_of(owned)]
         totals = more if totals is None else [a + b for a, b in zip(totals, more)]
@@ -386,18 +471,20 @@
 
 
 def next_sums_call(codes, blocks, chunks):
-    size, owned, unused = codes.shape
-    return pl.pallas_call(
-        functools.partial(next_sums_kernel, size),
+    owned = codes.shape[1]
+    held, rows = flat(chunks)
+    return pl.pallas_call(
+        functools.partial(next_sums_kernel, held),
         out_shape=jax.ShapeDtypeStruct((pack_layout(owned, False)[2], 128), BF16),
-        in_specs=[vmem_spec()] * (1 + len(blocks) + len(chunks)),
+        in_specs=[vmem_spec()] * (1 + len(blocks) + len(rows)),
         out_specs=vmem_spec(),
-        compiler_params=params(*chunks),
+        compiler_params=params(*rows),
+        cost_estimate=cost(0),
         name="next_sums",
-    )(codes, *blocks, *chunks)
-
-
-def final_kernel(size, place_ref, upper_ref, lower_ref, *refs):
+    )(codes, *blocks, *rows)
+
+
+def final_kernel(size, place_ref, residual_ref, *refs):
     parts, out_ref, whole = refs[:size], refs[size], refs[size + 1]
     height = parts[0].shape[0]
     for k, ref in enumerate(parts):
@@ -405,41 +492,51 @@
         whole[pl.ds(at, height), :] = ref[...].astype(whole.dtype)
     x = first_step(whole[...].astype(BF16))
     xb = jnp.concatenate([band.astype(BF16) for band in x], axis=0)
-    residual = jnp.concatenate([upper_ref[...], lower_ref[...]], axis=0)
+    residual = residual_ref[...]
     for i, band in enumerate(x):
         gram = mm(xb[i * BAND : (i + 1) * BAND], xb, NT).astype(BF16)
         rotation = (1.5 * band - 0.5 * mm(gram, xb)).astype(BF16)
         out_ref[:, i * BAND : (i + 1) * BAND] = mm(residual, rotation, NT).astype(BF16)
 
 
-def final_call(place, upper, lower, blocks):
-    rows, width = upper.shape
+def final_call(place, residual, blocks):
+    rows, width = residual.shape
     kind = BF16 if blocks[0].shape[0] % 16 == 0 else F32
     return pl.pallas_call(
         functools.partial(final_kernel, len(blocks)),
-        out_shape=jax.ShapeDtypeStruct((2 * rows, width), BF16),
-        in_specs=[smem_spec()] + [vmem_spec()] * (2 + len(blocks)),
+        out_shape=jax.ShapeDtypeStruct((rows, width), BF16),
+        in_specs=[smem_spec()] + [vmem_spec()] * (1 + len(blocks)),
         out_specs=vmem_spec(),
         scratch_shapes=[pltpu.VMEM((width, width), kind)],
         compiler_params=params(),
+        cost_estimate=cost(0),
         name="final",
-    )(place, upper, lower, *blocks)
-
-
-def gather_rows(halves, size):
-    bits = [1 << b for b in range(1, size.bit_length() - 1)]
-    held = [{0: half} for half in halves]
-    for h in range(2):
-        held[h][1] = swap(held[h][0], "within", size, 1)
-    for step in range(len(bits)):
-        for h in range(2):
-            bit = bits[step] if h == 0 else bits[len(bits) - 1 - step]
-            for k in [k for k in held[h] if k % 2 == 0]:
-                held[h][k ^ bit] = swap(held[h][k], "within", size, bit)
-    for h in range(2):
-        for k in [k for k in held[h] if k % 2 == 0 and k]:
-            held[h][k ^ 1] = swap(held[h][k], "within", size, 1)
-    return [held[h][k] for k in range(size) for h in range(2)]
+    )(place, residual, *blocks)
+
+
+def after(x, *first):
+    return lax.optimization_barrier((x,) + first)[0]
+
+
+def near_rows(rows, size):
+    return {1 << b: swap(rows, "within", size, 1 << b) for b in range(1, size.bit_length() - 1)}
+
+
+def far_rows(rows, near, size):
+    bits = list(near)
+    half = rows.shape[0] // 2
+    halves = []
+    for order, cut in ((bits, slice(0, half)), (bits[::-1], slice(half, None))):
+        here = {0: rows, order[0]: near[order[0]][cut]}
+        for bit in order[1:]:
+            for k in list(here):
+                here[k ^ bit] = swap(here[k], "within", size, bit) if k else near[bit][cut]
+        halves.append(here)
+    return {k: (halves[0][k], halves[1][k]) for k in halves[0] if k and k not in near}
+
+
+def both_cores(whole, size):
+    return {k ^ 1: tuple(swap(piece, "within", size, 1) for piece in pieces) for k, pieces in whole.items()}
 
 
 def gather_group(x, size):
@@ -449,14 +546,17 @@
     return [blocks[k] for k in range(size)]
 
 
-def scatter_sums(even, odd, owned, rows, size):
-    merged = merge_cores_call(even, swap(odd, "within", size, 1), owned)
+def scatter_sums(merged, owned, rows, size):
     parts = [merged[0]] + [swap(merged[k // 2], "within", size, k) for k in range(2, size, 2)]
     return merge_chips_call(parts, owned, rows)
 
 
 def everywhere(x, size):
     return [x] + [swap(x, "group", size, k) for k in range(1, size)]
+
+
+def reduce_cross(cross, size):
+    return tree([p.astype(F32) for p in everywhere(cross, size)]).astype(BF16)
 
 
 def per_device(vectors, centroids, list_ids, codes, rotation):
@@ -466,22 +566,34 @@
     owned = codes.shape[1] // size
     total_rows = rows * size * groups
     place = lax.axis_index("within").astype(jnp.int32).reshape(1)
-    upper, lower = residual_call(vectors, centroids, list_ids)
-    chunks = gather_rows((upper, lower), size)
-    even, odd = local_sums_call(place, rotation, codes.T, upper, lower, size)
-    sums, own_codes = scatter_sums(even, odd, owned, rows, size)
-    counts = None
-    for alternation in range(ALTS):
-        parts = everywhere(sums, groups)
-        cross, extra = cross_call(own_codes, parts, counts, chunks, total_rows)
-        block = tree([p.astype(F32) for p in everywhere(cross, groups)]).astype(BF16)
-        blocks = gather_group(block, size)
-        if alternation + 1 < ALTS:
-            counts = extra
-            sums = next_sums_call(own_codes, blocks, chunks)
-    rotated_out = final_call(place, upper, lower, blocks)
+    residual = residual_call(vectors, centroids, list_ids)
+    near = near_rows(residual, size)
+    twin = swap(residual, "within", size, 1)
+    even, odd = local_sums_call(place, rotation, codes.T, after(residual, twin), size)
+    merged = merge_cores_call(even, swap(odd, "within", size, 1), owned)
+    sums, own_codes = scatter_sums(merged, owned, rows, size)
+    far = far_rows(residual, near, size)
+    near = {k: after(rows_near, sums) for k, rows_near in near.items()}
+    for bit in [1 << b for b in range(groups.bit_length() - 2)]:
+        sums = merge_call(sums, swap(sums, "group", groups, bit), owned)
+    parts = [sums, swap(sums, "group", groups, groups // 2)]
+    chunks = {0: (residual,), 1: (twin,)}
+    for k, rows_near in near.items():
+        chunks[k] = (rows_near,)
+        chunks[k ^ 1] = (swap(rows_near, "within", size, 1),)
+    total, wide, counts = cross_near_call(own_codes, parts, chunks)
+    far = {k: tuple(after(piece, parts[1]) for piece in pieces) for k, pieces in far.items()}
+    far = {**far, **both_cores(far, size)}
+    cross = cross_far_call(own_codes, total, wide, far, total_rows)
+    chunks.update(far)
+    for alternation in range(1, ALTS):
+        blocks = gather_group(reduce_cross(cross, groups), size)
+        parts = everywhere(next_sums_call(own_codes, blocks, chunks), groups)
+        cross, book = cross_call(own_codes, parts, counts, chunks, total_rows)
+    blocks = gather_group(reduce_cross(cross, groups), size)
+    rotated_out = final_call(place, residual, blocks)
     packs = len(packs_of(owned))
-    book = extra.reshape(packs, LO * SUB, PACK, HI).transpose(0, 2, 3, 1).reshape(packs * PACK, K * SUB)
+    book = book.reshape(packs, LO * SUB, PACK, HI).transpose(0, 2, 3, 1).reshape(packs * PACK, K * SUB)
     return (rotated_out, book[:owned])
 
 

time: 133 us -> 122 us (0.917)
  waiting for transfers between devices: 63.2 us -> 51.5 us
    ppermute x44 -> x38, waiting for transfers between devices: 63.2 us -> 51.5 us  [swap(): return lax.ppermute(x, axis, [(i, i ^ bits) for i in range(size)])]
    ppermute x44 -> x38, starting transfers between devices: 38.7 us -> 39.8 us  [swap(): return lax.ppermute(x, axis, [(i, i ^ bits) for i in range(size)])]
    pallas_call x4 -> x6, Pallas kernels: 13.5 us -> 13.9 us  [the longest x1 6.83 us: next_sums_call(): pl.pallas_call(functools.partial(next_sums_kernel, held), out_shape=jax.S...]
  transfers between devices with their start and end apart: 44 -> 38, of which waited for: 25 -> 21; matrix products, arithmetic and copies ran while one was open for 1% -> 1% of each run, Pallas kernels for 0% -> 5%
where the time goes in v3:
time: 122 us
  waiting for transfers between devices  51.5 us (42%)
  starting transfers between devices  39.8 us (33%)
  Pallas kernels  23.5 us (19%)
  local copies, waits for them, and re-layouts  6.38 us (5%)
    ppermute x38, waiting for transfers between devices, swap(): return lax.ppermute(x, axis, [(i, i ^ bits) for i in range(size)])  51.5 us
    ppermute x38, starting transfers between devices, swap(): return lax.ppermute(x, axis, [(i, i ^ bits) for i in range(size)])  39.8 us
    pallas_call x1, Pallas kernels, next_sums_call(): pl.pallas_call(functools.partial(next_sums_kernel, held), out_shape=jax.S...  6.83 us
    pallas_call x1, Pallas kernels, final_call(): pl.pallas_call(functools.partial(final_kernel, len(blocks)), out_shape=ja...  6.21 us
    unnamed x10, local copies, waits for them, and re-layouts  5.33 us
    pallas_call x1, Pallas kernels, local_sums_call(): pl.pallas_call(functools.partial(local_sums_kernel, size), out_shape=(sha...  3.27 us
    pallas_call x1, Pallas kernels, cross_call(): pl.pallas_call(functools.partial(cross_kernel, held, len(sums), total_row...  2.97 us
  transfers between devices with their start and end apart: 38, of which 21 were waited for; matrix products, arithmetic and copies ran while one was open for 1% of the time, Pallas kernels for 5%

profile of v3, /device:TPU:0, one launch (start us, length us, event | category | flops | bytes accessed | tf_op | source)
XLA Modules:
  0.0 122.1 jit_solution(6666223547413389616)
XLA Ops:
  4.7 2.6 %collective-permute-start.9 = (bf16[512,768]{1,0:T(8,128)(2,1)S(1)}, bf16[512,768]{1,0:T(8,128)(2,1)S(1)}, u32[]{:S(2)}, u32[]{:S(2)}) collective-permute-start(bf16[512,768]{1,0:T(8,128)(2,1)S(1)} %residual.1.residual_ref.refs_2_.refs_8_.refs_5_), channel_id=1, source_target_pairs={{0,4},{1,5},{2,6},{3,7},{4,0},{5,1},{6,2},{7,3},{8,12},{9,13},{10,... | collective-permute-start | bytes 2359304 | tf_op jit(solution)/shard_map/ppermute | solution.py:50
  8.8 1.7 %copy-done = f32[768,768]{1,0:T(8,128)S(1)} copy-done((f32[768,768]{1,0:T(8,128)S(1)}, f32[768,768]{1,0:T(8,128)}, u32[]{:S(2)}) %copy-start) | copy-done | bytes 2359320
  11.4 3.3 %local_sums.1 = (bf16[4,304,128]{2,1,0:T(8,128)(2,1)S(1)}, bf16[4,304,128]{2,1,0:T(8,128)(2,1)S(1)}) custom-call(s32[1]{0:T(128)} %bitcast.place_ref, f32[768,768]{1,0:T(8,128)S(1)} %copy-done, s32[96,512]{1,0:T(8,128)S(1)} %bitcast.8, bf16[512,768]{1,0:T(8,128)(2,1)S(1)} %residual.1.residual_ref.refs_2_.refs_8_.refs_5_), custom_call_target="tpu_custom_call" | custom-call | tf_op jit(solution)/shard_map/local_sums/pallas_call | solution.py:197
  14.7 1.6 %collective-permute-done.1.came_ref = bf16[4,304,128]{2,1,0:T(8,128)(2,1)S(1)} collective-permute-done((bf16[4,304,128]{2,1,0:T(8,128)(2,1)S(1)}, bf16[4,304,128]{2,1,0:T(8,128)(2,1)S(1)}, u32[]{:S(2)}, u32[]{:S(2)}) %collective-permute-start.1) | collective-permute-done | bytes 311328 | tf_op jit(solution)/shard_map/ppermute | solution.py:50
  17.2 1.5 %collective-permute-start.3 = (bf16[368,128]{1,0:T(8,128)(2,1)S(1)}, bf16[368,128]{1,0:T(8,128)(2,1)S(1)}, u32[]{:S(2)}, u32[]{:S(2)}) collective-permute-start(bf16[368,128]{1,0:T(8,128)(2,1)S(1)} %get-tuple-element.25), channel_id=1, source_target_pairs={{0,4},{1,5},{2,6},{3,7},{4,0},{5,1},{6,2},{7,3},{8,12},{9,13},{10,... | collective-permute-start | bytes 282632 | tf_op jit(solution)/shard_map/ppermute | solution.py:50
  20.0 5.7 %collective-permute-done.9.refs_6_.refs_12_.refs_9_ = bf16[512,768]{1,0:T(8,128)(2,1)S(1)} collective-permute-done((bf16[512,768]{1,0:T(8,128)(2,1)S(1)}, bf16[512,768]{1,0:T(8,128)(2,1)S(1)}, u32[]{:S(2)}, u32[]{:S(2)}) %collective-permute-start.9) | collective-permute-done | bytes 786464 | tf_op jit(solution)/shard_map/ppermute | solution.py:50
  25.7 2.0 %collective-permute-start.12 = (bf16[256,768]{1,0:T(8,128)(2,1)S(1)}, bf16[256,768]{1,0:T(8,128)(2,1)S(1)}, u32[]{:S(2)}, u32[]{:S(2)}) collective-permute-start(bf16[256,768]{1,0:T(8,128)(2,1)S(1)} %slice.9), channel_id=1, source_target_pairs={{0,2},{1,3},{2,0},{3,1},{4,6},{5,7},{6,4},{7,5},{8,10},{9,11},{10,... | collective-permute-start | bytes 1179656 | tf_op jit(solution)/shard_map/ppermute | solution.py:50
  27.7 1.6 %collective-permute-start.11 = (bf16[256,768]{1,0:T(8,128)(2,1)S(1)}, bf16[256,768]{1,0:T(8,128)(2,1)S(1)}, u32[]{:S(2)}, u32[]{:S(2)}) collective-permute-start(bf16[256,768]{1,0:T(8,128)(2,1)S(1)} %slice.8), channel_id=1, source_target_pairs={{0,4},{1,5},{2,6},{3,7},{4,0},{5,1},{6,2},{7,3},{8,12},{9,13},{10,... | collective-permute-start | bytes 1179656 | tf_op jit(solution)/shard_map/ppermute | solution.py:50
  31.8 2.0 %collective-permute-start.5 = (bf16[240,128]{1,0:T(8,128)(2,1)S(1)}, bf16[240,128]{1,0:T(8,128)(2,1)S(1)}, u32[]{:S(2)}, u32[]{:S(2)}) collective-permute-start(bf16[240,128]{1,0:T(8,128)(2,1)S(1)} %get-tuple-element.28.first_ref), channel_id=1, source_target_pairs={{0,8},{8,0},{16,24},{24,16},{1,9},{9,1},{17,25},{25,17},{2,10},{10... | collective-permute-start | bytes 184328 | tf_op jit(solution)/shard_map/ppermute | solution.py:50
  33.9 2.2 %collective-permute-done.5.second_ref = bf16[240,128]{1,0:T(8,128)(2,1)S(1)} collective-permute-done((bf16[240,128]{1,0:T(8,128)(2,1)S(1)}, bf16[240,128]{1,0:T(8,128)(2,1)S(1)}, u32[]{:S(2)}, u32[]{:S(2)}) %collective-permute-start.5) | collective-permute-done | bytes 61472 | tf_op jit(solution)/shard_map/ppermute | solution.py:50
  36.2 3.1 %collective-permute-start.6 = (bf16[240,128]{1,0:T(8,128)(2,1)S(1)}, bf16[240,128]{1,0:T(8,128)(2,1)S(1)}, u32[]{:S(2)}, u32[]{:S(2)}) collective-permute-start(bf16[240,128]{1,0:T(8,128)(2,1)S(1)} %merge_groups.1.refs_0_), channel_id=1, source_target_pairs={{0,16},{8,24},{16,0},{24,8},{1,17},{9,25},{17,1},{25,9},{2,18},{10... | collective-permute-start | bytes 184328 | tf_op jit(solution)/shard_map/ppermute | solution.py:50
  39.4 2.3 %collective-permute-done.6.refs_1_ = bf16[240,128]{1,0:T(8,128)(2,1)S(1)} collective-permute-done((bf16[240,128]{1,0:T(8,128)(2,1)S(1)}, bf16[240,128]{1,0:T(8,128)(2,1)S(1)}, u32[]{:S(2)}, u32[]{:S(2)}) %collective-permute-start.6) | collective-permute-done | bytes 61472 | tf_op jit(solution)/shard_map/ppermute | solution.py:50
  42.2 2.3 %cross_near.1 = (f32[96,768]{1,0:T(8,128)S(1)}, bf16[3,256,128]{2,1,0:T(8,128)(2,1)S(1)}, f32[24,128]{1,0:T(8,128)S(1)}) custom-call(s32[8,12,512]{2,1,0:T(8,128)S(1)} %get-tuple-element.27.codes_ref, bf16[240,128]{1,0:T(8,128)(2,1)S(1)} %merge_groups.1.refs_0_, bf16[240,128]{1,0:T(8,128)(2,1)S(1)} %collective-permute-done.6.refs_1_, ...), custom_call_target="tpu_custom_call" | custom-call | tf_op jit(solution)/shard_map/cross_near/pallas_call | solution.py:365
  45.5 4.3 %collective-permute-start.17 = (bf16[96,768]{1,0:T(8,128)(2,1)S(1)}, bf16[96,768]{1,0:T(8,128)(2,1)S(1)}, u32[]{:S(2)}, u32[]{:S(2)}) collective-permute-start(bf16[96,768]{1,0:T(8,128)(2,1)S(1)} %cross_far.1), channel_id=1, source_target_pairs={{0,24},{8,16},{16,8},{24,0},{1,25},{9,17},{17,9},{25,1},{2,26},{10... | collective-permute-start | bytes 442376 | tf_op jit(solution)/shard_map/ppermute | solution.py:50
  50.4 4.1 %collective-permute-done.17 = bf16[96,768]{1,0:T(8,128)(2,1)S(1)} collective-permute-done((bf16[96,768]{1,0:T(8,128)(2,1)S(1)}, bf16[96,768]{1,0:T(8,128)(2,1)S(1)}, u32[]{:S(2)}, u32[]{:S(2)}) %collective-permute-start.17) | collective-permute-done | bytes 147488 | tf_op jit(solution)/shard_map/ppermute | solution.py:50
  54.5 7.3 %collective-permute-done.16 = bf16[96,768]{1,0:T(8,128)(2,1)S(1)} collective-permute-done((bf16[96,768]{1,0:T(8,128)(2,1)S(1)}, bf16[96,768]{1,0:T(8,128)(2,1)S(1)}, u32[]{:S(2)}, u32[]{:S(2)}) %collective-permute-start.16) | collective-permute-done | bytes 147488 | tf_op jit(solution)/shard_map/ppermute | solution.py:50
  61.9 2.5 %collective-permute-start.23 = (bf16[96,768]{1,0:T(8,128)(2,1)S(1)}, bf16[96,768]{1,0:T(8,128)(2,1)S(1)}, u32[]{:S(2)}, u32[]{:S(2)}) collective-permute-start(bf16[96,768]{1,0:T(8,128)(2,1)S(1)} %add_convert_fusion.1.refs_0_), channel_id=1, source_target_pairs={{0,6},{1,7},{2,4},{3,5},{4,2},{5,3},{6,0},{7,1},{8,14},{9,15},{10,... | collective-permute-start | bytes 442376 | tf_op jit(solution)/shard_map/ppermute | solution.py:50
  65.5 3.5 %collective-permute-done.23.refs_6_ = bf16[96,768]{1,0:T(8,128)(2,1)S(1)} collective-permute-done((bf16[96,768]{1,0:T(8,128)(2,1)S(1)}, bf16[96,768]{1,0:T(8,128)(2,1)S(1)}, u32[]{:S(2)}, u32[]{:S(2)}) %collective-permute-start.23) | collective-permute-done | bytes 147488 | tf_op jit(solution)/shard_map/ppermute | solution.py:50
  69.0 1.9 %collective-permute-done.21.refs_4_ = bf16[96,768]{1,0:T(8,128)(2,1)S(1)} collective-permute-done((bf16[96,768]{1,0:T(8,128)(2,1)S(1)}, bf16[96,768]{1,0:T(8,128)(2,1)S(1)}, u32[]{:S(2)}, u32[]{:S(2)}) %collective-permute-start.21) | collective-permute-done | bytes 147488 | tf_op jit(solution)/shard_map/ppermute | solution.py:50
  72.5 6.8 %next_sums.1.refs_0_ = bf16[192,128]{1,0:T(8,128)(2,1)S(1)} custom-call(s32[8,12,512]{2,1,0:T(8,128)S(1)} %get-tuple-element.27.codes_ref, bf16[96,768]{1,0:T(8,128)(2,1)S(1)} %add_convert_fusion.1.refs_0_, bf16[96,768]{1,0:T(8,128)(2,1)S(1)} %collective-permute-done.18.refs_1_, bf16[96,768]{1,0:T(8,128)(2,1)S(1)} %collective-permute-done.19.refs_2_, ...), custom_call_target="tpu_custom_call" | custom-call | tf_op jit(solution)/shard_map/next_sums/pallas_call | solution.py:476
  79.4 2.7 %collective-permute-start.27 = (bf16[192,128]{1,0:T(8,128)(2,1)S(1)}, bf16[192,128]{1,0:T(8,128)(2,1)S(1)}, u32[]{:S(2)}, u32[]{:S(2)}) collective-permute-start(bf16[192,128]{1,0:T(8,128)(2,1)S(1)} %next_sums.1.refs_0_), channel_id=1, source_target_pairs={{0,24},{8,16},{16,8},{24,0},{1,25},{9,17},{17,9},{25,1},{2,26},{10... | collective-permute-start | bytes 147464 | tf_op jit(solution)/shard_map/ppermute | solution.py:50
  82.1 1.8 %collective-permute-start.25 = (bf16[192,128]{1,0:T(8,128)(2,1)S(1)}, bf16[192,128]{1,0:T(8,128)(2,1)S(1)}, u32[]{:S(2)}, u32[]{:S(2)}) collective-permute-start(bf16[192,128]{1,0:T(8,128)(2,1)S(1)} %next_sums.1.refs_0_), channel_id=1, source_target_pairs={{0,8},{8,0},{16,24},{24,16},{1,9},{9,1},{17,25},{25,17},{2,10},{10... | collective-permute-start | bytes 147464 | tf_op jit(solution)/shard_map/ppermute | solution.py:50
  83.8 1.9 %collective-permute-done.27.refs_3_ = bf16[192,128]{1,0:T(8,128)(2,1)S(1)} collective-permute-done((bf16[192,128]{1,0:T(8,128)(2,1)S(1)}, bf16[192,128]{1,0:T(8,128)(2,1)S(1)}, u32[]{:S(2)}, u32[]{:S(2)}) %collective-permute-start.27) | collective-permute-done | bytes 49184 | tf_op jit(solution)/shard_map/ppermute | solution.py:50
  85.8 1.6 %collective-permute-done.26.refs_2_ = bf16[192,128]{1,0:T(8,128)(2,1)S(1)} collective-permute-done((bf16[192,128]{1,0:T(8,128)(2,1)S(1)}, bf16[192,128]{1,0:T(8,128)(2,1)S(1)}, u32[]{:S(2)}, u32[]{:S(2)}) %collective-permute-start.26) | collective-permute-done | bytes 49184 | tf_op jit(solution)/shard_map/ppermute | solution.py:50
  87.3 3.0 %cross.1 = (bf16[96,768]{1,0:T(8,128)(2,1)S(1)}, f32[192,128]{1,0:T(8,128)S(1)}) custom-call(s32[8,12,512]{2,1,0:T(8,128)S(1)} %get-tuple-element.27.codes_ref, bf16[192,128]{1,0:T(8,128)(2,1)S(1)} %next_sums.1.refs_0_, bf16[192,128]{1,0:T(8,128)(2,1)S(1)} %collective-permute-done.25.refs_1_, bf16[192,128]{1,0:T(8,128)(2,1)S(1)} %collective-permute-done.26.refs_2_, ...), custom_call_target="tpu_custom_call" | custom-call | tf_op jit(solution)/shard_map/cross/pallas_call | solution.py:416
  90.3 2.7 %collective-permute-start.30 = (bf16[96,768]{1,0:T(8,128)(2,1)S(1)}, bf16[96,768]{1,0:T(8,128)(2,1)S(1)}, u32[]{:S(2)}, u32[]{:S(2)}) collective-permute-start(bf16[96,768]{1,0:T(8,128)(2,1)S(1)} %get-tuple-element.36), channel_id=1, source_target_pairs={{0,24},{8,16},{16,8},{24,0},{1,25},{9,17},{17,9},{25,1},{2,26},{10... | collective-permute-start | bytes 442376 | tf_op jit(solution)/shard_map/ppermute | solution.py:50
  93.0 1.8 %collective-permute-start.28 = (bf16[96,768]{1,0:T(8,128)(2,1)S(1)}, bf16[96,768]{1,0:T(8,128)(2,1)S(1)}, u32[]{:S(2)}, u32[]{:S(2)}) collective-permute-start(bf16[96,768]{1,0:T(8,128)(2,1)S(1)} %get-tuple-element.36), channel_id=1, source_target_pairs={{0,8},{8,0},{16,24},{24,16},{1,9},{9,1},{17,25},{25,17},{2,10},{10... | collective-permute-start | bytes 442376 | tf_op jit(solution)/shard_map/ppermute | solution.py:50
  94.7 4.2 %collective-permute-done.30 = bf16[96,768]{1,0:T(8,128)(2,1)S(1)} collective-permute-done((bf16[96,768]{1,0:T(8,128)(2,1)S(1)}, bf16[96,768]{1,0:T(8,128)(2,1)S(1)}, u32[]{:S(2)}, u32[]{:S(2)}) %collective-permute-start.30) | collective-permute-done | bytes 147488 | tf_op jit(solution)/shard_map/ppermute | solution.py:50
  98.9 6.3 %collective-permute-done.29 = bf16[96,768]{1,0:T(8,128)(2,1)S(1)} collective-permute-done((bf16[96,768]{1,0:T(8,128)(2,1)S(1)}, bf16[96,768]{1,0:T(8,128)(2,1)S(1)}, u32[]{:S(2)}, u32[]{:S(2)}) %collective-permute-start.29) | collective-permute-done | bytes 147488 | tf_op jit(solution)/shard_map/ppermute | solution.py:50
  105.3 1.8 %collective-permute-start.36 = (bf16[96,768]{1,0:T(8,128)(2,1)S(1)}, bf16[96,768]{1,0:T(8,128)(2,1)S(1)}, u32[]{:S(2)}, u32[]{:S(2)}) collective-permute-start(bf16[96,768]{1,0:T(8,128)(2,1)S(1)} %add_convert_fusion.refs_0_), channel_id=1, source_target_pairs={{0,6},{1,7},{2,4},{3,5},{4,2},{5,3},{6,0},{7,1},{8,14},{9,15},{10,... | collective-permute-start | bytes 442376 | tf_op jit(solution)/shard_map/ppermute | solution.py:50
  108.9 4.1 %collective-permute-done.36.refs_6_ = bf16[96,768]{1,0:T(8,128)(2,1)S(1)} collective-permute-done((bf16[96,768]{1,0:T(8,128)(2,1)S(1)}, bf16[96,768]{1,0:T(8,128)(2,1)S(1)}, u32[]{:S(2)}, u32[]{:S(2)}) %collective-permute-start.36) | collective-permute-done | bytes 147488 | tf_op jit(solution)/shard_map/ppermute | solution.py:50
  115.9 6.2 %final.1 = bf16[512,768]{1,0:T(8,128)(2,1)} custom-call(s32[1]{0:T(128)} %bitcast.place_ref, bf16[512,768]{1,0:T(8,128)(2,1)S(1)} %residual.1.residual_ref.refs_2_.refs_8_.refs_5_, bf16[96,768]{1,0:T(8,128)(2,1)S(1)} %add_convert_fusion.refs_0_, bf16[96,768]{1,0:T(8,128)(2,1)S(1)} %collective-permute-done.31.refs_1_, ...), custom_call_target="tpu_custom_call" | custom-call | tf_op jit(solution)/shard_map/final/pallas_call | solution.py:505
  (72 shorter events, 21.0 us)
Async XLA Ops:
  4.2 4.6 %collective-permute-start = (bf16[512,768]{1,0:T(8,128)(2,1)S(1)}, bf16[512,768]{1,0:T(8,128)(2,1)S(1)}, u32[]{:S(2)}, u32[]{:S(2)}) collective-permute-start(bf16[512,768]{1,0:T(8,128)(2,1)S(1)} %residual.1.residual_ref.refs_2_.refs_8_.refs_5_), channel_id=1, source_target_pairs={{0,1},{1,0},{2,3},{3,2},{4,5},{5,4},{6,7},{7,6},{8,9},{9,8},{10,11... | collective-permute-start | bytes 2359304 | tf_op jit(solution)/shard_map/ppermute | solution.py:50
  4.7 21.0 %collective-permute-start.9 = (bf16[512,768]{1,0:T(8,128)(2,1)S(1)}, bf16[512,768]{1,0:T(8,128)(2,1)S(1)}, u32[]{:S(2)}, u32[]{:S(2)}) collective-permute-start(bf16[512,768]{1,0:T(8,128)(2,1)S(1)} %residual.1.residual_ref.refs_2_.refs_8_.refs_5_), channel_id=1, source_target_pairs={{0,4},{1,5},{2,6},{3,7},{4,0},{5,1},{6,2},{7,3},{8,12},{9,13},{10,... | collective-permute-start | bytes 2359304 | tf_op jit(solution)/shard_map/ppermute | solution.py:50
  7.3 20.4 %collective-permute-start.7 = (bf16[512,768]{1,0:T(8,128)(2,1)S(1)}, bf16[512,768]{1,0:T(8,128)(2,1)S(1)}, u32[]{:S(2)}, u32[]{:S(2)}) collective-permute-start(bf16[512,768]{1,0:T(8,128)(2,1)S(1)} %residual.1.residual_ref.refs_2_.refs_8_.refs_5_), channel_id=1, source_target_pairs={{0,2},{1,3},{2,0},{3,1},{4,6},{5,7},{6,4},{7,5},{8,10},{9,11},{10,... | collective-permute-start | bytes 2359304 | tf_op jit(solution)/shard_map/ppermute | solution.py:50
  16.4 13.3 %collective-permute-start.2 = (bf16[368,128]{1,0:T(8,128)(2,1)S(1)}, bf16[368,128]{1,0:T(8,128)(2,1)S(1)}, u32[]{:S(2)}, u32[]{:S(2)}) collective-permute-start(bf16[368,128]{1,0:T(8,128)(2,1)S(1)} %get-tuple-element.24), channel_id=1, source_target_pairs={{0,2},{1,3},{2,0},{3,1},{4,6},{5,7},{6,4},{7,5},{8,10},{9,11},{10,... | collective-permute-start | bytes 282632 | tf_op jit(solution)/shard_map/ppermute | solution.py:50
  17.2 12.6 %collective-permute-start.3 = (bf16[368,128]{1,0:T(8,128)(2,1)S(1)}, bf16[368,128]{1,0:T(8,128)(2,1)S(1)}, u32[]{:S(2)}, u32[]{:S(2)}) collective-permute-start(bf16[368,128]{1,0:T(8,128)(2,1)S(1)} %get-tuple-element.25), channel_id=1, source_target_pairs={{0,4},{1,5},{2,6},{3,7},{4,0},{5,1},{6,2},{7,3},{8,12},{9,13},{10,... | collective-permute-start | bytes 282632 | tf_op jit(solution)/shard_map/ppermute | solution.py:50
  18.7 12.5 %collective-permute-start.4 = (bf16[368,128]{1,0:T(8,128)(2,1)S(1)}, bf16[368,128]{1,0:T(8,128)(2,1)S(1)}, u32[]{:S(2)}, u32[]{:S(2)}) collective-permute-start(bf16[368,128]{1,0:T(8,128)(2,1)S(1)} %get-tuple-element.26), channel_id=1, source_target_pairs={{0,6},{1,7},{2,4},{3,5},{4,2},{5,3},{6,0},{7,1},{8,14},{9,15},{10,... | collective-permute-start | bytes 282632 | tf_op jit(solution)/shard_map/ppermute | solution.py:50
  25.7 13.7 %collective-permute-start.12 = (bf16[256,768]{1,0:T(8,128)(2,1)S(1)}, bf16[256,768]{1,0:T(8,128)(2,1)S(1)}, u32[]{:S(2)}, u32[]{:S(2)}) collective-permute-start(bf16[256,768]{1,0:T(8,128)(2,1)S(1)} %slice.9), channel_id=1, source_target_pairs={{0,2},{1,3},{2,0},{3,1},{4,6},{5,7},{6,4},{7,5},{8,10},{9,11},{10,... | collective-permute-start | bytes 1179656 | tf_op jit(solution)/shard_map/ppermute | solution.py:50
  27.7 13.9 %collective-permute-start.11 = (bf16[256,768]{1,0:T(8,128)(2,1)S(1)}, bf16[256,768]{1,0:T(8,128)(2,1)S(1)}, u32[]{:S(2)}, u32[]{:S(2)}) collective-permute-start(bf16[256,768]{1,0:T(8,128)(2,1)S(1)} %slice.8), channel_id=1, source_target_pairs={{0,4},{1,5},{2,6},{3,7},{4,0},{5,1},{6,2},{7,3},{8,12},{9,13},{10,... | collective-permute-start | bytes 1179656 | tf_op jit(solution)/shard_map/ppermute | solution.py:50
  31.3 10.9 %collective-permute-start.8 = (bf16[512,768]{1,0:T(8,128)(2,1)S(1)}, bf16[512,768]{1,0:T(8,128)(2,1)S(1)}, u32[]{:S(2)}, u32[]{:S(2)}) collective-permute-start(bf16[512,768]{1,0:T(8,128)(2,1)S(1)} %collective-permute-done.7.refs_4_.refs_10_.refs_7_), channel_id=1, source_target_pairs={{0,1},{1,0},{2,3},{3,2},{4,5},{5,4},{6,7},{7,6},{8,9},{9,8},{10,11... | collective-permute-start | bytes 2359304 | tf_op jit(solution)/shard_map/ppermute | solution.py:50
  31.3 10.8 %collective-permute-start.10 = (bf16[512,768]{1,0:T(8,128)(2,1)S(1)}, bf16[512,768]{1,0:T(8,128)(2,1)S(1)}, u32[]{:S(2)}, u32[]{:S(2)}) collective-permute-start(bf16[512,768]{1,0:T(8,128)(2,1)S(1)} %collective-permute-done.9.refs_6_.refs_12_.refs_9_), channel_id=1, source_target_pairs={{0,1},{1,0},{2,3},{3,2},{4,5},{5,4},{6,7},{7,6},{8,9},{9,8},{10,11... | collective-permute-start | bytes 2359304 | tf_op jit(solution)/shard_map/ppermute | solution.py:50
  31.8 4.3 %collective-permute-start.5 = (bf16[240,128]{1,0:T(8,128)(2,1)S(1)}, bf16[240,128]{1,0:T(8,128)(2,1)S(1)}, u32[]{:S(2)}, u32[]{:S(2)}) collective-permute-start(bf16[240,128]{1,0:T(8,128)(2,1)S(1)} %get-tuple-element.28.first_ref), channel_id=1, source_target_pairs={{0,8},{8,0},{16,24},{24,16},{1,9},{9,1},{17,25},{25,17},{2,10},{10... | collective-permute-start | bytes 184328 | tf_op jit(solution)/shard_map/ppermute | solution.py:50
  36.2 5.5 %collective-permute-start.6 = (bf16[240,128]{1,0:T(8,128)(2,1)S(1)}, bf16[240,128]{1,0:T(8,128)(2,1)S(1)}, u32[]{:S(2)}, u32[]{:S(2)}) collective-permute-start(bf16[240,128]{1,0:T(8,128)(2,1)S(1)} %merge_groups.1.refs_0_), channel_id=1, source_target_pairs={{0,16},{8,24},{16,0},{24,8},{1,17},{9,25},{17,1},{25,9},{2,18},{10... | collective-permute-start | bytes 184328 | tf_op jit(solution)/shard_map/ppermute | solution.py:50
  41.7 2.9 %collective-permute-start.13 = (bf16[256,768]{1,0:T(8,128)(2,1)S(1)}, bf16[256,768]{1,0:T(8,128)(2,1)S(1)}, u32[]{:S(2)}, u32[]{:S(2)}) collective-permute-start(bf16[256,768]{1,0:T(8,128)(2,1)S(1)} %collective-permute-done.11.refs_0_.refs_14_.refs_11_), channel_id=1, source_target_pairs={{0,1},{1,0},{2,3},{3,2},{4,5},{5,4},{6,7},{7,6},{8,9},{9,8},{10,11... | collective-permute-start | bytes 1179656 | tf_op jit(solution)/shard_map/ppermute | solution.py:50
  41.7 2.9 %collective-permute-start.14 = (bf16[256,768]{1,0:T(8,128)(2,1)S(1)}, bf16[256,768]{1,0:T(8,128)(2,1)S(1)}, u32[]{:S(2)}, u32[]{:S(2)}) collective-permute-start(bf16[256,768]{1,0:T(8,128)(2,1)S(1)} %collective-permute-done.12.refs_1_.refs_15_.refs_12_), channel_id=1, source_target_pairs={{0,1},{1,0},{2,3},{3,2},{4,5},{5,4},{6,7},{7,6},{8,9},{9,8},{10,11... | collective-permute-start | bytes 1179656 | tf_op jit(solution)/shard_map/ppermute | solution.py:50
  45.5 9.0 %collective-permute-start.17 = (bf16[96,768]{1,0:T(8,128)(2,1)S(1)}, bf16[96,768]{1,0:T(8,128)(2,1)S(1)}, u32[]{:S(2)}, u32[]{:S(2)}) collective-permute-start(bf16[96,768]{1,0:T(8,128)(2,1)S(1)} %cross_far.1), channel_id=1, source_target_pairs={{0,24},{8,16},{16,8},{24,0},{1,25},{9,17},{17,9},{25,1},{2,26},{10... | collective-permute-start | bytes 442376 | tf_op jit(solution)/shard_map/ppermute | solution.py:50
  49.8 12.1 %collective-permute-start.16 = (bf16[96,768]{1,0:T(8,128)(2,1)S(1)}, bf16[96,768]{1,0:T(8,128)(2,1)S(1)}, u32[]{:S(2)}, u32[]{:S(2)}) collective-permute-start(bf16[96,768]{1,0:T(8,128)(2,1)S(1)} %cross_far.1), channel_id=1, source_target_pairs={{0,16},{8,24},{16,0},{24,8},{1,17},{9,25},{17,1},{25,9},{2,18},{10... | collective-permute-start | bytes 442376 | tf_op jit(solution)/shard_map/ppermute | solution.py:50
  49.8 12.1 %collective-permute-start.15 = (bf16[96,768]{1,0:T(8,128)(2,1)S(1)}, bf16[96,768]{1,0:T(8,128)(2,1)S(1)}, u32[]{:S(2)}, u32[]{:S(2)}) collective-permute-start(bf16[96,768]{1,0:T(8,128)(2,1)S(1)} %cross_far.1), channel_id=1, source_target_pairs={{0,8},{8,0},{16,24},{24,16},{1,9},{9,1},{17,25},{25,17},{2,10},{10... | collective-permute-start | bytes 442376 | tf_op jit(solution)/shard_map/ppermute | solution.py:50
  61.9 7.1 %collective-permute-start.23 = (bf16[96,768]{1,0:T(8,128)(2,1)S(1)}, bf16[96,768]{1,0:T(8,128)(2,1)S(1)}, u32[]{:S(2)}, u32[]{:S(2)}) collective-permute-start(bf16[96,768]{1,0:T(8,128)(2,1)S(1)} %add_convert_fusion.1.refs_0_), channel_id=1, source_target_pairs={{0,6},{1,7},{2,4},{3,5},{4,2},{5,3},{6,0},{7,1},{8,14},{9,15},{10,... | collective-permute-start | bytes 442376 | tf_op jit(solution)/shard_map/ppermute | solution.py:50
  64.5 6.5 %collective-permute-start.21 = (bf16[96,768]{1,0:T(8,128)(2,1)S(1)}, bf16[96,768]{1,0:T(8,128)(2,1)S(1)}, u32[]{:S(2)}, u32[]{:S(2)}) collective-permute-start(bf16[96,768]{1,0:T(8,128)(2,1)S(1)} %add_convert_fusion.1.refs_0_), channel_id=1, source_target_pairs={{0,4},{1,5},{2,6},{3,7},{4,0},{5,1},{6,2},{7,3},{8,12},{9,13},{10,... | collective-permute-start | bytes 442376 | tf_op jit(solution)/shard_map/ppermute | solution.py:50
  65.0 6.1 %collective-permute-start.19 = (bf16[96,768]{1,0:T(8,128)(2,1)S(1)}, bf16[96,768]{1,0:T(8,128)(2,1)S(1)}, u32[]{:S(2)}, u32[]{:S(2)}) collective-permute-start(bf16[96,768]{1,0:T(8,128)(2,1)S(1)} %add_convert_fusion.1.refs_0_), channel_id=1, source_target_pairs={{0,2},{1,3},{2,0},{3,1},{4,6},{5,7},{6,4},{7,5},{8,10},{9,11},{10,... | collective-permute-start | bytes 442376 | tf_op jit(solution)/shard_map/ppermute | solution.py:50
  65.5 6.0 %collective-permute-start.18 = (bf16[96,768]{1,0:T(8,128)(2,1)S(1)}, bf16[96,768]{1,0:T(8,128)(2,1)S(1)}, u32[]{:S(2)}, u32[]{:S(2)}) collective-permute-start(bf16[96,768]{1,0:T(8,128)(2,1)S(1)} %add_convert_fusion.1.refs_0_), channel_id=1, source_target_pairs={{0,1},{1,0},{2,3},{3,2},{4,5},{5,4},{6,7},{7,6},{8,9},{9,8},{10,11... | collective-permute-start | bytes 442376 | tf_op jit(solution)/shard_map/ppermute | solution.py:50
  79.4 6.4 %collective-permute-start.27 = (bf16[192,128]{1,0:T(8,128)(2,1)S(1)}, bf16[192,128]{1,0:T(8,128)(2,1)S(1)}, u32[]{:S(2)}, u32[]{:S(2)}) collective-permute-start(bf16[192,128]{1,0:T(8,128)(2,1)S(1)} %next_sums.1.refs_0_), channel_id=1, source_target_pairs={{0,24},{8,16},{16,8},{24,0},{1,25},{9,17},{17,9},{25,1},{2,26},{10... | collective-permute-start | bytes 147464 | tf_op jit(solution)/shard_map/ppermute | solution.py:50
  82.1 5.3 %collective-permute-start.26 = (bf16[192,128]{1,0:T(8,128)(2,1)S(1)}, bf16[192,128]{1,0:T(8,128)(2,1)S(1)}, u32[]{:S(2)}, u32[]{:S(2)}) collective-permute-start(bf16[192,128]{1,0:T(8,128)(2,1)S(1)} %next_sums.1.refs_0_), channel_id=1, source_target_pairs={{0,16},{8,24},{16,0},{24,8},{1,17},{9,25},{17,1},{25,9},{2,18},{10... | collective-permute-start | bytes 147464 | tf_op jit(solution)/shard_map/ppermute | solution.py:50
  82.1 5.3 %collective-permute-start.25 = (bf16[192,128]{1,0:T(8,128)(2,1)S(1)}, bf16[192,128]{1,0:T(8,128)(2,1)S(1)}, u32[]{:S(2)}, u32[]{:S(2)}) collective-permute-start(bf16[192,128]{1,0:T(8,128)(2,1)S(1)} %next_sums.1.refs_0_), channel_id=1, source_target_pairs={{0,8},{8,0},{16,24},{24,16},{1,9},{9,1},{17,25},{25,17},{2,10},{10... | collective-permute-start | bytes 147464 | tf_op jit(solution)/shard_map/ppermute | solution.py:50
  90.3 8.7 %collective-permute-start.30 = (bf16[96,768]{1,0:T(8,128)(2,1)S(1)}, bf16[96,768]{1,0:T(8,128)(2,1)S(1)}, u32[]{:S(2)}, u32[]{:S(2)}) collective-permute-start(bf16[96,768]{1,0:T(8,128)(2,1)S(1)} %get-tuple-element.36), channel_id=1, source_target_pairs={{0,24},{8,16},{16,8},{24,0},{1,25},{9,17},{17,9},{25,1},{2,26},{10... | collective-permute-start | bytes 442376 | tf_op jit(solution)/shard_map/ppermute | solution.py:50
  93.0 12.3 %collective-permute-start.29 = (bf16[96,768]{1,0:T(8,128)(2,1)S(1)}, bf16[96,768]{1,0:T(8,128)(2,1)S(1)}, u32[]{:S(2)}, u32[]{:S(2)}) collective-permute-start(bf16[96,768]{1,0:T(8,128)(2,1)S(1)} %get-tuple-element.36), channel_id=1, source_target_pairs={{0,16},{8,24},{16,0},{24,8},{1,17},{9,25},{17,1},{25,9},{2,18},{10... | collective-permute-start | bytes 442376 | tf_op jit(solution)/shard_map/ppermute | solution.py:50
  93.0 12.3 %collective-permute-start.28 = (bf16[96,768]{1,0:T(8,128)(2,1)S(1)}, bf16[96,768]{1,0:T(8,128)(2,1)S(1)}, u32[]{:S(2)}, u32[]{:S(2)}) collective-permute-start(bf16[96,768]{1,0:T(8,128)(2,1)S(1)} %get-tuple-element.36), channel_id=1, source_target_pairs={{0,8},{8,0},{16,24},{24,16},{1,9},{9,1},{17,25},{25,17},{2,10},{10... | collective-permute-start | bytes 442376 | tf_op jit(solution)/shard_map/ppermute | solution.py:50
  105.3 7.6 %collective-permute-start.36 = (bf16[96,768]{1,0:T(8,128)(2,1)S(1)}, bf16[96,768]{1,0:T(8,128)(2,1)S(1)}, u32[]{:S(2)}, u32[]{:S(2)}) collective-permute-start(bf16[96,768]{1,0:T(8,128)(2,1)S(1)} %add_convert_fusion.refs_0_), channel_id=1, source_target_pairs={{0,6},{1,7},{2,4},{3,5},{4,2},{5,3},{6,0},{7,1},{8,14},{9,15},{10,... | collective-permute-start | bytes 442376 | tf_op jit(solution)/shard_map/ppermute | solution.py:50
  107.1 7.2 %collective-permute-start.34 = (bf16[96,768]{1,0:T(8,128)(2,1)S(1)}, bf16[96,768]{1,0:T(8,128)(2,1)S(1)}, u32[]{:S(2)}, u32[]{:S(2)}) collective-permute-start(bf16[96,768]{1,0:T(8,128)(2,1)S(1)} %add_convert_fusion.refs_0_), channel_id=1, source_target_pairs={{0,4},{1,5},{2,6},{3,7},{4,0},{5,1},{6,2},{7,3},{8,12},{9,13},{10,... | collective-permute-start | bytes 442376 | tf_op jit(solution)/shard_map/ppermute | solution.py:50
  108.3 6.1 %collective-permute-start.32 = (bf16[96,768]{1,0:T(8,128)(2,1)S(1)}, bf16[96,768]{1,0:T(8,128)(2,1)S(1)}, u32[]{:S(2)}, u32[]{:S(2)}) collective-permute-start(bf16[96,768]{1,0:T(8,128)(2,1)S(1)} %add_convert_fusion.refs_0_), channel_id=1, source_target_pairs={{0,2},{1,3},{2,0},{3,1},{4,6},{5,7},{6,4},{7,5},{8,10},{9,11},{10,... | collective-permute-start | bytes 442376 | tf_op jit(solution)/shard_map/ppermute | solution.py:50
  108.9 7.0 %collective-permute-start.31 = (bf16[96,768]{1,0:T(8,128)(2,1)S(1)}, bf16[96,768]{1,0:T(8,128)(2,1)S(1)}, u32[]{:S(2)}, u32[]{:S(2)}) collective-permute-start(bf16[96,768]{1,0:T(8,128)(2,1)S(1)} %add_convert_fusion.refs_0_), channel_id=1, source_target_pairs={{0,1},{1,0},{2,3},{3,2},{4,5},{5,4},{6,7},{7,6},{8,9},{9,8},{10,11... | collective-permute-start | bytes 442376 | tf_op jit(solution)/shard_map/ppermute | solution.py:50
  112.9 2.9 %collective-permute-start.37 = (bf16[96,768]{1,0:T(8,128)(2,1)S(1)}, bf16[96,768]{1,0:T(8,128)(2,1)S(1)}, u32[]{:S(2)}, u32[]{:S(2)}) collective-permute-start(bf16[96,768]{1,0:T(8,128)(2,1)S(1)} %collective-permute-done.36.refs_6_), channel_id=1, source_target_pairs={{0,1},{1,0},{2,3},{3,2},{4,5},{5,4},{6,7},{7,6},{8,9},{9,8},{10,11... | collective-permute-start | bytes 442376 | tf_op jit(solution)/shard_map/ppermute | solution.py:50
  (11 other events, 15.4 us)

commit v4 on v3

--- a/solution.py
+++ b/solution.py
@@ -50,12 +50,27 @@
     return lax.ppermute(x, axis, [(i, i ^ bits) for i in range(size)])
 
 
-def residual_kernel(vectors_ref, centroids_ref, ids_ref, out_ref):
-    lists = centroids_ref.shape[0]
-    rows = vectors_ref.shape[0]
+def pick_kernel(lists, ids_ref, table_ref):
     local = lax.rem(ids_ref[...], lists)
-    level = lax.broadcasted_iota(jnp.int32, (lists, rows), 0)
-    table = jnp.where(level == local, 1.0, 0.0).astype(BF16)
+    level = lax.broadcasted_iota(jnp.int32, table_ref.shape, 0)
+    table_ref[...] = jnp.where(level == local, 1.0, 0.0).astype(BF16)
+
+
+def pick_call(ids, lists):
+    rows = ids.shape[0]
+    return pl.pallas_call(
+        functools.partial(pick_kernel, lists),
+        out_shape=jax.ShapeDtypeStruct((lists, rows), BF16),
+        in_specs=[vmem_spec()],
+        out_specs=vmem_spec(),
+        compiler_params=params(),
+        cost_estimate=cost(10),
+        name="pick",
+    )(ids.reshape(1, rows))
+
+
+def residual_kernel(vectors_ref, centroids_ref, table_ref, out_ref):
+    table = table_ref[...]
     center = centroids_ref[...]
     first = center.astype(BF16)
     rest = center - first.astype(F32)
@@ -66,15 +81,15 @@
 
 
 def residual_call(vectors, centroids, ids):
-    rows, width = vectors.shape
     return pl.pallas_call(
         residual_kernel,
-        out_shape=jax.ShapeDtypeStruct((rows, width), BF16),
+        out_shape=jax.ShapeDtypeStruct(vectors.shape, BF16),
         in_specs=[vmem_spec()] * 3,
         out_specs=vmem_spec(),
         compiler_params=params(),
+        cost_estimate=cost(10),
         name="residual",
-    )(vectors, centroids, ids.reshape(1, rows))
+    )(vectors, centroids, pick_call(ids, centroids.shape[0]))
 
 
 def packs_of(owned):
@@ -101,10 +116,9 @@
     return total
 
 
-def pack_sums(rotated, codes, pack, with_counts):
+def pack_sums(rotated, codes, pack, with_counts, table=None):
     rows = codes.shape[1]
     hi, lo = codes >> 3, codes & 7
-    table = hi_table(hi, pack)
     parts = []
     for m in pack:
         value = rotated[m * SUB : (m + 1) * SUB, :]
@@ -113,7 +127,8 @@
     if with_counts:
         low_level = lax.broadcasted_iota(jnp.int32, (LO, rows), 0)
         parts += [jnp.where(low_level == lo[m : m + 1, :], 1.0, 0.0) for m in pack]
-    return mm(jnp.concatenate(parts, axis=0).astype(BF16), table, NT)
+    marked = jnp.concatenate(parts, axis=0).astype(BF16)
+    return mm(marked, hi_table(hi, pack), NT) if table is None else mm(marked, table)
 
 
 def pack_layout(owned, with_counts):
@@ -321,15 +336,16 @@
     ]
 
 
-def add_spans(total, wide, codes_ref, pieces, spans):
+def add_spans(total, wide, codes_ref, pieces, spans, tables=None):
     owned = codes_ref.shape[1]
-    for span in spans:
+    for i, span in enumerate(spans):
         codes = span_codes(codes_ref, span)
         hi, lo = codes >> 3, codes & 7
         rows = codes.shape[1]
         rebuilt = []
         for g, pack in enumerate(packs_of(owned)):
-            spread = mm(wide[g], hi_table(hi, pack))
+            table = hi_table(hi, pack) if tables is None else tables[i, g * 128 : (g + 1) * 128, :]
+            spread = mm(wide[g], table)
             for j, m in enumerate(pack):
                 low = jnp.broadcast_to(lo[m : m + 1, :], (SUB, rows))
                 at = j * LO * SUB
@@ -398,7 +414,8 @@
     )(codes, total, wide, *rows)
 
 
-def cross_kernel(held, groups, total_rows, codes_ref, *refs):
+def cross_kernel(held, groups, total_rows, ready, codes_ref, *refs):
+    tables, refs = (refs[0], refs[1:]) if ready else (None, refs)
     sums, counts_in, pieces = refs[:groups], refs[groups], pieces_of(held, refs[groups + 1 :])
     cross_ref, book_ref = refs[-2:]
     owned = codes_ref.shape[1]
@@ -406,25 +423,63 @@
     books, unused = read_books(sums, counts_in, owned)
     for g, book in enumerate(books):
         book_ref[g * block : (g + 1) * block, :] = book
-    total = add_spans(None, widen(books, owned), codes_ref, pieces, spans_of(held))
+    total = add_spans(None, widen(books, owned), codes_ref, pieces, spans_of(held), tables)
     cross_ref[...] = (total * (1.0 / total_rows)).astype(BF16)
 
 
-def cross_call(codes, sums, counts, chunks, total_rows):
+def cross_call(codes, ready, sums, counts, chunks, total_rows):
     owned = codes.shape[1]
     held, rows = flat(chunks)
-    return pl.pallas_call(
-        functools.partial(cross_kernel, held, len(sums), total_rows),
+    tables = [ready[2]] if ready else []
+    return pl.pallas_call(
+        functools.partial(cross_kernel, held, len(sums), total_rows, bool(ready)),
         out_shape=(
             jax.ShapeDtypeStruct((owned * SUB, rows[0].shape[1]), BF16),
             jax.ShapeDtypeStruct((len(packs_of(owned)) * LO * SUB, 128), F32),
         ),
-        in_specs=[vmem_spec()] * (2 + len(sums) + len(rows)),
+        in_specs=[vmem_spec()] * (2 + len(tables) + len(sums) + len(rows)),
         out_specs=(vmem_spec(), vmem_spec()),
-        compiler_params=params(*rows),
+        compiler_params=params(*rows, *tables),
         cost_estimate=cost(0),
         name="cross",
-    )(codes, *sums, counts, *rows)
+    )(codes, *tables, *sums, counts, *rows)
+
+
+def prepare_kernel(held, codes_ref, *refs):
+    pieces, (turned_ref, table_ref, across_ref) = pieces_of(held, refs), refs[-3:]
+    packs = packs_of(codes_ref.shape[1])
+    for i, span in enumerate(spans_of(held)):
+        turned_ref[i, :, :] = span_rows(pieces, span).T
+        hi = span_codes(codes_ref, span) >> 3
+        for g, pack in enumerate(packs):
+            table = hi_table(hi, pack)
+            across_ref[i, g * 128 : (g + 1) * 128, :] = table
+            table_ref[i, :, g * 128 : (g + 1) * 128] = table.T
+
+
+def prepare_call(codes, chunks):
+    size, owned, rows = codes.shape
+    held, pieces = flat(chunks)
+    lanes = 128 * len(packs_of(owned))
+    width = pieces[0].shape[1]
+    spans = len(spans_of(held))
+    each = size // spans * rows
+    shapes = (
+        jax.ShapeDtypeStruct((spans, width, each), BF16),
+        jax.ShapeDtypeStruct((spans, each, lanes), BF16),
+        jax.ShapeDtypeStruct((spans, lanes, each), BF16),
+    )
+    if sum(math.prod(a.shape) * 2 for a in shapes) > 16 * MIB:
+        return None
+    return pl.pallas_call(
+        functools.partial(prepare_kernel, held),
+        out_shape=shapes,
+        in_specs=[vmem_spec()] * (1 + len(pieces)),
+        out_specs=(vmem_spec(),) * 3,
+        compiler_params=params(*pieces, *shapes),
+        cost_estimate=cost(0),
+        name="prepare",
+    )(codes, *pieces)
 
 
 def bands(x):
@@ -451,9 +506,13 @@
     return jnp.concatenate([p.astype(F32) for p in parts], axis=0).astype(BF16)
 
 
-def next_sums_kernel(held, codes_ref, *refs):
+def next_sums_kernel(held, ready, codes_ref, *refs):
     size = len(held)
-    parts, pieces, out_ref = refs[:size], pieces_of(held, refs[size:]), refs[-1]
+    parts, out_ref = refs[:size], refs[-1]
+    if ready:
+        turned_ref, table_ref = refs[size : size + 2]
+    else:
+        pieces = pieces_of(held, refs[size:])
     owned = codes_ref.shape[1]
     height = parts[0].shape[0]
     x = first_step(join([ref[...] for ref in parts]))
@@ -462,26 +521,34 @@
     gram = mm(mine.astype(BF16), xb, NT)
     rotation_rows = (1.5 * mine - 0.5 * mm(gram.astype(BF16), xb)).astype(BF16)
     totals = None
-    for span in spans_of(held):
-        rotated = mm(rotation_rows, span_rows(pieces, span), NT).astype(BF16).astype(F32)
+    for i, span in enumerate(spans_of(held)):
+        if ready:
+            rotated = mm(rotation_rows, turned_ref[i])
+        else:
+            rotated = mm(rotation_rows, span_rows(pieces, span), NT)
+        rotated = rotated.astype(BF16).astype(F32)
         codes = span_codes(codes_ref, span)
-        more = [pack_sums(rotated, codes, pack, False) for pack in packs_of(owned)]
+        more = []
+        for g, pack in enumerate(packs_of(owned)):
+            table = table_ref[i, :, g * 128 : (g + 1) * 128] if ready else None
+            more.append(pack_sums(rotated, codes, pack, False, table))
         totals = more if totals is None else [a + b for a, b in zip(totals, more)]
     write_sums(pack_diagonals(totals, owned, False)[0], None, owned, out_ref)
 
 
-def next_sums_call(codes, blocks, chunks):
+def next_sums_call(codes, ready, blocks, chunks):
     owned = codes.shape[1]
     held, rows = flat(chunks)
-    return pl.pallas_call(
-        functools.partial(next_sums_kernel, held),
+    given = list(ready[:2]) if ready else rows
+    return pl.pallas_call(
+        functools.partial(next_sums_kernel, held, bool(ready)),
         out_shape=jax.ShapeDtypeStruct((pack_layout(owned, False)[2], 128), BF16),
-        in_specs=[vmem_spec()] * (1 + len(blocks) + len(rows)),
+        in_specs=[vmem_spec()] * (1 + len(blocks) + len(given)),
         out_specs=vmem_spec(),
-        compiler_params=params(*rows),
+        compiler_params=params(*given),
         cost_estimate=cost(0),
         name="next_sums",
-    )(codes, *blocks, *rows)
+    )(codes, *blocks, *given)
 
 
 def final_kernel(size, place_ref, residual_ref, *refs):
@@ -492,11 +559,10 @@
         whole[pl.ds(at, height), :] = ref[...].astype(whole.dtype)
     x = first_step(whole[...].astype(BF16))
     xb = jnp.concatenate([band.astype(BF16) for band in x], axis=0)
-    residual = residual_ref[...]
-    for i, band in enumerate(x):
-        gram = mm(xb[i * BAND : (i + 1) * BAND], xb, NT).astype(BF16)
-        rotation = (1.5 * band - 0.5 * mm(gram, xb)).astype(BF16)
-        out_ref[:, i * BAND : (i + 1) * BAND] = mm(residual, rotation, NT).astype(BF16)
+    for i in range(0, residual_ref.shape[0], BAND):
+        once = mm(residual_ref[i : i + BAND, :], xb, NT)
+        less = mm(mm(once.astype(BF16), xb).astype(BF16), xb, NT)
+        out_ref[i : i + BAND, :] = (1.5 * once - 0.5 * less).astype(BF16)
 
 
 def final_call(place, residual, blocks):
@@ -551,12 +617,15 @@
     return merge_chips_call(parts, owned, rows)
 
 
-def everywhere(x, size):
-    return [x] + [swap(x, "group", size, k) for k in range(1, size)]
-
-
-def reduce_cross(cross, size):
-    return tree([p.astype(F32) for p in everywhere(cross, size)]).astype(BF16)
+def add_over_groups(x, size, last):
+    for bit in [1 << b for b in range(size.bit_length() - 2)]:
+        x = (x.astype(F32) + swap(x, "group", size, bit).astype(F32)).astype(BF16)
+    x = after(x, *last)
+    return [x, swap(x, "group", size, size // 2)]
+
+
+def reduce_cross(cross, size, *last):
+    return tree([part.astype(F32) for part in add_over_groups(cross, size, last)]).astype(BF16)
 
 
 def per_device(vectors, centroids, list_ids, codes, rotation):
@@ -586,15 +655,18 @@
     far = {**far, **both_cores(far, size)}
     cross = cross_far_call(own_codes, total, wide, far, total_rows)
     chunks.update(far)
+    ready = prepare_call(after(own_codes, cross), chunks)
     for alternation in range(1, ALTS):
-        blocks = gather_group(reduce_cross(cross, groups), size)
-        parts = everywhere(next_sums_call(own_codes, blocks, chunks), groups)
-        cross, book = cross_call(own_codes, parts, counts, chunks, total_rows)
-    blocks = gather_group(reduce_cross(cross, groups), size)
+        block = reduce_cross(cross, groups)
+        if ready:
+            block = after(block, *ready)
+        parts = add_over_groups(next_sums_call(own_codes, ready, gather_group(block, size), chunks), groups, ())
+        cross, book = cross_call(own_codes, ready, parts, counts, chunks, total_rows)
+    packs = len(packs_of(owned))
+    book = book.reshape(packs, LO * SUB, PACK, HI).transpose(0, 2, 3, 1).reshape(packs * PACK, K * SUB)[:owned]
+    blocks = gather_group(reduce_cross(cross, groups, book), size)
     rotated_out = final_call(place, residual, blocks)
-    packs = len(packs_of(owned))
-    book = book.reshape(packs, LO * SUB, PACK, HI).transpose(0, 2, 3, 1).reshape(packs * PACK, K * SUB)
-    return (rotated_out, book[:owned])
+    return (rotated_out, book)
 
 
 def solution(mesh):

time: 122 us -> 118 us (0.967)
  waiting for transfers between devices: 51.5 us -> 47.7 us
  local copies, waits for them, and re-layouts: 6.38 us -> 4.54 us
  Pallas kernels: 23.5 us -> 25.1 us
    ppermute x38 -> x35, waiting for transfers between devices: 51.5 us -> 47.7 us  [swap(): return lax.ppermute(x, axis, [(i, i ^ bits) for i in range(size)])]
    pallas_call x2 -> x4, Pallas kernels: 7.63 us -> 9.79 us  [the longest x1 6.18 us: next_sums_call(): pl.pallas_call(functools.partial(next_sums_kernel, held, bool(ready)), ou...]
    unnamed x10, local copies, waits for them, and re-layouts: 5.33 us -> 3.48 us
    ppermute x38 -> x35, starting transfers between devices: 39.8 us -> 39.5 us  [swap(): return lax.ppermute(x, axis, [(i, i ^ bits) for i in range(size)])]
  transfers between devices with their start and end apart: 38 -> 35, of which waited for: 21 -> 22; matrix products, arithmetic and copies ran while one was open for 1% -> 1% of each run, Pallas kernels for 5% -> 7%
where the time goes in v4:
time: 118 us
  waiting for transfers between devices  47.7 us (40%)
  starting transfers between devices  39.5 us (33%)
  Pallas kernels  25.1 us (21%)
  local copies, waits for them, and re-layouts  4.54 us (4%)
    ppermute x35, waiting for transfers between devices, swap(): return lax.ppermute(x, axis, [(i, i ^ bits) for i in range(size)])  47.7 us
    ppermute x35, starting transfers between devices, swap(): return lax.ppermute(x, axis, [(i, i ^ bits) for i in range(size)])  39.5 us
    pallas_call x1, Pallas kernels, next_sums_call(): pl.pallas_call(functools.partial(next_sums_kernel, held, bool(ready)), ou...  6.18 us
    pallas_call x1, Pallas kernels, final_call(): pl.pallas_call(functools.partial(final_kernel, len(blocks)), out_shape=ja...  5.83 us
    unnamed x10, local copies, waits for them, and re-layouts  3.48 us
    pallas_call x1, Pallas kernels, local_sums_call(): pl.pallas_call(functools.partial(local_sums_kernel, size), out_shape=(sha...  3.27 us
    pallas_call x1, Pallas kernels, prepare_call(): pl.pallas_call(functools.partial(prepare_kernel, held), out_shape=shapes,...  2.79 us
    pallas_call x1, Pallas kernels, cross_call(): pl.pallas_call(functools.partial(cross_kernel, held, len(sums), total_row...  2.79 us
  transfers between devices with their start and end apart: 35, of which 22 were waited for; matrix products, arithmetic and copies ran while one was open for 1% of the time, Pallas kernels for 7%

profile of v4, /device:TPU:0, one launch (start us, length us, event | category | flops | bytes accessed | tf_op | source)
XLA Modules:
  0.0 117.8 jit_solution(2584974457682731402)
XLA Ops:
  3.8 2.6 %collective-permute-start.9 = (bf16[512,768]{1,0:T(8,128)(2,1)S(1)}, bf16[512,768]{1,0:T(8,128)(2,1)S(1)}, u32[]{:S(2)}, u32[]{:S(2)}) collective-permute-start(bf16[512,768]{1,0:T(8,128)(2,1)S(1)} %residual.1.residual_ref.refs_2_.refs_0_.refs_4_), channel_id=1, source_target_pairs={{0,4},{1,5},{2,6},{3,7},{4,0},{5,1},{6,2},{7,3},{8,12},{9,13},{10,... | collective-permute-start | bytes 2359304 | tf_op jit(solution)/shard_map/ppermute | solution.py:50
  7.9 1.7 %copy-done = f32[768,768]{1,0:T(8,128)S(1)} copy-done((f32[768,768]{1,0:T(8,128)S(1)}, f32[768,768]{1,0:T(8,128)}, u32[]{:S(2)}) %copy-start) | copy-done | bytes 2359320
  9.6 3.3 %local_sums.1 = (bf16[4,304,128]{2,1,0:T(8,128)(2,1)S(1)}, bf16[4,304,128]{2,1,0:T(8,128)(2,1)S(1)}) custom-call(s32[1]{0:T(128)} %bitcast.place_ref, f32[768,768]{1,0:T(8,128)S(1)} %copy-done, s32[96,512]{1,0:T(8,128)S(1)} %bitcast.8, bf16[512,768]{1,0:T(8,128)(2,1)S(1)} %residual.1.residual_ref.refs_2_.refs_0_.refs_4_), custom_call_target="tpu_custom_call" | custom-call | tf_op jit(solution)/shard_map/local_sums/pallas_call | solution.py:212
  12.9 1.6 %collective-permute-done.1.came_ref = bf16[4,304,128]{2,1,0:T(8,128)(2,1)S(1)} collective-permute-done((bf16[4,304,128]{2,1,0:T(8,128)(2,1)S(1)}, bf16[4,304,128]{2,1,0:T(8,128)(2,1)S(1)}, u32[]{:S(2)}, u32[]{:S(2)}) %collective-permute-start.1) | collective-permute-done | bytes 311328 | tf_op jit(solution)/shard_map/ppermute | solution.py:50
  18.1 6.7 %collective-permute-done.9.refs_6_.refs_4_.refs_8_ = bf16[512,768]{1,0:T(8,128)(2,1)S(1)} collective-permute-done((bf16[512,768]{1,0:T(8,128)(2,1)S(1)}, bf16[512,768]{1,0:T(8,128)(2,1)S(1)}, u32[]{:S(2)}, u32[]{:S(2)}) %collective-permute-start.9) | collective-permute-done | bytes 786464 | tf_op jit(solution)/shard_map/ppermute | solution.py:50
  24.8 2.0 %collective-permute-start.12 = (bf16[256,768]{1,0:T(8,128)(2,1)S(1)}, bf16[256,768]{1,0:T(8,128)(2,1)S(1)}, u32[]{:S(2)}, u32[]{:S(2)}) collective-permute-start(bf16[256,768]{1,0:T(8,128)(2,1)S(1)} %slice.9), channel_id=1, source_target_pairs={{0,2},{1,3},{2,0},{3,1},{4,6},{5,7},{6,4},{7,5},{8,10},{9,11},{10,... | collective-permute-start | bytes 1179656 | tf_op jit(solution)/shard_map/ppermute | solution.py:50
  30.9 2.0 %collective-permute-start.5 = (bf16[240,128]{1,0:T(8,128)(2,1)S(1)}, bf16[240,128]{1,0:T(8,128)(2,1)S(1)}, u32[]{:S(2)}, u32[]{:S(2)}) collective-permute-start(bf16[240,128]{1,0:T(8,128)(2,1)S(1)} %get-tuple-element.34.first_ref), channel_id=1, source_target_pairs={{0,8},{8,0},{16,24},{24,16},{1,9},{9,1},{17,25},{25,17},{2,10},{10... | collective-permute-start | bytes 184328 | tf_op jit(solution)/shard_map/ppermute | solution.py:50
  33.0 2.2 %collective-permute-done.5.second_ref = bf16[240,128]{1,0:T(8,128)(2,1)S(1)} collective-permute-done((bf16[240,128]{1,0:T(8,128)(2,1)S(1)}, bf16[240,128]{1,0:T(8,128)(2,1)S(1)}, u32[]{:S(2)}, u32[]{:S(2)}) %collective-permute-start.5) | collective-permute-done | bytes 61472 | tf_op jit(solution)/shard_map/ppermute | solution.py:50
  35.2 3.1 %collective-permute-start.6 = (bf16[240,128]{1,0:T(8,128)(2,1)S(1)}, bf16[240,128]{1,0:T(8,128)(2,1)S(1)}, u32[]{:S(2)}, u32[]{:S(2)}) collective-permute-start(bf16[240,128]{1,0:T(8,128)(2,1)S(1)} %merge_groups.1.refs_0_), channel_id=1, source_target_pairs={{0,16},{8,24},{16,0},{24,8},{1,17},{9,25},{17,1},{25,9},{2,18},{10... | collective-permute-start | bytes 184328 | tf_op jit(solution)/shard_map/ppermute | solution.py:50
  38.5 2.3 %collective-permute-done.6.refs_1_ = bf16[240,128]{1,0:T(8,128)(2,1)S(1)} collective-permute-done((bf16[240,128]{1,0:T(8,128)(2,1)S(1)}, bf16[240,128]{1,0:T(8,128)(2,1)S(1)}, u32[]{:S(2)}, u32[]{:S(2)}) %collective-permute-start.6) | collective-permute-done | bytes 61472 | tf_op jit(solution)/shard_map/ppermute | solution.py:50
  41.3 2.3 %cross_near.1 = (f32[96,768]{1,0:T(8,128)S(1)}, bf16[3,256,128]{2,1,0:T(8,128)(2,1)S(1)}, f32[24,128]{1,0:T(8,128)S(1)}) custom-call(s32[8,12,512]{2,1,0:T(8,128)S(1)} %get-tuple-element.41.codes_ref, bf16[240,128]{1,0:T(8,128)(2,1)S(1)} %merge_groups.1.refs_0_, bf16[240,128]{1,0:T(8,128)(2,1)S(1)} %collective-permute-done.6.refs_1_, ...), custom_call_target="tpu_custom_call" | custom-call | tf_op jit(solution)/shard_map/cross_near/pallas_call | solution.py:381
  44.6 1.7 %collective-permute-start.15 = (bf16[96,768]{1,0:T(8,128)(2,1)S(1)}, bf16[96,768]{1,0:T(8,128)(2,1)S(1)}, u32[]{:S(2)}, u32[]{:S(2)}) collective-permute-start(bf16[96,768]{1,0:T(8,128)(2,1)S(1)} %cross_far.1), channel_id=1, source_target_pairs={{0,8},{8,0},{16,24},{24,16},{1,9},{9,1},{17,25},{25,17},{2,10},{10... | collective-permute-start | bytes 442376 | tf_op jit(solution)/shard_map/ppermute | solution.py:50
  46.3 4.1 %collective-permute-done.15 = bf16[96,768]{1,0:T(8,128)(2,1)S(1)} collective-permute-done((bf16[96,768]{1,0:T(8,128)(2,1)S(1)}, bf16[96,768]{1,0:T(8,128)(2,1)S(1)}, u32[]{:S(2)}, u32[]{:S(2)}) %collective-permute-start.15) | collective-permute-done | bytes 147488 | tf_op jit(solution)/shard_map/ppermute | solution.py:50
  50.4 3.1 %collective-permute-start.16 = (bf16[96,768]{1,0:T(8,128)(2,1)S(1)}, bf16[96,768]{1,0:T(8,128)(2,1)S(1)}, u32[]{:S(2)}, u32[]{:S(2)}) collective-permute-start(bf16[96,768]{1,0:T(8,128)(2,1)S(1)} %add_convert_fusion.3), channel_id=1, source_target_pairs={{0,16},{8,24},{16,0},{24,8},{1,17},{9,25},{17,1},{25,9},{2,18},{10... | collective-permute-start | bytes 442376 | tf_op jit(solution)/shard_map/ppermute | solution.py:50
  53.5 2.8 %prepare.1 = (bf16[4,768,1024]{2,1,0:T(8,128)(2,1)S(1)}, bf16[4,1024,384]{2,1,0:T(8,128)(2,1)S(1)}, bf16[4,384,1024]{2,1,0:T(8,128)(2,1)S(1)}) custom-call(s32[8,12,512]{2,1,0:T(8,128)S(1)} %get-tuple-element.41.codes_ref, bf16[512,768]{1,0:T(8,128)(2,1)S(1)} %residual.1.residual_ref.refs_2_.refs_0_.refs_4_, ...), custom_call_target="tpu_custom_call" | custom-call | tf_op jit(solution)/shard_map/prepare/pallas_call | solution.py:474
  56.3 3.9 %collective-permute-done.16 = bf16[96,768]{1,0:T(8,128)(2,1)S(1)} collective-permute-done((bf16[96,768]{1,0:T(8,128)(2,1)S(1)}, bf16[96,768]{1,0:T(8,128)(2,1)S(1)}, u32[]{:S(2)}, u32[]{:S(2)}) %collective-permute-start.16) | collective-permute-done | bytes 147488 | tf_op jit(solution)/shard_map/ppermute | solution.py:50
  60.3 2.5 %collective-permute-start.22 = (bf16[96,768]{1,0:T(8,128)(2,1)S(1)}, bf16[96,768]{1,0:T(8,128)(2,1)S(1)}, u32[]{:S(2)}, u32[]{:S(2)}) collective-permute-start(bf16[96,768]{1,0:T(8,128)(2,1)S(1)} %add_convert_fusion.2.refs_0_), channel_id=1, source_target_pairs={{0,6},{1,7},{2,4},{3,5},{4,2},{5,3},{6,0},{7,1},{8,14},{9,15},{10,... | collective-permute-start | bytes 442376 | tf_op jit(solution)/shard_map/ppermute | solution.py:50
  63.8 3.6 %collective-permute-done.22.refs_6_ = bf16[96,768]{1,0:T(8,128)(2,1)S(1)} collective-permute-done((bf16[96,768]{1,0:T(8,128)(2,1)S(1)}, bf16[96,768]{1,0:T(8,128)(2,1)S(1)}, u32[]{:S(2)}, u32[]{:S(2)}) %collective-permute-start.22) | collective-permute-done | bytes 147488 | tf_op jit(solution)/shard_map/ppermute | solution.py:50
  67.4 1.8 %collective-permute-done.20.refs_4_ = bf16[96,768]{1,0:T(8,128)(2,1)S(1)} collective-permute-done((bf16[96,768]{1,0:T(8,128)(2,1)S(1)}, bf16[96,768]{1,0:T(8,128)(2,1)S(1)}, u32[]{:S(2)}, u32[]{:S(2)}) %collective-permute-start.20) | collective-permute-done | bytes 147488 | tf_op jit(solution)/shard_map/ppermute | solution.py:50
  70.8 6.2 %next_sums.1 = bf16[192,128]{1,0:T(8,128)(2,1)S(1)} custom-call(s32[8,12,512]{2,1,0:T(8,128)S(1)} %get-tuple-element.41.codes_ref, bf16[96,768]{1,0:T(8,128)(2,1)S(1)} %add_convert_fusion.2.refs_0_, bf16[96,768]{1,0:T(8,128)(2,1)S(1)} %collective-permute-done.17.refs_1_, bf16[96,768]{1,0:T(8,128)(2,1)S(1)} %collective-permute-done.18.refs_2_, ...), custom_call_target="tpu_custom_call" | custom-call | tf_op jit(solution)/shard_map/next_sums/pallas_call | solution.py:543
  77.0 1.6 %collective-permute-start.24 = (bf16[192,128]{1,0:T(8,128)(2,1)S(1)}, bf16[192,128]{1,0:T(8,128)(2,1)S(1)}, u32[]{:S(2)}, u32[]{:S(2)}) collective-permute-start(bf16[192,128]{1,0:T(8,128)(2,1)S(1)} %next_sums.1), channel_id=1, source_target_pairs={{0,8},{8,0},{16,24},{24,16},{1,9},{9,1},{17,25},{25,17},{2,10},{10... | collective-permute-start | bytes 147464 | tf_op jit(solution)/shard_map/ppermute | solution.py:50
  78.6 2.6 %collective-permute-done.24 = bf16[192,128]{1,0:T(8,128)(2,1)S(1)} collective-permute-done((bf16[192,128]{1,0:T(8,128)(2,1)S(1)}, bf16[192,128]{1,0:T(8,128)(2,1)S(1)}, u32[]{:S(2)}, u32[]{:S(2)}) %collective-permute-start.24) | collective-permute-done | bytes 49184 | tf_op jit(solution)/shard_map/ppermute | solution.py:50
  81.2 3.1 %collective-permute-start.25 = (bf16[192,128]{1,0:T(8,128)(2,1)S(1)}, bf16[192,128]{1,0:T(8,128)(2,1)S(1)}, u32[]{:S(2)}, u32[]{:S(2)}) collective-permute-start(bf16[192,128]{1,0:T(8,128)(2,1)S(1)} %add_convert_fusion.4.refs_1_), channel_id=1, source_target_pairs={{0,16},{8,24},{16,0},{24,8},{1,17},{9,25},{17,1},{25,9},{2,18},{10... | collective-permute-start | bytes 147464 | tf_op jit(solution)/shard_map/ppermute | solution.py:50
  84.3 2.4 %collective-permute-done.25.refs_2_ = bf16[192,128]{1,0:T(8,128)(2,1)S(1)} collective-permute-done((bf16[192,128]{1,0:T(8,128)(2,1)S(1)}, bf16[192,128]{1,0:T(8,128)(2,1)S(1)}, u32[]{:S(2)}, u32[]{:S(2)}) %collective-permute-start.25) | collective-permute-done | bytes 49184 | tf_op jit(solution)/shard_map/ppermute | solution.py:50
  86.7 2.8 %cross.1 = (bf16[96,768]{1,0:T(8,128)(2,1)S(1)}, f32[192,128]{1,0:T(8,128)S(1)}) custom-call(s32[8,12,512]{2,1,0:T(8,128)S(1)} %get-tuple-element.41.codes_ref, bf16[4,384,1024]{2,1,0:T(8,128)(2,1)S(1)} %get-tuple-element.42.refs_0_, bf16[192,128]{1,0:T(8,128)(2,1)S(1)} %add_convert_fusion.4.refs_1_, bf16[192,128]{1,0:T(8,128)(2,1)S(1)} %collective-permute-done.25.refs_2_, ...), custom_call_target="tpu_custom_call" | custom-call | tf_op jit(solution)/shard_map/cross/pallas_call | solution.py:434
  89.5 1.6 %collective-permute-start.26 = (bf16[96,768]{1,0:T(8,128)(2,1)S(1)}, bf16[96,768]{1,0:T(8,128)(2,1)S(1)}, u32[]{:S(2)}, u32[]{:S(2)}) collective-permute-start(bf16[96,768]{1,0:T(8,128)(2,1)S(1)} %get-tuple-element.47), channel_id=1, source_target_pairs={{0,8},{8,0},{16,24},{24,16},{1,9},{9,1},{17,25},{25,17},{2,10},{10... | collective-permute-start | bytes 442376 | tf_op jit(solution)/shard_map/ppermute | solution.py:50
  92.1 2.5 %collective-permute-done.26 = bf16[96,768]{1,0:T(8,128)(2,1)S(1)} collective-permute-done((bf16[96,768]{1,0:T(8,128)(2,1)S(1)}, bf16[96,768]{1,0:T(8,128)(2,1)S(1)}, u32[]{:S(2)}, u32[]{:S(2)}) %collective-permute-start.26) | collective-permute-done | bytes 147488 | tf_op jit(solution)/shard_map/ppermute | solution.py:50
  94.7 2.7 %collective-permute-start.27 = (bf16[96,768]{1,0:T(8,128)(2,1)S(1)}, bf16[96,768]{1,0:T(8,128)(2,1)S(1)}, u32[]{:S(2)}, u32[]{:S(2)}) collective-permute-start(bf16[96,768]{1,0:T(8,128)(2,1)S(1)} %add_convert_fusion.1), channel_id=1, source_target_pairs={{0,16},{8,24},{16,0},{24,8},{1,17},{9,25},{17,1},{25,9},{2,18},{10... | collective-permute-start | bytes 442376 | tf_op jit(solution)/shard_map/ppermute | solution.py:50
  97.4 5.0 %collective-permute-done.27 = bf16[96,768]{1,0:T(8,128)(2,1)S(1)} collective-permute-done((bf16[96,768]{1,0:T(8,128)(2,1)S(1)}, bf16[96,768]{1,0:T(8,128)(2,1)S(1)}, u32[]{:S(2)}, u32[]{:S(2)}) %collective-permute-start.27) | collective-permute-done | bytes 147488 | tf_op jit(solution)/shard_map/ppermute | solution.py:50
  102.4 1.8 %collective-permute-start.33 = (bf16[96,768]{1,0:T(8,128)(2,1)S(1)}, bf16[96,768]{1,0:T(8,128)(2,1)S(1)}, u32[]{:S(2)}, u32[]{:S(2)}) collective-permute-start(bf16[96,768]{1,0:T(8,128)(2,1)S(1)} %add_convert_fusion.refs_0_), channel_id=1, source_target_pairs={{0,6},{1,7},{2,4},{3,5},{4,2},{5,3},{6,0},{7,1},{8,14},{9,15},{10,... | collective-permute-start | bytes 442376 | tf_op jit(solution)/shard_map/ppermute | solution.py:50
  106.0 2.6 %collective-permute-done.33.refs_6_ = bf16[96,768]{1,0:T(8,128)(2,1)S(1)} collective-permute-done((bf16[96,768]{1,0:T(8,128)(2,1)S(1)}, bf16[96,768]{1,0:T(8,128)(2,1)S(1)}, u32[]{:S(2)}, u32[]{:S(2)}) %collective-permute-start.33) | collective-permute-done | bytes 147488 | tf_op jit(solution)/shard_map/ppermute | solution.py:50
  112.0 5.8 %final.1 = bf16[512,768]{1,0:T(8,128)(2,1)} custom-call(s32[1]{0:T(128)} %bitcast.place_ref, bf16[512,768]{1,0:T(8,128)(2,1)S(1)} %residual.1.residual_ref.refs_2_.refs_0_.refs_4_, bf16[96,768]{1,0:T(8,128)(2,1)S(1)} %add_convert_fusion.refs_0_, bf16[96,768]{1,0:T(8,128)(2,1)S(1)} %collective-permute-done.28.refs_1_, ...), custom_call_target="tpu_custom_call" | custom-call | tf_op jit(solution)/shard_map/final/pallas_call | solution.py:571
  (71 shorter events, 23.0 us)
Async XLA Ops:
  3.3 4.6 %collective-permute-start = (bf16[512,768]{1,0:T(8,128)(2,1)S(1)}, bf16[512,768]{1,0:T(8,128)(2,1)S(1)}, u32[]{:S(2)}, u32[]{:S(2)}) collective-permute-start(bf16[512,768]{1,0:T(8,128)(2,1)S(1)} %residual.1.residual_ref.refs_2_.refs_0_.refs_4_), channel_id=1, source_target_pairs={{0,1},{1,0},{2,3},{3,2},{4,5},{5,4},{6,7},{7,6},{8,9},{9,8},{10,11... | collective-permute-start | bytes 2359304 | tf_op jit(solution)/shard_map/ppermute | solution.py:50
  3.8 21.0 %collective-permute-start.9 = (bf16[512,768]{1,0:T(8,128)(2,1)S(1)}, bf16[512,768]{1,0:T(8,128)(2,1)S(1)}, u32[]{:S(2)}, u32[]{:S(2)}) collective-permute-start(bf16[512,768]{1,0:T(8,128)(2,1)S(1)} %residual.1.residual_ref.refs_2_.refs_0_.refs_4_), channel_id=1, source_target_pairs={{0,4},{1,5},{2,6},{3,7},{4,0},{5,1},{6,2},{7,3},{8,12},{9,13},{10,... | collective-permute-start | bytes 2359304 | tf_op jit(solution)/shard_map/ppermute | solution.py:50
  6.4 20.4 %collective-permute-start.7 = (bf16[512,768]{1,0:T(8,128)(2,1)S(1)}, bf16[512,768]{1,0:T(8,128)(2,1)S(1)}, u32[]{:S(2)}, u32[]{:S(2)}) collective-permute-start(bf16[512,768]{1,0:T(8,128)(2,1)S(1)} %residual.1.residual_ref.refs_2_.refs_0_.refs_4_), channel_id=1, source_target_pairs={{0,2},{1,3},{2,0},{3,1},{4,6},{5,7},{6,4},{7,5},{8,10},{9,11},{10,... | collective-permute-start | bytes 2359304 | tf_op jit(solution)/shard_map/ppermute | solution.py:50
  12.8 1.7 %collective-permute-start.1 = (bf16[4,304,128]{2,1,0:T(8,128)(2,1)S(1)}, bf16[4,304,128]{2,1,0:T(8,128)(2,1)S(1)}, u32[]{:S(2)}, u32[]{:S(2)}) collective-permute-start(bf16[4,304,128]{2,1,0:T(8,128)(2,1)S(1)} %get-tuple-element.28), channel_id=1, source_target_pairs={{0,1},{1,0},{2,3},{3,2},{4,5},{5,4},{6,7},{7,6},{8,9},{9,8},{10,11... | collective-permute-start | bytes 933896 | tf_op jit(solution)/shard_map/ppermute | solution.py:50
  14.6 14.2 %collective-permute-start.2 = (bf16[368,128]{1,0:T(8,128)(2,1)S(1)}, bf16[368,128]{1,0:T(8,128)(2,1)S(1)}, u32[]{:S(2)}, u32[]{:S(2)}) collective-permute-start(bf16[368,128]{1,0:T(8,128)(2,1)S(1)} %get-tuple-element.30), channel_id=1, source_target_pairs={{0,2},{1,3},{2,0},{3,1},{4,6},{5,7},{6,4},{7,5},{8,10},{9,11},{10,... | collective-permute-start | bytes 282632 | tf_op jit(solution)/shard_map/ppermute | solution.py:50
  15.3 13.5 %collective-permute-start.3 = (bf16[368,128]{1,0:T(8,128)(2,1)S(1)}, bf16[368,128]{1,0:T(8,128)(2,1)S(1)}, u32[]{:S(2)}, u32[]{:S(2)}) collective-permute-start(bf16[368,128]{1,0:T(8,128)(2,1)S(1)} %get-tuple-element.31), channel_id=1, source_target_pairs={{0,4},{1,5},{2,6},{3,7},{4,0},{5,1},{6,2},{7,3},{8,12},{9,13},{10,... | collective-permute-start | bytes 282632 | tf_op jit(solution)/shard_map/ppermute | solution.py:50
  16.8 13.5 %collective-permute-start.4 = (bf16[368,128]{1,0:T(8,128)(2,1)S(1)}, bf16[368,128]{1,0:T(8,128)(2,1)S(1)}, u32[]{:S(2)}, u32[]{:S(2)}) collective-permute-start(bf16[368,128]{1,0:T(8,128)(2,1)S(1)} %get-tuple-element.32), channel_id=1, source_target_pairs={{0,6},{1,7},{2,4},{3,5},{4,2},{5,3},{6,0},{7,1},{8,14},{9,15},{10,... | collective-permute-start | bytes 282632 | tf_op jit(solution)/shard_map/ppermute | solution.py:50
  24.8 13.7 %collective-permute-start.12 = (bf16[256,768]{1,0:T(8,128)(2,1)S(1)}, bf16[256,768]{1,0:T(8,128)(2,1)S(1)}, u32[]{:S(2)}, u32[]{:S(2)}) collective-permute-start(bf16[256,768]{1,0:T(8,128)(2,1)S(1)} %slice.9), channel_id=1, source_target_pairs={{0,2},{1,3},{2,0},{3,1},{4,6},{5,7},{6,4},{7,5},{8,10},{9,11},{10,... | collective-permute-start | bytes 1179656 | tf_op jit(solution)/shard_map/ppermute | solution.py:50
  26.8 13.9 %collective-permute-start.11 = (bf16[256,768]{1,0:T(8,128)(2,1)S(1)}, bf16[256,768]{1,0:T(8,128)(2,1)S(1)}, u32[]{:S(2)}, u32[]{:S(2)}) collective-permute-start(bf16[256,768]{1,0:T(8,128)(2,1)S(1)} %slice.8), channel_id=1, source_target_pairs={{0,4},{1,5},{2,6},{3,7},{4,0},{5,1},{6,2},{7,3},{8,12},{9,13},{10,... | collective-permute-start | bytes 1179656 | tf_op jit(solution)/shard_map/ppermute | solution.py:50
  30.4 10.9 %collective-permute-start.8 = (bf16[512,768]{1,0:T(8,128)(2,1)S(1)}, bf16[512,768]{1,0:T(8,128)(2,1)S(1)}, u32[]{:S(2)}, u32[]{:S(2)}) collective-permute-start(bf16[512,768]{1,0:T(8,128)(2,1)S(1)} %collective-permute-done.7.refs_4_.refs_2_.refs_6_), channel_id=1, source_target_pairs={{0,1},{1,0},{2,3},{3,2},{4,5},{5,4},{6,7},{7,6},{8,9},{9,8},{10,11... | collective-permute-start | bytes 2359304 | tf_op jit(solution)/shard_map/ppermute | solution.py:50
  30.4 10.8 %collective-permute-start.10 = (bf16[512,768]{1,0:T(8,128)(2,1)S(1)}, bf16[512,768]{1,0:T(8,128)(2,1)S(1)}, u32[]{:S(2)}, u32[]{:S(2)}) collective-permute-start(bf16[512,768]{1,0:T(8,128)(2,1)S(1)} %collective-permute-done.9.refs_6_.refs_4_.refs_8_), channel_id=1, source_target_pairs={{0,1},{1,0},{2,3},{3,2},{4,5},{5,4},{6,7},{7,6},{8,9},{9,8},{10,11... | collective-permute-start | bytes 2359304 | tf_op jit(solution)/shard_map/ppermute | solution.py:50
  30.9 4.3 %collective-permute-start.5 = (bf16[240,128]{1,0:T(8,128)(2,1)S(1)}, bf16[240,128]{1,0:T(8,128)(2,1)S(1)}, u32[]{:S(2)}, u32[]{:S(2)}) collective-permute-start(bf16[240,128]{1,0:T(8,128)(2,1)S(1)} %get-tuple-element.34.first_ref), channel_id=1, source_target_pairs={{0,8},{8,0},{16,24},{24,16},{1,9},{9,1},{17,25},{25,17},{2,10},{10... | collective-permute-start | bytes 184328 | tf_op jit(solution)/shard_map/ppermute | solution.py:50
  35.2 5.5 %collective-permute-start.6 = (bf16[240,128]{1,0:T(8,128)(2,1)S(1)}, bf16[240,128]{1,0:T(8,128)(2,1)S(1)}, u32[]{:S(2)}, u32[]{:S(2)}) collective-permute-start(bf16[240,128]{1,0:T(8,128)(2,1)S(1)} %merge_groups.1.refs_0_), channel_id=1, source_target_pairs={{0,16},{8,24},{16,0},{24,8},{1,17},{9,25},{17,1},{25,9},{2,18},{10... | collective-permute-start | bytes 184328 | tf_op jit(solution)/shard_map/ppermute | solution.py:50
  40.8 2.9 %collective-permute-start.13 = (bf16[256,768]{1,0:T(8,128)(2,1)S(1)}, bf16[256,768]{1,0:T(8,128)(2,1)S(1)}, u32[]{:S(2)}, u32[]{:S(2)}) collective-permute-start(bf16[256,768]{1,0:T(8,128)(2,1)S(1)} %collective-permute-done.11.refs_0_.refs_6_.refs_10_), channel_id=1, source_target_pairs={{0,1},{1,0},{2,3},{3,2},{4,5},{5,4},{6,7},{7,6},{8,9},{9,8},{10,11... | collective-permute-start | bytes 1179656 | tf_op jit(solution)/shard_map/ppermute | solution.py:50
  40.8 2.9 %collective-permute-start.14 = (bf16[256,768]{1,0:T(8,128)(2,1)S(1)}, bf16[256,768]{1,0:T(8,128)(2,1)S(1)}, u32[]{:S(2)}, u32[]{:S(2)}) collective-permute-start(bf16[256,768]{1,0:T(8,128)(2,1)S(1)} %collective-permute-done.12.refs_1_.refs_7_.refs_11_), channel_id=1, source_target_pairs={{0,1},{1,0},{2,3},{3,2},{4,5},{5,4},{6,7},{7,6},{8,9},{9,8},{10,11... | collective-permute-start | bytes 1179656 | tf_op jit(solution)/shard_map/ppermute | solution.py:50
  44.6 5.8 %collective-permute-start.15 = (bf16[96,768]{1,0:T(8,128)(2,1)S(1)}, bf16[96,768]{1,0:T(8,128)(2,1)S(1)}, u32[]{:S(2)}, u32[]{:S(2)}) collective-permute-start(bf16[96,768]{1,0:T(8,128)(2,1)S(1)} %cross_far.1), channel_id=1, source_target_pairs={{0,8},{8,0},{16,24},{24,16},{1,9},{9,1},{17,25},{25,17},{2,10},{10... | collective-permute-start | bytes 442376 | tf_op jit(solution)/shard_map/ppermute | solution.py:50
  50.4 9.8 %collective-permute-start.16 = (bf16[96,768]{1,0:T(8,128)(2,1)S(1)}, bf16[96,768]{1,0:T(8,128)(2,1)S(1)}, u32[]{:S(2)}, u32[]{:S(2)}) collective-permute-start(bf16[96,768]{1,0:T(8,128)(2,1)S(1)} %add_convert_fusion.3), channel_id=1, source_target_pairs={{0,16},{8,24},{16,0},{24,8},{1,17},{9,25},{17,1},{25,9},{2,18},{10... | collective-permute-start | bytes 442376 | tf_op jit(solution)/shard_map/ppermute | solution.py:50
  60.3 7.2 %collective-permute-start.22 = (bf16[96,768]{1,0:T(8,128)(2,1)S(1)}, bf16[96,768]{1,0:T(8,128)(2,1)S(1)}, u32[]{:S(2)}, u32[]{:S(2)}) collective-permute-start(bf16[96,768]{1,0:T(8,128)(2,1)S(1)} %add_convert_fusion.2.refs_0_), channel_id=1, source_target_pairs={{0,6},{1,7},{2,4},{3,5},{4,2},{5,3},{6,0},{7,1},{8,14},{9,15},{10,... | collective-permute-start | bytes 442376 | tf_op jit(solution)/shard_map/ppermute | solution.py:50
  62.7 6.5 %collective-permute-start.20 = (bf16[96,768]{1,0:T(8,128)(2,1)S(1)}, bf16[96,768]{1,0:T(8,128)(2,1)S(1)}, u32[]{:S(2)}, u32[]{:S(2)}) collective-permute-start(bf16[96,768]{1,0:T(8,128)(2,1)S(1)} %add_convert_fusion.2.refs_0_), channel_id=1, source_target_pairs={{0,4},{1,5},{2,6},{3,7},{4,0},{5,1},{6,2},{7,3},{8,12},{9,13},{10,... | collective-permute-start | bytes 442376 | tf_op jit(solution)/shard_map/ppermute | solution.py:50
  63.2 6.0 %collective-permute-start.18 = (bf16[96,768]{1,0:T(8,128)(2,1)S(1)}, bf16[96,768]{1,0:T(8,128)(2,1)S(1)}, u32[]{:S(2)}, u32[]{:S(2)}) collective-permute-start(bf16[96,768]{1,0:T(8,128)(2,1)S(1)} %add_convert_fusion.2.refs_0_), channel_id=1, source_target_pairs={{0,2},{1,3},{2,0},{3,1},{4,6},{5,7},{6,4},{7,5},{8,10},{9,11},{10,... | collective-permute-start | bytes 442376 | tf_op jit(solution)/shard_map/ppermute | solution.py:50
  63.8 6.0 %collective-permute-start.17 = (bf16[96,768]{1,0:T(8,128)(2,1)S(1)}, bf16[96,768]{1,0:T(8,128)(2,1)S(1)}, u32[]{:S(2)}, u32[]{:S(2)}) collective-permute-start(bf16[96,768]{1,0:T(8,128)(2,1)S(1)} %add_convert_fusion.2.refs_0_), channel_id=1, source_target_pairs={{0,1},{1,0},{2,3},{3,2},{4,5},{5,4},{6,7},{7,6},{8,9},{9,8},{10,11... | collective-permute-start | bytes 442376 | tf_op jit(solution)/shard_map/ppermute | solution.py:50
  67.4 2.4 %collective-permute-start.23 = (bf16[96,768]{1,0:T(8,128)(2,1)S(1)}, bf16[96,768]{1,0:T(8,128)(2,1)S(1)}, u32[]{:S(2)}, u32[]{:S(2)}) collective-permute-start(bf16[96,768]{1,0:T(8,128)(2,1)S(1)} %collective-permute-done.22.refs_6_), channel_id=1, source_target_pairs={{0,1},{1,0},{2,3},{3,2},{4,5},{5,4},{6,7},{7,6},{8,9},{9,8},{10,11... | collective-permute-start | bytes 442376 | tf_op jit(solution)/shard_map/ppermute | solution.py:50
  69.3 1.6 %collective-permute-start.19 = (bf16[96,768]{1,0:T(8,128)(2,1)S(1)}, bf16[96,768]{1,0:T(8,128)(2,1)S(1)}, u32[]{:S(2)}, u32[]{:S(2)}) collective-permute-start(bf16[96,768]{1,0:T(8,128)(2,1)S(1)} %collective-permute-done.18.refs_2_), channel_id=1, source_target_pairs={{0,1},{1,0},{2,3},{3,2},{4,5},{5,4},{6,7},{7,6},{8,9},{9,8},{10,11... | collective-permute-start | bytes 442376 | tf_op jit(solution)/shard_map/ppermute | solution.py:50
  77.0 4.2 %collective-permute-start.24 = (bf16[192,128]{1,0:T(8,128)(2,1)S(1)}, bf16[192,128]{1,0:T(8,128)(2,1)S(1)}, u32[]{:S(2)}, u32[]{:S(2)}) collective-permute-start(bf16[192,128]{1,0:T(8,128)(2,1)S(1)} %next_sums.1), channel_id=1, source_target_pairs={{0,8},{8,0},{16,24},{24,16},{1,9},{9,1},{17,25},{25,17},{2,10},{10... | collective-permute-start | bytes 147464 | tf_op jit(solution)/shard_map/ppermute | solution.py:50
  81.2 5.5 %collective-permute-start.25 = (bf16[192,128]{1,0:T(8,128)(2,1)S(1)}, bf16[192,128]{1,0:T(8,128)(2,1)S(1)}, u32[]{:S(2)}, u32[]{:S(2)}) collective-permute-start(bf16[192,128]{1,0:T(8,128)(2,1)S(1)} %add_convert_fusion.4.refs_1_), channel_id=1, source_target_pairs={{0,16},{8,24},{16,0},{24,8},{1,17},{9,25},{17,1},{25,9},{2,18},{10... | collective-permute-start | bytes 147464 | tf_op jit(solution)/shard_map/ppermute | solution.py:50
  89.5 5.2 %collective-permute-start.26 = (bf16[96,768]{1,0:T(8,128)(2,1)S(1)}, bf16[96,768]{1,0:T(8,128)(2,1)S(1)}, u32[]{:S(2)}, u32[]{:S(2)}) collective-permute-start(bf16[96,768]{1,0:T(8,128)(2,1)S(1)} %get-tuple-element.47), channel_id=1, source_target_pairs={{0,8},{8,0},{16,24},{24,16},{1,9},{9,1},{17,25},{25,17},{2,10},{10... | collective-permute-start | bytes 442376 | tf_op jit(solution)/shard_map/ppermute | solution.py:50
  94.7 7.7 %collective-permute-start.27 = (bf16[96,768]{1,0:T(8,128)(2,1)S(1)}, bf16[96,768]{1,0:T(8,128)(2,1)S(1)}, u32[]{:S(2)}, u32[]{:S(2)}) collective-permute-start(bf16[96,768]{1,0:T(8,128)(2,1)S(1)} %add_convert_fusion.1), channel_id=1, source_target_pairs={{0,16},{8,24},{16,0},{24,8},{1,17},{9,25},{17,1},{25,9},{2,18},{10... | collective-permute-start | bytes 442376 | tf_op jit(solution)/shard_map/ppermute | solution.py:50
  102.4 6.2 %collective-permute-start.33 = (bf16[96,768]{1,0:T(8,128)(2,1)S(1)}, bf16[96,768]{1,0:T(8,128)(2,1)S(1)}, u32[]{:S(2)}, u32[]{:S(2)}) collective-permute-start(bf16[96,768]{1,0:T(8,128)(2,1)S(1)} %add_convert_fusion.refs_0_), channel_id=1, source_target_pairs={{0,6},{1,7},{2,4},{3,5},{4,2},{5,3},{6,0},{7,1},{8,14},{9,15},{10,... | collective-permute-start | bytes 442376 | tf_op jit(solution)/shard_map/ppermute | solution.py:50
  104.3 5.9 %collective-permute-start.31 = (bf16[96,768]{1,0:T(8,128)(2,1)S(1)}, bf16[96,768]{1,0:T(8,128)(2,1)S(1)}, u32[]{:S(2)}, u32[]{:S(2)}) collective-permute-start(bf16[96,768]{1,0:T(8,128)(2,1)S(1)} %add_convert_fusion.refs_0_), channel_id=1, source_target_pairs={{0,4},{1,5},{2,6},{3,7},{4,0},{5,1},{6,2},{7,3},{8,12},{9,13},{10,... | collective-permute-start | bytes 442376 | tf_op jit(solution)/shard_map/ppermute | solution.py:50
  105.4 5.1 %collective-permute-start.29 = (bf16[96,768]{1,0:T(8,128)(2,1)S(1)}, bf16[96,768]{1,0:T(8,128)(2,1)S(1)}, u32[]{:S(2)}, u32[]{:S(2)}) collective-permute-start(bf16[96,768]{1,0:T(8,128)(2,1)S(1)} %add_convert_fusion.refs_0_), channel_id=1, source_target_pairs={{0,2},{1,3},{2,0},{3,1},{4,6},{5,7},{6,4},{7,5},{8,10},{9,11},{10,... | collective-permute-start | bytes 442376 | tf_op jit(solution)/shard_map/ppermute | solution.py:50
  106.0 4.7 %collective-permute-start.28 = (bf16[96,768]{1,0:T(8,128)(2,1)S(1)}, bf16[96,768]{1,0:T(8,128)(2,1)S(1)}, u32[]{:S(2)}, u32[]{:S(2)}) collective-permute-start(bf16[96,768]{1,0:T(8,128)(2,1)S(1)} %add_convert_fusion.refs_0_), channel_id=1, source_target_pairs={{0,1},{1,0},{2,3},{3,2},{4,5},{5,4},{6,7},{7,6},{8,9},{9,8},{10,11... | collective-permute-start | bytes 442376 | tf_op jit(solution)/shard_map/ppermute | solution.py:50
  108.6 2.0 %collective-permute-start.34 = (bf16[96,768]{1,0:T(8,128)(2,1)S(1)}, bf16[96,768]{1,0:T(8,128)(2,1)S(1)}, u32[]{:S(2)}, u32[]{:S(2)}) collective-permute-start(bf16[96,768]{1,0:T(8,128)(2,1)S(1)} %collective-permute-done.33.refs_6_), channel_id=1, source_target_pairs={{0,1},{1,0},{2,3},{3,2},{4,5},{5,4},{6,7},{7,6},{8,9},{9,8},{10,11... | collective-permute-start | bytes 442376 | tf_op jit(solution)/shard_map/ppermute | solution.py:50
  (8 other events, 14.2 us)

commit v5 on v4

--- a/solution.py
+++ b/solution.py
@@ -10,10 +10,12 @@
 
 K = 256
 ALTS = 2
-LO = 8
+LO = 4
 HI = K // LO
 SUB = 8
-PACK = 128 // HI
+LANES = 256
+PACK = LANES // HI
+MARKS = 8
 EPSILON = 1e-06
 MIB = 1024 * 1024
 BAND = 256
@@ -92,6 +94,10 @@
     )(vectors, centroids, pick_call(ids, centroids.shape[0]))
 
 
+def split(codes):
+    return codes >> 2, codes & 3
+
+
 def packs_of(owned):
     return [range(first, min(first + PACK, owned)) for first in range(0, owned, PACK)]
 
@@ -105,12 +111,12 @@
 
 
 def lane_owner(rows):
-    return lax.broadcasted_iota(jnp.int32, (rows, 128), 1) // HI
+    return lax.broadcasted_iota(jnp.int32, (rows, LANES), 1) // HI
 
 
 def diagonal(wide, block):
     owner = lane_owner(block)
-    total = jnp.zeros((block, 128), F32)
+    total = jnp.zeros((block, LANES), F32)
     for i in range(wide.shape[0] // block):
         total = jnp.where(owner == i, wide[i * block : (i + 1) * block, :], total)
     return total
@@ -118,14 +124,14 @@
 
 def pack_sums(rotated, codes, pack, with_counts, table=None):
     rows = codes.shape[1]
-    hi, lo = codes >> 3, codes & 7
+    hi, lo = split(codes)
     parts = []
     for m in pack:
         value = rotated[m * SUB : (m + 1) * SUB, :]
         low = jnp.broadcast_to(lo[m : m + 1, :], (SUB, rows))
         parts += [jnp.where(low == level, value, 0.0) for level in range(LO)]
     if with_counts:
-        low_level = lax.broadcasted_iota(jnp.int32, (LO, rows), 0)
+        low_level = lax.broadcasted_iota(jnp.int32, (MARKS, rows), 0)
         parts += [jnp.where(low_level == lo[m : m + 1, :], 1.0, 0.0) for m in pack]
     marked = jnp.concatenate(parts, axis=0).astype(BF16)
     return mm(marked, hi_table(hi, pack), NT) if table is None else mm(marked, table)
@@ -133,8 +139,8 @@
 
 def pack_layout(owned, with_counts):
     packs = len(packs_of(owned))
-    base, height = packs * LO * SUB, packs * LO
-    return base, height, base + (-(-2 * height // 16) * 16 if with_counts else 0)
+    base, height = packs * LO * SUB, packs * MARKS
+    return base, height, base + (-(-height // 16) * 16 if with_counts else 0)
 
 
 def write_sums(sums, counts, owned, out_ref):
@@ -142,9 +148,12 @@
     out_ref[:base, :] = sums.astype(BF16)
     if counts is not None:
         above = jnp.floor(counts * (1.0 / 256.0))
-        pieces = [above, counts - above * 256.0]
-        pad = total - base - 2 * height
-        pieces += [jnp.zeros((pad, 128), F32)] if pad else []
+        below = counts - above * 256.0
+        pieces = []
+        for at in range(0, height, MARKS):
+            pieces.append(jnp.concatenate([above[at : at + LO], below[at : at + LO]], axis=0))
+        if total > base + height:
+            pieces.append(jnp.zeros((total - base - height, LANES), F32))
         out_ref[base:, :] = jnp.concatenate(pieces, axis=0).astype(BF16)
 
 
@@ -155,7 +164,7 @@
         size = len(pack)
         sums.append(diagonal(total[: size * block], block))
         if with_counts:
-            counts.append(diagonal(total[size * block :], LO))
+            counts.append(diagonal(total[size * block :], MARKS))
     return jnp.concatenate(sums, axis=0), jnp.concatenate(counts, axis=0) if with_counts else None
 
 
@@ -170,18 +179,22 @@
     whole = tree([ref[...].astype(F32) for ref in parts])
     if not with_counts:
         return whole, None
-    return whole[:base], whole[base : base + height] * 256.0 + whole[base + height : base + 2 * height]
+    counts = []
+    for at in range(base, base + height, MARKS):
+        count = whole[at : at + LO] * 256.0 + whole[at + LO : at + MARKS]
+        counts.append(jnp.concatenate([count, jnp.zeros((MARKS - LO, LANES), F32)], axis=0))
+    return whole[:base], jnp.concatenate(counts, axis=0)
 
 
 def code_rows(rows):
-    return rows // 128 * 16
+    return rows // LANES * 16
 
 
 def write_codes(codes, out_ref, at):
     owned, rows = codes.shape
     filled = jnp.concatenate([codes, jnp.zeros((16 - owned, rows), F32)], axis=0).astype(BF16)
-    for c in range(rows // 128):
-        out_ref[at + 16 * c : at + 16 * c + 16, :] = filled[:, 128 * c : 128 * c + 128]
+    for c in range(rows // LANES):
+        out_ref[at + 16 * c : at + 16 * c + 16, :] = filled[:, LANES * c : LANES * (c + 1)]
 
 
 def local_sums_kernel(size, place_ref, rotation_ref, codes_ref, residual_ref, *refs):
@@ -208,7 +221,7 @@
     subspaces, rows = codes.shape
     owned = subspaces // size
     height = -(-owned // 8) * 8
-    shape = jax.ShapeDtypeStruct((size // 2, pack_layout(owned, True)[2] + code_rows(rows), 128), BF16)
+    shape = jax.ShapeDtypeStruct((size // 2, pack_layout(owned, True)[2] + code_rows(rows), LANES), BF16)
     return pl.pallas_call(
         functools.partial(local_sums_kernel, size),
         out_shape=(shape,) * 2,
@@ -256,7 +269,7 @@
             for c in range(length // 16):
                 at = base + core * length + 16 * c
                 piece = part[at : at + 16, :].astype(F32)
-                codes_ref[2 * i + core, :, 128 * c : 128 * c + 128] = piece[:owned].astype(jnp.int32)
+                codes_ref[2 * i + core, :, LANES * c : LANES * (c + 1)] = piece[:owned].astype(jnp.int32)
 
 
 def merge_chips_call(parts, owned, rows):
@@ -264,7 +277,7 @@
     return pl.pallas_call(
         functools.partial(merge_chips_kernel, owned),
         out_shape=(
-            jax.ShapeDtypeStruct((pack_layout(owned, True)[2], 128), BF16),
+            jax.ShapeDtypeStruct((pack_layout(owned, True)[2], LANES), BF16),
             jax.ShapeDtypeStruct((size, owned, rows), jnp.int32),
         ),
         in_specs=[vmem_spec()] * len(parts),
@@ -323,7 +336,7 @@
         rows = []
         for level in range(LO):
             at = g * block + level * SUB
-            rows.append(everything[at : at + SUB] / (counts[g * LO + level : g * LO + level + 1] + 1.0))
+            rows.append(everything[at : at + SUB] / (counts[g * MARKS + level : g * MARKS + level + 1] + 1.0))
         books.append(jnp.concatenate(rows, axis=0))
     return books, counts
 
@@ -340,11 +353,11 @@
     owned = codes_ref.shape[1]
     for i, span in enumerate(spans):
         codes = span_codes(codes_ref, span)
-        hi, lo = codes >> 3, codes & 7
+        hi, lo = split(codes)
         rows = codes.shape[1]
         rebuilt = []
         for g, pack in enumerate(packs_of(owned)):
-            table = hi_table(hi, pack) if tables is None else tables[i, g * 128 : (g + 1) * 128, :]
+            table = hi_table(hi, pack) if tables is None else tables[i, g * LANES : (g + 1) * LANES, :]
             spread = mm(wide[g], table)
             for j, m in enumerate(pack):
                 low = jnp.broadcast_to(lo[m : m + 1, :], (SUB, rows))
@@ -382,8 +395,8 @@
         functools.partial(cross_near_kernel, held, len(sums)),
         out_shape=(
             jax.ShapeDtypeStruct((owned * SUB, rows[0].shape[1]), F32),
-            jax.ShapeDtypeStruct((packs, PACK * LO * SUB, 128), BF16),
-            jax.ShapeDtypeStruct((packs * LO, 128), F32),
+            jax.ShapeDtypeStruct((packs, PACK * LO * SUB, LANES), BF16),
+            jax.ShapeDtypeStruct((packs * MARKS, LANES), F32),
         ),
         in_specs=[vmem_spec()] * (1 + len(sums) + len(rows)),
         out_specs=(vmem_spec(),) * 3,
@@ -435,7 +448,7 @@
         functools.partial(cross_kernel, held, len(sums), total_rows, bool(ready)),
         out_shape=(
             jax.ShapeDtypeStruct((owned * SUB, rows[0].shape[1]), BF16),
-            jax.ShapeDtypeStruct((len(packs_of(owned)) * LO * SUB, 128), F32),
+            jax.ShapeDtypeStruct((len(packs_of(owned)) * LO * SUB, LANES), F32),
         ),
         in_specs=[vmem_spec()] * (2 + len(tables) + len(sums) + len(rows)),
         out_specs=(vmem_spec(), vmem_spec()),
@@ -445,41 +458,55 @@
     )(codes, *tables, *sums, counts, *rows)
 
 
-def prepare_kernel(held, codes_ref, *refs):
-    pieces, (turned_ref, table_ref, across_ref) = pieces_of(held, refs), refs[-3:]
-    packs = packs_of(codes_ref.shape[1])
+def turn_kernel(held, *refs):
+    pieces, turned_ref = pieces_of(held, refs), refs[-1]
     for i, span in enumerate(spans_of(held)):
         turned_ref[i, :, :] = span_rows(pieces, span).T
-        hi = span_codes(codes_ref, span) >> 3
+
+
+def tables_kernel(spans, codes_ref, table_ref, across_ref):
+    packs = packs_of(codes_ref.shape[1])
+    for i, span in enumerate(spans):
+        hi = split(span_codes(codes_ref, span))[0]
         for g, pack in enumerate(packs):
             table = hi_table(hi, pack)
-            across_ref[i, g * 128 : (g + 1) * 128, :] = table
-            table_ref[i, :, g * 128 : (g + 1) * 128] = table.T
-
-
-def prepare_call(codes, chunks):
+            across_ref[i, g * LANES : (g + 1) * LANES, :] = table
+            table_ref[i, :, g * LANES : (g + 1) * LANES] = table.T
+
+
+def prepare_call(codes, chunks, after_codes, after_rows):
     size, owned, rows = codes.shape
     held, pieces = flat(chunks)
-    lanes = 128 * len(packs_of(owned))
+    lanes = LANES * len(packs_of(owned))
     width = pieces[0].shape[1]
-    spans = len(spans_of(held))
-    each = size // spans * rows
-    shapes = (
-        jax.ShapeDtypeStruct((spans, width, each), BF16),
-        jax.ShapeDtypeStruct((spans, each, lanes), BF16),
-        jax.ShapeDtypeStruct((spans, lanes, each), BF16),
+    spans = spans_of(held)
+    each = size // len(spans) * rows
+    turned = jax.ShapeDtypeStruct((len(spans), width, each), BF16)
+    tables = (
+        jax.ShapeDtypeStruct((len(spans), each, lanes), BF16),
+        jax.ShapeDtypeStruct((len(spans), lanes, each), BF16),
     )
-    if sum(math.prod(a.shape) * 2 for a in shapes) > 16 * MIB:
+    if sum(math.prod(a.shape) * 2 for a in (turned, *tables)) > 20 * MIB:
         return None
-    return pl.pallas_call(
-        functools.partial(prepare_kernel, held),
-        out_shape=shapes,
-        in_specs=[vmem_spec()] * (1 + len(pieces)),
-        out_specs=(vmem_spec(),) * 3,
-        compiler_params=params(*pieces, *shapes),
-        cost_estimate=cost(0),
-        name="prepare",
-    )(codes, *pieces)
+    rows_turned = pl.pallas_call(
+        functools.partial(turn_kernel, held),
+        out_shape=turned,
+        in_specs=[vmem_spec()] * len(pieces),
+        out_specs=vmem_spec(),
+        compiler_params=params(turned),
+        cost_estimate=cost(0),
+        name="turn_rows",
+    )(after(pieces[0], *after_rows), *pieces[1:])
+    two = pl.pallas_call(
+        functools.partial(tables_kernel, spans),
+        out_shape=tables,
+        in_specs=[vmem_spec()],
+        out_specs=(vmem_spec(),) * 2,
+        compiler_params=params(*tables),
+        cost_estimate=cost(0),
+        name="tables",
+    )(after(codes, *after_codes))
+    return (rows_turned, *two)
 
 
 def bands(x):
@@ -530,7 +557,7 @@
         codes = span_codes(codes_ref, span)
         more = []
         for g, pack in enumerate(packs_of(owned)):
-            table = table_ref[i, :, g * 128 : (g + 1) * 128] if ready else None
+            table = table_ref[i, :, g * LANES : (g + 1) * LANES] if ready else None
             more.append(pack_sums(rotated, codes, pack, False, table))
         totals = more if totals is None else [a + b for a, b in zip(totals, more)]
     write_sums(pack_diagonals(totals, owned, False)[0], None, owned, out_ref)
@@ -542,7 +569,7 @@
     given = list(ready[:2]) if ready else rows
     return pl.pallas_call(
         functools.partial(next_sums_kernel, held, bool(ready)),
-        out_shape=jax.ShapeDtypeStruct((pack_layout(owned, False)[2], 128), BF16),
+        out_shape=jax.ShapeDtypeStruct((pack_layout(owned, False)[2], LANES), BF16),
         in_specs=[vmem_spec()] * (1 + len(blocks) + len(given)),
         out_specs=vmem_spec(),
         compiler_params=params(*given),
@@ -617,15 +644,17 @@
     return merge_chips_call(parts, owned, rows)
 
 
-def add_over_groups(x, size, last):
-    for bit in [1 << b for b in range(size.bit_length() - 2)]:
-        x = (x.astype(F32) + swap(x, "group", size, bit).astype(F32)).astype(BF16)
-    x = after(x, *last)
-    return [x, swap(x, "group", size, size // 2)]
-
-
-def reduce_cross(cross, size, *last):
-    return tree([part.astype(F32) for part in add_over_groups(cross, size, last)]).astype(BF16)
+def direct(x, size):
+    return [x] + [swap(x, "group", size, k) for k in range(1, size)]
+
+
+def reduce_cross(cross, size, last):
+    bits = [1 << b for b in range(size.bit_length() - 1)]
+    for bit in bits:
+        if bit == bits[-1]:
+            cross = after(cross, *last)
+        cross = (cross.astype(F32) + swap(cross, "group", size, bit).astype(F32)).astype(BF16)
+    return cross
 
 
 def per_device(vectors, centroids, list_ids, codes, rotation):
@@ -655,16 +684,16 @@
     far = {**far, **both_cores(far, size)}
     cross = cross_far_call(own_codes, total, wide, far, total_rows)
     chunks.update(far)
-    ready = prepare_call(after(own_codes, cross), chunks)
+    ready = prepare_call(own_codes, chunks, (cross,), (cross,))
     for alternation in range(1, ALTS):
-        block = reduce_cross(cross, groups)
+        block = reduce_cross(cross, groups, ready[:1] if ready else ())
         if ready:
             block = after(block, *ready)
-        parts = add_over_groups(next_sums_call(own_codes, ready, gather_group(block, size), chunks), groups, ())
+        parts = direct(next_sums_call(own_codes, ready, gather_group(block, size), chunks), groups)
         cross, book = cross_call(own_codes, ready, parts, counts, chunks, total_rows)
     packs = len(packs_of(owned))
     book = book.reshape(packs, LO * SUB, PACK, HI).transpose(0, 2, 3, 1).reshape(packs * PACK, K * SUB)[:owned]
-    blocks = gather_group(reduce_cross(cross, groups, book), size)
+    blocks = gather_group(reduce_cross(cross, groups, (book,)), size)
     rotated_out = final_call(place, residual, blocks)
     return (rotated_out, book)
 

time: 118 us -> 116 us (0.983)
    pallas_call x1 -> x2, Pallas kernels: 2.79 us -> 3.89 us  [the longest x1 2.08 us: prepare_call(): pl.pallas_call(functools.partial(tables_kernel, spans), out_shape=tables,...]
    ppermute x35 -> x36, starting transfers between devices: 39.5 us -> 38.4 us  [swap(): return lax.ppermute(x, axis, [(i, i ^ bits) for i in range(size)])]
    ppermute x35 -> x36, waiting for transfers between devices: 47.7 us -> 47.5 us  [swap(): return lax.ppermute(x, axis, [(i, i ^ bits) for i in range(size)])]
  transfers between devices with their start and end apart: 35 -> 36, of which waited for: 22 -> 22; matrix products, arithmetic and copies ran while one was open for 1% -> 1% of each run, Pallas kernels for 7% -> 8%
where the time goes in v5:
time: 116 us
  waiting for transfers between devices  47.5 us (41%)
  starting transfers between devices  38.4 us (33%)
  Pallas kernels  24.7 us (21%)
  local copies, waits for them, and re-layouts  4.68 us (4%)
    ppermute x36, waiting for transfers between devices, swap(): return lax.ppermute(x, axis, [(i, i ^ bits) for i in range(size)])  47.5 us
    ppermute x36, starting transfers between devices, swap(): return lax.ppermute(x, axis, [(i, i ^ bits) for i in range(size)])  38.4 us
    pallas_call x1, Pallas kernels, final_call(): pl.pallas_call(functools.partial(final_kernel, len(blocks)), out_shape=ja...  5.82 us
    pallas_call x1, Pallas kernels, next_sums_call(): pl.pallas_call(functools.partial(next_sums_kernel, held, bool(ready)), ou...  5.43 us
    unnamed x10, local copies, waits for them, and re-layouts  3.48 us
    pallas_call x1, Pallas kernels, local_sums_call(): pl.pallas_call(functools.partial(local_sums_kernel, size), out_shape=(sha...  3.45 us
  transfers between devices with their start and end apart: 36, of which 22 were waited for; matrix products, arithmetic and copies ran while one was open for 1% of the time, Pallas kernels for 8%

profile of v5, /device:TPU:0, one launch (start us, length us, event | category | flops | bytes accessed | tf_op | source)
XLA Modules:
  0.0 116.3 jit_solution(1839909173216970035)
XLA Ops:
  3.8 2.6 %collective-permute-start.9 = (bf16[512,768]{1,0:T(8,128)(2,1)S(1)}, bf16[512,768]{1,0:T(8,128)(2,1)S(1)}, u32[]{:S(2)}, u32[]{:S(2)}) collective-permute-start(bf16[512,768]{1,0:T(8,128)(2,1)S(1)} %residual.1.residual_ref.refs_2_.refs_0_.refs_6_), channel_id=1, source_target_pairs={{0,4},{1,5},{2,6},{3,7},{4,0},{5,1},{6,2},{7,3},{8,12},{9,13},{10,... | collective-permute-start | bytes 2359304 | tf_op jit(solution)/shard_map/ppermute | solution.py:52
  7.9 1.7 %copy-done = f32[768,768]{1,0:T(8,128)S(1)} copy-done((f32[768,768]{1,0:T(8,128)S(1)}, f32[768,768]{1,0:T(8,128)}, u32[]{:S(2)}) %copy-start) | copy-done | bytes 2359320
  9.6 3.4 %local_sums.1 = (bf16[4,160,256]{2,1,0:T(8,128)(2,1)S(1)}, bf16[4,160,256]{2,1,0:T(8,128)(2,1)S(1)}) custom-call(s32[1]{0:T(128)} %bitcast.place_ref, f32[768,768]{1,0:T(8,128)S(1)} %copy-done, s32[96,512]{1,0:T(8,128)S(1)} %bitcast.6, bf16[512,768]{1,0:T(8,128)(2,1)S(1)} %residual.1.residual_ref.refs_2_.refs_0_.refs_6_), custom_call_target="tpu_custom_call" | custom-call | tf_op jit(solution)/shard_map/local_sums/pallas_call | solution.py:225
  13.1 1.6 %collective-permute-done.1.came_ref = bf16[4,160,256]{2,1,0:T(8,128)(2,1)S(1)} collective-permute-done((bf16[4,160,256]{2,1,0:T(8,128)(2,1)S(1)}, bf16[4,160,256]{2,1,0:T(8,128)(2,1)S(1)}, u32[]{:S(2)}, u32[]{:S(2)}) %collective-permute-start.1) | collective-permute-done | bytes 327712 | tf_op jit(solution)/shard_map/ppermute | solution.py:52
  18.4 6.4 %collective-permute-done.9.refs_6_.refs_4_.refs_10_ = bf16[512,768]{1,0:T(8,128)(2,1)S(1)} collective-permute-done((bf16[512,768]{1,0:T(8,128)(2,1)S(1)}, bf16[512,768]{1,0:T(8,128)(2,1)S(1)}, u32[]{:S(2)}, u32[]{:S(2)}) %collective-permute-start.9) | collective-permute-done | bytes 786464 | tf_op jit(solution)/shard_map/ppermute | solution.py:52
  24.8 2.0 %collective-permute-start.12 = (bf16[256,768]{1,0:T(8,128)(2,1)S(1)}, bf16[256,768]{1,0:T(8,128)(2,1)S(1)}, u32[]{:S(2)}, u32[]{:S(2)}) collective-permute-start(bf16[256,768]{1,0:T(8,128)(2,1)S(1)} %slice.9), channel_id=1, source_target_pairs={{0,2},{1,3},{2,0},{3,1},{4,6},{5,7},{6,4},{7,5},{8,10},{9,11},{10,... | collective-permute-start | bytes 1179656 | tf_op jit(solution)/shard_map/ppermute | solution.py:52
  28.9 1.6 %collective-permute-done.4.refs_3_ = bf16[192,256]{1,0:T(8,128)(2,1)S(1)} collective-permute-done((bf16[192,256]{1,0:T(8,128)(2,1)S(1)}, bf16[192,256]{1,0:T(8,128)(2,1)S(1)}, u32[]{:S(2)}, u32[]{:S(2)}) %collective-permute-start.4) | collective-permute-done | bytes 98336 | tf_op jit(solution)/shard_map/ppermute | solution.py:52
  31.1 2.0 %collective-permute-start.5 = (bf16[128,256]{1,0:T(8,128)(2,1)S(1)}, bf16[128,256]{1,0:T(8,128)(2,1)S(1)}, u32[]{:S(2)}, u32[]{:S(2)}) collective-permute-start(bf16[128,256]{1,0:T(8,128)(2,1)S(1)} %get-tuple-element.35.first_ref), channel_id=1, source_target_pairs={{0,8},{8,0},{16,24},{24,16},{1,9},{9,1},{17,25},{25,17},{2,10},{10... | collective-permute-start | bytes 196616 | tf_op jit(solution)/shard_map/ppermute | solution.py:52
  33.2 2.3 %collective-permute-done.5.second_ref = bf16[128,256]{1,0:T(8,128)(2,1)S(1)} collective-permute-done((bf16[128,256]{1,0:T(8,128)(2,1)S(1)}, bf16[128,256]{1,0:T(8,128)(2,1)S(1)}, u32[]{:S(2)}, u32[]{:S(2)}) %collective-permute-start.5) | collective-permute-done | bytes 65568 | tf_op jit(solution)/shard_map/ppermute | solution.py:52
  35.5 3.0 %collective-permute-start.6 = (bf16[128,256]{1,0:T(8,128)(2,1)S(1)}, bf16[128,256]{1,0:T(8,128)(2,1)S(1)}, u32[]{:S(2)}, u32[]{:S(2)}) collective-permute-start(bf16[128,256]{1,0:T(8,128)(2,1)S(1)} %merge_groups.1.refs_0_), channel_id=1, source_target_pairs={{0,16},{8,24},{16,0},{24,8},{1,17},{9,25},{17,1},{25,9},{2,18},{10... | collective-permute-start | bytes 196616 | tf_op jit(solution)/shard_map/ppermute | solution.py:52
  38.6 2.4 %collective-permute-done.6.refs_1_ = bf16[128,256]{1,0:T(8,128)(2,1)S(1)} collective-permute-done((bf16[128,256]{1,0:T(8,128)(2,1)S(1)}, bf16[128,256]{1,0:T(8,128)(2,1)S(1)}, u32[]{:S(2)}, u32[]{:S(2)}) %collective-permute-start.6) | collective-permute-done | bytes 65568 | tf_op jit(solution)/shard_map/ppermute | solution.py:52
  41.6 2.1 %cross_near.1 = (f32[96,768]{1,0:T(8,128)S(1)}, bf16[3,128,256]{2,1,0:T(8,128)(2,1)S(1)}, f32[24,256]{1,0:T(8,128)S(1)}) custom-call(s32[8,12,512]{2,1,0:T(8,128)S(1)} %get-tuple-element.42.codes_ref, bf16[128,256]{1,0:T(8,128)(2,1)S(1)} %merge_groups.1.refs_0_, bf16[128,256]{1,0:T(8,128)(2,1)S(1)} %collective-permute-done.6.refs_1_, ...), custom_call_target="tpu_custom_call" | custom-call | tf_op jit(solution)/shard_map/cross_near/pallas_call | solution.py:394
  44.5 1.7 %collective-permute-start.15 = (bf16[96,768]{1,0:T(8,128)(2,1)S(1)}, bf16[96,768]{1,0:T(8,128)(2,1)S(1)}, u32[]{:S(2)}, u32[]{:S(2)}) collective-permute-start(bf16[96,768]{1,0:T(8,128)(2,1)S(1)} %cross_far.1), channel_id=1, source_target_pairs={{0,8},{8,0},{16,24},{24,16},{1,9},{9,1},{17,25},{25,17},{2,10},{10... | collective-permute-start | bytes 442376 | tf_op jit(solution)/shard_map/ppermute | solution.py:52
  46.1 1.8 %turn_rows.1.refs_8_ = bf16[4,768,1024]{2,1,0:T(8,128)(2,1)S(1)} custom-call(bf16[512,768]{1,0:T(8,128)(2,1)S(1)} %residual.1.residual_ref.refs_2_.refs_0_.refs_6_, bf16[512,768]{1,0:T(8,128)(2,1)S(1)} %collective-permute-done.refs_3_.refs_1_.refs_7_, bf16[512,768]{1,0:T(8,128)(2,1)S(1)} %collective-permute-done.7.refs_4_.refs_2_.refs_8_, ...), custom_call_target="tpu_custom_call" | custom-call | tf_op jit(solution)/shard_map/turn_rows/pallas_call | solution.py:491
  48.0 2.3 %collective-permute-done.15 = bf16[96,768]{1,0:T(8,128)(2,1)S(1)} collective-permute-done((bf16[96,768]{1,0:T(8,128)(2,1)S(1)}, bf16[96,768]{1,0:T(8,128)(2,1)S(1)}, u32[]{:S(2)}, u32[]{:S(2)}) %collective-permute-start.15) | collective-permute-done | bytes 147488 | tf_op jit(solution)/shard_map/ppermute | solution.py:52
  50.3 3.1 %collective-permute-start.16 = (bf16[96,768]{1,0:T(8,128)(2,1)S(1)}, bf16[96,768]{1,0:T(8,128)(2,1)S(1)}, u32[]{:S(2)}, u32[]{:S(2)}) collective-permute-start(bf16[96,768]{1,0:T(8,128)(2,1)S(1)} %add_convert_fusion.3), channel_id=1, source_target_pairs={{0,16},{8,24},{16,0},{24,8},{1,17},{9,25},{17,1},{25,9},{2,18},{10... | collective-permute-start | bytes 442376 | tf_op jit(solution)/shard_map/ppermute | solution.py:52
  53.4 2.1 %tables.1 = (bf16[4,1024,768]{2,1,0:T(8,128)(2,1)S(1)}, bf16[4,768,1024]{2,1,0:T(8,128)(2,1)S(1)}) custom-call(s32[8,12,512]{2,1,0:T(8,128)S(1)} %get-tuple-element.42.codes_ref), custom_call_target="tpu_custom_call" | custom-call | tf_op jit(solution)/shard_map/tables/pallas_call | solution.py:500
  55.5 4.6 %collective-permute-done.16 = bf16[96,768]{1,0:T(8,128)(2,1)S(1)} collective-permute-done((bf16[96,768]{1,0:T(8,128)(2,1)S(1)}, bf16[96,768]{1,0:T(8,128)(2,1)S(1)}, u32[]{:S(2)}, u32[]{:S(2)}) %collective-permute-start.16) | collective-permute-done | bytes 147488 | tf_op jit(solution)/shard_map/ppermute | solution.py:52
  60.1 2.5 %collective-permute-start.22 = (bf16[96,768]{1,0:T(8,128)(2,1)S(1)}, bf16[96,768]{1,0:T(8,128)(2,1)S(1)}, u32[]{:S(2)}, u32[]{:S(2)}) collective-permute-start(bf16[96,768]{1,0:T(8,128)(2,1)S(1)} %add_convert_fusion.2.refs_0_), channel_id=1, source_target_pairs={{0,6},{1,7},{2,4},{3,5},{4,2},{5,3},{6,0},{7,1},{8,14},{9,15},{10,... | collective-permute-start | bytes 442376 | tf_op jit(solution)/shard_map/ppermute | solution.py:52
  63.7 3.6 %collective-permute-done.22.refs_6_ = bf16[96,768]{1,0:T(8,128)(2,1)S(1)} collective-permute-done((bf16[96,768]{1,0:T(8,128)(2,1)S(1)}, bf16[96,768]{1,0:T(8,128)(2,1)S(1)}, u32[]{:S(2)}, u32[]{:S(2)}) %collective-permute-start.22) | collective-permute-done | bytes 147488 | tf_op jit(solution)/shard_map/ppermute | solution.py:52
  67.3 1.9 %collective-permute-done.20.refs_4_ = bf16[96,768]{1,0:T(8,128)(2,1)S(1)} collective-permute-done((bf16[96,768]{1,0:T(8,128)(2,1)S(1)}, bf16[96,768]{1,0:T(8,128)(2,1)S(1)}, u32[]{:S(2)}, u32[]{:S(2)}) %collective-permute-start.20) | collective-permute-done | bytes 147488 | tf_op jit(solution)/shard_map/ppermute | solution.py:52
  70.7 5.4 %next_sums.1.refs_1_ = bf16[96,256]{1,0:T(8,128)(2,1)S(1)} custom-call(s32[8,12,512]{2,1,0:T(8,128)S(1)} %get-tuple-element.42.codes_ref, bf16[96,768]{1,0:T(8,128)(2,1)S(1)} %add_convert_fusion.2.refs_0_, bf16[96,768]{1,0:T(8,128)(2,1)S(1)} %collective-permute-done.17.refs_1_, bf16[96,768]{1,0:T(8,128)(2,1)S(1)} %collective-permute-done.18.refs_2_, ...), custom_call_target="tpu_custom_call" | custom-call | tf_op jit(solution)/shard_map/next_sums/pallas_call | solution.py:570
  76.2 4.4 %collective-permute-start.26 = (bf16[96,256]{1,0:T(8,128)(2,1)S(1)}, bf16[96,256]{1,0:T(8,128)(2,1)S(1)}, u32[]{:S(2)}, u32[]{:S(2)}) collective-permute-start(bf16[96,256]{1,0:T(8,128)(2,1)S(1)} %next_sums.1.refs_1_), channel_id=1, source_target_pairs={{0,24},{8,16},{16,8},{24,0},{1,25},{9,17},{17,9},{25,1},{2,26},{10... | collective-permute-start | bytes 147464 | tf_op jit(solution)/shard_map/ppermute | solution.py:52
  81.2 1.9 %collective-permute-done.26.refs_4_ = bf16[96,256]{1,0:T(8,128)(2,1)S(1)} collective-permute-done((bf16[96,256]{1,0:T(8,128)(2,1)S(1)}, bf16[96,256]{1,0:T(8,128)(2,1)S(1)}, u32[]{:S(2)}, u32[]{:S(2)}) %collective-permute-start.26) | collective-permute-done | bytes 49184 | tf_op jit(solution)/shard_map/ppermute | solution.py:52
  83.1 2.5 %collective-permute-done.25.refs_3_ = bf16[96,256]{1,0:T(8,128)(2,1)S(1)} collective-permute-done((bf16[96,256]{1,0:T(8,128)(2,1)S(1)}, bf16[96,256]{1,0:T(8,128)(2,1)S(1)}, u32[]{:S(2)}, u32[]{:S(2)}) %collective-permute-start.25) | collective-permute-done | bytes 49184 | tf_op jit(solution)/shard_map/ppermute | solution.py:52
  85.7 2.3 %cross.1 = (bf16[96,768]{1,0:T(8,128)(2,1)S(1)}, f32[96,256]{1,0:T(8,128)S(1)}) custom-call(s32[8,12,512]{2,1,0:T(8,128)S(1)} %get-tuple-element.42.codes_ref, bf16[4,768,1024]{2,1,0:T(8,128)(2,1)S(1)} %get-tuple-element.43.refs_0_, bf16[96,256]{1,0:T(8,128)(2,1)S(1)} %next_sums.1.refs_1_, bf16[96,256]{1,0:T(8,128)(2,1)S(1)} %collective-permute-done.24.refs_2_, ...), custom_call_target="tpu_custom_call" | custom-call | tf_op jit(solution)/shard_map/cross/pallas_call | solution.py:447
  90.1 3.0 %collective-permute-done.27 = bf16[96,768]{1,0:T(8,128)(2,1)S(1)} collective-permute-done((bf16[96,768]{1,0:T(8,128)(2,1)S(1)}, bf16[96,768]{1,0:T(8,128)(2,1)S(1)}, u32[]{:S(2)}, u32[]{:S(2)}) %collective-permute-start.27) | collective-permute-done | bytes 147488 | tf_op jit(solution)/shard_map/ppermute | solution.py:52
  93.2 2.0 %collective-permute-start.28 = (bf16[96,768]{1,0:T(8,128)(2,1)S(1)}, bf16[96,768]{1,0:T(8,128)(2,1)S(1)}, u32[]{:S(2)}, u32[]{:S(2)}) collective-permute-start(bf16[96,768]{1,0:T(8,128)(2,1)S(1)} %add_convert_fusion.1), channel_id=1, source_target_pairs={{0,16},{8,24},{16,0},{24,8},{1,17},{9,25},{17,1},{25,9},{2,18},{10... | collective-permute-start | bytes 442376 | tf_op jit(solution)/shard_map/ppermute | solution.py:52
  95.2 5.7 %collective-permute-done.28 = bf16[96,768]{1,0:T(8,128)(2,1)S(1)} collective-permute-done((bf16[96,768]{1,0:T(8,128)(2,1)S(1)}, bf16[96,768]{1,0:T(8,128)(2,1)S(1)}, u32[]{:S(2)}, u32[]{:S(2)}) %collective-permute-start.28) | collective-permute-done | bytes 147488 | tf_op jit(solution)/shard_map/ppermute | solution.py:52
  100.9 1.8 %collective-permute-start.34 = (bf16[96,768]{1,0:T(8,128)(2,1)S(1)}, bf16[96,768]{1,0:T(8,128)(2,1)S(1)}, u32[]{:S(2)}, u32[]{:S(2)}) collective-permute-start(bf16[96,768]{1,0:T(8,128)(2,1)S(1)} %add_convert_fusion.refs_0_), channel_id=1, source_target_pairs={{0,6},{1,7},{2,4},{3,5},{4,2},{5,3},{6,0},{7,1},{8,14},{9,15},{10,... | collective-permute-start | bytes 442376 | tf_op jit(solution)/shard_map/ppermute | solution.py:52
  104.5 2.6 %collective-permute-done.34.refs_6_ = bf16[96,768]{1,0:T(8,128)(2,1)S(1)} collective-permute-done((bf16[96,768]{1,0:T(8,128)(2,1)S(1)}, bf16[96,768]{1,0:T(8,128)(2,1)S(1)}, u32[]{:S(2)}, u32[]{:S(2)}) %collective-permute-start.34) | collective-permute-done | bytes 147488 | tf_op jit(solution)/shard_map/ppermute | solution.py:52
  110.4 5.8 %final.1 = bf16[512,768]{1,0:T(8,128)(2,1)} custom-call(s32[1]{0:T(128)} %bitcast.place_ref, bf16[512,768]{1,0:T(8,128)(2,1)S(1)} %residual.1.residual_ref.refs_2_.refs_0_.refs_6_, bf16[96,768]{1,0:T(8,128)(2,1)S(1)} %add_convert_fusion.refs_0_, bf16[96,768]{1,0:T(8,128)(2,1)S(1)} %collective-permute-done.29.refs_1_, ...), custom_call_target="tpu_custom_call" | custom-call | tf_op jit(solution)/shard_map/final/pallas_call | solution.py:598
  (72 shorter events, 23.3 us)
Async XLA Ops:
  3.3 4.6 %collective-permute-start = (bf16[512,768]{1,0:T(8,128)(2,1)S(1)}, bf16[512,768]{1,0:T(8,128)(2,1)S(1)}, u32[]{:S(2)}, u32[]{:S(2)}) collective-permute-start(bf16[512,768]{1,0:T(8,128)(2,1)S(1)} %residual.1.residual_ref.refs_2_.refs_0_.refs_6_), channel_id=1, source_target_pairs={{0,1},{1,0},{2,3},{3,2},{4,5},{5,4},{6,7},{7,6},{8,9},{9,8},{10,11... | collective-permute-start | bytes 2359304 | tf_op jit(solution)/shard_map/ppermute | solution.py:52
  3.8 21.0 %collective-permute-start.9 = (bf16[512,768]{1,0:T(8,128)(2,1)S(1)}, bf16[512,768]{1,0:T(8,128)(2,1)S(1)}, u32[]{:S(2)}, u32[]{:S(2)}) collective-permute-start(bf16[512,768]{1,0:T(8,128)(2,1)S(1)} %residual.1.residual_ref.refs_2_.refs_0_.refs_6_), channel_id=1, source_target_pairs={{0,4},{1,5},{2,6},{3,7},{4,0},{5,1},{6,2},{7,3},{8,12},{9,13},{10,... | collective-permute-start | bytes 2359304 | tf_op jit(solution)/shard_map/ppermute | solution.py:52
  6.4 20.4 %collective-permute-start.7 = (bf16[512,768]{1,0:T(8,128)(2,1)S(1)}, bf16[512,768]{1,0:T(8,128)(2,1)S(1)}, u32[]{:S(2)}, u32[]{:S(2)}) collective-permute-start(bf16[512,768]{1,0:T(8,128)(2,1)S(1)} %residual.1.residual_ref.refs_2_.refs_0_.refs_6_), channel_id=1, source_target_pairs={{0,2},{1,3},{2,0},{3,1},{4,6},{5,7},{6,4},{7,5},{8,10},{9,11},{10,... | collective-permute-start | bytes 2359304 | tf_op jit(solution)/shard_map/ppermute | solution.py:52
  13.0 1.7 %collective-permute-start.1 = (bf16[4,160,256]{2,1,0:T(8,128)(2,1)S(1)}, bf16[4,160,256]{2,1,0:T(8,128)(2,1)S(1)}, u32[]{:S(2)}, u32[]{:S(2)}) collective-permute-start(bf16[4,160,256]{2,1,0:T(8,128)(2,1)S(1)} %get-tuple-element.29), channel_id=1, source_target_pairs={{0,1},{1,0},{2,3},{3,2},{4,5},{5,4},{6,7},{7,6},{8,9},{9,8},{10,11... | collective-permute-start | bytes 983048 | tf_op jit(solution)/shard_map/ppermute | solution.py:52
  14.8 14.1 %collective-permute-start.2 = (bf16[192,256]{1,0:T(8,128)(2,1)S(1)}, bf16[192,256]{1,0:T(8,128)(2,1)S(1)}, u32[]{:S(2)}, u32[]{:S(2)}) collective-permute-start(bf16[192,256]{1,0:T(8,128)(2,1)S(1)} %get-tuple-element.31), channel_id=1, source_target_pairs={{0,2},{1,3},{2,0},{3,1},{4,6},{5,7},{6,4},{7,5},{8,10},{9,11},{10,... | collective-permute-start | bytes 294920 | tf_op jit(solution)/shard_map/ppermute | solution.py:52
  15.5 13.3 %collective-permute-start.3 = (bf16[192,256]{1,0:T(8,128)(2,1)S(1)}, bf16[192,256]{1,0:T(8,128)(2,1)S(1)}, u32[]{:S(2)}, u32[]{:S(2)}) collective-permute-start(bf16[192,256]{1,0:T(8,128)(2,1)S(1)} %get-tuple-element.32), channel_id=1, source_target_pairs={{0,4},{1,5},{2,6},{3,7},{4,0},{5,1},{6,2},{7,3},{8,12},{9,13},{10,... | collective-permute-start | bytes 294920 | tf_op jit(solution)/shard_map/ppermute | solution.py:52
  17.1 13.4 %collective-permute-start.4 = (bf16[192,256]{1,0:T(8,128)(2,1)S(1)}, bf16[192,256]{1,0:T(8,128)(2,1)S(1)}, u32[]{:S(2)}, u32[]{:S(2)}) collective-permute-start(bf16[192,256]{1,0:T(8,128)(2,1)S(1)} %get-tuple-element.33), channel_id=1, source_target_pairs={{0,6},{1,7},{2,4},{3,5},{4,2},{5,3},{6,0},{7,1},{8,14},{9,15},{10,... | collective-permute-start | bytes 294920 | tf_op jit(solution)/shard_map/ppermute | solution.py:52
  24.8 13.8 %collective-permute-start.12 = (bf16[256,768]{1,0:T(8,128)(2,1)S(1)}, bf16[256,768]{1,0:T(8,128)(2,1)S(1)}, u32[]{:S(2)}, u32[]{:S(2)}) collective-permute-start(bf16[256,768]{1,0:T(8,128)(2,1)S(1)} %slice.9), channel_id=1, source_target_pairs={{0,2},{1,3},{2,0},{3,1},{4,6},{5,7},{6,4},{7,5},{8,10},{9,11},{10,... | collective-permute-start | bytes 1179656 | tf_op jit(solution)/shard_map/ppermute | solution.py:52
  26.8 14.2 %collective-permute-start.11 = (bf16[256,768]{1,0:T(8,128)(2,1)S(1)}, bf16[256,768]{1,0:T(8,128)(2,1)S(1)}, u32[]{:S(2)}, u32[]{:S(2)}) collective-permute-start(bf16[256,768]{1,0:T(8,128)(2,1)S(1)} %slice.8), channel_id=1, source_target_pairs={{0,4},{1,5},{2,6},{3,7},{4,0},{5,1},{6,2},{7,3},{8,12},{9,13},{10,... | collective-permute-start | bytes 1179656 | tf_op jit(solution)/shard_map/ppermute | solution.py:52
  30.5 11.0 %collective-permute-start.8 = (bf16[512,768]{1,0:T(8,128)(2,1)S(1)}, bf16[512,768]{1,0:T(8,128)(2,1)S(1)}, u32[]{:S(2)}, u32[]{:S(2)}) collective-permute-start(bf16[512,768]{1,0:T(8,128)(2,1)S(1)} %collective-permute-done.7.refs_4_.refs_2_.refs_8_), channel_id=1, source_target_pairs={{0,1},{1,0},{2,3},{3,2},{4,5},{5,4},{6,7},{7,6},{8,9},{9,8},{10,11... | collective-permute-start | bytes 2359304 | tf_op jit(solution)/shard_map/ppermute | solution.py:52
  30.6 11.0 %collective-permute-start.10 = (bf16[512,768]{1,0:T(8,128)(2,1)S(1)}, bf16[512,768]{1,0:T(8,128)(2,1)S(1)}, u32[]{:S(2)}, u32[]{:S(2)}) collective-permute-start(bf16[512,768]{1,0:T(8,128)(2,1)S(1)} %collective-permute-done.9.refs_6_.refs_4_.refs_10_), channel_id=1, source_target_pairs={{0,1},{1,0},{2,3},{3,2},{4,5},{5,4},{6,7},{7,6},{8,9},{9,8},{10,11... | collective-permute-start | bytes 2359304 | tf_op jit(solution)/shard_map/ppermute | solution.py:52
  31.1 4.4 %collective-permute-start.5 = (bf16[128,256]{1,0:T(8,128)(2,1)S(1)}, bf16[128,256]{1,0:T(8,128)(2,1)S(1)}, u32[]{:S(2)}, u32[]{:S(2)}) collective-permute-start(bf16[128,256]{1,0:T(8,128)(2,1)S(1)} %get-tuple-element.35.first_ref), channel_id=1, source_target_pairs={{0,8},{8,0},{16,24},{24,16},{1,9},{9,1},{17,25},{25,17},{2,10},{10... | collective-permute-start | bytes 196616 | tf_op jit(solution)/shard_map/ppermute | solution.py:52
  35.5 5.6 %collective-permute-start.6 = (bf16[128,256]{1,0:T(8,128)(2,1)S(1)}, bf16[128,256]{1,0:T(8,128)(2,1)S(1)}, u32[]{:S(2)}, u32[]{:S(2)}) collective-permute-start(bf16[128,256]{1,0:T(8,128)(2,1)S(1)} %merge_groups.1.refs_0_), channel_id=1, source_target_pairs={{0,16},{8,24},{16,0},{24,8},{1,17},{9,25},{17,1},{25,9},{2,18},{10... | collective-permute-start | bytes 196616 | tf_op jit(solution)/shard_map/ppermute | solution.py:52
  41.1 2.6 %collective-permute-start.13 = (bf16[256,768]{1,0:T(8,128)(2,1)S(1)}, bf16[256,768]{1,0:T(8,128)(2,1)S(1)}, u32[]{:S(2)}, u32[]{:S(2)}) collective-permute-start(bf16[256,768]{1,0:T(8,128)(2,1)S(1)} %collective-permute-done.11.refs_0_.refs_6_.refs_12_), channel_id=1, source_target_pairs={{0,1},{1,0},{2,3},{3,2},{4,5},{5,4},{6,7},{7,6},{8,9},{9,8},{10,11... | collective-permute-start | bytes 1179656 | tf_op jit(solution)/shard_map/ppermute | solution.py:52
  41.1 2.6 %collective-permute-start.14 = (bf16[256,768]{1,0:T(8,128)(2,1)S(1)}, bf16[256,768]{1,0:T(8,128)(2,1)S(1)}, u32[]{:S(2)}, u32[]{:S(2)}) collective-permute-start(bf16[256,768]{1,0:T(8,128)(2,1)S(1)} %collective-permute-done.12.refs_1_.refs_7_.refs_13_), channel_id=1, source_target_pairs={{0,1},{1,0},{2,3},{3,2},{4,5},{5,4},{6,7},{7,6},{8,9},{9,8},{10,11... | collective-permute-start | bytes 1179656 | tf_op jit(solution)/shard_map/ppermute | solution.py:52
  44.5 5.8 %collective-permute-start.15 = (bf16[96,768]{1,0:T(8,128)(2,1)S(1)}, bf16[96,768]{1,0:T(8,128)(2,1)S(1)}, u32[]{:S(2)}, u32[]{:S(2)}) collective-permute-start(bf16[96,768]{1,0:T(8,128)(2,1)S(1)} %cross_far.1), channel_id=1, source_target_pairs={{0,8},{8,0},{16,24},{24,16},{1,9},{9,1},{17,25},{25,17},{2,10},{10... | collective-permute-start | bytes 442376 | tf_op jit(solution)/shard_map/ppermute | solution.py:52
  50.3 9.8 %collective-permute-start.16 = (bf16[96,768]{1,0:T(8,128)(2,1)S(1)}, bf16[96,768]{1,0:T(8,128)(2,1)S(1)}, u32[]{:S(2)}, u32[]{:S(2)}) collective-permute-start(bf16[96,768]{1,0:T(8,128)(2,1)S(1)} %add_convert_fusion.3), channel_id=1, source_target_pairs={{0,16},{8,24},{16,0},{24,8},{1,17},{9,25},{17,1},{25,9},{2,18},{10... | collective-permute-start | bytes 442376 | tf_op jit(solution)/shard_map/ppermute | solution.py:52
  60.1 7.1 %collective-permute-start.22 = (bf16[96,768]{1,0:T(8,128)(2,1)S(1)}, bf16[96,768]{1,0:T(8,128)(2,1)S(1)}, u32[]{:S(2)}, u32[]{:S(2)}) collective-permute-start(bf16[96,768]{1,0:T(8,128)(2,1)S(1)} %add_convert_fusion.2.refs_0_), channel_id=1, source_target_pairs={{0,6},{1,7},{2,4},{3,5},{4,2},{5,3},{6,0},{7,1},{8,14},{9,15},{10,... | collective-permute-start | bytes 442376 | tf_op jit(solution)/shard_map/ppermute | solution.py:52
  62.6 6.5 %collective-permute-start.20 = (bf16[96,768]{1,0:T(8,128)(2,1)S(1)}, bf16[96,768]{1,0:T(8,128)(2,1)S(1)}, u32[]{:S(2)}, u32[]{:S(2)}) collective-permute-start(bf16[96,768]{1,0:T(8,128)(2,1)S(1)} %add_convert_fusion.2.refs_0_), channel_id=1, source_target_pairs={{0,4},{1,5},{2,6},{3,7},{4,0},{5,1},{6,2},{7,3},{8,12},{9,13},{10,... | collective-permute-start | bytes 442376 | tf_op jit(solution)/shard_map/ppermute | solution.py:52
  63.2 6.0 %collective-permute-start.18 = (bf16[96,768]{1,0:T(8,128)(2,1)S(1)}, bf16[96,768]{1,0:T(8,128)(2,1)S(1)}, u32[]{:S(2)}, u32[]{:S(2)}) collective-permute-start(bf16[96,768]{1,0:T(8,128)(2,1)S(1)} %add_convert_fusion.2.refs_0_), channel_id=1, source_target_pairs={{0,2},{1,3},{2,0},{3,1},{4,6},{5,7},{6,4},{7,5},{8,10},{9,11},{10,... | collective-permute-start | bytes 442376 | tf_op jit(solution)/shard_map/ppermute | solution.py:52
  63.7 6.0 %collective-permute-start.17 = (bf16[96,768]{1,0:T(8,128)(2,1)S(1)}, bf16[96,768]{1,0:T(8,128)(2,1)S(1)}, u32[]{:S(2)}, u32[]{:S(2)}) collective-permute-start(bf16[96,768]{1,0:T(8,128)(2,1)S(1)} %add_convert_fusion.2.refs_0_), channel_id=1, source_target_pairs={{0,1},{1,0},{2,3},{3,2},{4,5},{5,4},{6,7},{7,6},{8,9},{9,8},{10,11... | collective-permute-start | bytes 442376 | tf_op jit(solution)/shard_map/ppermute | solution.py:52
  67.3 2.4 %collective-permute-start.23 = (bf16[96,768]{1,0:T(8,128)(2,1)S(1)}, bf16[96,768]{1,0:T(8,128)(2,1)S(1)}, u32[]{:S(2)}, u32[]{:S(2)}) collective-permute-start(bf16[96,768]{1,0:T(8,128)(2,1)S(1)} %collective-permute-done.22.refs_6_), channel_id=1, source_target_pairs={{0,1},{1,0},{2,3},{3,2},{4,5},{5,4},{6,7},{7,6},{8,9},{9,8},{10,11... | collective-permute-start | bytes 442376 | tf_op jit(solution)/shard_map/ppermute | solution.py:52
  76.2 6.9 %collective-permute-start.26 = (bf16[96,256]{1,0:T(8,128)(2,1)S(1)}, bf16[96,256]{1,0:T(8,128)(2,1)S(1)}, u32[]{:S(2)}, u32[]{:S(2)}) collective-permute-start(bf16[96,256]{1,0:T(8,128)(2,1)S(1)} %next_sums.1.refs_1_), channel_id=1, source_target_pairs={{0,24},{8,16},{16,8},{24,0},{1,25},{9,17},{17,9},{25,1},{2,26},{10... | collective-permute-start | bytes 147464 | tf_op jit(solution)/shard_map/ppermute | solution.py:52
  80.6 5.0 %collective-permute-start.25 = (bf16[96,256]{1,0:T(8,128)(2,1)S(1)}, bf16[96,256]{1,0:T(8,128)(2,1)S(1)}, u32[]{:S(2)}, u32[]{:S(2)}) collective-permute-start(bf16[96,256]{1,0:T(8,128)(2,1)S(1)} %next_sums.1.refs_1_), channel_id=1, source_target_pairs={{0,16},{8,24},{16,0},{24,8},{1,17},{9,25},{17,1},{25,9},{2,18},{10... | collective-permute-start | bytes 147464 | tf_op jit(solution)/shard_map/ppermute | solution.py:52
  80.6 5.1 %collective-permute-start.24 = (bf16[96,256]{1,0:T(8,128)(2,1)S(1)}, bf16[96,256]{1,0:T(8,128)(2,1)S(1)}, u32[]{:S(2)}, u32[]{:S(2)}) collective-permute-start(bf16[96,256]{1,0:T(8,128)(2,1)S(1)} %next_sums.1.refs_1_), channel_id=1, source_target_pairs={{0,8},{8,0},{16,24},{24,16},{1,9},{9,1},{17,25},{25,17},{2,10},{10... | collective-permute-start | bytes 147464 | tf_op jit(solution)/shard_map/ppermute | solution.py:52
  87.9 5.2 %collective-permute-start.27 = (bf16[96,768]{1,0:T(8,128)(2,1)S(1)}, bf16[96,768]{1,0:T(8,128)(2,1)S(1)}, u32[]{:S(2)}, u32[]{:S(2)}) collective-permute-start(bf16[96,768]{1,0:T(8,128)(2,1)S(1)} %get-tuple-element.49), channel_id=1, source_target_pairs={{0,8},{8,0},{16,24},{24,16},{1,9},{9,1},{17,25},{25,17},{2,10},{10... | collective-permute-start | bytes 442376 | tf_op jit(solution)/shard_map/ppermute | solution.py:52
  93.2 7.7 %collective-permute-start.28 = (bf16[96,768]{1,0:T(8,128)(2,1)S(1)}, bf16[96,768]{1,0:T(8,128)(2,1)S(1)}, u32[]{:S(2)}, u32[]{:S(2)}) collective-permute-start(bf16[96,768]{1,0:T(8,128)(2,1)S(1)} %add_convert_fusion.1), channel_id=1, source_target_pairs={{0,16},{8,24},{16,0},{24,8},{1,17},{9,25},{17,1},{25,9},{2,18},{10... | collective-permute-start | bytes 442376 | tf_op jit(solution)/shard_map/ppermute | solution.py:52
  100.9 6.2 %collective-permute-start.34 = (bf16[96,768]{1,0:T(8,128)(2,1)S(1)}, bf16[96,768]{1,0:T(8,128)(2,1)S(1)}, u32[]{:S(2)}, u32[]{:S(2)}) collective-permute-start(bf16[96,768]{1,0:T(8,128)(2,1)S(1)} %add_convert_fusion.refs_0_), channel_id=1, source_target_pairs={{0,6},{1,7},{2,4},{3,5},{4,2},{5,3},{6,0},{7,1},{8,14},{9,15},{10,... | collective-permute-start | bytes 442376 | tf_op jit(solution)/shard_map/ppermute | solution.py:52
  102.7 5.9 %collective-permute-start.32 = (bf16[96,768]{1,0:T(8,128)(2,1)S(1)}, bf16[96,768]{1,0:T(8,128)(2,1)S(1)}, u32[]{:S(2)}, u32[]{:S(2)}) collective-permute-start(bf16[96,768]{1,0:T(8,128)(2,1)S(1)} %add_convert_fusion.refs_0_), channel_id=1, source_target_pairs={{0,4},{1,5},{2,6},{3,7},{4,0},{5,1},{6,2},{7,3},{8,12},{9,13},{10,... | collective-permute-start | bytes 442376 | tf_op jit(solution)/shard_map/ppermute | solution.py:52
  103.9 5.1 %collective-permute-start.30 = (bf16[96,768]{1,0:T(8,128)(2,1)S(1)}, bf16[96,768]{1,0:T(8,128)(2,1)S(1)}, u32[]{:S(2)}, u32[]{:S(2)}) collective-permute-start(bf16[96,768]{1,0:T(8,128)(2,1)S(1)} %add_convert_fusion.refs_0_), channel_id=1, source_target_pairs={{0,2},{1,3},{2,0},{3,1},{4,6},{5,7},{6,4},{7,5},{8,10},{9,11},{10,... | collective-permute-start | bytes 442376 | tf_op jit(solution)/shard_map/ppermute | solution.py:52
  104.4 4.7 %collective-permute-start.29 = (bf16[96,768]{1,0:T(8,128)(2,1)S(1)}, bf16[96,768]{1,0:T(8,128)(2,1)S(1)}, u32[]{:S(2)}, u32[]{:S(2)}) collective-permute-start(bf16[96,768]{1,0:T(8,128)(2,1)S(1)} %add_convert_fusion.refs_0_), channel_id=1, source_target_pairs={{0,1},{1,0},{2,3},{3,2},{4,5},{5,4},{6,7},{7,6},{8,9},{9,8},{10,11... | collective-permute-start | bytes 442376 | tf_op jit(solution)/shard_map/ppermute | solution.py:52
  107.1 2.0 %collective-permute-start.35 = (bf16[96,768]{1,0:T(8,128)(2,1)S(1)}, bf16[96,768]{1,0:T(8,128)(2,1)S(1)}, u32[]{:S(2)}, u32[]{:S(2)}) collective-permute-start(bf16[96,768]{1,0:T(8,128)(2,1)S(1)} %collective-permute-done.34.refs_6_), channel_id=1, source_target_pairs={{0,1},{1,0},{2,3},{3,2},{4,5},{5,4},{6,7},{7,6},{8,9},{9,8},{10,11... | collective-permute-start | bytes 442376 | tf_op jit(solution)/shard_map/ppermute | solution.py:52
  (9 other events, 15.7 us)

commit v6 on v5

--- a/solution.py
+++ b/solution.py
@@ -16,6 +16,7 @@
 LANES = 256
 PACK = LANES // HI
 MARKS = 8
+SPAN = 2
 EPSILON = 1e-06
 MIB = 1024 * 1024
 BAND = 256
@@ -52,23 +53,34 @@
     return lax.ppermute(x, axis, [(i, i ^ bits) for i in range(size)])
 
 
-def pick_kernel(lists, ids_ref, table_ref):
+def levels_kernel(out_ref):
+    out_ref[...] = lax.broadcasted_iota(jnp.int32, out_ref.shape, 0)
+
+
+def pick_kernel(lists, ids_ref, levels_ref, table_ref):
     local = lax.rem(ids_ref[...], lists)
-    level = lax.broadcasted_iota(jnp.int32, table_ref.shape, 0)
-    table_ref[...] = jnp.where(level == local, 1.0, 0.0).astype(BF16)
+    table_ref[...] = jnp.where(levels_ref[...] == local, 1.0, 0.0).astype(BF16)
 
 
 def pick_call(ids, lists):
     rows = ids.shape[0]
-    return pl.pallas_call(
-        functools.partial(pick_kernel, lists),
-        out_shape=jax.ShapeDtypeStruct((lists, rows), BF16),
-        in_specs=[vmem_spec()],
+    levels = pl.pallas_call(
+        levels_kernel,
+        out_shape=jax.ShapeDtypeStruct((lists, rows), jnp.int32),
         out_specs=vmem_spec(),
         compiler_params=params(),
         cost_estimate=cost(10),
+        name="levels",
+    )()
+    return pl.pallas_call(
+        functools.partial(pick_kernel, lists),
+        out_shape=jax.ShapeDtypeStruct((lists, rows), BF16),
+        in_specs=[vmem_spec()] * 2,
+        out_specs=vmem_spec(),
+        compiler_params=params(),
+        cost_estimate=cost(0),
         name="pick",
-    )(ids.reshape(1, rows))
+    )(ids.reshape(1, rows), levels)
 
 
 def residual_kernel(vectors_ref, centroids_ref, table_ref, out_ref):
@@ -306,7 +318,8 @@
 
 
 def spans_of(held):
-    return [(k, k ^ 1) for k in held if k % 2 == 0]
+    peers = [k for even in held if even % 2 == 0 for k in (even, even ^ 1)]
+    return [tuple(peers[i : i + SPAN]) for i in range(0, len(peers), SPAN)]
 
 
 def span_codes(codes_ref, span):
@@ -480,7 +493,7 @@
     lanes = LANES * len(packs_of(owned))
     width = pieces[0].shape[1]
     spans = spans_of(held)
-    each = size // len(spans) * rows
+    each = len(spans[0]) * rows
     turned = jax.ShapeDtypeStruct((len(spans), width, each), BF16)
     tables = (
         jax.ShapeDtypeStruct((len(spans), each, lanes), BF16),
@@ -586,10 +599,9 @@
         whole[pl.ds(at, height), :] = ref[...].astype(whole.dtype)
     x = first_step(whole[...].astype(BF16))
     xb = jnp.concatenate([band.astype(BF16) for band in x], axis=0)
-    for i in range(0, residual_ref.shape[0], BAND):
-        once = mm(residual_ref[i : i + BAND, :], xb, NT)
-        less = mm(mm(once.astype(BF16), xb).astype(BF16), xb, NT)
-        out_ref[i : i + BAND, :] = (1.5 * once - 0.5 * less).astype(BF16)
+    once = mm(residual_ref[...], xb, NT)
+    less = mm(mm(once.astype(BF16), xb).astype(BF16), xb, NT)
+    out_ref[...] = (1.5 * once - 0.5 * less).astype(BF16)
 
 
 def final_call(place, residual, blocks):

time: 116 us -> 115 us (level)
  transfers between devices with their start and end apart: 36 -> 36, of which waited for: 22 -> 23; matrix products, arithmetic and copies ran while one was open for 1% -> 1% of each run, Pallas kernels for 8% -> 8%
where the time goes in v6:
time: 115 us
  waiting for transfers between devices  47.5 us (41%)
  starting transfers between devices  38.5 us (33%)
  Pallas kernels  24.2 us (21%)
  local copies, waits for them, and re-layouts  4.06 us (4%)
    ppermute x36, waiting for transfers between devices, swap(): return lax.ppermute(x, axis, [(i, i ^ bits) for i in range(size)])  47.5 us
    ppermute x36, starting transfers between devices, swap(): return lax.ppermute(x, axis, [(i, i ^ bits) for i in range(size)])  38.5 us
    pallas_call x1, Pallas kernels, next_sums_call(): pl.pallas_call(functools.partial(next_sums_kernel, held, bool(ready)), ou...  5.41 us
    pallas_call x1, Pallas kernels, final_call(): pl.pallas_call(functools.partial(final_kernel, len(blocks)), out_shape=ja...  5.33 us
    pallas_call x1, Pallas kernels, local_sums_call(): pl.pallas_call(functools.partial(local_sums_kernel, size), out_shape=(sha...  3.44 us
    unnamed x10, local copies, waits for them, and re-layouts  2.86 us
  transfers between devices with their start and end apart: 36, of which 23 were waited for; matrix products, arithmetic and copies ran while one was open for 1% of the time, Pallas kernels for 8%

profile of v6, /device:TPU:0, one launch (start us, length us, event | category | flops | bytes accessed | tf_op | source)
XLA Modules:
  0.0 115.2 jit_solution(6800409335915668956)
XLA Ops:
  3.2 2.6 %collective-permute-start.9 = (bf16[512,768]{1,0:T(8,128)(2,1)S(1)}, bf16[512,768]{1,0:T(8,128)(2,1)S(1)}, u32[]{:S(2)}, u32[]{:S(2)}) collective-permute-start(bf16[512,768]{1,0:T(8,128)(2,1)S(1)} %residual.1.residual_ref.refs_2_.refs_0_.refs_6_), channel_id=1, source_target_pairs={{0,4},{1,5},{2,6},{3,7},{4,0},{5,1},{6,2},{7,3},{8,12},{9,13},{10,... | collective-permute-start | bytes 2359304 | tf_op jit(solution)/shard_map/ppermute | solution.py:53
  7.3 1.7 %copy-done = f32[768,768]{1,0:T(8,128)S(1)} copy-done((f32[768,768]{1,0:T(8,128)S(1)}, f32[768,768]{1,0:T(8,128)}, u32[]{:S(2)}) %copy-start) | copy-done | bytes 2359320
  9.0 3.4 %local_sums.1 = (bf16[4,160,256]{2,1,0:T(8,128)(2,1)S(1)}, bf16[4,160,256]{2,1,0:T(8,128)(2,1)S(1)}) custom-call(s32[1]{0:T(128)} %bitcast.place_ref, f32[768,768]{1,0:T(8,128)S(1)} %copy-done, s32[96,512]{1,0:T(8,128)S(1)} %bitcast.6, bf16[512,768]{1,0:T(8,128)(2,1)S(1)} %residual.1.residual_ref.refs_2_.refs_0_.refs_6_), custom_call_target="tpu_custom_call" | custom-call | tf_op jit(solution)/shard_map/local_sums/pallas_call | solution.py:237
  12.5 1.6 %collective-permute-done.1.came_ref = bf16[4,160,256]{2,1,0:T(8,128)(2,1)S(1)} collective-permute-done((bf16[4,160,256]{2,1,0:T(8,128)(2,1)S(1)}, bf16[4,160,256]{2,1,0:T(8,128)(2,1)S(1)}, u32[]{:S(2)}, u32[]{:S(2)}) %collective-permute-start.1) | collective-permute-done | bytes 327712 | tf_op jit(solution)/shard_map/ppermute | solution.py:53
  17.8 6.4 %collective-permute-done.9.refs_6_.refs_4_.refs_10_ = bf16[512,768]{1,0:T(8,128)(2,1)S(1)} collective-permute-done((bf16[512,768]{1,0:T(8,128)(2,1)S(1)}, bf16[512,768]{1,0:T(8,128)(2,1)S(1)}, u32[]{:S(2)}, u32[]{:S(2)}) %collective-permute-start.9) | collective-permute-done | bytes 786464 | tf_op jit(solution)/shard_map/ppermute | solution.py:53
  24.2 2.0 %collective-permute-start.12 = (bf16[256,768]{1,0:T(8,128)(2,1)S(1)}, bf16[256,768]{1,0:T(8,128)(2,1)S(1)}, u32[]{:S(2)}, u32[]{:S(2)}) collective-permute-start(bf16[256,768]{1,0:T(8,128)(2,1)S(1)} %slice.9), channel_id=1, source_target_pairs={{0,2},{1,3},{2,0},{3,1},{4,6},{5,7},{6,4},{7,5},{8,10},{9,11},{10,... | collective-permute-start | bytes 1179656 | tf_op jit(solution)/shard_map/ppermute | solution.py:53
  28.3 1.6 %collective-permute-done.4.refs_3_ = bf16[192,256]{1,0:T(8,128)(2,1)S(1)} collective-permute-done((bf16[192,256]{1,0:T(8,128)(2,1)S(1)}, bf16[192,256]{1,0:T(8,128)(2,1)S(1)}, u32[]{:S(2)}, u32[]{:S(2)}) %collective-permute-start.4) | collective-permute-done | bytes 98336 | tf_op jit(solution)/shard_map/ppermute | solution.py:53
  30.5 2.0 %collective-permute-start.5 = (bf16[128,256]{1,0:T(8,128)(2,1)S(1)}, bf16[128,256]{1,0:T(8,128)(2,1)S(1)}, u32[]{:S(2)}, u32[]{:S(2)}) collective-permute-start(bf16[128,256]{1,0:T(8,128)(2,1)S(1)} %get-tuple-element.35.first_ref), channel_id=1, source_target_pairs={{0,8},{8,0},{16,24},{24,16},{1,9},{9,1},{17,25},{25,17},{2,10},{10... | collective-permute-start | bytes 196616 | tf_op jit(solution)/shard_map/ppermute | solution.py:53
  32.6 2.3 %collective-permute-done.5.second_ref = bf16[128,256]{1,0:T(8,128)(2,1)S(1)} collective-permute-done((bf16[128,256]{1,0:T(8,128)(2,1)S(1)}, bf16[128,256]{1,0:T(8,128)(2,1)S(1)}, u32[]{:S(2)}, u32[]{:S(2)}) %collective-permute-start.5) | collective-permute-done | bytes 65568 | tf_op jit(solution)/shard_map/ppermute | solution.py:53
  34.9 3.0 %collective-permute-start.6 = (bf16[128,256]{1,0:T(8,128)(2,1)S(1)}, bf16[128,256]{1,0:T(8,128)(2,1)S(1)}, u32[]{:S(2)}, u32[]{:S(2)}) collective-permute-start(bf16[128,256]{1,0:T(8,128)(2,1)S(1)} %merge_groups.1.refs_0_), channel_id=1, source_target_pairs={{0,16},{8,24},{16,0},{24,8},{1,17},{9,25},{17,1},{25,9},{2,18},{10... | collective-permute-start | bytes 196616 | tf_op jit(solution)/shard_map/ppermute | solution.py:53
  38.1 2.4 %collective-permute-done.6.refs_1_ = bf16[128,256]{1,0:T(8,128)(2,1)S(1)} collective-permute-done((bf16[128,256]{1,0:T(8,128)(2,1)S(1)}, bf16[128,256]{1,0:T(8,128)(2,1)S(1)}, u32[]{:S(2)}, u32[]{:S(2)}) %collective-permute-start.6) | collective-permute-done | bytes 65568 | tf_op jit(solution)/shard_map/ppermute | solution.py:53
  41.0 2.1 %cross_near.1 = (f32[96,768]{1,0:T(8,128)S(1)}, bf16[3,128,256]{2,1,0:T(8,128)(2,1)S(1)}, f32[24,256]{1,0:T(8,128)S(1)}) custom-call(s32[8,12,512]{2,1,0:T(8,128)S(1)} %get-tuple-element.42.codes_ref, bf16[128,256]{1,0:T(8,128)(2,1)S(1)} %merge_groups.1.refs_0_, bf16[128,256]{1,0:T(8,128)(2,1)S(1)} %collective-permute-done.6.refs_1_, ...), custom_call_target="tpu_custom_call" | custom-call | tf_op jit(solution)/shard_map/cross_near/pallas_call | solution.py:407
  43.9 1.7 %collective-permute-start.15 = (bf16[96,768]{1,0:T(8,128)(2,1)S(1)}, bf16[96,768]{1,0:T(8,128)(2,1)S(1)}, u32[]{:S(2)}, u32[]{:S(2)}) collective-permute-start(bf16[96,768]{1,0:T(8,128)(2,1)S(1)} %cross_far.1), channel_id=1, source_target_pairs={{0,8},{8,0},{16,24},{24,16},{1,9},{9,1},{17,25},{25,17},{2,10},{10... | collective-permute-start | bytes 442376 | tf_op jit(solution)/shard_map/ppermute | solution.py:53
  45.6 1.8 %turn_rows.1.refs_8_ = bf16[4,768,1024]{2,1,0:T(8,128)(2,1)S(1)} custom-call(bf16[512,768]{1,0:T(8,128)(2,1)S(1)} %residual.1.residual_ref.refs_2_.refs_0_.refs_6_, bf16[512,768]{1,0:T(8,128)(2,1)S(1)} %collective-permute-done.refs_3_.refs_1_.refs_7_, bf16[512,768]{1,0:T(8,128)(2,1)S(1)} %collective-permute-done.7.refs_4_.refs_2_.refs_8_, ...), custom_call_target="tpu_custom_call" | custom-call | tf_op jit(solution)/shard_map/turn_rows/pallas_call | solution.py:504
  47.4 2.3 %collective-permute-done.15 = bf16[96,768]{1,0:T(8,128)(2,1)S(1)} collective-permute-done((bf16[96,768]{1,0:T(8,128)(2,1)S(1)}, bf16[96,768]{1,0:T(8,128)(2,1)S(1)}, u32[]{:S(2)}, u32[]{:S(2)}) %collective-permute-start.15) | collective-permute-done | bytes 147488 | tf_op jit(solution)/shard_map/ppermute | solution.py:53
  49.7 3.1 %collective-permute-start.16 = (bf16[96,768]{1,0:T(8,128)(2,1)S(1)}, bf16[96,768]{1,0:T(8,128)(2,1)S(1)}, u32[]{:S(2)}, u32[]{:S(2)}) collective-permute-start(bf16[96,768]{1,0:T(8,128)(2,1)S(1)} %add_convert_fusion.3), channel_id=1, source_target_pairs={{0,16},{8,24},{16,0},{24,8},{1,17},{9,25},{17,1},{25,9},{2,18},{10... | collective-permute-start | bytes 442376 | tf_op jit(solution)/shard_map/ppermute | solution.py:53
  52.9 2.1 %tables.1 = (bf16[4,1024,768]{2,1,0:T(8,128)(2,1)S(1)}, bf16[4,768,1024]{2,1,0:T(8,128)(2,1)S(1)}) custom-call(s32[8,12,512]{2,1,0:T(8,128)S(1)} %get-tuple-element.42.codes_ref), custom_call_target="tpu_custom_call" | custom-call | tf_op jit(solution)/shard_map/tables/pallas_call | solution.py:513
  54.9 4.6 %collective-permute-done.16 = bf16[96,768]{1,0:T(8,128)(2,1)S(1)} collective-permute-done((bf16[96,768]{1,0:T(8,128)(2,1)S(1)}, bf16[96,768]{1,0:T(8,128)(2,1)S(1)}, u32[]{:S(2)}, u32[]{:S(2)}) %collective-permute-start.16) | collective-permute-done | bytes 147488 | tf_op jit(solution)/shard_map/ppermute | solution.py:53
  59.6 2.5 %collective-permute-start.22 = (bf16[96,768]{1,0:T(8,128)(2,1)S(1)}, bf16[96,768]{1,0:T(8,128)(2,1)S(1)}, u32[]{:S(2)}, u32[]{:S(2)}) collective-permute-start(bf16[96,768]{1,0:T(8,128)(2,1)S(1)} %add_convert_fusion.2.refs_0_), channel_id=1, source_target_pairs={{0,6},{1,7},{2,4},{3,5},{4,2},{5,3},{6,0},{7,1},{8,14},{9,15},{10,... | collective-permute-start | bytes 442376 | tf_op jit(solution)/shard_map/ppermute | solution.py:53
  63.1 3.6 %collective-permute-done.22.refs_6_ = bf16[96,768]{1,0:T(8,128)(2,1)S(1)} collective-permute-done((bf16[96,768]{1,0:T(8,128)(2,1)S(1)}, bf16[96,768]{1,0:T(8,128)(2,1)S(1)}, u32[]{:S(2)}, u32[]{:S(2)}) %collective-permute-start.22) | collective-permute-done | bytes 147488 | tf_op jit(solution)/shard_map/ppermute | solution.py:53
  66.7 1.9 %collective-permute-done.20.refs_4_ = bf16[96,768]{1,0:T(8,128)(2,1)S(1)} collective-permute-done((bf16[96,768]{1,0:T(8,128)(2,1)S(1)}, bf16[96,768]{1,0:T(8,128)(2,1)S(1)}, u32[]{:S(2)}, u32[]{:S(2)}) %collective-permute-start.20) | collective-permute-done | bytes 147488 | tf_op jit(solution)/shard_map/ppermute | solution.py:53
  70.2 5.4 %next_sums.1.refs_1_ = bf16[96,256]{1,0:T(8,128)(2,1)S(1)} custom-call(s32[8,12,512]{2,1,0:T(8,128)S(1)} %get-tuple-element.42.codes_ref, bf16[96,768]{1,0:T(8,128)(2,1)S(1)} %add_convert_fusion.2.refs_0_, bf16[96,768]{1,0:T(8,128)(2,1)S(1)} %collective-permute-done.17.refs_1_, bf16[96,768]{1,0:T(8,128)(2,1)S(1)} %collective-permute-done.18.refs_2_, ...), custom_call_target="tpu_custom_call" | custom-call | tf_op jit(solution)/shard_map/next_sums/pallas_call | solution.py:583
  75.6 4.4 %collective-permute-start.26 = (bf16[96,256]{1,0:T(8,128)(2,1)S(1)}, bf16[96,256]{1,0:T(8,128)(2,1)S(1)}, u32[]{:S(2)}, u32[]{:S(2)}) collective-permute-start(bf16[96,256]{1,0:T(8,128)(2,1)S(1)} %next_sums.1.refs_1_), channel_id=1, source_target_pairs={{0,24},{8,16},{16,8},{24,0},{1,25},{9,17},{17,9},{25,1},{2,26},{10... | collective-permute-start | bytes 147464 | tf_op jit(solution)/shard_map/ppermute | solution.py:53
  80.6 1.9 %collective-permute-done.26.refs_4_ = bf16[96,256]{1,0:T(8,128)(2,1)S(1)} collective-permute-done((bf16[96,256]{1,0:T(8,128)(2,1)S(1)}, bf16[96,256]{1,0:T(8,128)(2,1)S(1)}, u32[]{:S(2)}, u32[]{:S(2)}) %collective-permute-start.26) | collective-permute-done | bytes 49184 | tf_op jit(solution)/shard_map/ppermute | solution.py:53
  82.5 2.5 %collective-permute-done.25.refs_3_ = bf16[96,256]{1,0:T(8,128)(2,1)S(1)} collective-permute-done((bf16[96,256]{1,0:T(8,128)(2,1)S(1)}, bf16[96,256]{1,0:T(8,128)(2,1)S(1)}, u32[]{:S(2)}, u32[]{:S(2)}) %collective-permute-start.25) | collective-permute-done | bytes 49184 | tf_op jit(solution)/shard_map/ppermute | solution.py:53
  85.1 2.2 %cross.1 = (bf16[96,768]{1,0:T(8,128)(2,1)S(1)}, f32[96,256]{1,0:T(8,128)S(1)}) custom-call(s32[8,12,512]{2,1,0:T(8,128)S(1)} %get-tuple-element.42.codes_ref, bf16[4,768,1024]{2,1,0:T(8,128)(2,1)S(1)} %get-tuple-element.43.refs_0_, bf16[96,256]{1,0:T(8,128)(2,1)S(1)} %next_sums.1.refs_1_, bf16[96,256]{1,0:T(8,128)(2,1)S(1)} %collective-permute-done.24.refs_2_, ...), custom_call_target="tpu_custom_call" | custom-call | tf_op jit(solution)/shard_map/cross/pallas_call | solution.py:460
  89.5 3.0 %collective-permute-done.27 = bf16[96,768]{1,0:T(8,128)(2,1)S(1)} collective-permute-done((bf16[96,768]{1,0:T(8,128)(2,1)S(1)}, bf16[96,768]{1,0:T(8,128)(2,1)S(1)}, u32[]{:S(2)}, u32[]{:S(2)}) %collective-permute-start.27) | collective-permute-done | bytes 147488 | tf_op jit(solution)/shard_map/ppermute | solution.py:53
  92.6 2.0 %collective-permute-start.28 = (bf16[96,768]{1,0:T(8,128)(2,1)S(1)}, bf16[96,768]{1,0:T(8,128)(2,1)S(1)}, u32[]{:S(2)}, u32[]{:S(2)}) collective-permute-start(bf16[96,768]{1,0:T(8,128)(2,1)S(1)} %add_convert_fusion.1), channel_id=1, source_target_pairs={{0,16},{8,24},{16,0},{24,8},{1,17},{9,25},{17,1},{25,9},{2,18},{10... | collective-permute-start | bytes 442376 | tf_op jit(solution)/shard_map/ppermute | solution.py:53
  94.6 5.7 %collective-permute-done.28 = bf16[96,768]{1,0:T(8,128)(2,1)S(1)} collective-permute-done((bf16[96,768]{1,0:T(8,128)(2,1)S(1)}, bf16[96,768]{1,0:T(8,128)(2,1)S(1)}, u32[]{:S(2)}, u32[]{:S(2)}) %collective-permute-start.28) | collective-permute-done | bytes 147488 | tf_op jit(solution)/shard_map/ppermute | solution.py:53
  100.3 1.8 %collective-permute-start.34 = (bf16[96,768]{1,0:T(8,128)(2,1)S(1)}, bf16[96,768]{1,0:T(8,128)(2,1)S(1)}, u32[]{:S(2)}, u32[]{:S(2)}) collective-permute-start(bf16[96,768]{1,0:T(8,128)(2,1)S(1)} %add_convert_fusion.refs_0_), channel_id=1, source_target_pairs={{0,6},{1,7},{2,4},{3,5},{4,2},{5,3},{6,0},{7,1},{8,14},{9,15},{10,... | collective-permute-start | bytes 442376 | tf_op jit(solution)/shard_map/ppermute | solution.py:53
  103.8 2.6 %collective-permute-done.34.refs_6_ = bf16[96,768]{1,0:T(8,128)(2,1)S(1)} collective-permute-done((bf16[96,768]{1,0:T(8,128)(2,1)S(1)}, bf16[96,768]{1,0:T(8,128)(2,1)S(1)}, u32[]{:S(2)}, u32[]{:S(2)}) %collective-permute-start.34) | collective-permute-done | bytes 147488 | tf_op jit(solution)/shard_map/ppermute | solution.py:53
  109.8 5.3 %final.1 = bf16[512,768]{1,0:T(8,128)(2,1)} custom-call(s32[1]{0:T(128)} %bitcast.place_ref, bf16[512,768]{1,0:T(8,128)(2,1)S(1)} %residual.1.residual_ref.refs_2_.refs_0_.refs_6_, bf16[96,768]{1,0:T(8,128)(2,1)S(1)} %add_convert_fusion.refs_0_, bf16[96,768]{1,0:T(8,128)(2,1)S(1)} %collective-permute-done.29.refs_1_, ...), custom_call_target="tpu_custom_call" | custom-call | tf_op jit(solution)/shard_map/final/pallas_call | solution.py:610
  (73 shorter events, 22.7 us)
Async XLA Ops:
  2.7 4.6 %collective-permute-start = (bf16[512,768]{1,0:T(8,128)(2,1)S(1)}, bf16[512,768]{1,0:T(8,128)(2,1)S(1)}, u32[]{:S(2)}, u32[]{:S(2)}) collective-permute-start(bf16[512,768]{1,0:T(8,128)(2,1)S(1)} %residual.1.residual_ref.refs_2_.refs_0_.refs_6_), channel_id=1, source_target_pairs={{0,1},{1,0},{2,3},{3,2},{4,5},{5,4},{6,7},{7,6},{8,9},{9,8},{10,11... | collective-permute-start | bytes 2359304 | tf_op jit(solution)/shard_map/ppermute | solution.py:53
  3.2 21.0 %collective-permute-start.9 = (bf16[512,768]{1,0:T(8,128)(2,1)S(1)}, bf16[512,768]{1,0:T(8,128)(2,1)S(1)}, u32[]{:S(2)}, u32[]{:S(2)}) collective-permute-start(bf16[512,768]{1,0:T(8,128)(2,1)S(1)} %residual.1.residual_ref.refs_2_.refs_0_.refs_6_), channel_id=1, source_target_pairs={{0,4},{1,5},{2,6},{3,7},{4,0},{5,1},{6,2},{7,3},{8,12},{9,13},{10,... | collective-permute-start | bytes 2359304 | tf_op jit(solution)/shard_map/ppermute | solution.py:53
  5.8 20.4 %collective-permute-start.7 = (bf16[512,768]{1,0:T(8,128)(2,1)S(1)}, bf16[512,768]{1,0:T(8,128)(2,1)S(1)}, u32[]{:S(2)}, u32[]{:S(2)}) collective-permute-start(bf16[512,768]{1,0:T(8,128)(2,1)S(1)} %residual.1.residual_ref.refs_2_.refs_0_.refs_6_), channel_id=1, source_target_pairs={{0,2},{1,3},{2,0},{3,1},{4,6},{5,7},{6,4},{7,5},{8,10},{9,11},{10,... | collective-permute-start | bytes 2359304 | tf_op jit(solution)/shard_map/ppermute | solution.py:53
  12.4 1.7 %collective-permute-start.1 = (bf16[4,160,256]{2,1,0:T(8,128)(2,1)S(1)}, bf16[4,160,256]{2,1,0:T(8,128)(2,1)S(1)}, u32[]{:S(2)}, u32[]{:S(2)}) collective-permute-start(bf16[4,160,256]{2,1,0:T(8,128)(2,1)S(1)} %get-tuple-element.29), channel_id=1, source_target_pairs={{0,1},{1,0},{2,3},{3,2},{4,5},{5,4},{6,7},{7,6},{8,9},{9,8},{10,11... | collective-permute-start | bytes 983048 | tf_op jit(solution)/shard_map/ppermute | solution.py:53
  14.2 14.1 %collective-permute-start.2 = (bf16[192,256]{1,0:T(8,128)(2,1)S(1)}, bf16[192,256]{1,0:T(8,128)(2,1)S(1)}, u32[]{:S(2)}, u32[]{:S(2)}) collective-permute-start(bf16[192,256]{1,0:T(8,128)(2,1)S(1)} %get-tuple-element.31), channel_id=1, source_target_pairs={{0,2},{1,3},{2,0},{3,1},{4,6},{5,7},{6,4},{7,5},{8,10},{9,11},{10,... | collective-permute-start | bytes 294920 | tf_op jit(solution)/shard_map/ppermute | solution.py:53
  15.0 13.3 %collective-permute-start.3 = (bf16[192,256]{1,0:T(8,128)(2,1)S(1)}, bf16[192,256]{1,0:T(8,128)(2,1)S(1)}, u32[]{:S(2)}, u32[]{:S(2)}) collective-permute-start(bf16[192,256]{1,0:T(8,128)(2,1)S(1)} %get-tuple-element.32), channel_id=1, source_target_pairs={{0,4},{1,5},{2,6},{3,7},{4,0},{5,1},{6,2},{7,3},{8,12},{9,13},{10,... | collective-permute-start | bytes 294920 | tf_op jit(solution)/shard_map/ppermute | solution.py:53
  16.5 13.4 %collective-permute-start.4 = (bf16[192,256]{1,0:T(8,128)(2,1)S(1)}, bf16[192,256]{1,0:T(8,128)(2,1)S(1)}, u32[]{:S(2)}, u32[]{:S(2)}) collective-permute-start(bf16[192,256]{1,0:T(8,128)(2,1)S(1)} %get-tuple-element.33), channel_id=1, source_target_pairs={{0,6},{1,7},{2,4},{3,5},{4,2},{5,3},{6,0},{7,1},{8,14},{9,15},{10,... | collective-permute-start | bytes 294920 | tf_op jit(solution)/shard_map/ppermute | solution.py:53
  24.2 13.8 %collective-permute-start.12 = (bf16[256,768]{1,0:T(8,128)(2,1)S(1)}, bf16[256,768]{1,0:T(8,128)(2,1)S(1)}, u32[]{:S(2)}, u32[]{:S(2)}) collective-permute-start(bf16[256,768]{1,0:T(8,128)(2,1)S(1)} %slice.9), channel_id=1, source_target_pairs={{0,2},{1,3},{2,0},{3,1},{4,6},{5,7},{6,4},{7,5},{8,10},{9,11},{10,... | collective-permute-start | bytes 1179656 | tf_op jit(solution)/shard_map/ppermute | solution.py:53
  26.2 14.2 %collective-permute-start.11 = (bf16[256,768]{1,0:T(8,128)(2,1)S(1)}, bf16[256,768]{1,0:T(8,128)(2,1)S(1)}, u32[]{:S(2)}, u32[]{:S(2)}) collective-permute-start(bf16[256,768]{1,0:T(8,128)(2,1)S(1)} %slice.8), channel_id=1, source_target_pairs={{0,4},{1,5},{2,6},{3,7},{4,0},{5,1},{6,2},{7,3},{8,12},{9,13},{10,... | collective-permute-start | bytes 1179656 | tf_op jit(solution)/shard_map/ppermute | solution.py:53
  30.0 11.1 %collective-permute-start.8 = (bf16[512,768]{1,0:T(8,128)(2,1)S(1)}, bf16[512,768]{1,0:T(8,128)(2,1)S(1)}, u32[]{:S(2)}, u32[]{:S(2)}) collective-permute-start(bf16[512,768]{1,0:T(8,128)(2,1)S(1)} %collective-permute-done.7.refs_4_.refs_2_.refs_8_), channel_id=1, source_target_pairs={{0,1},{1,0},{2,3},{3,2},{4,5},{5,4},{6,7},{7,6},{8,9},{9,8},{10,11... | collective-permute-start | bytes 2359304 | tf_op jit(solution)/shard_map/ppermute | solution.py:53
  30.0 11.0 %collective-permute-start.10 = (bf16[512,768]{1,0:T(8,128)(2,1)S(1)}, bf16[512,768]{1,0:T(8,128)(2,1)S(1)}, u32[]{:S(2)}, u32[]{:S(2)}) collective-permute-start(bf16[512,768]{1,0:T(8,128)(2,1)S(1)} %collective-permute-done.9.refs_6_.refs_4_.refs_10_), channel_id=1, source_target_pairs={{0,1},{1,0},{2,3},{3,2},{4,5},{5,4},{6,7},{7,6},{8,9},{9,8},{10,11... | collective-permute-start | bytes 2359304 | tf_op jit(solution)/shard_map/ppermute | solution.py:53
  30.5 4.4 %collective-permute-start.5 = (bf16[128,256]{1,0:T(8,128)(2,1)S(1)}, bf16[128,256]{1,0:T(8,128)(2,1)S(1)}, u32[]{:S(2)}, u32[]{:S(2)}) collective-permute-start(bf16[128,256]{1,0:T(8,128)(2,1)S(1)} %get-tuple-element.35.first_ref), channel_id=1, source_target_pairs={{0,8},{8,0},{16,24},{24,16},{1,9},{9,1},{17,25},{25,17},{2,10},{10... | collective-permute-start | bytes 196616 | tf_op jit(solution)/shard_map/ppermute | solution.py:53
  34.9 5.6 %collective-permute-start.6 = (bf16[128,256]{1,0:T(8,128)(2,1)S(1)}, bf16[128,256]{1,0:T(8,128)(2,1)S(1)}, u32[]{:S(2)}, u32[]{:S(2)}) collective-permute-start(bf16[128,256]{1,0:T(8,128)(2,1)S(1)} %merge_groups.1.refs_0_), channel_id=1, source_target_pairs={{0,16},{8,24},{16,0},{24,8},{1,17},{9,25},{17,1},{25,9},{2,18},{10... | collective-permute-start | bytes 196616 | tf_op jit(solution)/shard_map/ppermute | solution.py:53
  40.5 2.6 %collective-permute-start.13 = (bf16[256,768]{1,0:T(8,128)(2,1)S(1)}, bf16[256,768]{1,0:T(8,128)(2,1)S(1)}, u32[]{:S(2)}, u32[]{:S(2)}) collective-permute-start(bf16[256,768]{1,0:T(8,128)(2,1)S(1)} %collective-permute-done.11.refs_0_.refs_6_.refs_12_), channel_id=1, source_target_pairs={{0,1},{1,0},{2,3},{3,2},{4,5},{5,4},{6,7},{7,6},{8,9},{9,8},{10,11... | collective-permute-start | bytes 1179656 | tf_op jit(solution)/shard_map/ppermute | solution.py:53
  40.5 2.6 %collective-permute-start.14 = (bf16[256,768]{1,0:T(8,128)(2,1)S(1)}, bf16[256,768]{1,0:T(8,128)(2,1)S(1)}, u32[]{:S(2)}, u32[]{:S(2)}) collective-permute-start(bf16[256,768]{1,0:T(8,128)(2,1)S(1)} %collective-permute-done.12.refs_1_.refs_7_.refs_13_), channel_id=1, source_target_pairs={{0,1},{1,0},{2,3},{3,2},{4,5},{5,4},{6,7},{7,6},{8,9},{9,8},{10,11... | collective-permute-start | bytes 1179656 | tf_op jit(solution)/shard_map/ppermute | solution.py:53
  43.9 5.8 %collective-permute-start.15 = (bf16[96,768]{1,0:T(8,128)(2,1)S(1)}, bf16[96,768]{1,0:T(8,128)(2,1)S(1)}, u32[]{:S(2)}, u32[]{:S(2)}) collective-permute-start(bf16[96,768]{1,0:T(8,128)(2,1)S(1)} %cross_far.1), channel_id=1, source_target_pairs={{0,8},{8,0},{16,24},{24,16},{1,9},{9,1},{17,25},{25,17},{2,10},{10... | collective-permute-start | bytes 442376 | tf_op jit(solution)/shard_map/ppermute | solution.py:53
  49.7 9.8 %collective-permute-start.16 = (bf16[96,768]{1,0:T(8,128)(2,1)S(1)}, bf16[96,768]{1,0:T(8,128)(2,1)S(1)}, u32[]{:S(2)}, u32[]{:S(2)}) collective-permute-start(bf16[96,768]{1,0:T(8,128)(2,1)S(1)} %add_convert_fusion.3), channel_id=1, source_target_pairs={{0,16},{8,24},{16,0},{24,8},{1,17},{9,25},{17,1},{25,9},{2,18},{10... | collective-permute-start | bytes 442376 | tf_op jit(solution)/shard_map/ppermute | solution.py:53
  59.6 7.1 %collective-permute-start.22 = (bf16[96,768]{1,0:T(8,128)(2,1)S(1)}, bf16[96,768]{1,0:T(8,128)(2,1)S(1)}, u32[]{:S(2)}, u32[]{:S(2)}) collective-permute-start(bf16[96,768]{1,0:T(8,128)(2,1)S(1)} %add_convert_fusion.2.refs_0_), channel_id=1, source_target_pairs={{0,6},{1,7},{2,4},{3,5},{4,2},{5,3},{6,0},{7,1},{8,14},{9,15},{10,... | collective-permute-start | bytes 442376 | tf_op jit(solution)/shard_map/ppermute | solution.py:53
  62.1 6.5 %collective-permute-start.20 = (bf16[96,768]{1,0:T(8,128)(2,1)S(1)}, bf16[96,768]{1,0:T(8,128)(2,1)S(1)}, u32[]{:S(2)}, u32[]{:S(2)}) collective-permute-start(bf16[96,768]{1,0:T(8,128)(2,1)S(1)} %add_convert_fusion.2.refs_0_), channel_id=1, source_target_pairs={{0,4},{1,5},{2,6},{3,7},{4,0},{5,1},{6,2},{7,3},{8,12},{9,13},{10,... | collective-permute-start | bytes 442376 | tf_op jit(solution)/shard_map/ppermute | solution.py:53
  62.6 6.0 %collective-permute-start.18 = (bf16[96,768]{1,0:T(8,128)(2,1)S(1)}, bf16[96,768]{1,0:T(8,128)(2,1)S(1)}, u32[]{:S(2)}, u32[]{:S(2)}) collective-permute-start(bf16[96,768]{1,0:T(8,128)(2,1)S(1)} %add_convert_fusion.2.refs_0_), channel_id=1, source_target_pairs={{0,2},{1,3},{2,0},{3,1},{4,6},{5,7},{6,4},{7,5},{8,10},{9,11},{10,... | collective-permute-start | bytes 442376 | tf_op jit(solution)/shard_map/ppermute | solution.py:53
  63.1 6.0 %collective-permute-start.17 = (bf16[96,768]{1,0:T(8,128)(2,1)S(1)}, bf16[96,768]{1,0:T(8,128)(2,1)S(1)}, u32[]{:S(2)}, u32[]{:S(2)}) collective-permute-start(bf16[96,768]{1,0:T(8,128)(2,1)S(1)} %add_convert_fusion.2.refs_0_), channel_id=1, source_target_pairs={{0,1},{1,0},{2,3},{3,2},{4,5},{5,4},{6,7},{7,6},{8,9},{9,8},{10,11... | collective-permute-start | bytes 442376 | tf_op jit(solution)/shard_map/ppermute | solution.py:53
  66.7 2.4 %collective-permute-start.23 = (bf16[96,768]{1,0:T(8,128)(2,1)S(1)}, bf16[96,768]{1,0:T(8,128)(2,1)S(1)}, u32[]{:S(2)}, u32[]{:S(2)}) collective-permute-start(bf16[96,768]{1,0:T(8,128)(2,1)S(1)} %collective-permute-done.22.refs_6_), channel_id=1, source_target_pairs={{0,1},{1,0},{2,3},{3,2},{4,5},{5,4},{6,7},{7,6},{8,9},{9,8},{10,11... | collective-permute-start | bytes 442376 | tf_op jit(solution)/shard_map/ppermute | solution.py:53
  75.6 6.9 %collective-permute-start.26 = (bf16[96,256]{1,0:T(8,128)(2,1)S(1)}, bf16[96,256]{1,0:T(8,128)(2,1)S(1)}, u32[]{:S(2)}, u32[]{:S(2)}) collective-permute-start(bf16[96,256]{1,0:T(8,128)(2,1)S(1)} %next_sums.1.refs_1_), channel_id=1, source_target_pairs={{0,24},{8,16},{16,8},{24,0},{1,25},{9,17},{17,9},{25,1},{2,26},{10... | collective-permute-start | bytes 147464 | tf_op jit(solution)/shard_map/ppermute | solution.py:53
  80.0 5.0 %collective-permute-start.25 = (bf16[96,256]{1,0:T(8,128)(2,1)S(1)}, bf16[96,256]{1,0:T(8,128)(2,1)S(1)}, u32[]{:S(2)}, u32[]{:S(2)}) collective-permute-start(bf16[96,256]{1,0:T(8,128)(2,1)S(1)} %next_sums.1.refs_1_), channel_id=1, source_target_pairs={{0,16},{8,24},{16,0},{24,8},{1,17},{9,25},{17,1},{25,9},{2,18},{10... | collective-permute-start | bytes 147464 | tf_op jit(solution)/shard_map/ppermute | solution.py:53
  80.0 5.1 %collective-permute-start.24 = (bf16[96,256]{1,0:T(8,128)(2,1)S(1)}, bf16[96,256]{1,0:T(8,128)(2,1)S(1)}, u32[]{:S(2)}, u32[]{:S(2)}) collective-permute-start(bf16[96,256]{1,0:T(8,128)(2,1)S(1)} %next_sums.1.refs_1_), channel_id=1, source_target_pairs={{0,8},{8,0},{16,24},{24,16},{1,9},{9,1},{17,25},{25,17},{2,10},{10... | collective-permute-start | bytes 147464 | tf_op jit(solution)/shard_map/ppermute | solution.py:53
  87.3 5.2 %collective-permute-start.27 = (bf16[96,768]{1,0:T(8,128)(2,1)S(1)}, bf16[96,768]{1,0:T(8,128)(2,1)S(1)}, u32[]{:S(2)}, u32[]{:S(2)}) collective-permute-start(bf16[96,768]{1,0:T(8,128)(2,1)S(1)} %get-tuple-element.49), channel_id=1, source_target_pairs={{0,8},{8,0},{16,24},{24,16},{1,9},{9,1},{17,25},{25,17},{2,10},{10... | collective-permute-start | bytes 442376 | tf_op jit(solution)/shard_map/ppermute | solution.py:53
  92.6 7.7 %collective-permute-start.28 = (bf16[96,768]{1,0:T(8,128)(2,1)S(1)}, bf16[96,768]{1,0:T(8,128)(2,1)S(1)}, u32[]{:S(2)}, u32[]{:S(2)}) collective-permute-start(bf16[96,768]{1,0:T(8,128)(2,1)S(1)} %add_convert_fusion.1), channel_id=1, source_target_pairs={{0,16},{8,24},{16,0},{24,8},{1,17},{9,25},{17,1},{25,9},{2,18},{10... | collective-permute-start | bytes 442376 | tf_op jit(solution)/shard_map/ppermute | solution.py:53
  100.3 6.2 %collective-permute-start.34 = (bf16[96,768]{1,0:T(8,128)(2,1)S(1)}, bf16[96,768]{1,0:T(8,128)(2,1)S(1)}, u32[]{:S(2)}, u32[]{:S(2)}) collective-permute-start(bf16[96,768]{1,0:T(8,128)(2,1)S(1)} %add_convert_fusion.refs_0_), channel_id=1, source_target_pairs={{0,6},{1,7},{2,4},{3,5},{4,2},{5,3},{6,0},{7,1},{8,14},{9,15},{10,... | collective-permute-start | bytes 442376 | tf_op jit(solution)/shard_map/ppermute | solution.py:53
  102.1 5.9 %collective-permute-start.32 = (bf16[96,768]{1,0:T(8,128)(2,1)S(1)}, bf16[96,768]{1,0:T(8,128)(2,1)S(1)}, u32[]{:S(2)}, u32[]{:S(2)}) collective-permute-start(bf16[96,768]{1,0:T(8,128)(2,1)S(1)} %add_convert_fusion.refs_0_), channel_id=1, source_target_pairs={{0,4},{1,5},{2,6},{3,7},{4,0},{5,1},{6,2},{7,3},{8,12},{9,13},{10,... | collective-permute-start | bytes 442376 | tf_op jit(solution)/shard_map/ppermute | solution.py:53
  103.3 5.1 %collective-permute-start.30 = (bf16[96,768]{1,0:T(8,128)(2,1)S(1)}, bf16[96,768]{1,0:T(8,128)(2,1)S(1)}, u32[]{:S(2)}, u32[]{:S(2)}) collective-permute-start(bf16[96,768]{1,0:T(8,128)(2,1)S(1)} %add_convert_fusion.refs_0_), channel_id=1, source_target_pairs={{0,2},{1,3},{2,0},{3,1},{4,6},{5,7},{6,4},{7,5},{8,10},{9,11},{10,... | collective-permute-start | bytes 442376 | tf_op jit(solution)/shard_map/ppermute | solution.py:53
  103.8 4.7 %collective-permute-start.29 = (bf16[96,768]{1,0:T(8,128)(2,1)S(1)}, bf16[96,768]{1,0:T(8,128)(2,1)S(1)}, u32[]{:S(2)}, u32[]{:S(2)}) collective-permute-start(bf16[96,768]{1,0:T(8,128)(2,1)S(1)} %add_convert_fusion.refs_0_), channel_id=1, source_target_pairs={{0,1},{1,0},{2,3},{3,2},{4,5},{5,4},{6,7},{7,6},{8,9},{9,8},{10,11... | collective-permute-start | bytes 442376 | tf_op jit(solution)/shard_map/ppermute | solution.py:53
  106.5 2.0 %collective-permute-start.35 = (bf16[96,768]{1,0:T(8,128)(2,1)S(1)}, bf16[96,768]{1,0:T(8,128)(2,1)S(1)}, u32[]{:S(2)}, u32[]{:S(2)}) collective-permute-start(bf16[96,768]{1,0:T(8,128)(2,1)S(1)} %collective-permute-done.34.refs_6_), channel_id=1, source_target_pairs={{0,1},{1,0},{2,3},{3,2},{4,5},{5,4},{6,7},{7,6},{8,9},{9,8},{10,11... | collective-permute-start | bytes 442376 | tf_op jit(solution)/shard_map/ppermute | solution.py:53
  (9 other events, 15.6 us)

commit v7 on v6

--- a/solution.py
+++ b/solution.py
@@ -19,7 +19,6 @@
 SPAN = 2
 EPSILON = 1e-06
 MIB = 1024 * 1024
-BAND = 256
 
 F32 = jnp.float32
 BF16 = jnp.bfloat16
@@ -522,22 +521,12 @@
     return (rows_turned, *two)
 
 
-def bands(x):
-    return [x[i : i + BAND] for i in range(0, x.shape[0], BAND)]
-
-
 def first_step(xb):
-    steps = []
-    square = None
-    for band in bands(xb):
-        gram = mm(band, xb, NT)
-        part = jnp.sum(gram * gram, keepdims=True)
-        square = part if square is None else square + part
-        steps.append(mm(gram.astype(BF16), xb))
-    norm_square = jnp.sqrt(square + EPSILON)
+    gram = mm(xb, xb, NT)
+    norm_square = jnp.sqrt(jnp.sum(gram * gram, keepdims=True) + EPSILON)
     scale = lax.rsqrt(norm_square)
-    less = 0.5 * scale / norm_square
-    return [(1.5 * scale) * band.astype(F32) - less * step for band, step in zip(bands(xb), steps)]
+    step = mm(gram.astype(BF16), xb)
+    return (1.5 * scale) * xb.astype(F32) - (0.5 * scale / norm_square) * step
 
 
 def join(parts):
@@ -556,8 +545,8 @@
     owned = codes_ref.shape[1]
     height = parts[0].shape[0]
     x = first_step(join([ref[...] for ref in parts]))
-    xb = jnp.concatenate([band.astype(BF16) for band in x], axis=0)
-    mine = x[0][:height]
+    xb = x.astype(BF16)
+    mine = x[:height]
     gram = mm(mine.astype(BF16), xb, NT)
     rotation_rows = (1.5 * mine - 0.5 * mm(gram.astype(BF16), xb)).astype(BF16)
     totals = None
@@ -597,8 +586,7 @@
     for k, ref in enumerate(parts):
         at = pl.multiple_of((place_ref[0] ^ k) * height, 16 if whole.dtype == BF16 else 8)
         whole[pl.ds(at, height), :] = ref[...].astype(whole.dtype)
-    x = first_step(whole[...].astype(BF16))
-    xb = jnp.concatenate([band.astype(BF16) for band in x], axis=0)
+    xb = first_step(whole[...].astype(BF16)).astype(BF16)
     once = mm(residual_ref[...], xb, NT)
     less = mm(mm(once.astype(BF16), xb).astype(BF16), xb, NT)
     out_ref[...] = (1.5 * once - 0.5 * less).astype(BF16)

time: 115 us -> 115 us (level)
  transfers between devices with their start and end apart: 36 -> 36, of which waited for: 23 -> 24; matrix products, arithmetic and copies ran while one was open for 1% -> 1% of each run, Pallas kernels for 8% -> 8%
where the time goes in v7:
time: 115 us
  waiting for transfers between devices  47.6 us (41%)
  starting transfers between devices  38.4 us (33%)
  Pallas kernels  23.6 us (21%)
  local copies, waits for them, and re-layouts  4.06 us (4%)
    ppermute x36, waiting for transfers between devices, swap(): return lax.ppermute(x, axis, [(i, i ^ bits) for i in range(size)])  47.6 us
    ppermute x36, starting transfers between devices, swap(): return lax.ppermute(x, axis, [(i, i ^ bits) for i in range(size)])  38.4 us
    pallas_call x1, Pallas kernels, next_sums_call(): pl.pallas_call(functools.partial(next_sums_kernel, held, bool(ready)), ou...  5.16 us
    pallas_call x1, Pallas kernels, final_call(): pl.pallas_call(functools.partial(final_kernel, len(blocks)), out_shape=ja...  5.03 us
    pallas_call x1, Pallas kernels, local_sums_call(): pl.pallas_call(functools.partial(local_sums_kernel, size), out_shape=(sha...  3.44 us
    unnamed x10, local copies, waits for them, and re-layouts  2.86 us
  transfers between devices with their start and end apart: 36, of which 24 were waited for; matrix products, arithmetic and copies ran while one was open for 1% of the time, Pallas kernels for 8%

profile of v7, /device:TPU:0, one launch (start us, length us, event | category | flops | bytes accessed | tf_op | source)
XLA Modules:
  0.0 114.6 jit_solution(6740727327808483667)
XLA Ops:
  3.2 2.6 %collective-permute-start.9 = (bf16[512,768]{1,0:T(8,128)(2,1)S(1)}, bf16[512,768]{1,0:T(8,128)(2,1)S(1)}, u32[]{:S(2)}, u32[]{:S(2)}) collective-permute-start(bf16[512,768]{1,0:T(8,128)(2,1)S(1)} %residual.1.residual_ref.refs_2_.refs_0_.refs_6_), channel_id=1, source_target_pairs={{0,4},{1,5},{2,6},{3,7},{4,0},{5,1},{6,2},{7,3},{8,12},{9,13},{10,... | collective-permute-start | bytes 2359304 | tf_op jit(solution)/shard_map/ppermute | solution.py:52
  7.3 1.7 %copy-done = f32[768,768]{1,0:T(8,128)S(1)} copy-done((f32[768,768]{1,0:T(8,128)S(1)}, f32[768,768]{1,0:T(8,128)}, u32[]{:S(2)}) %copy-start) | copy-done | bytes 2359320
  9.0 3.4 %local_sums.1 = (bf16[4,160,256]{2,1,0:T(8,128)(2,1)S(1)}, bf16[4,160,256]{2,1,0:T(8,128)(2,1)S(1)}) custom-call(s32[1]{0:T(128)} %bitcast.place_ref, f32[768,768]{1,0:T(8,128)S(1)} %copy-done, s32[96,512]{1,0:T(8,128)S(1)} %bitcast.6, bf16[512,768]{1,0:T(8,128)(2,1)S(1)} %residual.1.residual_ref.refs_2_.refs_0_.refs_6_), custom_call_target="tpu_custom_call" | custom-call | tf_op jit(solution)/shard_map/local_sums/pallas_call | solution.py:236
  12.5 1.6 %collective-permute-done.1.came_ref = bf16[4,160,256]{2,1,0:T(8,128)(2,1)S(1)} collective-permute-done((bf16[4,160,256]{2,1,0:T(8,128)(2,1)S(1)}, bf16[4,160,256]{2,1,0:T(8,128)(2,1)S(1)}, u32[]{:S(2)}, u32[]{:S(2)}) %collective-permute-start.1) | collective-permute-done | bytes 327712 | tf_op jit(solution)/shard_map/ppermute | solution.py:52
  17.8 6.4 %collective-permute-done.9.refs_6_.refs_4_.refs_10_ = bf16[512,768]{1,0:T(8,128)(2,1)S(1)} collective-permute-done((bf16[512,768]{1,0:T(8,128)(2,1)S(1)}, bf16[512,768]{1,0:T(8,128)(2,1)S(1)}, u32[]{:S(2)}, u32[]{:S(2)}) %collective-permute-start.9) | collective-permute-done | bytes 786464 | tf_op jit(solution)/shard_map/ppermute | solution.py:52
  24.2 2.0 %collective-permute-start.12 = (bf16[256,768]{1,0:T(8,128)(2,1)S(1)}, bf16[256,768]{1,0:T(8,128)(2,1)S(1)}, u32[]{:S(2)}, u32[]{:S(2)}) collective-permute-start(bf16[256,768]{1,0:T(8,128)(2,1)S(1)} %slice.9), channel_id=1, source_target_pairs={{0,2},{1,3},{2,0},{3,1},{4,6},{5,7},{6,4},{7,5},{8,10},{9,11},{10,... | collective-permute-start | bytes 1179656 | tf_op jit(solution)/shard_map/ppermute | solution.py:52
  28.3 1.6 %collective-permute-done.4.refs_3_ = bf16[192,256]{1,0:T(8,128)(2,1)S(1)} collective-permute-done((bf16[192,256]{1,0:T(8,128)(2,1)S(1)}, bf16[192,256]{1,0:T(8,128)(2,1)S(1)}, u32[]{:S(2)}, u32[]{:S(2)}) %collective-permute-start.4) | collective-permute-done | bytes 98336 | tf_op jit(solution)/shard_map/ppermute | solution.py:52
  30.5 2.0 %collective-permute-start.5 = (bf16[128,256]{1,0:T(8,128)(2,1)S(1)}, bf16[128,256]{1,0:T(8,128)(2,1)S(1)}, u32[]{:S(2)}, u32[]{:S(2)}) collective-permute-start(bf16[128,256]{1,0:T(8,128)(2,1)S(1)} %get-tuple-element.35.first_ref), channel_id=1, source_target_pairs={{0,8},{8,0},{16,24},{24,16},{1,9},{9,1},{17,25},{25,17},{2,10},{10... | collective-permute-start | bytes 196616 | tf_op jit(solution)/shard_map/ppermute | solution.py:52
  32.6 2.3 %collective-permute-done.5.second_ref = bf16[128,256]{1,0:T(8,128)(2,1)S(1)} collective-permute-done((bf16[128,256]{1,0:T(8,128)(2,1)S(1)}, bf16[128,256]{1,0:T(8,128)(2,1)S(1)}, u32[]{:S(2)}, u32[]{:S(2)}) %collective-permute-start.5) | collective-permute-done | bytes 65568 | tf_op jit(solution)/shard_map/ppermute | solution.py:52
  34.9 3.0 %collective-permute-start.6 = (bf16[128,256]{1,0:T(8,128)(2,1)S(1)}, bf16[128,256]{1,0:T(8,128)(2,1)S(1)}, u32[]{:S(2)}, u32[]{:S(2)}) collective-permute-start(bf16[128,256]{1,0:T(8,128)(2,1)S(1)} %merge_groups.1.refs_0_), channel_id=1, source_target_pairs={{0,16},{8,24},{16,0},{24,8},{1,17},{9,25},{17,1},{25,9},{2,18},{10... | collective-permute-start | bytes 196616 | tf_op jit(solution)/shard_map/ppermute | solution.py:52
  38.1 2.4 %collective-permute-done.6.refs_1_ = bf16[128,256]{1,0:T(8,128)(2,1)S(1)} collective-permute-done((bf16[128,256]{1,0:T(8,128)(2,1)S(1)}, bf16[128,256]{1,0:T(8,128)(2,1)S(1)}, u32[]{:S(2)}, u32[]{:S(2)}) %collective-permute-start.6) | collective-permute-done | bytes 65568 | tf_op jit(solution)/shard_map/ppermute | solution.py:52
  41.0 2.1 %cross_near.1 = (f32[96,768]{1,0:T(8,128)S(1)}, bf16[3,128,256]{2,1,0:T(8,128)(2,1)S(1)}, f32[24,256]{1,0:T(8,128)S(1)}) custom-call(s32[8,12,512]{2,1,0:T(8,128)S(1)} %get-tuple-element.42.codes_ref, bf16[128,256]{1,0:T(8,128)(2,1)S(1)} %merge_groups.1.refs_0_, bf16[128,256]{1,0:T(8,128)(2,1)S(1)} %collective-permute-done.6.refs_1_, ...), custom_call_target="tpu_custom_call" | custom-call | tf_op jit(solution)/shard_map/cross_near/pallas_call | solution.py:406
  43.9 1.7 %collective-permute-start.15 = (bf16[96,768]{1,0:T(8,128)(2,1)S(1)}, bf16[96,768]{1,0:T(8,128)(2,1)S(1)}, u32[]{:S(2)}, u32[]{:S(2)}) collective-permute-start(bf16[96,768]{1,0:T(8,128)(2,1)S(1)} %cross_far.1), channel_id=1, source_target_pairs={{0,8},{8,0},{16,24},{24,16},{1,9},{9,1},{17,25},{25,17},{2,10},{10... | collective-permute-start | bytes 442376 | tf_op jit(solution)/shard_map/ppermute | solution.py:52
  45.6 1.8 %turn_rows.1.refs_8_ = bf16[4,768,1024]{2,1,0:T(8,128)(2,1)S(1)} custom-call(bf16[512,768]{1,0:T(8,128)(2,1)S(1)} %residual.1.residual_ref.refs_2_.refs_0_.refs_6_, bf16[512,768]{1,0:T(8,128)(2,1)S(1)} %collective-permute-done.refs_3_.refs_1_.refs_7_, bf16[512,768]{1,0:T(8,128)(2,1)S(1)} %collective-permute-done.7.refs_4_.refs_2_.refs_8_, ...), custom_call_target="tpu_custom_call" | custom-call | tf_op jit(solution)/shard_map/turn_rows/pallas_call | solution.py:503
  47.4 2.3 %collective-permute-done.15 = bf16[96,768]{1,0:T(8,128)(2,1)S(1)} collective-permute-done((bf16[96,768]{1,0:T(8,128)(2,1)S(1)}, bf16[96,768]{1,0:T(8,128)(2,1)S(1)}, u32[]{:S(2)}, u32[]{:S(2)}) %collective-permute-start.15) | collective-permute-done | bytes 147488 | tf_op jit(solution)/shard_map/ppermute | solution.py:52
  49.7 3.1 %collective-permute-start.16 = (bf16[96,768]{1,0:T(8,128)(2,1)S(1)}, bf16[96,768]{1,0:T(8,128)(2,1)S(1)}, u32[]{:S(2)}, u32[]{:S(2)}) collective-permute-start(bf16[96,768]{1,0:T(8,128)(2,1)S(1)} %add_convert_fusion.3), channel_id=1, source_target_pairs={{0,16},{8,24},{16,0},{24,8},{1,17},{9,25},{17,1},{25,9},{2,18},{10... | collective-permute-start | bytes 442376 | tf_op jit(solution)/shard_map/ppermute | solution.py:52
  52.9 2.1 %tables.1 = (bf16[4,1024,768]{2,1,0:T(8,128)(2,1)S(1)}, bf16[4,768,1024]{2,1,0:T(8,128)(2,1)S(1)}) custom-call(s32[8,12,512]{2,1,0:T(8,128)S(1)} %get-tuple-element.42.codes_ref), custom_call_target="tpu_custom_call" | custom-call | tf_op jit(solution)/shard_map/tables/pallas_call | solution.py:512
  54.9 4.6 %collective-permute-done.16 = bf16[96,768]{1,0:T(8,128)(2,1)S(1)} collective-permute-done((bf16[96,768]{1,0:T(8,128)(2,1)S(1)}, bf16[96,768]{1,0:T(8,128)(2,1)S(1)}, u32[]{:S(2)}, u32[]{:S(2)}) %collective-permute-start.16) | collective-permute-done | bytes 147488 | tf_op jit(solution)/shard_map/ppermute | solution.py:52
  59.6 2.5 %collective-permute-start.22 = (bf16[96,768]{1,0:T(8,128)(2,1)S(1)}, bf16[96,768]{1,0:T(8,128)(2,1)S(1)}, u32[]{:S(2)}, u32[]{:S(2)}) collective-permute-start(bf16[96,768]{1,0:T(8,128)(2,1)S(1)} %add_convert_fusion.2.refs_0_), channel_id=1, source_target_pairs={{0,6},{1,7},{2,4},{3,5},{4,2},{5,3},{6,0},{7,1},{8,14},{9,15},{10,... | collective-permute-start | bytes 442376 | tf_op jit(solution)/shard_map/ppermute | solution.py:52
  63.1 3.6 %collective-permute-done.22.refs_6_ = bf16[96,768]{1,0:T(8,128)(2,1)S(1)} collective-permute-done((bf16[96,768]{1,0:T(8,128)(2,1)S(1)}, bf16[96,768]{1,0:T(8,128)(2,1)S(1)}, u32[]{:S(2)}, u32[]{:S(2)}) %collective-permute-start.22) | collective-permute-done | bytes 147488 | tf_op jit(solution)/shard_map/ppermute | solution.py:52
  66.7 1.9 %collective-permute-done.20.refs_4_ = bf16[96,768]{1,0:T(8,128)(2,1)S(1)} collective-permute-done((bf16[96,768]{1,0:T(8,128)(2,1)S(1)}, bf16[96,768]{1,0:T(8,128)(2,1)S(1)}, u32[]{:S(2)}, u32[]{:S(2)}) %collective-permute-start.20) | collective-permute-done | bytes 147488 | tf_op jit(solution)/shard_map/ppermute | solution.py:52
  70.2 5.2 %next_sums.1.refs_1_ = bf16[96,256]{1,0:T(8,128)(2,1)S(1)} custom-call(s32[8,12,512]{2,1,0:T(8,128)S(1)} %get-tuple-element.42.codes_ref, bf16[96,768]{1,0:T(8,128)(2,1)S(1)} %add_convert_fusion.2.refs_0_, bf16[96,768]{1,0:T(8,128)(2,1)S(1)} %collective-permute-done.17.refs_1_, bf16[96,768]{1,0:T(8,128)(2,1)S(1)} %collective-permute-done.18.refs_2_, ...), custom_call_target="tpu_custom_call" | custom-call | tf_op jit(solution)/shard_map/next_sums/pallas_call | solution.py:572
  75.3 4.4 %collective-permute-start.26 = (bf16[96,256]{1,0:T(8,128)(2,1)S(1)}, bf16[96,256]{1,0:T(8,128)(2,1)S(1)}, u32[]{:S(2)}, u32[]{:S(2)}) collective-permute-start(bf16[96,256]{1,0:T(8,128)(2,1)S(1)} %next_sums.1.refs_1_), channel_id=1, source_target_pairs={{0,24},{8,16},{16,8},{24,0},{1,25},{9,17},{17,9},{25,1},{2,26},{10... | collective-permute-start | bytes 147464 | tf_op jit(solution)/shard_map/ppermute | solution.py:52
  80.3 1.9 %collective-permute-done.26.refs_4_ = bf16[96,256]{1,0:T(8,128)(2,1)S(1)} collective-permute-done((bf16[96,256]{1,0:T(8,128)(2,1)S(1)}, bf16[96,256]{1,0:T(8,128)(2,1)S(1)}, u32[]{:S(2)}, u32[]{:S(2)}) %collective-permute-start.26) | collective-permute-done | bytes 49184 | tf_op jit(solution)/shard_map/ppermute | solution.py:52
  82.2 2.5 %collective-permute-done.25.refs_3_ = bf16[96,256]{1,0:T(8,128)(2,1)S(1)} collective-permute-done((bf16[96,256]{1,0:T(8,128)(2,1)S(1)}, bf16[96,256]{1,0:T(8,128)(2,1)S(1)}, u32[]{:S(2)}, u32[]{:S(2)}) %collective-permute-start.25) | collective-permute-done | bytes 49184 | tf_op jit(solution)/shard_map/ppermute | solution.py:52
  84.8 2.2 %cross.1 = (bf16[96,768]{1,0:T(8,128)(2,1)S(1)}, f32[96,256]{1,0:T(8,128)S(1)}) custom-call(s32[8,12,512]{2,1,0:T(8,128)S(1)} %get-tuple-element.42.codes_ref, bf16[4,768,1024]{2,1,0:T(8,128)(2,1)S(1)} %get-tuple-element.43.refs_0_, bf16[96,256]{1,0:T(8,128)(2,1)S(1)} %next_sums.1.refs_1_, bf16[96,256]{1,0:T(8,128)(2,1)S(1)} %collective-permute-done.24.refs_2_, ...), custom_call_target="tpu_custom_call" | custom-call | tf_op jit(solution)/shard_map/cross/pallas_call | solution.py:459
  89.3 3.0 %collective-permute-done.27 = bf16[96,768]{1,0:T(8,128)(2,1)S(1)} collective-permute-done((bf16[96,768]{1,0:T(8,128)(2,1)S(1)}, bf16[96,768]{1,0:T(8,128)(2,1)S(1)}, u32[]{:S(2)}, u32[]{:S(2)}) %collective-permute-start.27) | collective-permute-done | bytes 147488 | tf_op jit(solution)/shard_map/ppermute | solution.py:52
  92.3 2.0 %collective-permute-start.28 = (bf16[96,768]{1,0:T(8,128)(2,1)S(1)}, bf16[96,768]{1,0:T(8,128)(2,1)S(1)}, u32[]{:S(2)}, u32[]{:S(2)}) collective-permute-start(bf16[96,768]{1,0:T(8,128)(2,1)S(1)} %add_convert_fusion.1), channel_id=1, source_target_pairs={{0,16},{8,24},{16,0},{24,8},{1,17},{9,25},{17,1},{25,9},{2,18},{10... | collective-permute-start | bytes 442376 | tf_op jit(solution)/shard_map/ppermute | solution.py:52
  94.3 5.7 %collective-permute-done.28 = bf16[96,768]{1,0:T(8,128)(2,1)S(1)} collective-permute-done((bf16[96,768]{1,0:T(8,128)(2,1)S(1)}, bf16[96,768]{1,0:T(8,128)(2,1)S(1)}, u32[]{:S(2)}, u32[]{:S(2)}) %collective-permute-start.28) | collective-permute-done | bytes 147488 | tf_op jit(solution)/shard_map/ppermute | solution.py:52
  100.0 1.8 %collective-permute-start.34 = (bf16[96,768]{1,0:T(8,128)(2,1)S(1)}, bf16[96,768]{1,0:T(8,128)(2,1)S(1)}, u32[]{:S(2)}, u32[]{:S(2)}) collective-permute-start(bf16[96,768]{1,0:T(8,128)(2,1)S(1)} %add_convert_fusion.refs_0_), channel_id=1, source_target_pairs={{0,6},{1,7},{2,4},{3,5},{4,2},{5,3},{6,0},{7,1},{8,14},{9,15},{10,... | collective-permute-start | bytes 442376 | tf_op jit(solution)/shard_map/ppermute | solution.py:52
  103.6 2.6 %collective-permute-done.34.refs_6_ = bf16[96,768]{1,0:T(8,128)(2,1)S(1)} collective-permute-done((bf16[96,768]{1,0:T(8,128)(2,1)S(1)}, bf16[96,768]{1,0:T(8,128)(2,1)S(1)}, u32[]{:S(2)}, u32[]{:S(2)}) %collective-permute-start.34) | collective-permute-done | bytes 147488 | tf_op jit(solution)/shard_map/ppermute | solution.py:52
  109.6 5.0 %final.1 = bf16[512,768]{1,0:T(8,128)(2,1)} custom-call(s32[1]{0:T(128)} %bitcast.place_ref, bf16[512,768]{1,0:T(8,128)(2,1)S(1)} %residual.1.residual_ref.refs_2_.refs_0_.refs_6_, bf16[96,768]{1,0:T(8,128)(2,1)S(1)} %add_convert_fusion.refs_0_, bf16[96,768]{1,0:T(8,128)(2,1)S(1)} %collective-permute-done.29.refs_1_, ...), custom_call_target="tpu_custom_call" | custom-call | tf_op jit(solution)/shard_map/final/pallas_call | solution.py:598
  (73 shorter events, 22.7 us)
Async XLA Ops:
  2.7 4.6 %collective-permute-start = (bf16[512,768]{1,0:T(8,128)(2,1)S(1)}, bf16[512,768]{1,0:T(8,128)(2,1)S(1)}, u32[]{:S(2)}, u32[]{:S(2)}) collective-permute-start(bf16[512,768]{1,0:T(8,128)(2,1)S(1)} %residual.1.residual_ref.refs_2_.refs_0_.refs_6_), channel_id=1, source_target_pairs={{0,1},{1,0},{2,3},{3,2},{4,5},{5,4},{6,7},{7,6},{8,9},{9,8},{10,11... | collective-permute-start | bytes 2359304 | tf_op jit(solution)/shard_map/ppermute | solution.py:52
  3.2 21.0 %collective-permute-start.9 = (bf16[512,768]{1,0:T(8,128)(2,1)S(1)}, bf16[512,768]{1,0:T(8,128)(2,1)S(1)}, u32[]{:S(2)}, u32[]{:S(2)}) collective-permute-start(bf16[512,768]{1,0:T(8,128)(2,1)S(1)} %residual.1.residual_ref.refs_2_.refs_0_.refs_6_), channel_id=1, source_target_pairs={{0,4},{1,5},{2,6},{3,7},{4,0},{5,1},{6,2},{7,3},{8,12},{9,13},{10,... | collective-permute-start | bytes 2359304 | tf_op jit(solution)/shard_map/ppermute | solution.py:52
  5.8 20.4 %collective-permute-start.7 = (bf16[512,768]{1,0:T(8,128)(2,1)S(1)}, bf16[512,768]{1,0:T(8,128)(2,1)S(1)}, u32[]{:S(2)}, u32[]{:S(2)}) collective-permute-start(bf16[512,768]{1,0:T(8,128)(2,1)S(1)} %residual.1.residual_ref.refs_2_.refs_0_.refs_6_), channel_id=1, source_target_pairs={{0,2},{1,3},{2,0},{3,1},{4,6},{5,7},{6,4},{7,5},{8,10},{9,11},{10,... | collective-permute-start | bytes 2359304 | tf_op jit(solution)/shard_map/ppermute | solution.py:52
  12.4 1.7 %collective-permute-start.1 = (bf16[4,160,256]{2,1,0:T(8,128)(2,1)S(1)}, bf16[4,160,256]{2,1,0:T(8,128)(2,1)S(1)}, u32[]{:S(2)}, u32[]{:S(2)}) collective-permute-start(bf16[4,160,256]{2,1,0:T(8,128)(2,1)S(1)} %get-tuple-element.29), channel_id=1, source_target_pairs={{0,1},{1,0},{2,3},{3,2},{4,5},{5,4},{6,7},{7,6},{8,9},{9,8},{10,11... | collective-permute-start | bytes 983048 | tf_op jit(solution)/shard_map/ppermute | solution.py:52
  14.2 14.1 %collective-permute-start.2 = (bf16[192,256]{1,0:T(8,128)(2,1)S(1)}, bf16[192,256]{1,0:T(8,128)(2,1)S(1)}, u32[]{:S(2)}, u32[]{:S(2)}) collective-permute-start(bf16[192,256]{1,0:T(8,128)(2,1)S(1)} %get-tuple-element.31), channel_id=1, source_target_pairs={{0,2},{1,3},{2,0},{3,1},{4,6},{5,7},{6,4},{7,5},{8,10},{9,11},{10,... | collective-permute-start | bytes 294920 | tf_op jit(solution)/shard_map/ppermute | solution.py:52
  15.0 13.3 %collective-permute-start.3 = (bf16[192,256]{1,0:T(8,128)(2,1)S(1)}, bf16[192,256]{1,0:T(8,128)(2,1)S(1)}, u32[]{:S(2)}, u32[]{:S(2)}) collective-permute-start(bf16[192,256]{1,0:T(8,128)(2,1)S(1)} %get-tuple-element.32), channel_id=1, source_target_pairs={{0,4},{1,5},{2,6},{3,7},{4,0},{5,1},{6,2},{7,3},{8,12},{9,13},{10,... | collective-permute-start | bytes 294920 | tf_op jit(solution)/shard_map/ppermute | solution.py:52
  16.5 13.4 %collective-permute-start.4 = (bf16[192,256]{1,0:T(8,128)(2,1)S(1)}, bf16[192,256]{1,0:T(8,128)(2,1)S(1)}, u32[]{:S(2)}, u32[]{:S(2)}) collective-permute-start(bf16[192,256]{1,0:T(8,128)(2,1)S(1)} %get-tuple-element.33), channel_id=1, source_target_pairs={{0,6},{1,7},{2,4},{3,5},{4,2},{5,3},{6,0},{7,1},{8,14},{9,15},{10,... | collective-permute-start | bytes 294920 | tf_op jit(solution)/shard_map/ppermute | solution.py:52
  24.2 13.8 %collective-permute-start.12 = (bf16[256,768]{1,0:T(8,128)(2,1)S(1)}, bf16[256,768]{1,0:T(8,128)(2,1)S(1)}, u32[]{:S(2)}, u32[]{:S(2)}) collective-permute-start(bf16[256,768]{1,0:T(8,128)(2,1)S(1)} %slice.9), channel_id=1, source_target_pairs={{0,2},{1,3},{2,0},{3,1},{4,6},{5,7},{6,4},{7,5},{8,10},{9,11},{10,... | collective-permute-start | bytes 1179656 | tf_op jit(solution)/shard_map/ppermute | solution.py:52
  26.2 14.2 %collective-permute-start.11 = (bf16[256,768]{1,0:T(8,128)(2,1)S(1)}, bf16[256,768]{1,0:T(8,128)(2,1)S(1)}, u32[]{:S(2)}, u32[]{:S(2)}) collective-permute-start(bf16[256,768]{1,0:T(8,128)(2,1)S(1)} %slice.8), channel_id=1, source_target_pairs={{0,4},{1,5},{2,6},{3,7},{4,0},{5,1},{6,2},{7,3},{8,12},{9,13},{10,... | collective-permute-start | bytes 1179656 | tf_op jit(solution)/shard_map/ppermute | solution.py:52
  30.0 11.1 %collective-permute-start.8 = (bf16[512,768]{1,0:T(8,128)(2,1)S(1)}, bf16[512,768]{1,0:T(8,128)(2,1)S(1)}, u32[]{:S(2)}, u32[]{:S(2)}) collective-permute-start(bf16[512,768]{1,0:T(8,128)(2,1)S(1)} %collective-permute-done.7.refs_4_.refs_2_.refs_8_), channel_id=1, source_target_pairs={{0,1},{1,0},{2,3},{3,2},{4,5},{5,4},{6,7},{7,6},{8,9},{9,8},{10,11... | collective-permute-start | bytes 2359304 | tf_op jit(solution)/shard_map/ppermute | solution.py:52
  30.0 11.0 %collective-permute-start.10 = (bf16[512,768]{1,0:T(8,128)(2,1)S(1)}, bf16[512,768]{1,0:T(8,128)(2,1)S(1)}, u32[]{:S(2)}, u32[]{:S(2)}) collective-permute-start(bf16[512,768]{1,0:T(8,128)(2,1)S(1)} %collective-permute-done.9.refs_6_.refs_4_.refs_10_), channel_id=1, source_target_pairs={{0,1},{1,0},{2,3},{3,2},{4,5},{5,4},{6,7},{7,6},{8,9},{9,8},{10,11... | collective-permute-start | bytes 2359304 | tf_op jit(solution)/shard_map/ppermute | solution.py:52
  30.5 4.4 %collective-permute-start.5 = (bf16[128,256]{1,0:T(8,128)(2,1)S(1)}, bf16[128,256]{1,0:T(8,128)(2,1)S(1)}, u32[]{:S(2)}, u32[]{:S(2)}) collective-permute-start(bf16[128,256]{1,0:T(8,128)(2,1)S(1)} %get-tuple-element.35.first_ref), channel_id=1, source_target_pairs={{0,8},{8,0},{16,24},{24,16},{1,9},{9,1},{17,25},{25,17},{2,10},{10... | collective-permute-start | bytes 196616 | tf_op jit(solution)/shard_map/ppermute | solution.py:52
  34.9 5.6 %collective-permute-start.6 = (bf16[128,256]{1,0:T(8,128)(2,1)S(1)}, bf16[128,256]{1,0:T(8,128)(2,1)S(1)}, u32[]{:S(2)}, u32[]{:S(2)}) collective-permute-start(bf16[128,256]{1,0:T(8,128)(2,1)S(1)} %merge_groups.1.refs_0_), channel_id=1, source_target_pairs={{0,16},{8,24},{16,0},{24,8},{1,17},{9,25},{17,1},{25,9},{2,18},{10... | collective-permute-start | bytes 196616 | tf_op jit(solution)/shard_map/ppermute | solution.py:52
  40.5 2.6 %collective-permute-start.13 = (bf16[256,768]{1,0:T(8,128)(2,1)S(1)}, bf16[256,768]{1,0:T(8,128)(2,1)S(1)}, u32[]{:S(2)}, u32[]{:S(2)}) collective-permute-start(bf16[256,768]{1,0:T(8,128)(2,1)S(1)} %collective-permute-done.11.refs_0_.refs_6_.refs_12_), channel_id=1, source_target_pairs={{0,1},{1,0},{2,3},{3,2},{4,5},{5,4},{6,7},{7,6},{8,9},{9,8},{10,11... | collective-permute-start | bytes 1179656 | tf_op jit(solution)/shard_map/ppermute | solution.py:52
  40.5 2.6 %collective-permute-start.14 = (bf16[256,768]{1,0:T(8,128)(2,1)S(1)}, bf16[256,768]{1,0:T(8,128)(2,1)S(1)}, u32[]{:S(2)}, u32[]{:S(2)}) collective-permute-start(bf16[256,768]{1,0:T(8,128)(2,1)S(1)} %collective-permute-done.12.refs_1_.refs_7_.refs_13_), channel_id=1, source_target_pairs={{0,1},{1,0},{2,3},{3,2},{4,5},{5,4},{6,7},{7,6},{8,9},{9,8},{10,11... | collective-permute-start | bytes 1179656 | tf_op jit(solution)/shard_map/ppermute | solution.py:52
  43.9 5.8 %collective-permute-start.15 = (bf16[96,768]{1,0:T(8,128)(2,1)S(1)}, bf16[96,768]{1,0:T(8,128)(2,1)S(1)}, u32[]{:S(2)}, u32[]{:S(2)}) collective-permute-start(bf16[96,768]{1,0:T(8,128)(2,1)S(1)} %cross_far.1), channel_id=1, source_target_pairs={{0,8},{8,0},{16,24},{24,16},{1,9},{9,1},{17,25},{25,17},{2,10},{10... | collective-permute-start | bytes 442376 | tf_op jit(solution)/shard_map/ppermute | solution.py:52
  49.7 9.8 %collective-permute-start.16 = (bf16[96,768]{1,0:T(8,128)(2,1)S(1)}, bf16[96,768]{1,0:T(8,128)(2,1)S(1)}, u32[]{:S(2)}, u32[]{:S(2)}) collective-permute-start(bf16[96,768]{1,0:T(8,128)(2,1)S(1)} %add_convert_fusion.3), channel_id=1, source_target_pairs={{0,16},{8,24},{16,0},{24,8},{1,17},{9,25},{17,1},{25,9},{2,18},{10... | collective-permute-start | bytes 442376 | tf_op jit(solution)/shard_map/ppermute | solution.py:52
  59.6 7.1 %collective-permute-start.22 = (bf16[96,768]{1,0:T(8,128)(2,1)S(1)}, bf16[96,768]{1,0:T(8,128)(2,1)S(1)}, u32[]{:S(2)}, u32[]{:S(2)}) collective-permute-start(bf16[96,768]{1,0:T(8,128)(2,1)S(1)} %add_convert_fusion.2.refs_0_), channel_id=1, source_target_pairs={{0,6},{1,7},{2,4},{3,5},{4,2},{5,3},{6,0},{7,1},{8,14},{9,15},{10,... | collective-permute-start | bytes 442376 | tf_op jit(solution)/shard_map/ppermute | solution.py:52
  62.1 6.5 %collective-permute-start.20 = (bf16[96,768]{1,0:T(8,128)(2,1)S(1)}, bf16[96,768]{1,0:T(8,128)(2,1)S(1)}, u32[]{:S(2)}, u32[]{:S(2)}) collective-permute-start(bf16[96,768]{1,0:T(8,128)(2,1)S(1)} %add_convert_fusion.2.refs_0_), channel_id=1, source_target_pairs={{0,4},{1,5},{2,6},{3,7},{4,0},{5,1},{6,2},{7,3},{8,12},{9,13},{10,... | collective-permute-start | bytes 442376 | tf_op jit(solution)/shard_map/ppermute | solution.py:52
  62.6 6.0 %collective-permute-start.18 = (bf16[96,768]{1,0:T(8,128)(2,1)S(1)}, bf16[96,768]{1,0:T(8,128)(2,1)S(1)}, u32[]{:S(2)}, u32[]{:S(2)}) collective-permute-start(bf16[96,768]{1,0:T(8,128)(2,1)S(1)} %add_convert_fusion.2.refs_0_), channel_id=1, source_target_pairs={{0,2},{1,3},{2,0},{3,1},{4,6},{5,7},{6,4},{7,5},{8,10},{9,11},{10,... | collective-permute-start | bytes 442376 | tf_op jit(solution)/shard_map/ppermute | solution.py:52
  63.1 6.0 %collective-permute-start.17 = (bf16[96,768]{1,0:T(8,128)(2,1)S(1)}, bf16[96,768]{1,0:T(8,128)(2,1)S(1)}, u32[]{:S(2)}, u32[]{:S(2)}) collective-permute-start(bf16[96,768]{1,0:T(8,128)(2,1)S(1)} %add_convert_fusion.2.refs_0_), channel_id=1, source_target_pairs={{0,1},{1,0},{2,3},{3,2},{4,5},{5,4},{6,7},{7,6},{8,9},{9,8},{10,11... | collective-permute-start | bytes 442376 | tf_op jit(solution)/shard_map/ppermute | solution.py:52
  66.7 2.4 %collective-permute-start.23 = (bf16[96,768]{1,0:T(8,128)(2,1)S(1)}, bf16[96,768]{1,0:T(8,128)(2,1)S(1)}, u32[]{:S(2)}, u32[]{:S(2)}) collective-permute-start(bf16[96,768]{1,0:T(8,128)(2,1)S(1)} %collective-permute-done.22.refs_6_), channel_id=1, source_target_pairs={{0,1},{1,0},{2,3},{3,2},{4,5},{5,4},{6,7},{7,6},{8,9},{9,8},{10,11... | collective-permute-start | bytes 442376 | tf_op jit(solution)/shard_map/ppermute | solution.py:52
  75.3 6.9 %collective-permute-start.26 = (bf16[96,256]{1,0:T(8,128)(2,1)S(1)}, bf16[96,256]{1,0:T(8,128)(2,1)S(1)}, u32[]{:S(2)}, u32[]{:S(2)}) collective-permute-start(bf16[96,256]{1,0:T(8,128)(2,1)S(1)} %next_sums.1.refs_1_), channel_id=1, source_target_pairs={{0,24},{8,16},{16,8},{24,0},{1,25},{9,17},{17,9},{25,1},{2,26},{10... | collective-permute-start | bytes 147464 | tf_op jit(solution)/shard_map/ppermute | solution.py:52
  79.7 5.0 %collective-permute-start.25 = (bf16[96,256]{1,0:T(8,128)(2,1)S(1)}, bf16[96,256]{1,0:T(8,128)(2,1)S(1)}, u32[]{:S(2)}, u32[]{:S(2)}) collective-permute-start(bf16[96,256]{1,0:T(8,128)(2,1)S(1)} %next_sums.1.refs_1_), channel_id=1, source_target_pairs={{0,16},{8,24},{16,0},{24,8},{1,17},{9,25},{17,1},{25,9},{2,18},{10... | collective-permute-start | bytes 147464 | tf_op jit(solution)/shard_map/ppermute | solution.py:52
  79.7 5.1 %collective-permute-start.24 = (bf16[96,256]{1,0:T(8,128)(2,1)S(1)}, bf16[96,256]{1,0:T(8,128)(2,1)S(1)}, u32[]{:S(2)}, u32[]{:S(2)}) collective-permute-start(bf16[96,256]{1,0:T(8,128)(2,1)S(1)} %next_sums.1.refs_1_), channel_id=1, source_target_pairs={{0,8},{8,0},{16,24},{24,16},{1,9},{9,1},{17,25},{25,17},{2,10},{10... | collective-permute-start | bytes 147464 | tf_op jit(solution)/shard_map/ppermute | solution.py:52
  87.1 5.2 %collective-permute-start.27 = (bf16[96,768]{1,0:T(8,128)(2,1)S(1)}, bf16[96,768]{1,0:T(8,128)(2,1)S(1)}, u32[]{:S(2)}, u32[]{:S(2)}) collective-permute-start(bf16[96,768]{1,0:T(8,128)(2,1)S(1)} %get-tuple-element.49), channel_id=1, source_target_pairs={{0,8},{8,0},{16,24},{24,16},{1,9},{9,1},{17,25},{25,17},{2,10},{10... | collective-permute-start | bytes 442376 | tf_op jit(solution)/shard_map/ppermute | solution.py:52
  92.3 7.7 %collective-permute-start.28 = (bf16[96,768]{1,0:T(8,128)(2,1)S(1)}, bf16[96,768]{1,0:T(8,128)(2,1)S(1)}, u32[]{:S(2)}, u32[]{:S(2)}) collective-permute-start(bf16[96,768]{1,0:T(8,128)(2,1)S(1)} %add_convert_fusion.1), channel_id=1, source_target_pairs={{0,16},{8,24},{16,0},{24,8},{1,17},{9,25},{17,1},{25,9},{2,18},{10... | collective-permute-start | bytes 442376 | tf_op jit(solution)/shard_map/ppermute | solution.py:52
  100.0 6.2 %collective-permute-start.34 = (bf16[96,768]{1,0:T(8,128)(2,1)S(1)}, bf16[96,768]{1,0:T(8,128)(2,1)S(1)}, u32[]{:S(2)}, u32[]{:S(2)}) collective-permute-start(bf16[96,768]{1,0:T(8,128)(2,1)S(1)} %add_convert_fusion.refs_0_), channel_id=1, source_target_pairs={{0,6},{1,7},{2,4},{3,5},{4,2},{5,3},{6,0},{7,1},{8,14},{9,15},{10,... | collective-permute-start | bytes 442376 | tf_op jit(solution)/shard_map/ppermute | solution.py:52
  101.8 5.9 %collective-permute-start.32 = (bf16[96,768]{1,0:T(8,128)(2,1)S(1)}, bf16[96,768]{1,0:T(8,128)(2,1)S(1)}, u32[]{:S(2)}, u32[]{:S(2)}) collective-permute-start(bf16[96,768]{1,0:T(8,128)(2,1)S(1)} %add_convert_fusion.refs_0_), channel_id=1, source_target_pairs={{0,4},{1,5},{2,6},{3,7},{4,0},{5,1},{6,2},{7,3},{8,12},{9,13},{10,... | collective-permute-start | bytes 442376 | tf_op jit(solution)/shard_map/ppermute | solution.py:52
  103.1 5.1 %collective-permute-start.30 = (bf16[96,768]{1,0:T(8,128)(2,1)S(1)}, bf16[96,768]{1,0:T(8,128)(2,1)S(1)}, u32[]{:S(2)}, u32[]{:S(2)}) collective-permute-start(bf16[96,768]{1,0:T(8,128)(2,1)S(1)} %add_convert_fusion.refs_0_), channel_id=1, source_target_pairs={{0,2},{1,3},{2,0},{3,1},{4,6},{5,7},{6,4},{7,5},{8,10},{9,11},{10,... | collective-permute-start | bytes 442376 | tf_op jit(solution)/shard_map/ppermute | solution.py:52
  103.6 4.7 %collective-permute-start.29 = (bf16[96,768]{1,0:T(8,128)(2,1)S(1)}, bf16[96,768]{1,0:T(8,128)(2,1)S(1)}, u32[]{:S(2)}, u32[]{:S(2)}) collective-permute-start(bf16[96,768]{1,0:T(8,128)(2,1)S(1)} %add_convert_fusion.refs_0_), channel_id=1, source_target_pairs={{0,1},{1,0},{2,3},{3,2},{4,5},{5,4},{6,7},{7,6},{8,9},{9,8},{10,11... | collective-permute-start | bytes 442376 | tf_op jit(solution)/shard_map/ppermute | solution.py:52
  106.2 2.0 %collective-permute-start.35 = (bf16[96,768]{1,0:T(8,128)(2,1)S(1)}, bf16[96,768]{1,0:T(8,128)(2,1)S(1)}, u32[]{:S(2)}, u32[]{:S(2)}) collective-permute-start(bf16[96,768]{1,0:T(8,128)(2,1)S(1)} %collective-permute-done.34.refs_6_), channel_id=1, source_target_pairs={{0,1},{1,0},{2,3},{3,2},{4,5},{5,4},{6,7},{7,6},{8,9},{9,8},{10,11... | collective-permute-start | bytes 442376 | tf_op jit(solution)/shard_map/ppermute | solution.py:52
  (9 other events, 15.6 us)

commit v8 on v7

--- a/solution.py
+++ b/solution.py
@@ -361,7 +361,7 @@
     ]
 
 
-def add_spans(total, wide, codes_ref, pieces, spans, tables=None):
+def add_spans(total, wide, codes_ref, pieces, spans, tables=None, first=0):
     owned = codes_ref.shape[1]
     for i, span in enumerate(spans):
         codes = span_codes(codes_ref, span)
@@ -369,7 +369,7 @@
         rows = codes.shape[1]
         rebuilt = []
         for g, pack in enumerate(packs_of(owned)):
-            table = hi_table(hi, pack) if tables is None else tables[i, g * LANES : (g + 1) * LANES, :]
+            table = hi_table(hi, pack) if tables is None else tables[first + i, g * LANES : (g + 1) * LANES, :]
             spread = mm(wide[g], table)
             for j, m in enumerate(pack):
                 low = jnp.broadcast_to(lo[m : m + 1, :], (SUB, rows))
@@ -387,7 +387,8 @@
     return {k: len(c) for k, c in chunks.items()}, [piece for c in chunks.values() for piece in c]
 
 
-def cross_near_kernel(held, groups, codes_ref, *refs):
+def cross_near_kernel(held, groups, ready, codes_ref, *refs):
+    tables, refs = (refs[0], refs[1:]) if ready else (None, refs)
     sums, pieces, outs = refs[:groups], pieces_of(held, refs[groups:]), refs[groups + sum(held.values()) :]
     total_ref, wide_ref, counts_ref = outs
     owned = codes_ref.shape[1]
@@ -396,47 +397,48 @@
     wide = widen(books, owned)
     for g, one in enumerate(wide):
         wide_ref[g, : one.shape[0], :] = one
-    total_ref[...] = add_spans(None, wide, codes_ref, pieces, spans_of(held))
-
-
-def cross_near_call(codes, sums, chunks):
+    total_ref[...] = add_spans(None, wide, codes_ref, pieces, spans_of(held), tables)
+
+
+def cross_near_call(codes, tables, sums, chunks):
     owned = codes.shape[1]
     packs = len(packs_of(owned))
     held, rows = flat(chunks)
     return pl.pallas_call(
-        functools.partial(cross_near_kernel, held, len(sums)),
+        functools.partial(cross_near_kernel, held, len(sums), bool(tables)),
         out_shape=(
             jax.ShapeDtypeStruct((owned * SUB, rows[0].shape[1]), F32),
             jax.ShapeDtypeStruct((packs, PACK * LO * SUB, LANES), BF16),
             jax.ShapeDtypeStruct((packs * MARKS, LANES), F32),
         ),
-        in_specs=[vmem_spec()] * (1 + len(sums) + len(rows)),
+        in_specs=[vmem_spec()] * (1 + len(tables) + len(sums) + len(rows)),
         out_specs=(vmem_spec(),) * 3,
         compiler_params=params(*rows),
         cost_estimate=cost(0),
         name="cross_near",
-    )(codes, *sums, *rows)
-
-
-def cross_far_kernel(held, total_rows, codes_ref, total_ref, wide_ref, *refs):
+    )(codes, *tables, *sums, *rows)
+
+
+def cross_far_kernel(held, total_rows, first, codes_ref, total_ref, wide_ref, *refs):
+    tables, refs = (refs[0], refs[1:]) if first else (None, refs)
     pieces, cross_ref = pieces_of(held, refs), refs[-1]
     packs = packs_of(codes_ref.shape[1])
     wide = [wide_ref[g, : len(pack) * LO * SUB, :] for g, pack in enumerate(packs)]
-    total = add_spans(total_ref[...], wide, codes_ref, pieces, spans_of(held))
+    total = add_spans(total_ref[...], wide, codes_ref, pieces, spans_of(held), tables, first)
     cross_ref[...] = (total * (1.0 / total_rows)).astype(BF16)
 
 
-def cross_far_call(codes, total, wide, chunks, total_rows):
+def cross_far_call(codes, tables, first, total, wide, chunks, total_rows):
     held, rows = flat(chunks)
     return pl.pallas_call(
-        functools.partial(cross_far_kernel, held, total_rows),
+        functools.partial(cross_far_kernel, held, total_rows, first if tables else 0),
         out_shape=jax.ShapeDtypeStruct(total.shape, BF16),
-        in_specs=[vmem_spec()] * (3 + len(rows)),
+        in_specs=[vmem_spec()] * (3 + len(tables) + len(rows)),
         out_specs=vmem_spec(),
         compiler_params=params(*rows),
         cost_estimate=cost(0),
         name="cross_far",
-    )(codes, total, wide, *rows)
+    )(codes, total, wide, *tables, *rows)
 
 
 def cross_kernel(held, groups, total_rows, ready, codes_ref, *refs):
@@ -486,21 +488,34 @@
             table_ref[i, :, g * LANES : (g + 1) * LANES] = table.T
 
 
-def prepare_call(codes, chunks, after_codes, after_rows):
-    size, owned, rows = codes.shape
-    held, pieces = flat(chunks)
+def tables_call(codes, peers):
+    owned, rows = codes.shape[1:]
     lanes = LANES * len(packs_of(owned))
-    width = pieces[0].shape[1]
-    spans = spans_of(held)
+    spans = spans_of(dict.fromkeys(peers))
     each = len(spans[0]) * rows
-    turned = jax.ShapeDtypeStruct((len(spans), width, each), BF16)
-    tables = (
+    shapes = (
         jax.ShapeDtypeStruct((len(spans), each, lanes), BF16),
         jax.ShapeDtypeStruct((len(spans), lanes, each), BF16),
     )
-    if sum(math.prod(a.shape) * 2 for a in (turned, *tables)) > 20 * MIB:
-        return None
-    rows_turned = pl.pallas_call(
+    if sum(math.prod(a.shape) * 2 for a in shapes) > 14 * MIB:
+        return ()
+    return pl.pallas_call(
+        functools.partial(tables_kernel, spans),
+        out_shape=shapes,
+        in_specs=[vmem_spec()],
+        out_specs=(vmem_spec(),) * 2,
+        compiler_params=params(*shapes),
+        cost_estimate=cost(0),
+        name="tables",
+    )(codes)
+
+
+def turn_call(chunks):
+    held, pieces = flat(chunks)
+    spans = spans_of(held)
+    each = len(spans[0]) * chunks[0][0].shape[0]
+    turned = jax.ShapeDtypeStruct((len(spans), pieces[0].shape[1], each), BF16)
+    return pl.pallas_call(
         functools.partial(turn_kernel, held),
         out_shape=turned,
         in_specs=[vmem_spec()] * len(pieces),
@@ -508,17 +523,7 @@
         compiler_params=params(turned),
         cost_estimate=cost(0),
         name="turn_rows",
-    )(after(pieces[0], *after_rows), *pieces[1:])
-    two = pl.pallas_call(
-        functools.partial(tables_kernel, spans),
-        out_shape=tables,
-        in_specs=[vmem_spec()],
-        out_specs=(vmem_spec(),) * 2,
-        compiler_params=params(*tables),
-        cost_estimate=cost(0),
-        name="tables",
-    )(after(codes, *after_codes))
-    return (rows_turned, *two)
+    )(*pieces)
 
 
 def first_step(xb):
@@ -674,21 +679,22 @@
     near = {k: after(rows_near, sums) for k, rows_near in near.items()}
     for bit in [1 << b for b in range(groups.bit_length() - 2)]:
         sums = merge_call(sums, swap(sums, "group", groups, bit), owned)
-    parts = [sums, swap(sums, "group", groups, groups // 2)]
     chunks = {0: (residual,), 1: (twin,)}
     for k, rows_near in near.items():
         chunks[k] = (rows_near,)
         chunks[k ^ 1] = (swap(rows_near, "within", size, 1),)
-    total, wide, counts = cross_near_call(own_codes, parts, chunks)
+    tables = tables_call(after(own_codes, sums), list(chunks) + [peer for k in far for peer in (k, k ^ 1)])
+    parts = [sums, after(swap(sums, "group", groups, groups // 2), *tables)]
+    total, wide, counts = cross_near_call(own_codes, tables[1:], parts, chunks)
     far = {k: tuple(after(piece, parts[1]) for piece in pieces) for k, pieces in far.items()}
     far = {**far, **both_cores(far, size)}
-    cross = cross_far_call(own_codes, total, wide, far, total_rows)
-    chunks.update(far)
-    ready = prepare_call(own_codes, chunks, (cross,), (cross,))
+    cross = cross_far_call(own_codes, tables[1:], len(spans_of(chunks)), total, wide, far, total_rows)
+    chunks.update({k: far[k] for even in far if even % 2 == 0 for k in (even, even ^ 1)})
+    ready = ()
+    if tables:
+        ready = (turn_call({**chunks, 0: (after(residual, cross),)}), *tables)
     for alternation in range(1, ALTS):
-        block = reduce_cross(cross, groups, ready[:1] if ready else ())
-        if ready:
-            block = after(block, *ready)
+        block = reduce_cross(cross, groups, ready[:1])
         parts = direct(next_sums_call(own_codes, ready, gather_group(block, size), chunks), groups)
         cross, book = cross_call(own_codes, ready, parts, counts, chunks, total_rows)
     packs = len(packs_of(owned))

time: 115 us -> 115 us (level)
  transfers between devices with their start and end apart: 36 -> 36, of which waited for: 24 -> 23; matrix products, arithmetic and copies ran while one was open for 1% -> 1% of each run, Pallas kernels for 8% -> 8%
where the time goes in v8:
time: 115 us
  waiting for transfers between devices  47.8 us (42%)
  starting transfers between devices  38.4 us (33%)
  Pallas kernels  23.3 us (20%)
  local copies, waits for them, and re-layouts  4.06 us (4%)
    ppermute x36, waiting for transfers between devices, swap(): return lax.ppermute(x, axis, [(i, i ^ bits) for i in range(size)])  47.8 us
    ppermute x36, starting transfers between devices, swap(): return lax.ppermute(x, axis, [(i, i ^ bits) for i in range(size)])  38.4 us
    pallas_call x1, Pallas kernels, next_sums_call(): pl.pallas_call(functools.partial(next_sums_kernel, held, bool(ready)), ou...  5.15 us
    pallas_call x1, Pallas kernels, final_call(): pl.pallas_call(functools.partial(final_kernel, len(blocks)), out_shape=ja...  5.03 us
    pallas_call x1, Pallas kernels, local_sums_call(): pl.pallas_call(functools.partial(local_sums_kernel, size), out_shape=(sha...  3.44 us
    unnamed x10, local copies, waits for them, and re-layouts  2.86 us
  transfers between devices with their start and end apart: 36, of which 23 were waited for; matrix products, arithmetic and copies ran while one was open for 1% of the time, Pallas kernels for 8%

profile of v8, /device:TPU:0, one launch (start us, length us, event | category | flops | bytes accessed | tf_op | source)
XLA Modules:
  0.0 114.5 jit_solution(3470839746145516356)
XLA Ops:
  3.2 2.6 %collective-permute-start.9 = (bf16[512,768]{1,0:T(8,128)(2,1)S(1)}, bf16[512,768]{1,0:T(8,128)(2,1)S(1)}, u32[]{:S(2)}, u32[]{:S(2)}) collective-permute-start(bf16[512,768]{1,0:T(8,128)(2,1)S(1)} %residual.1.residual_ref.refs_3_.refs_0_.refs_6_), channel_id=1, source_target_pairs={{0,4},{1,5},{2,6},{3,7},{4,0},{5,1},{6,2},{7,3},{8,12},{9,13},{10,... | collective-permute-start | bytes 2359304 | tf_op jit(solution)/shard_map/ppermute | solution.py:52
  7.3 1.7 %copy-done = f32[768,768]{1,0:T(8,128)S(1)} copy-done((f32[768,768]{1,0:T(8,128)S(1)}, f32[768,768]{1,0:T(8,128)}, u32[]{:S(2)}) %copy-start) | copy-done | bytes 2359320
  9.0 3.4 %local_sums.1 = (bf16[4,160,256]{2,1,0:T(8,128)(2,1)S(1)}, bf16[4,160,256]{2,1,0:T(8,128)(2,1)S(1)}) custom-call(s32[1]{0:T(128)} %bitcast.place_ref, f32[768,768]{1,0:T(8,128)S(1)} %copy-done, s32[96,512]{1,0:T(8,128)S(1)} %bitcast.6, bf16[512,768]{1,0:T(8,128)(2,1)S(1)} %residual.1.residual_ref.refs_3_.refs_0_.refs_6_), custom_call_target="tpu_custom_call" | custom-call | tf_op jit(solution)/shard_map/local_sums/pallas_call | solution.py:236
  12.5 1.6 %collective-permute-done.1.came_ref = bf16[4,160,256]{2,1,0:T(8,128)(2,1)S(1)} collective-permute-done((bf16[4,160,256]{2,1,0:T(8,128)(2,1)S(1)}, bf16[4,160,256]{2,1,0:T(8,128)(2,1)S(1)}, u32[]{:S(2)}, u32[]{:S(2)}) %collective-permute-start.1) | collective-permute-done | bytes 327712 | tf_op jit(solution)/shard_map/ppermute | solution.py:52
  17.8 6.4 %collective-permute-done.9.refs_7_.refs_4_.refs_10_ = bf16[512,768]{1,0:T(8,128)(2,1)S(1)} collective-permute-done((bf16[512,768]{1,0:T(8,128)(2,1)S(1)}, bf16[512,768]{1,0:T(8,128)(2,1)S(1)}, u32[]{:S(2)}, u32[]{:S(2)}) %collective-permute-start.9) | collective-permute-done | bytes 786464 | tf_op jit(solution)/shard_map/ppermute | solution.py:52
  24.2 2.0 %collective-permute-start.12 = (bf16[256,768]{1,0:T(8,128)(2,1)S(1)}, bf16[256,768]{1,0:T(8,128)(2,1)S(1)}, u32[]{:S(2)}, u32[]{:S(2)}) collective-permute-start(bf16[256,768]{1,0:T(8,128)(2,1)S(1)} %slice.9), channel_id=1, source_target_pairs={{0,2},{1,3},{2,0},{3,1},{4,6},{5,7},{6,4},{7,5},{8,10},{9,11},{10,... | collective-permute-start | bytes 1179656 | tf_op jit(solution)/shard_map/ppermute | solution.py:52
  26.2 1.6 %collective-permute-start.11 = (bf16[256,768]{1,0:T(8,128)(2,1)S(1)}, bf16[256,768]{1,0:T(8,128)(2,1)S(1)}, u32[]{:S(2)}, u32[]{:S(2)}) collective-permute-start(bf16[256,768]{1,0:T(8,128)(2,1)S(1)} %slice.8), channel_id=1, source_target_pairs={{0,4},{1,5},{2,6},{3,7},{4,0},{5,1},{6,2},{7,3},{8,12},{9,13},{10,... | collective-permute-start | bytes 1179656 | tf_op jit(solution)/shard_map/ppermute | solution.py:52
  28.3 1.6 %collective-permute-done.4.refs_3_ = bf16[192,256]{1,0:T(8,128)(2,1)S(1)} collective-permute-done((bf16[192,256]{1,0:T(8,128)(2,1)S(1)}, bf16[192,256]{1,0:T(8,128)(2,1)S(1)}, u32[]{:S(2)}, u32[]{:S(2)}) %collective-permute-start.4) | collective-permute-done | bytes 98336 | tf_op jit(solution)/shard_map/ppermute | solution.py:52
  30.5 2.0 %collective-permute-start.5 = (bf16[128,256]{1,0:T(8,128)(2,1)S(1)}, bf16[128,256]{1,0:T(8,128)(2,1)S(1)}, u32[]{:S(2)}, u32[]{:S(2)}) collective-permute-start(bf16[128,256]{1,0:T(8,128)(2,1)S(1)} %get-tuple-element.35.first_ref), channel_id=1, source_target_pairs={{0,8},{8,0},{16,24},{24,16},{1,9},{9,1},{17,25},{25,17},{2,10},{10... | collective-permute-start | bytes 196616 | tf_op jit(solution)/shard_map/ppermute | solution.py:52
  32.6 2.3 %collective-permute-done.5.second_ref = bf16[128,256]{1,0:T(8,128)(2,1)S(1)} collective-permute-done((bf16[128,256]{1,0:T(8,128)(2,1)S(1)}, bf16[128,256]{1,0:T(8,128)(2,1)S(1)}, u32[]{:S(2)}, u32[]{:S(2)}) %collective-permute-start.5) | collective-permute-done | bytes 65568 | tf_op jit(solution)/shard_map/ppermute | solution.py:52
  34.9 3.0 %collective-permute-start.6 = (bf16[128,256]{1,0:T(8,128)(2,1)S(1)}, bf16[128,256]{1,0:T(8,128)(2,1)S(1)}, u32[]{:S(2)}, u32[]{:S(2)}) collective-permute-start(bf16[128,256]{1,0:T(8,128)(2,1)S(1)} %merge_groups.1.refs_1_), channel_id=1, source_target_pairs={{0,16},{8,24},{16,0},{24,8},{1,17},{9,25},{17,1},{25,9},{2,18},{10... | collective-permute-start | bytes 196616 | tf_op jit(solution)/shard_map/ppermute | solution.py:52
  37.9 2.1 %tables.1 = (bf16[4,1024,768]{2,1,0:T(8,128)(2,1)S(1)}, bf16[4,768,1024]{2,1,0:T(8,128)(2,1)S(1)}) custom-call(s32[8,12,512]{2,1,0:T(8,128)S(1)} %get-tuple-element.36.codes_ref), custom_call_target="tpu_custom_call" | custom-call | tf_op jit(solution)/shard_map/tables/pallas_call | solution.py:502
  41.0 1.7 %cross_near.1 = (f32[96,768]{1,0:T(8,128)S(1)}, bf16[3,128,256]{2,1,0:T(8,128)(2,1)S(1)}, f32[24,256]{1,0:T(8,128)S(1)}) custom-call(s32[8,12,512]{2,1,0:T(8,128)S(1)} %get-tuple-element.36.codes_ref, bf16[4,768,1024]{2,1,0:T(8,128)(2,1)S(1)} %get-tuple-element.37.refs_0_, bf16[128,256]{1,0:T(8,128)(2,1)S(1)} %merge_groups.1.refs_1_, ...), custom_call_target="tpu_custom_call" | custom-call | tf_op jit(solution)/shard_map/cross_near/pallas_call | solution.py:407
  43.5 1.7 %collective-permute-start.15 = (bf16[96,768]{1,0:T(8,128)(2,1)S(1)}, bf16[96,768]{1,0:T(8,128)(2,1)S(1)}, u32[]{:S(2)}, u32[]{:S(2)}) collective-permute-start(bf16[96,768]{1,0:T(8,128)(2,1)S(1)} %cross_far.1), channel_id=1, source_target_pairs={{0,8},{8,0},{16,24},{24,16},{1,9},{9,1},{17,25},{25,17},{2,10},{10... | collective-permute-start | bytes 442376 | tf_op jit(solution)/shard_map/ppermute | solution.py:52
  45.2 1.8 %turn_rows.1.refs_8_ = bf16[4,768,1024]{2,1,0:T(8,128)(2,1)S(1)} custom-call(bf16[512,768]{1,0:T(8,128)(2,1)S(1)} %residual.1.residual_ref.refs_3_.refs_0_.refs_6_, bf16[512,768]{1,0:T(8,128)(2,1)S(1)} %collective-permute-done.refs_4_.refs_1_.refs_7_, bf16[512,768]{1,0:T(8,128)(2,1)S(1)} %collective-permute-done.7.refs_5_.refs_2_.refs_8_, ...), custom_call_target="tpu_custom_call" | custom-call | tf_op jit(solution)/shard_map/turn_rows/pallas_call | solution.py:518
  47.0 2.5 %collective-permute-done.15 = bf16[96,768]{1,0:T(8,128)(2,1)S(1)} collective-permute-done((bf16[96,768]{1,0:T(8,128)(2,1)S(1)}, bf16[96,768]{1,0:T(8,128)(2,1)S(1)}, u32[]{:S(2)}, u32[]{:S(2)}) %collective-permute-start.15) | collective-permute-done | bytes 147488 | tf_op jit(solution)/shard_map/ppermute | solution.py:52
  49.6 3.1 %collective-permute-start.16 = (bf16[96,768]{1,0:T(8,128)(2,1)S(1)}, bf16[96,768]{1,0:T(8,128)(2,1)S(1)}, u32[]{:S(2)}, u32[]{:S(2)}) collective-permute-start(bf16[96,768]{1,0:T(8,128)(2,1)S(1)} %add_convert_fusion.3), channel_id=1, source_target_pairs={{0,16},{8,24},{16,0},{24,8},{1,17},{9,25},{17,1},{25,9},{2,18},{10... | collective-permute-start | bytes 442376 | tf_op jit(solution)/shard_map/ppermute | solution.py:52
  52.7 6.8 %collective-permute-done.16 = bf16[96,768]{1,0:T(8,128)(2,1)S(1)} collective-permute-done((bf16[96,768]{1,0:T(8,128)(2,1)S(1)}, bf16[96,768]{1,0:T(8,128)(2,1)S(1)}, u32[]{:S(2)}, u32[]{:S(2)}) %collective-permute-start.16) | collective-permute-done | bytes 147488 | tf_op jit(solution)/shard_map/ppermute | solution.py:52
  59.5 2.5 %collective-permute-start.22 = (bf16[96,768]{1,0:T(8,128)(2,1)S(1)}, bf16[96,768]{1,0:T(8,128)(2,1)S(1)}, u32[]{:S(2)}, u32[]{:S(2)}) collective-permute-start(bf16[96,768]{1,0:T(8,128)(2,1)S(1)} %add_convert_fusion.2.refs_0_), channel_id=1, source_target_pairs={{0,6},{1,7},{2,4},{3,5},{4,2},{5,3},{6,0},{7,1},{8,14},{9,15},{10,... | collective-permute-start | bytes 442376 | tf_op jit(solution)/shard_map/ppermute | solution.py:52
  63.0 3.5 %collective-permute-done.22.refs_6_ = bf16[96,768]{1,0:T(8,128)(2,1)S(1)} collective-permute-done((bf16[96,768]{1,0:T(8,128)(2,1)S(1)}, bf16[96,768]{1,0:T(8,128)(2,1)S(1)}, u32[]{:S(2)}, u32[]{:S(2)}) %collective-permute-start.22) | collective-permute-done | bytes 147488 | tf_op jit(solution)/shard_map/ppermute | solution.py:52
  66.6 1.9 %collective-permute-done.20.refs_4_ = bf16[96,768]{1,0:T(8,128)(2,1)S(1)} collective-permute-done((bf16[96,768]{1,0:T(8,128)(2,1)S(1)}, bf16[96,768]{1,0:T(8,128)(2,1)S(1)}, u32[]{:S(2)}, u32[]{:S(2)}) %collective-permute-start.20) | collective-permute-done | bytes 147488 | tf_op jit(solution)/shard_map/ppermute | solution.py:52
  70.1 5.1 %next_sums.1.refs_1_ = bf16[96,256]{1,0:T(8,128)(2,1)S(1)} custom-call(s32[8,12,512]{2,1,0:T(8,128)S(1)} %get-tuple-element.36.codes_ref, bf16[96,768]{1,0:T(8,128)(2,1)S(1)} %add_convert_fusion.2.refs_0_, bf16[96,768]{1,0:T(8,128)(2,1)S(1)} %collective-permute-done.17.refs_1_, bf16[96,768]{1,0:T(8,128)(2,1)S(1)} %collective-permute-done.18.refs_2_, ...), custom_call_target="tpu_custom_call" | custom-call | tf_op jit(solution)/shard_map/next_sums/pallas_call | solution.py:577
  75.3 4.4 %collective-permute-start.26 = (bf16[96,256]{1,0:T(8,128)(2,1)S(1)}, bf16[96,256]{1,0:T(8,128)(2,1)S(1)}, u32[]{:S(2)}, u32[]{:S(2)}) collective-permute-start(bf16[96,256]{1,0:T(8,128)(2,1)S(1)} %next_sums.1.refs_1_), channel_id=1, source_target_pairs={{0,24},{8,16},{16,8},{24,0},{1,25},{9,17},{17,9},{25,1},{2,26},{10... | collective-permute-start | bytes 147464 | tf_op jit(solution)/shard_map/ppermute | solution.py:52
  80.3 1.9 %collective-permute-done.26.refs_4_ = bf16[96,256]{1,0:T(8,128)(2,1)S(1)} collective-permute-done((bf16[96,256]{1,0:T(8,128)(2,1)S(1)}, bf16[96,256]{1,0:T(8,128)(2,1)S(1)}, u32[]{:S(2)}, u32[]{:S(2)}) %collective-permute-start.26) | collective-permute-done | bytes 49184 | tf_op jit(solution)/shard_map/ppermute | solution.py:52
  82.1 2.5 %collective-permute-done.25.refs_3_ = bf16[96,256]{1,0:T(8,128)(2,1)S(1)} collective-permute-done((bf16[96,256]{1,0:T(8,128)(2,1)S(1)}, bf16[96,256]{1,0:T(8,128)(2,1)S(1)}, u32[]{:S(2)}, u32[]{:S(2)}) %collective-permute-start.25) | collective-permute-done | bytes 49184 | tf_op jit(solution)/shard_map/ppermute | solution.py:52
  84.7 2.2 %cross.1 = (bf16[96,768]{1,0:T(8,128)(2,1)S(1)}, f32[96,256]{1,0:T(8,128)S(1)}) custom-call(s32[8,12,512]{2,1,0:T(8,128)S(1)} %get-tuple-element.36.codes_ref, bf16[4,768,1024]{2,1,0:T(8,128)(2,1)S(1)} %get-tuple-element.37.refs_0_, bf16[96,256]{1,0:T(8,128)(2,1)S(1)} %next_sums.1.refs_1_, bf16[96,256]{1,0:T(8,128)(2,1)S(1)} %collective-permute-done.24.refs_2_, ...), custom_call_target="tpu_custom_call" | custom-call | tf_op jit(solution)/shard_map/cross/pallas_call | solution.py:461
  89.2 3.0 %collective-permute-done.27 = bf16[96,768]{1,0:T(8,128)(2,1)S(1)} collective-permute-done((bf16[96,768]{1,0:T(8,128)(2,1)S(1)}, bf16[96,768]{1,0:T(8,128)(2,1)S(1)}, u32[]{:S(2)}, u32[]{:S(2)}) %collective-permute-start.27) | collective-permute-done | bytes 147488 | tf_op jit(solution)/shard_map/ppermute | solution.py:52
  92.2 2.0 %collective-permute-start.28 = (bf16[96,768]{1,0:T(8,128)(2,1)S(1)}, bf16[96,768]{1,0:T(8,128)(2,1)S(1)}, u32[]{:S(2)}, u32[]{:S(2)}) collective-permute-start(bf16[96,768]{1,0:T(8,128)(2,1)S(1)} %add_convert_fusion.1), channel_id=1, source_target_pairs={{0,16},{8,24},{16,0},{24,8},{1,17},{9,25},{17,1},{25,9},{2,18},{10... | collective-permute-start | bytes 442376 | tf_op jit(solution)/shard_map/ppermute | solution.py:52
  94.2 5.7 %collective-permute-done.28 = bf16[96,768]{1,0:T(8,128)(2,1)S(1)} collective-permute-done((bf16[96,768]{1,0:T(8,128)(2,1)S(1)}, bf16[96,768]{1,0:T(8,128)(2,1)S(1)}, u32[]{:S(2)}, u32[]{:S(2)}) %collective-permute-start.28) | collective-permute-done | bytes 147488 | tf_op jit(solution)/shard_map/ppermute | solution.py:52
  100.0 1.8 %collective-permute-start.34 = (bf16[96,768]{1,0:T(8,128)(2,1)S(1)}, bf16[96,768]{1,0:T(8,128)(2,1)S(1)}, u32[]{:S(2)}, u32[]{:S(2)}) collective-permute-start(bf16[96,768]{1,0:T(8,128)(2,1)S(1)} %add_convert_fusion.refs_0_), channel_id=1, source_target_pairs={{0,6},{1,7},{2,4},{3,5},{4,2},{5,3},{6,0},{7,1},{8,14},{9,15},{10,... | collective-permute-start | bytes 442376 | tf_op jit(solution)/shard_map/ppermute | solution.py:52
  103.5 2.6 %collective-permute-done.34.refs_6_ = bf16[96,768]{1,0:T(8,128)(2,1)S(1)} collective-permute-done((bf16[96,768]{1,0:T(8,128)(2,1)S(1)}, bf16[96,768]{1,0:T(8,128)(2,1)S(1)}, u32[]{:S(2)}, u32[]{:S(2)}) %collective-permute-start.34) | collective-permute-done | bytes 147488 | tf_op jit(solution)/shard_map/ppermute | solution.py:52
  109.5 5.0 %final.1 = bf16[512,768]{1,0:T(8,128)(2,1)} custom-call(s32[1]{0:T(128)} %bitcast.place_ref, bf16[512,768]{1,0:T(8,128)(2,1)S(1)} %residual.1.residual_ref.refs_3_.refs_0_.refs_6_, bf16[96,768]{1,0:T(8,128)(2,1)S(1)} %add_convert_fusion.refs_0_, bf16[96,768]{1,0:T(8,128)(2,1)S(1)} %collective-permute-done.29.refs_1_, ...), custom_call_target="tpu_custom_call" | custom-call | tf_op jit(solution)/shard_map/final/pallas_call | solution.py:603
  (73 shorter events, 21.5 us)
Async XLA Ops:
  2.7 4.6 %collective-permute-start = (bf16[512,768]{1,0:T(8,128)(2,1)S(1)}, bf16[512,768]{1,0:T(8,128)(2,1)S(1)}, u32[]{:S(2)}, u32[]{:S(2)}) collective-permute-start(bf16[512,768]{1,0:T(8,128)(2,1)S(1)} %residual.1.residual_ref.refs_3_.refs_0_.refs_6_), channel_id=1, source_target_pairs={{0,1},{1,0},{2,3},{3,2},{4,5},{5,4},{6,7},{7,6},{8,9},{9,8},{10,11... | collective-permute-start | bytes 2359304 | tf_op jit(solution)/shard_map/ppermute | solution.py:52
  3.2 21.0 %collective-permute-start.9 = (bf16[512,768]{1,0:T(8,128)(2,1)S(1)}, bf16[512,768]{1,0:T(8,128)(2,1)S(1)}, u32[]{:S(2)}, u32[]{:S(2)}) collective-permute-start(bf16[512,768]{1,0:T(8,128)(2,1)S(1)} %residual.1.residual_ref.refs_3_.refs_0_.refs_6_), channel_id=1, source_target_pairs={{0,4},{1,5},{2,6},{3,7},{4,0},{5,1},{6,2},{7,3},{8,12},{9,13},{10,... | collective-permute-start | bytes 2359304 | tf_op jit(solution)/shard_map/ppermute | solution.py:52
  5.8 20.4 %collective-permute-start.7 = (bf16[512,768]{1,0:T(8,128)(2,1)S(1)}, bf16[512,768]{1,0:T(8,128)(2,1)S(1)}, u32[]{:S(2)}, u32[]{:S(2)}) collective-permute-start(bf16[512,768]{1,0:T(8,128)(2,1)S(1)} %residual.1.residual_ref.refs_3_.refs_0_.refs_6_), channel_id=1, source_target_pairs={{0,2},{1,3},{2,0},{3,1},{4,6},{5,7},{6,4},{7,5},{8,10},{9,11},{10,... | collective-permute-start | bytes 2359304 | tf_op jit(solution)/shard_map/ppermute | solution.py:52
  12.4 1.7 %collective-permute-start.1 = (bf16[4,160,256]{2,1,0:T(8,128)(2,1)S(1)}, bf16[4,160,256]{2,1,0:T(8,128)(2,1)S(1)}, u32[]{:S(2)}, u32[]{:S(2)}) collective-permute-start(bf16[4,160,256]{2,1,0:T(8,128)(2,1)S(1)} %get-tuple-element.29), channel_id=1, source_target_pairs={{0,1},{1,0},{2,3},{3,2},{4,5},{5,4},{6,7},{7,6},{8,9},{9,8},{10,11... | collective-permute-start | bytes 983048 | tf_op jit(solution)/shard_map/ppermute | solution.py:52
  14.2 14.1 %collective-permute-start.2 = (bf16[192,256]{1,0:T(8,128)(2,1)S(1)}, bf16[192,256]{1,0:T(8,128)(2,1)S(1)}, u32[]{:S(2)}, u32[]{:S(2)}) collective-permute-start(bf16[192,256]{1,0:T(8,128)(2,1)S(1)} %get-tuple-element.31), channel_id=1, source_target_pairs={{0,2},{1,3},{2,0},{3,1},{4,6},{5,7},{6,4},{7,5},{8,10},{9,11},{10,... | collective-permute-start | bytes 294920 | tf_op jit(solution)/shard_map/ppermute | solution.py:52
  15.0 13.3 %collective-permute-start.3 = (bf16[192,256]{1,0:T(8,128)(2,1)S(1)}, bf16[192,256]{1,0:T(8,128)(2,1)S(1)}, u32[]{:S(2)}, u32[]{:S(2)}) collective-permute-start(bf16[192,256]{1,0:T(8,128)(2,1)S(1)} %get-tuple-element.32), channel_id=1, source_target_pairs={{0,4},{1,5},{2,6},{3,7},{4,0},{5,1},{6,2},{7,3},{8,12},{9,13},{10,... | collective-permute-start | bytes 294920 | tf_op jit(solution)/shard_map/ppermute | solution.py:52
  16.5 13.4 %collective-permute-start.4 = (bf16[192,256]{1,0:T(8,128)(2,1)S(1)}, bf16[192,256]{1,0:T(8,128)(2,1)S(1)}, u32[]{:S(2)}, u32[]{:S(2)}) collective-permute-start(bf16[192,256]{1,0:T(8,128)(2,1)S(1)} %get-tuple-element.33), channel_id=1, source_target_pairs={{0,6},{1,7},{2,4},{3,5},{4,2},{5,3},{6,0},{7,1},{8,14},{9,15},{10,... | collective-permute-start | bytes 294920 | tf_op jit(solution)/shard_map/ppermute | solution.py:52
  24.2 16.3 %collective-permute-start.12 = (bf16[256,768]{1,0:T(8,128)(2,1)S(1)}, bf16[256,768]{1,0:T(8,128)(2,1)S(1)}, u32[]{:S(2)}, u32[]{:S(2)}) collective-permute-start(bf16[256,768]{1,0:T(8,128)(2,1)S(1)} %slice.9), channel_id=1, source_target_pairs={{0,2},{1,3},{2,0},{3,1},{4,6},{5,7},{6,4},{7,5},{8,10},{9,11},{10,... | collective-permute-start | bytes 1179656 | tf_op jit(solution)/shard_map/ppermute | solution.py:52
  26.2 14.3 %collective-permute-start.11 = (bf16[256,768]{1,0:T(8,128)(2,1)S(1)}, bf16[256,768]{1,0:T(8,128)(2,1)S(1)}, u32[]{:S(2)}, u32[]{:S(2)}) collective-permute-start(bf16[256,768]{1,0:T(8,128)(2,1)S(1)} %slice.8), channel_id=1, source_target_pairs={{0,4},{1,5},{2,6},{3,7},{4,0},{5,1},{6,2},{7,3},{8,12},{9,13},{10,... | collective-permute-start | bytes 1179656 | tf_op jit(solution)/shard_map/ppermute | solution.py:52
  30.0 11.1 %collective-permute-start.8 = (bf16[512,768]{1,0:T(8,128)(2,1)S(1)}, bf16[512,768]{1,0:T(8,128)(2,1)S(1)}, u32[]{:S(2)}, u32[]{:S(2)}) collective-permute-start(bf16[512,768]{1,0:T(8,128)(2,1)S(1)} %collective-permute-done.7.refs_5_.refs_2_.refs_8_), channel_id=1, source_target_pairs={{0,1},{1,0},{2,3},{3,2},{4,5},{5,4},{6,7},{7,6},{8,9},{9,8},{10,11... | collective-permute-start | bytes 2359304 | tf_op jit(solution)/shard_map/ppermute | solution.py:52
  30.0 11.0 %collective-permute-start.10 = (bf16[512,768]{1,0:T(8,128)(2,1)S(1)}, bf16[512,768]{1,0:T(8,128)(2,1)S(1)}, u32[]{:S(2)}, u32[]{:S(2)}) collective-permute-start(bf16[512,768]{1,0:T(8,128)(2,1)S(1)} %collective-permute-done.9.refs_7_.refs_4_.refs_10_), channel_id=1, source_target_pairs={{0,1},{1,0},{2,3},{3,2},{4,5},{5,4},{6,7},{7,6},{8,9},{9,8},{10,11... | collective-permute-start | bytes 2359304 | tf_op jit(solution)/shard_map/ppermute | solution.py:52
  30.5 4.4 %collective-permute-start.5 = (bf16[128,256]{1,0:T(8,128)(2,1)S(1)}, bf16[128,256]{1,0:T(8,128)(2,1)S(1)}, u32[]{:S(2)}, u32[]{:S(2)}) collective-permute-start(bf16[128,256]{1,0:T(8,128)(2,1)S(1)} %get-tuple-element.35.first_ref), channel_id=1, source_target_pairs={{0,8},{8,0},{16,24},{24,16},{1,9},{9,1},{17,25},{25,17},{2,10},{10... | collective-permute-start | bytes 196616 | tf_op jit(solution)/shard_map/ppermute | solution.py:52
  34.9 5.6 %collective-permute-start.6 = (bf16[128,256]{1,0:T(8,128)(2,1)S(1)}, bf16[128,256]{1,0:T(8,128)(2,1)S(1)}, u32[]{:S(2)}, u32[]{:S(2)}) collective-permute-start(bf16[128,256]{1,0:T(8,128)(2,1)S(1)} %merge_groups.1.refs_1_), channel_id=1, source_target_pairs={{0,16},{8,24},{16,0},{24,8},{1,17},{9,25},{17,1},{25,9},{2,18},{10... | collective-permute-start | bytes 196616 | tf_op jit(solution)/shard_map/ppermute | solution.py:52
  40.5 2.3 %collective-permute-start.13 = (bf16[256,768]{1,0:T(8,128)(2,1)S(1)}, bf16[256,768]{1,0:T(8,128)(2,1)S(1)}, u32[]{:S(2)}, u32[]{:S(2)}) collective-permute-start(bf16[256,768]{1,0:T(8,128)(2,1)S(1)} %collective-permute-done.11.refs_1_.refs_6_.refs_12_), channel_id=1, source_target_pairs={{0,1},{1,0},{2,3},{3,2},{4,5},{5,4},{6,7},{7,6},{8,9},{9,8},{10,11... | collective-permute-start | bytes 1179656 | tf_op jit(solution)/shard_map/ppermute | solution.py:52
  40.5 2.3 %collective-permute-start.14 = (bf16[256,768]{1,0:T(8,128)(2,1)S(1)}, bf16[256,768]{1,0:T(8,128)(2,1)S(1)}, u32[]{:S(2)}, u32[]{:S(2)}) collective-permute-start(bf16[256,768]{1,0:T(8,128)(2,1)S(1)} %collective-permute-done.12.refs_2_.refs_7_.refs_13_), channel_id=1, source_target_pairs={{0,1},{1,0},{2,3},{3,2},{4,5},{5,4},{6,7},{7,6},{8,9},{9,8},{10,11... | collective-permute-start | bytes 1179656 | tf_op jit(solution)/shard_map/ppermute | solution.py:52
  43.5 6.0 %collective-permute-start.15 = (bf16[96,768]{1,0:T(8,128)(2,1)S(1)}, bf16[96,768]{1,0:T(8,128)(2,1)S(1)}, u32[]{:S(2)}, u32[]{:S(2)}) collective-permute-start(bf16[96,768]{1,0:T(8,128)(2,1)S(1)} %cross_far.1), channel_id=1, source_target_pairs={{0,8},{8,0},{16,24},{24,16},{1,9},{9,1},{17,25},{25,17},{2,10},{10... | collective-permute-start | bytes 442376 | tf_op jit(solution)/shard_map/ppermute | solution.py:52
  49.6 9.9 %collective-permute-start.16 = (bf16[96,768]{1,0:T(8,128)(2,1)S(1)}, bf16[96,768]{1,0:T(8,128)(2,1)S(1)}, u32[]{:S(2)}, u32[]{:S(2)}) collective-permute-start(bf16[96,768]{1,0:T(8,128)(2,1)S(1)} %add_convert_fusion.3), channel_id=1, source_target_pairs={{0,16},{8,24},{16,0},{24,8},{1,17},{9,25},{17,1},{25,9},{2,18},{10... | collective-permute-start | bytes 442376 | tf_op jit(solution)/shard_map/ppermute | solution.py:52
  59.5 7.1 %collective-permute-start.22 = (bf16[96,768]{1,0:T(8,128)(2,1)S(1)}, bf16[96,768]{1,0:T(8,128)(2,1)S(1)}, u32[]{:S(2)}, u32[]{:S(2)}) collective-permute-start(bf16[96,768]{1,0:T(8,128)(2,1)S(1)} %add_convert_fusion.2.refs_0_), channel_id=1, source_target_pairs={{0,6},{1,7},{2,4},{3,5},{4,2},{5,3},{6,0},{7,1},{8,14},{9,15},{10,... | collective-permute-start | bytes 442376 | tf_op jit(solution)/shard_map/ppermute | solution.py:52
  62.0 6.5 %collective-permute-start.20 = (bf16[96,768]{1,0:T(8,128)(2,1)S(1)}, bf16[96,768]{1,0:T(8,128)(2,1)S(1)}, u32[]{:S(2)}, u32[]{:S(2)}) collective-permute-start(bf16[96,768]{1,0:T(8,128)(2,1)S(1)} %add_convert_fusion.2.refs_0_), channel_id=1, source_target_pairs={{0,4},{1,5},{2,6},{3,7},{4,0},{5,1},{6,2},{7,3},{8,12},{9,13},{10,... | collective-permute-start | bytes 442376 | tf_op jit(solution)/shard_map/ppermute | solution.py:52
  62.5 6.1 %collective-permute-start.18 = (bf16[96,768]{1,0:T(8,128)(2,1)S(1)}, bf16[96,768]{1,0:T(8,128)(2,1)S(1)}, u32[]{:S(2)}, u32[]{:S(2)}) collective-permute-start(bf16[96,768]{1,0:T(8,128)(2,1)S(1)} %add_convert_fusion.2.refs_0_), channel_id=1, source_target_pairs={{0,2},{1,3},{2,0},{3,1},{4,6},{5,7},{6,4},{7,5},{8,10},{9,11},{10,... | collective-permute-start | bytes 442376 | tf_op jit(solution)/shard_map/ppermute | solution.py:52
  63.0 6.0 %collective-permute-start.17 = (bf16[96,768]{1,0:T(8,128)(2,1)S(1)}, bf16[96,768]{1,0:T(8,128)(2,1)S(1)}, u32[]{:S(2)}, u32[]{:S(2)}) collective-permute-start(bf16[96,768]{1,0:T(8,128)(2,1)S(1)} %add_convert_fusion.2.refs_0_), channel_id=1, source_target_pairs={{0,1},{1,0},{2,3},{3,2},{4,5},{5,4},{6,7},{7,6},{8,9},{9,8},{10,11... | collective-permute-start | bytes 442376 | tf_op jit(solution)/shard_map/ppermute | solution.py:52
  66.6 2.4 %collective-permute-start.23 = (bf16[96,768]{1,0:T(8,128)(2,1)S(1)}, bf16[96,768]{1,0:T(8,128)(2,1)S(1)}, u32[]{:S(2)}, u32[]{:S(2)}) collective-permute-start(bf16[96,768]{1,0:T(8,128)(2,1)S(1)} %collective-permute-done.22.refs_6_), channel_id=1, source_target_pairs={{0,1},{1,0},{2,3},{3,2},{4,5},{5,4},{6,7},{7,6},{8,9},{9,8},{10,11... | collective-permute-start | bytes 442376 | tf_op jit(solution)/shard_map/ppermute | solution.py:52
  75.3 6.9 %collective-permute-start.26 = (bf16[96,256]{1,0:T(8,128)(2,1)S(1)}, bf16[96,256]{1,0:T(8,128)(2,1)S(1)}, u32[]{:S(2)}, u32[]{:S(2)}) collective-permute-start(bf16[96,256]{1,0:T(8,128)(2,1)S(1)} %next_sums.1.refs_1_), channel_id=1, source_target_pairs={{0,24},{8,16},{16,8},{24,0},{1,25},{9,17},{17,9},{25,1},{2,26},{10... | collective-permute-start | bytes 147464 | tf_op jit(solution)/shard_map/ppermute | solution.py:52
  79.6 5.0 %collective-permute-start.25 = (bf16[96,256]{1,0:T(8,128)(2,1)S(1)}, bf16[96,256]{1,0:T(8,128)(2,1)S(1)}, u32[]{:S(2)}, u32[]{:S(2)}) collective-permute-start(bf16[96,256]{1,0:T(8,128)(2,1)S(1)} %next_sums.1.refs_1_), channel_id=1, source_target_pairs={{0,16},{8,24},{16,0},{24,8},{1,17},{9,25},{17,1},{25,9},{2,18},{10... | collective-permute-start | bytes 147464 | tf_op jit(solution)/shard_map/ppermute | solution.py:52
  79.6 5.1 %collective-permute-start.24 = (bf16[96,256]{1,0:T(8,128)(2,1)S(1)}, bf16[96,256]{1,0:T(8,128)(2,1)S(1)}, u32[]{:S(2)}, u32[]{:S(2)}) collective-permute-start(bf16[96,256]{1,0:T(8,128)(2,1)S(1)} %next_sums.1.refs_1_), channel_id=1, source_target_pairs={{0,8},{8,0},{16,24},{24,16},{1,9},{9,1},{17,25},{25,17},{2,10},{10... | collective-permute-start | bytes 147464 | tf_op jit(solution)/shard_map/ppermute | solution.py:52
  87.0 5.2 %collective-permute-start.27 = (bf16[96,768]{1,0:T(8,128)(2,1)S(1)}, bf16[96,768]{1,0:T(8,128)(2,1)S(1)}, u32[]{:S(2)}, u32[]{:S(2)}) collective-permute-start(bf16[96,768]{1,0:T(8,128)(2,1)S(1)} %get-tuple-element.49), channel_id=1, source_target_pairs={{0,8},{8,0},{16,24},{24,16},{1,9},{9,1},{17,25},{25,17},{2,10},{10... | collective-permute-start | bytes 442376 | tf_op jit(solution)/shard_map/ppermute | solution.py:52
  92.2 7.7 %collective-permute-start.28 = (bf16[96,768]{1,0:T(8,128)(2,1)S(1)}, bf16[96,768]{1,0:T(8,128)(2,1)S(1)}, u32[]{:S(2)}, u32[]{:S(2)}) collective-permute-start(bf16[96,768]{1,0:T(8,128)(2,1)S(1)} %add_convert_fusion.1), channel_id=1, source_target_pairs={{0,16},{8,24},{16,0},{24,8},{1,17},{9,25},{17,1},{25,9},{2,18},{10... | collective-permute-start | bytes 442376 | tf_op jit(solution)/shard_map/ppermute | solution.py:52
  100.0 6.2 %collective-permute-start.34 = (bf16[96,768]{1,0:T(8,128)(2,1)S(1)}, bf16[96,768]{1,0:T(8,128)(2,1)S(1)}, u32[]{:S(2)}, u32[]{:S(2)}) collective-permute-start(bf16[96,768]{1,0:T(8,128)(2,1)S(1)} %add_convert_fusion.refs_0_), channel_id=1, source_target_pairs={{0,6},{1,7},{2,4},{3,5},{4,2},{5,3},{6,0},{7,1},{8,14},{9,15},{10,... | collective-permute-start | bytes 442376 | tf_op jit(solution)/shard_map/ppermute | solution.py:52
  101.8 5.9 %collective-permute-start.32 = (bf16[96,768]{1,0:T(8,128)(2,1)S(1)}, bf16[96,768]{1,0:T(8,128)(2,1)S(1)}, u32[]{:S(2)}, u32[]{:S(2)}) collective-permute-start(bf16[96,768]{1,0:T(8,128)(2,1)S(1)} %add_convert_fusion.refs_0_), channel_id=1, source_target_pairs={{0,4},{1,5},{2,6},{3,7},{4,0},{5,1},{6,2},{7,3},{8,12},{9,13},{10,... | collective-permute-start | bytes 442376 | tf_op jit(solution)/shard_map/ppermute | solution.py:52
  103.0 5.1 %collective-permute-start.30 = (bf16[96,768]{1,0:T(8,128)(2,1)S(1)}, bf16[96,768]{1,0:T(8,128)(2,1)S(1)}, u32[]{:S(2)}, u32[]{:S(2)}) collective-permute-start(bf16[96,768]{1,0:T(8,128)(2,1)S(1)} %add_convert_fusion.refs_0_), channel_id=1, source_target_pairs={{0,2},{1,3},{2,0},{3,1},{4,6},{5,7},{6,4},{7,5},{8,10},{9,11},{10,... | collective-permute-start | bytes 442376 | tf_op jit(solution)/shard_map/ppermute | solution.py:52
  103.5 4.7 %collective-permute-start.29 = (bf16[96,768]{1,0:T(8,128)(2,1)S(1)}, bf16[96,768]{1,0:T(8,128)(2,1)S(1)}, u32[]{:S(2)}, u32[]{:S(2)}) collective-permute-start(bf16[96,768]{1,0:T(8,128)(2,1)S(1)} %add_convert_fusion.refs_0_), channel_id=1, source_target_pairs={{0,1},{1,0},{2,3},{3,2},{4,5},{5,4},{6,7},{7,6},{8,9},{9,8},{10,11... | collective-permute-start | bytes 442376 | tf_op jit(solution)/shard_map/ppermute | solution.py:52
  106.1 2.0 %collective-permute-start.35 = (bf16[96,768]{1,0:T(8,128)(2,1)S(1)}, bf16[96,768]{1,0:T(8,128)(2,1)S(1)}, u32[]{:S(2)}, u32[]{:S(2)}) collective-permute-start(bf16[96,768]{1,0:T(8,128)(2,1)S(1)} %collective-permute-done.34.refs_6_), channel_id=1, source_target_pairs={{0,1},{1,0},{2,3},{3,2},{4,5},{5,4},{6,7},{7,6},{8,9},{9,8},{10,11... | collective-permute-start | bytes 442376 | tf_op jit(solution)/shard_map/ppermute | solution.py:52
  (9 other events, 15.6 us)

commit v9 on v8

--- a/solution.py
+++ b/solution.py
@@ -586,7 +586,7 @@
 
 
 def final_kernel(size, place_ref, residual_ref, *refs):
-    parts, out_ref, whole = refs[:size], refs[size], refs[size + 1]
+    parts, (out_hbm, whole, out_ref, sems) = refs[:size], refs[size:]
     height = parts[0].shape[0]
     for k, ref in enumerate(parts):
         at = pl.multiple_of((place_ref[0] ^ k) * height, 16 if whole.dtype == BF16 else 8)
@@ -594,7 +594,15 @@
     xb = first_step(whole[...].astype(BF16)).astype(BF16)
     once = mm(residual_ref[...], xb, NT)
     less = mm(mm(once.astype(BF16), xb).astype(BF16), xb, NT)
-    out_ref[...] = (1.5 * once - 0.5 * less).astype(BF16)
+    half = out_ref.shape[0] // 2
+    copies = []
+    for h in range(2):
+        rows = slice(h * half, (h + 1) * half)
+        out_ref[rows, :] = (1.5 * once[rows] - 0.5 * less[rows]).astype(BF16)
+        copies.append(pltpu.make_async_copy(out_ref.at[pl.ds(h * half, half)], out_hbm.at[pl.ds(h * half, half)], sems.at[h]))
+        copies[-1].start()
+    for copy in copies:
+        copy.wait()
 
 
 def final_call(place, residual, blocks):
@@ -604,8 +612,8 @@
         functools.partial(final_kernel, len(blocks)),
         out_shape=jax.ShapeDtypeStruct((rows, width), BF16),
         in_specs=[smem_spec()] + [vmem_spec()] * (1 + len(blocks)),
-        out_specs=vmem_spec(),
-        scratch_shapes=[pltpu.VMEM((width, width), kind)],
+        out_specs=pl.BlockSpec(memory_space=pl.ANY),
+        scratch_shapes=[pltpu.VMEM((width, width), kind), pltpu.VMEM((rows, width), BF16), pltpu.SemaphoreType.DMA((2,))],
         compiler_params=params(),
         cost_estimate=cost(0),
         name="final",

time: 115 us -> 115 us (level)
  no operation moved by 1% of the time
where the time goes in v9:
time: 115 us
  waiting for transfers between devices  47.8 us (42%)
  starting transfers between devices  38.4 us (33%)
  Pallas kernels  23.2 us (20%)
  local copies, waits for them, and re-layouts  4.06 us (4%)
    ppermute x36, waiting for transfers between devices, swap(): return lax.ppermute(x, axis, [(i, i ^ bits) for i in range(size)])  47.8 us
    ppermute x36, starting transfers between devices, swap(): return lax.ppermute(x, axis, [(i, i ^ bits) for i in range(size)])  38.4 us
    pallas_call x1, Pallas kernels, next_sums_call(): pl.pallas_call(functools.partial(next_sums_kernel, held, bool(ready)), ou...  5.15 us
    pallas_call x1, Pallas kernels, final_call(): pl.pallas_call(functools.partial(final_kernel, len(blocks)), out_shape=ja...  4.97 us
    pallas_call x1, Pallas kernels, local_sums_call(): pl.pallas_call(functools.partial(local_sums_kernel, size), out_shape=(sha...  3.44 us
    unnamed x10, local copies, waits for them, and re-layouts  2.86 us
  transfers between devices with their start and end apart: 36, of which 23 were waited for; matrix products, arithmetic and copies ran while one was open for 1% of the time, Pallas kernels for 8%

profile of v9, /device:TPU:0, one launch (start us, length us, event | category | flops | bytes accessed | tf_op | source)
XLA Modules:
  0.0 114.6 jit_solution(12456155713835548531)
XLA Ops:
  3.2 2.6 %collective-permute-start.9 = (bf16[512,768]{1,0:T(8,128)(2,1)S(1)}, bf16[512,768]{1,0:T(8,128)(2,1)S(1)}, u32[]{:S(2)}, u32[]{:S(2)}) collective-permute-start(bf16[512,768]{1,0:T(8,128)(2,1)S(1)} %residual.1.residual_ref.refs_3_.refs_0_.refs_6_), channel_id=1, source_target_pairs={{0,4},{1,5},{2,6},{3,7},{4,0},{5,1},{6,2},{7,3},{8,12},{9,13},{10,... | collective-permute-start | bytes 2359304 | tf_op jit(solution)/shard_map/ppermute | solution.py:52
  7.3 1.7 %copy-done = f32[768,768]{1,0:T(8,128)S(1)} copy-done((f32[768,768]{1,0:T(8,128)S(1)}, f32[768,768]{1,0:T(8,128)}, u32[]{:S(2)}) %copy-start) | copy-done | bytes 2359320
  9.0 3.4 %local_sums.1 = (bf16[4,160,256]{2,1,0:T(8,128)(2,1)S(1)}, bf16[4,160,256]{2,1,0:T(8,128)(2,1)S(1)}) custom-call(s32[1]{0:T(128)} %bitcast.place_ref, f32[768,768]{1,0:T(8,128)S(1)} %copy-done, s32[96,512]{1,0:T(8,128)S(1)} %bitcast.6, bf16[512,768]{1,0:T(8,128)(2,1)S(1)} %residual.1.residual_ref.refs_3_.refs_0_.refs_6_), custom_call_target="tpu_custom_call" | custom-call | tf_op jit(solution)/shard_map/local_sums/pallas_call | solution.py:236
  12.5 1.6 %collective-permute-done.1.came_ref = bf16[4,160,256]{2,1,0:T(8,128)(2,1)S(1)} collective-permute-done((bf16[4,160,256]{2,1,0:T(8,128)(2,1)S(1)}, bf16[4,160,256]{2,1,0:T(8,128)(2,1)S(1)}, u32[]{:S(2)}, u32[]{:S(2)}) %collective-permute-start.1) | collective-permute-done | bytes 327712 | tf_op jit(solution)/shard_map/ppermute | solution.py:52
  17.8 6.4 %collective-permute-done.9.refs_7_.refs_4_.refs_10_ = bf16[512,768]{1,0:T(8,128)(2,1)S(1)} collective-permute-done((bf16[512,768]{1,0:T(8,128)(2,1)S(1)}, bf16[512,768]{1,0:T(8,128)(2,1)S(1)}, u32[]{:S(2)}, u32[]{:S(2)}) %collective-permute-start.9) | collective-permute-done | bytes 786464 | tf_op jit(solution)/shard_map/ppermute | solution.py:52
  24.2 2.0 %collective-permute-start.12 = (bf16[256,768]{1,0:T(8,128)(2,1)S(1)}, bf16[256,768]{1,0:T(8,128)(2,1)S(1)}, u32[]{:S(2)}, u32[]{:S(2)}) collective-permute-start(bf16[256,768]{1,0:T(8,128)(2,1)S(1)} %slice.9), channel_id=1, source_target_pairs={{0,2},{1,3},{2,0},{3,1},{4,6},{5,7},{6,4},{7,5},{8,10},{9,11},{10,... | collective-permute-start | bytes 1179656 | tf_op jit(solution)/shard_map/ppermute | solution.py:52
  26.2 1.6 %collective-permute-start.11 = (bf16[256,768]{1,0:T(8,128)(2,1)S(1)}, bf16[256,768]{1,0:T(8,128)(2,1)S(1)}, u32[]{:S(2)}, u32[]{:S(2)}) collective-permute-start(bf16[256,768]{1,0:T(8,128)(2,1)S(1)} %slice.8), channel_id=1, source_target_pairs={{0,4},{1,5},{2,6},{3,7},{4,0},{5,1},{6,2},{7,3},{8,12},{9,13},{10,... | collective-permute-start | bytes 1179656 | tf_op jit(solution)/shard_map/ppermute | solution.py:52
  28.3 1.6 %collective-permute-done.4.refs_3_ = bf16[192,256]{1,0:T(8,128)(2,1)S(1)} collective-permute-done((bf16[192,256]{1,0:T(8,128)(2,1)S(1)}, bf16[192,256]{1,0:T(8,128)(2,1)S(1)}, u32[]{:S(2)}, u32[]{:S(2)}) %collective-permute-start.4) | collective-permute-done | bytes 98336 | tf_op jit(solution)/shard_map/ppermute | solution.py:52
  30.5 2.0 %collective-permute-start.5 = (bf16[128,256]{1,0:T(8,128)(2,1)S(1)}, bf16[128,256]{1,0:T(8,128)(2,1)S(1)}, u32[]{:S(2)}, u32[]{:S(2)}) collective-permute-start(bf16[128,256]{1,0:T(8,128)(2,1)S(1)} %get-tuple-element.35.first_ref), channel_id=1, source_target_pairs={{0,8},{8,0},{16,24},{24,16},{1,9},{9,1},{17,25},{25,17},{2,10},{10... | collective-permute-start | bytes 196616 | tf_op jit(solution)/shard_map/ppermute | solution.py:52
  32.6 2.3 %collective-permute-done.5.second_ref = bf16[128,256]{1,0:T(8,128)(2,1)S(1)} collective-permute-done((bf16[128,256]{1,0:T(8,128)(2,1)S(1)}, bf16[128,256]{1,0:T(8,128)(2,1)S(1)}, u32[]{:S(2)}, u32[]{:S(2)}) %collective-permute-start.5) | collective-permute-done | bytes 65568 | tf_op jit(solution)/shard_map/ppermute | solution.py:52
  34.9 3.0 %collective-permute-start.6 = (bf16[128,256]{1,0:T(8,128)(2,1)S(1)}, bf16[128,256]{1,0:T(8,128)(2,1)S(1)}, u32[]{:S(2)}, u32[]{:S(2)}) collective-permute-start(bf16[128,256]{1,0:T(8,128)(2,1)S(1)} %merge_groups.1.refs_1_), channel_id=1, source_target_pairs={{0,16},{8,24},{16,0},{24,8},{1,17},{9,25},{17,1},{25,9},{2,18},{10... | collective-permute-start | bytes 196616 | tf_op jit(solution)/shard_map/ppermute | solution.py:52
  37.9 2.1 %tables.1 = (bf16[4,1024,768]{2,1,0:T(8,128)(2,1)S(1)}, bf16[4,768,1024]{2,1,0:T(8,128)(2,1)S(1)}) custom-call(s32[8,12,512]{2,1,0:T(8,128)S(1)} %get-tuple-element.36.codes_ref), custom_call_target="tpu_custom_call" | custom-call | tf_op jit(solution)/shard_map/tables/pallas_call | solution.py:502
  41.0 1.7 %cross_near.1 = (f32[96,768]{1,0:T(8,128)S(1)}, bf16[3,128,256]{2,1,0:T(8,128)(2,1)S(1)}, f32[24,256]{1,0:T(8,128)S(1)}) custom-call(s32[8,12,512]{2,1,0:T(8,128)S(1)} %get-tuple-element.36.codes_ref, bf16[4,768,1024]{2,1,0:T(8,128)(2,1)S(1)} %get-tuple-element.37.refs_0_, bf16[128,256]{1,0:T(8,128)(2,1)S(1)} %merge_groups.1.refs_1_, ...), custom_call_target="tpu_custom_call" | custom-call | tf_op jit(solution)/shard_map/cross_near/pallas_call | solution.py:407
  43.5 1.7 %collective-permute-start.15 = (bf16[96,768]{1,0:T(8,128)(2,1)S(1)}, bf16[96,768]{1,0:T(8,128)(2,1)S(1)}, u32[]{:S(2)}, u32[]{:S(2)}) collective-permute-start(bf16[96,768]{1,0:T(8,128)(2,1)S(1)} %cross_far.1), channel_id=1, source_target_pairs={{0,8},{8,0},{16,24},{24,16},{1,9},{9,1},{17,25},{25,17},{2,10},{10... | collective-permute-start | bytes 442376 | tf_op jit(solution)/shard_map/ppermute | solution.py:52
  45.2 1.8 %turn_rows.1.refs_8_ = bf16[4,768,1024]{2,1,0:T(8,128)(2,1)S(1)} custom-call(bf16[512,768]{1,0:T(8,128)(2,1)S(1)} %residual.1.residual_ref.refs_3_.refs_0_.refs_6_, bf16[512,768]{1,0:T(8,128)(2,1)S(1)} %collective-permute-done.refs_4_.refs_1_.refs_7_, bf16[512,768]{1,0:T(8,128)(2,1)S(1)} %collective-permute-done.7.refs_5_.refs_2_.refs_8_, ...), custom_call_target="tpu_custom_call" | custom-call | tf_op jit(solution)/shard_map/turn_rows/pallas_call | solution.py:518
  47.0 2.5 %collective-permute-done.15 = bf16[96,768]{1,0:T(8,128)(2,1)S(1)} collective-permute-done((bf16[96,768]{1,0:T(8,128)(2,1)S(1)}, bf16[96,768]{1,0:T(8,128)(2,1)S(1)}, u32[]{:S(2)}, u32[]{:S(2)}) %collective-permute-start.15) | collective-permute-done | bytes 147488 | tf_op jit(solution)/shard_map/ppermute | solution.py:52
  49.6 3.1 %collective-permute-start.16 = (bf16[96,768]{1,0:T(8,128)(2,1)S(1)}, bf16[96,768]{1,0:T(8,128)(2,1)S(1)}, u32[]{:S(2)}, u32[]{:S(2)}) collective-permute-start(bf16[96,768]{1,0:T(8,128)(2,1)S(1)} %add_convert_fusion.3), channel_id=1, source_target_pairs={{0,16},{8,24},{16,0},{24,8},{1,17},{9,25},{17,1},{25,9},{2,18},{10... | collective-permute-start | bytes 442376 | tf_op jit(solution)/shard_map/ppermute | solution.py:52
  52.7 6.8 %collective-permute-done.16 = bf16[96,768]{1,0:T(8,128)(2,1)S(1)} collective-permute-done((bf16[96,768]{1,0:T(8,128)(2,1)S(1)}, bf16[96,768]{1,0:T(8,128)(2,1)S(1)}, u32[]{:S(2)}, u32[]{:S(2)}) %collective-permute-start.16) | collective-permute-done | bytes 147488 | tf_op jit(solution)/shard_map/ppermute | solution.py:52
  59.5 2.5 %collective-permute-start.22 = (bf16[96,768]{1,0:T(8,128)(2,1)S(1)}, bf16[96,768]{1,0:T(8,128)(2,1)S(1)}, u32[]{:S(2)}, u32[]{:S(2)}) collective-permute-start(bf16[96,768]{1,0:T(8,128)(2,1)S(1)} %add_convert_fusion.2.refs_0_), channel_id=1, source_target_pairs={{0,6},{1,7},{2,4},{3,5},{4,2},{5,3},{6,0},{7,1},{8,14},{9,15},{10,... | collective-permute-start | bytes 442376 | tf_op jit(solution)/shard_map/ppermute | solution.py:52
  63.0 3.5 %collective-permute-done.22.refs_6_ = bf16[96,768]{1,0:T(8,128)(2,1)S(1)} collective-permute-done((bf16[96,768]{1,0:T(8,128)(2,1)S(1)}, bf16[96,768]{1,0:T(8,128)(2,1)S(1)}, u32[]{:S(2)}, u32[]{:S(2)}) %collective-permute-start.22) | collective-permute-done | bytes 147488 | tf_op jit(solution)/shard_map/ppermute | solution.py:52
  66.6 1.9 %collective-permute-done.20.refs_4_ = bf16[96,768]{1,0:T(8,128)(2,1)S(1)} collective-permute-done((bf16[96,768]{1,0:T(8,128)(2,1)S(1)}, bf16[96,768]{1,0:T(8,128)(2,1)S(1)}, u32[]{:S(2)}, u32[]{:S(2)}) %collective-permute-start.20) | collective-permute-done | bytes 147488 | tf_op jit(solution)/shard_map/ppermute | solution.py:52
  70.1 5.1 %next_sums.1.refs_1_ = bf16[96,256]{1,0:T(8,128)(2,1)S(1)} custom-call(s32[8,12,512]{2,1,0:T(8,128)S(1)} %get-tuple-element.36.codes_ref, bf16[96,768]{1,0:T(8,128)(2,1)S(1)} %add_convert_fusion.2.refs_0_, bf16[96,768]{1,0:T(8,128)(2,1)S(1)} %collective-permute-done.17.refs_1_, bf16[96,768]{1,0:T(8,128)(2,1)S(1)} %collective-permute-done.18.refs_2_, ...), custom_call_target="tpu_custom_call" | custom-call | tf_op jit(solution)/shard_map/next_sums/pallas_call | solution.py:577
  75.3 4.4 %collective-permute-start.26 = (bf16[96,256]{1,0:T(8,128)(2,1)S(1)}, bf16[96,256]{1,0:T(8,128)(2,1)S(1)}, u32[]{:S(2)}, u32[]{:S(2)}) collective-permute-start(bf16[96,256]{1,0:T(8,128)(2,1)S(1)} %next_sums.1.refs_1_), channel_id=1, source_target_pairs={{0,24},{8,16},{16,8},{24,0},{1,25},{9,17},{17,9},{25,1},{2,26},{10... | collective-permute-start | bytes 147464 | tf_op jit(solution)/shard_map/ppermute | solution.py:52
  80.3 1.9 %collective-permute-done.26.refs_4_ = bf16[96,256]{1,0:T(8,128)(2,1)S(1)} collective-permute-done((bf16[96,256]{1,0:T(8,128)(2,1)S(1)}, bf16[96,256]{1,0:T(8,128)(2,1)S(1)}, u32[]{:S(2)}, u32[]{:S(2)}) %collective-permute-start.26) | collective-permute-done | bytes 49184 | tf_op jit(solution)/shard_map/ppermute | solution.py:52
  82.1 2.5 %collective-permute-done.25.refs_3_ = bf16[96,256]{1,0:T(8,128)(2,1)S(1)} collective-permute-done((bf16[96,256]{1,0:T(8,128)(2,1)S(1)}, bf16[96,256]{1,0:T(8,128)(2,1)S(1)}, u32[]{:S(2)}, u32[]{:S(2)}) %collective-permute-start.25) | collective-permute-done | bytes 49184 | tf_op jit(solution)/shard_map/ppermute | solution.py:52
  84.7 2.2 %cross.1 = (bf16[96,768]{1,0:T(8,128)(2,1)S(1)}, f32[96,256]{1,0:T(8,128)S(1)}) custom-call(s32[8,12,512]{2,1,0:T(8,128)S(1)} %get-tuple-element.36.codes_ref, bf16[4,768,1024]{2,1,0:T(8,128)(2,1)S(1)} %get-tuple-element.37.refs_0_, bf16[96,256]{1,0:T(8,128)(2,1)S(1)} %next_sums.1.refs_1_, bf16[96,256]{1,0:T(8,128)(2,1)S(1)} %collective-permute-done.24.refs_2_, ...), custom_call_target="tpu_custom_call" | custom-call | tf_op jit(solution)/shard_map/cross/pallas_call | solution.py:461
  89.2 3.0 %collective-permute-done.27 = bf16[96,768]{1,0:T(8,128)(2,1)S(1)} collective-permute-done((bf16[96,768]{1,0:T(8,128)(2,1)S(1)}, bf16[96,768]{1,0:T(8,128)(2,1)S(1)}, u32[]{:S(2)}, u32[]{:S(2)}) %collective-permute-start.27) | collective-permute-done | bytes 147488 | tf_op jit(solution)/shard_map/ppermute | solution.py:52
  92.2 2.0 %collective-permute-start.28 = (bf16[96,768]{1,0:T(8,128)(2,1)S(1)}, bf16[96,768]{1,0:T(8,128)(2,1)S(1)}, u32[]{:S(2)}, u32[]{:S(2)}) collective-permute-start(bf16[96,768]{1,0:T(8,128)(2,1)S(1)} %add_convert_fusion.1), channel_id=1, source_target_pairs={{0,16},{8,24},{16,0},{24,8},{1,17},{9,25},{17,1},{25,9},{2,18},{10... | collective-permute-start | bytes 442376 | tf_op jit(solution)/shard_map/ppermute | solution.py:52
  94.2 5.7 %collective-permute-done.28 = bf16[96,768]{1,0:T(8,128)(2,1)S(1)} collective-permute-done((bf16[96,768]{1,0:T(8,128)(2,1)S(1)}, bf16[96,768]{1,0:T(8,128)(2,1)S(1)}, u32[]{:S(2)}, u32[]{:S(2)}) %collective-permute-start.28) | collective-permute-done | bytes 147488 | tf_op jit(solution)/shard_map/ppermute | solution.py:52
  100.0 1.8 %collective-permute-start.34 = (bf16[96,768]{1,0:T(8,128)(2,1)S(1)}, bf16[96,768]{1,0:T(8,128)(2,1)S(1)}, u32[]{:S(2)}, u32[]{:S(2)}) collective-permute-start(bf16[96,768]{1,0:T(8,128)(2,1)S(1)} %add_convert_fusion.refs_0_), channel_id=1, source_target_pairs={{0,6},{1,7},{2,4},{3,5},{4,2},{5,3},{6,0},{7,1},{8,14},{9,15},{10,... | collective-permute-start | bytes 442376 | tf_op jit(solution)/shard_map/ppermute | solution.py:52
  103.5 2.6 %collective-permute-done.34.refs_6_ = bf16[96,768]{1,0:T(8,128)(2,1)S(1)} collective-permute-done((bf16[96,768]{1,0:T(8,128)(2,1)S(1)}, bf16[96,768]{1,0:T(8,128)(2,1)S(1)}, u32[]{:S(2)}, u32[]{:S(2)}) %collective-permute-start.34) | collective-permute-done | bytes 147488 | tf_op jit(solution)/shard_map/ppermute | solution.py:52
  109.5 5.0 %final.1 = bf16[512,768]{1,0:T(8,128)(2,1)} custom-call(s32[1]{0:T(128)} %bitcast.place_ref, bf16[512,768]{1,0:T(8,128)(2,1)S(1)} %residual.1.residual_ref.refs_3_.refs_0_.refs_6_, bf16[96,768]{1,0:T(8,128)(2,1)S(1)} %add_convert_fusion.refs_0_, bf16[96,768]{1,0:T(8,128)(2,1)S(1)} %collective-permute-done.29.refs_1_, ...), custom_call_target="tpu_custom_call" | custom-call | tf_op jit(solution)/shard_map/final/pallas_call | solution.py:611
  (73 shorter events, 21.5 us)
Async XLA Ops:
  2.7 4.6 %collective-permute-start = (bf16[512,768]{1,0:T(8,128)(2,1)S(1)}, bf16[512,768]{1,0:T(8,128)(2,1)S(1)}, u32[]{:S(2)}, u32[]{:S(2)}) collective-permute-start(bf16[512,768]{1,0:T(8,128)(2,1)S(1)} %residual.1.residual_ref.refs_3_.refs_0_.refs_6_), channel_id=1, source_target_pairs={{0,1},{1,0},{2,3},{3,2},{4,5},{5,4},{6,7},{7,6},{8,9},{9,8},{10,11... | collective-permute-start | bytes 2359304 | tf_op jit(solution)/shard_map/ppermute | solution.py:52
  3.2 21.0 %collective-permute-start.9 = (bf16[512,768]{1,0:T(8,128)(2,1)S(1)}, bf16[512,768]{1,0:T(8,128)(2,1)S(1)}, u32[]{:S(2)}, u32[]{:S(2)}) collective-permute-start(bf16[512,768]{1,0:T(8,128)(2,1)S(1)} %residual.1.residual_ref.refs_3_.refs_0_.refs_6_), channel_id=1, source_target_pairs={{0,4},{1,5},{2,6},{3,7},{4,0},{5,1},{6,2},{7,3},{8,12},{9,13},{10,... | collective-permute-start | bytes 2359304 | tf_op jit(solution)/shard_map/ppermute | solution.py:52
  5.8 20.4 %collective-permute-start.7 = (bf16[512,768]{1,0:T(8,128)(2,1)S(1)}, bf16[512,768]{1,0:T(8,128)(2,1)S(1)}, u32[]{:S(2)}, u32[]{:S(2)}) collective-permute-start(bf16[512,768]{1,0:T(8,128)(2,1)S(1)} %residual.1.residual_ref.refs_3_.refs_0_.refs_6_), channel_id=1, source_target_pairs={{0,2},{1,3},{2,0},{3,1},{4,6},{5,7},{6,4},{7,5},{8,10},{9,11},{10,... | collective-permute-start | bytes 2359304 | tf_op jit(solution)/shard_map/ppermute | solution.py:52
  12.4 1.7 %collective-permute-start.1 = (bf16[4,160,256]{2,1,0:T(8,128)(2,1)S(1)}, bf16[4,160,256]{2,1,0:T(8,128)(2,1)S(1)}, u32[]{:S(2)}, u32[]{:S(2)}) collective-permute-start(bf16[4,160,256]{2,1,0:T(8,128)(2,1)S(1)} %get-tuple-element.29), channel_id=1, source_target_pairs={{0,1},{1,0},{2,3},{3,2},{4,5},{5,4},{6,7},{7,6},{8,9},{9,8},{10,11... | collective-permute-start | bytes 983048 | tf_op jit(solution)/shard_map/ppermute | solution.py:52
  14.2 14.1 %collective-permute-start.2 = (bf16[192,256]{1,0:T(8,128)(2,1)S(1)}, bf16[192,256]{1,0:T(8,128)(2,1)S(1)}, u32[]{:S(2)}, u32[]{:S(2)}) collective-permute-start(bf16[192,256]{1,0:T(8,128)(2,1)S(1)} %get-tuple-element.31), channel_id=1, source_target_pairs={{0,2},{1,3},{2,0},{3,1},{4,6},{5,7},{6,4},{7,5},{8,10},{9,11},{10,... | collective-permute-start | bytes 294920 | tf_op jit(solution)/shard_map/ppermute | solution.py:52
  15.0 13.3 %collective-permute-start.3 = (bf16[192,256]{1,0:T(8,128)(2,1)S(1)}, bf16[192,256]{1,0:T(8,128)(2,1)S(1)}, u32[]{:S(2)}, u32[]{:S(2)}) collective-permute-start(bf16[192,256]{1,0:T(8,128)(2,1)S(1)} %get-tuple-element.32), channel_id=1, source_target_pairs={{0,4},{1,5},{2,6},{3,7},{4,0},{5,1},{6,2},{7,3},{8,12},{9,13},{10,... | collective-permute-start | bytes 294920 | tf_op jit(solution)/shard_map/ppermute | solution.py:52
  16.5 13.4 %collective-permute-start.4 = (bf16[192,256]{1,0:T(8,128)(2,1)S(1)}, bf16[192,256]{1,0:T(8,128)(2,1)S(1)}, u32[]{:S(2)}, u32[]{:S(2)}) collective-permute-start(bf16[192,256]{1,0:T(8,128)(2,1)S(1)} %get-tuple-element.33), channel_id=1, source_target_pairs={{0,6},{1,7},{2,4},{3,5},{4,2},{5,3},{6,0},{7,1},{8,14},{9,15},{10,... | collective-permute-start | bytes 294920 | tf_op jit(solution)/shard_map/ppermute | solution.py:52
  24.2 16.3 %collective-permute-start.12 = (bf16[256,768]{1,0:T(8,128)(2,1)S(1)}, bf16[256,768]{1,0:T(8,128)(2,1)S(1)}, u32[]{:S(2)}, u32[]{:S(2)}) collective-permute-start(bf16[256,768]{1,0:T(8,128)(2,1)S(1)} %slice.9), channel_id=1, source_target_pairs={{0,2},{1,3},{2,0},{3,1},{4,6},{5,7},{6,4},{7,5},{8,10},{9,11},{10,... | collective-permute-start | bytes 1179656 | tf_op jit(solution)/shard_map/ppermute | solution.py:52
  26.2 14.3 %collective-permute-start.11 = (bf16[256,768]{1,0:T(8,128)(2,1)S(1)}, bf16[256,768]{1,0:T(8,128)(2,1)S(1)}, u32[]{:S(2)}, u32[]{:S(2)}) collective-permute-start(bf16[256,768]{1,0:T(8,128)(2,1)S(1)} %slice.8), channel_id=1, source_target_pairs={{0,4},{1,5},{2,6},{3,7},{4,0},{5,1},{6,2},{7,3},{8,12},{9,13},{10,... | collective-permute-start | bytes 1179656 | tf_op jit(solution)/shard_map/ppermute | solution.py:52
  30.0 11.1 %collective-permute-start.8 = (bf16[512,768]{1,0:T(8,128)(2,1)S(1)}, bf16[512,768]{1,0:T(8,128)(2,1)S(1)}, u32[]{:S(2)}, u32[]{:S(2)}) collective-permute-start(bf16[512,768]{1,0:T(8,128)(2,1)S(1)} %collective-permute-done.7.refs_5_.refs_2_.refs_8_), channel_id=1, source_target_pairs={{0,1},{1,0},{2,3},{3,2},{4,5},{5,4},{6,7},{7,6},{8,9},{9,8},{10,11... | collective-permute-start | bytes 2359304 | tf_op jit(solution)/shard_map/ppermute | solution.py:52
  30.0 11.0 %collective-permute-start.10 = (bf16[512,768]{1,0:T(8,128)(2,1)S(1)}, bf16[512,768]{1,0:T(8,128)(2,1)S(1)}, u32[]{:S(2)}, u32[]{:S(2)}) collective-permute-start(bf16[512,768]{1,0:T(8,128)(2,1)S(1)} %collective-permute-done.9.refs_7_.refs_4_.refs_10_), channel_id=1, source_target_pairs={{0,1},{1,0},{2,3},{3,2},{4,5},{5,4},{6,7},{7,6},{8,9},{9,8},{10,11... | collective-permute-start | bytes 2359304 | tf_op jit(solution)/shard_map/ppermute | solution.py:52
  30.5 4.4 %collective-permute-start.5 = (bf16[128,256]{1,0:T(8,128)(2,1)S(1)}, bf16[128,256]{1,0:T(8,128)(2,1)S(1)}, u32[]{:S(2)}, u32[]{:S(2)}) collective-permute-start(bf16[128,256]{1,0:T(8,128)(2,1)S(1)} %get-tuple-element.35.first_ref), channel_id=1, source_target_pairs={{0,8},{8,0},{16,24},{24,16},{1,9},{9,1},{17,25},{25,17},{2,10},{10... | collective-permute-start | bytes 196616 | tf_op jit(solution)/shard_map/ppermute | solution.py:52
  34.9 5.6 %collective-permute-start.6 = (bf16[128,256]{1,0:T(8,128)(2,1)S(1)}, bf16[128,256]{1,0:T(8,128)(2,1)S(1)}, u32[]{:S(2)}, u32[]{:S(2)}) collective-permute-start(bf16[128,256]{1,0:T(8,128)(2,1)S(1)} %merge_groups.1.refs_1_), channel_id=1, source_target_pairs={{0,16},{8,24},{16,0},{24,8},{1,17},{9,25},{17,1},{25,9},{2,18},{10... | collective-permute-start | bytes 196616 | tf_op jit(solution)/shard_map/ppermute | solution.py:52
  40.5 2.3 %collective-permute-start.13 = (bf16[256,768]{1,0:T(8,128)(2,1)S(1)}, bf16[256,768]{1,0:T(8,128)(2,1)S(1)}, u32[]{:S(2)}, u32[]{:S(2)}) collective-permute-start(bf16[256,768]{1,0:T(8,128)(2,1)S(1)} %collective-permute-done.11.refs_1_.refs_6_.refs_12_), channel_id=1, source_target_pairs={{0,1},{1,0},{2,3},{3,2},{4,5},{5,4},{6,7},{7,6},{8,9},{9,8},{10,11... | collective-permute-start | bytes 1179656 | tf_op jit(solution)/shard_map/ppermute | solution.py:52
  40.5 2.3 %collective-permute-start.14 = (bf16[256,768]{1,0:T(8,128)(2,1)S(1)}, bf16[256,768]{1,0:T(8,128)(2,1)S(1)}, u32[]{:S(2)}, u32[]{:S(2)}) collective-permute-start(bf16[256,768]{1,0:T(8,128)(2,1)S(1)} %collective-permute-done.12.refs_2_.refs_7_.refs_13_), channel_id=1, source_target_pairs={{0,1},{1,0},{2,3},{3,2},{4,5},{5,4},{6,7},{7,6},{8,9},{9,8},{10,11... | collective-permute-start | bytes 1179656 | tf_op jit(solution)/shard_map/ppermute | solution.py:52
  43.5 6.0 %collective-permute-start.15 = (bf16[96,768]{1,0:T(8,128)(2,1)S(1)}, bf16[96,768]{1,0:T(8,128)(2,1)S(1)}, u32[]{:S(2)}, u32[]{:S(2)}) collective-permute-start(bf16[96,768]{1,0:T(8,128)(2,1)S(1)} %cross_far.1), channel_id=1, source_target_pairs={{0,8},{8,0},{16,24},{24,16},{1,9},{9,1},{17,25},{25,17},{2,10},{10... | collective-permute-start | bytes 442376 | tf_op jit(solution)/shard_map/ppermute | solution.py:52
  49.6 9.9 %collective-permute-start.16 = (bf16[96,768]{1,0:T(8,128)(2,1)S(1)}, bf16[96,768]{1,0:T(8,128)(2,1)S(1)}, u32[]{:S(2)}, u32[]{:S(2)}) collective-permute-start(bf16[96,768]{1,0:T(8,128)(2,1)S(1)} %add_convert_fusion.3), channel_id=1, source_target_pairs={{0,16},{8,24},{16,0},{24,8},{1,17},{9,25},{17,1},{25,9},{2,18},{10... | collective-permute-start | bytes 442376 | tf_op jit(solution)/shard_map/ppermute | solution.py:52
  59.5 7.1 %collective-permute-start.22 = (bf16[96,768]{1,0:T(8,128)(2,1)S(1)}, bf16[96,768]{1,0:T(8,128)(2,1)S(1)}, u32[]{:S(2)}, u32[]{:S(2)}) collective-permute-start(bf16[96,768]{1,0:T(8,128)(2,1)S(1)} %add_convert_fusion.2.refs_0_), channel_id=1, source_target_pairs={{0,6},{1,7},{2,4},{3,5},{4,2},{5,3},{6,0},{7,1},{8,14},{9,15},{10,... | collective-permute-start | bytes 442376 | tf_op jit(solution)/shard_map/ppermute | solution.py:52
  62.0 6.5 %collective-permute-start.20 = (bf16[96,768]{1,0:T(8,128)(2,1)S(1)}, bf16[96,768]{1,0:T(8,128)(2,1)S(1)}, u32[]{:S(2)}, u32[]{:S(2)}) collective-permute-start(bf16[96,768]{1,0:T(8,128)(2,1)S(1)} %add_convert_fusion.2.refs_0_), channel_id=1, source_target_pairs={{0,4},{1,5},{2,6},{3,7},{4,0},{5,1},{6,2},{7,3},{8,12},{9,13},{10,... | collective-permute-start | bytes 442376 | tf_op jit(solution)/shard_map/ppermute | solution.py:52
  62.5 6.1 %collective-permute-start.18 = (bf16[96,768]{1,0:T(8,128)(2,1)S(1)}, bf16[96,768]{1,0:T(8,128)(2,1)S(1)}, u32[]{:S(2)}, u32[]{:S(2)}) collective-permute-start(bf16[96,768]{1,0:T(8,128)(2,1)S(1)} %add_convert_fusion.2.refs_0_), channel_id=1, source_target_pairs={{0,2},{1,3},{2,0},{3,1},{4,6},{5,7},{6,4},{7,5},{8,10},{9,11},{10,... | collective-permute-start | bytes 442376 | tf_op jit(solution)/shard_map/ppermute | solution.py:52
  63.0 6.0 %collective-permute-start.17 = (bf16[96,768]{1,0:T(8,128)(2,1)S(1)}, bf16[96,768]{1,0:T(8,128)(2,1)S(1)}, u32[]{:S(2)}, u32[]{:S(2)}) collective-permute-start(bf16[96,768]{1,0:T(8,128)(2,1)S(1)} %add_convert_fusion.2.refs_0_), channel_id=1, source_target_pairs={{0,1},{1,0},{2,3},{3,2},{4,5},{5,4},{6,7},{7,6},{8,9},{9,8},{10,11... | collective-permute-start | bytes 442376 | tf_op jit(solution)/shard_map/ppermute | solution.py:52
  66.6 2.4 %collective-permute-start.23 = (bf16[96,768]{1,0:T(8,128)(2,1)S(1)}, bf16[96,768]{1,0:T(8,128)(2,1)S(1)}, u32[]{:S(2)}, u32[]{:S(2)}) collective-permute-start(bf16[96,768]{1,0:T(8,128)(2,1)S(1)} %collective-permute-done.22.refs_6_), channel_id=1, source_target_pairs={{0,1},{1,0},{2,3},{3,2},{4,5},{5,4},{6,7},{7,6},{8,9},{9,8},{10,11... | collective-permute-start | bytes 442376 | tf_op jit(solution)/shard_map/ppermute | solution.py:52
  75.3 6.9 %collective-permute-start.26 = (bf16[96,256]{1,0:T(8,128)(2,1)S(1)}, bf16[96,256]{1,0:T(8,128)(2,1)S(1)}, u32[]{:S(2)}, u32[]{:S(2)}) collective-permute-start(bf16[96,256]{1,0:T(8,128)(2,1)S(1)} %next_sums.1.refs_1_), channel_id=1, source_target_pairs={{0,24},{8,16},{16,8},{24,0},{1,25},{9,17},{17,9},{25,1},{2,26},{10... | collective-permute-start | bytes 147464 | tf_op jit(solution)/shard_map/ppermute | solution.py:52
  79.6 5.0 %collective-permute-start.25 = (bf16[96,256]{1,0:T(8,128)(2,1)S(1)}, bf16[96,256]{1,0:T(8,128)(2,1)S(1)}, u32[]{:S(2)}, u32[]{:S(2)}) collective-permute-start(bf16[96,256]{1,0:T(8,128)(2,1)S(1)} %next_sums.1.refs_1_), channel_id=1, source_target_pairs={{0,16},{8,24},{16,0},{24,8},{1,17},{9,25},{17,1},{25,9},{2,18},{10... | collective-permute-start | bytes 147464 | tf_op jit(solution)/shard_map/ppermute | solution.py:52
  79.6 5.1 %collective-permute-start.24 = (bf16[96,256]{1,0:T(8,128)(2,1)S(1)}, bf16[96,256]{1,0:T(8,128)(2,1)S(1)}, u32[]{:S(2)}, u32[]{:S(2)}) collective-permute-start(bf16[96,256]{1,0:T(8,128)(2,1)S(1)} %next_sums.1.refs_1_), channel_id=1, source_target_pairs={{0,8},{8,0},{16,24},{24,16},{1,9},{9,1},{17,25},{25,17},{2,10},{10... | collective-permute-start | bytes 147464 | tf_op jit(solution)/shard_map/ppermute | solution.py:52
  87.0 5.2 %collective-permute-start.27 = (bf16[96,768]{1,0:T(8,128)(2,1)S(1)}, bf16[96,768]{1,0:T(8,128)(2,1)S(1)}, u32[]{:S(2)}, u32[]{:S(2)}) collective-permute-start(bf16[96,768]{1,0:T(8,128)(2,1)S(1)} %get-tuple-element.49), channel_id=1, source_target_pairs={{0,8},{8,0},{16,24},{24,16},{1,9},{9,1},{17,25},{25,17},{2,10},{10... | collective-permute-start | bytes 442376 | tf_op jit(solution)/shard_map/ppermute | solution.py:52
  92.2 7.7 %collective-permute-start.28 = (bf16[96,768]{1,0:T(8,128)(2,1)S(1)}, bf16[96,768]{1,0:T(8,128)(2,1)S(1)}, u32[]{:S(2)}, u32[]{:S(2)}) collective-permute-start(bf16[96,768]{1,0:T(8,128)(2,1)S(1)} %add_convert_fusion.1), channel_id=1, source_target_pairs={{0,16},{8,24},{16,0},{24,8},{1,17},{9,25},{17,1},{25,9},{2,18},{10... | collective-permute-start | bytes 442376 | tf_op jit(solution)/shard_map/ppermute | solution.py:52
  100.0 6.2 %collective-permute-start.34 = (bf16[96,768]{1,0:T(8,128)(2,1)S(1)}, bf16[96,768]{1,0:T(8,128)(2,1)S(1)}, u32[]{:S(2)}, u32[]{:S(2)}) collective-permute-start(bf16[96,768]{1,0:T(8,128)(2,1)S(1)} %add_convert_fusion.refs_0_), channel_id=1, source_target_pairs={{0,6},{1,7},{2,4},{3,5},{4,2},{5,3},{6,0},{7,1},{8,14},{9,15},{10,... | collective-permute-start | bytes 442376 | tf_op jit(solution)/shard_map/ppermute | solution.py:52
  101.8 5.9 %collective-permute-start.32 = (bf16[96,768]{1,0:T(8,128)(2,1)S(1)}, bf16[96,768]{1,0:T(8,128)(2,1)S(1)}, u32[]{:S(2)}, u32[]{:S(2)}) collective-permute-start(bf16[96,768]{1,0:T(8,128)(2,1)S(1)} %add_convert_fusion.refs_0_), channel_id=1, source_target_pairs={{0,4},{1,5},{2,6},{3,7},{4,0},{5,1},{6,2},{7,3},{8,12},{9,13},{10,... | collective-permute-start | bytes 442376 | tf_op jit(solution)/shard_map/ppermute | solution.py:52
  103.0 5.1 %collective-permute-start.30 = (bf16[96,768]{1,0:T(8,128)(2,1)S(1)}, bf16[96,768]{1,0:T(8,128)(2,1)S(1)}, u32[]{:S(2)}, u32[]{:S(2)}) collective-permute-start(bf16[96,768]{1,0:T(8,128)(2,1)S(1)} %add_convert_fusion.refs_0_), channel_id=1, source_target_pairs={{0,2},{1,3},{2,0},{3,1},{4,6},{5,7},{6,4},{7,5},{8,10},{9,11},{10,... | collective-permute-start | bytes 442376 | tf_op jit(solution)/shard_map/ppermute | solution.py:52
  103.5 4.7 %collective-permute-start.29 = (bf16[96,768]{1,0:T(8,128)(2,1)S(1)}, bf16[96,768]{1,0:T(8,128)(2,1)S(1)}, u32[]{:S(2)}, u32[]{:S(2)}) collective-permute-start(bf16[96,768]{1,0:T(8,128)(2,1)S(1)} %add_convert_fusion.refs_0_), channel_id=1, source_target_pairs={{0,1},{1,0},{2,3},{3,2},{4,5},{5,4},{6,7},{7,6},{8,9},{9,8},{10,11... | collective-permute-start | bytes 442376 | tf_op jit(solution)/shard_map/ppermute | solution.py:52
  106.1 2.0 %collective-permute-start.35 = (bf16[96,768]{1,0:T(8,128)(2,1)S(1)}, bf16[96,768]{1,0:T(8,128)(2,1)S(1)}, u32[]{:S(2)}, u32[]{:S(2)}) collective-permute-start(bf16[96,768]{1,0:T(8,128)(2,1)S(1)} %collective-permute-done.34.refs_6_), channel_id=1, source_target_pairs={{0,1},{1,0},{2,3},{3,2},{4,5},{5,4},{6,7},{7,6},{8,9},{9,8},{10,11... | collective-permute-start | bytes 442376 | tf_op jit(solution)/shard_map/ppermute | solution.py:52
  (9 other events, 15.6 us)
